TPU v7x, 32 devices: a whole 2x2x4 slice. The times are simulated.
32 devices in a mesh: energy: 2 (over y), trans: 8 (over z, x), cross: 2 (over core).
Axes of the slice: x: 2, y: 2, z: 4, core: 2. Of those that a mesh axis runs over, the one named last changes fastest.
Arguments:
- sources: float32 [64, 8, 64, 128], P(('energy', 'trans'), 'cross'), parts along dimension 0, may hold values from -6 to 6
- couplings: float32 [64, 8, 7, 64, 64], P(('energy', 'trans'), 'cross'), parts along dimension 0
- block_cols: int32 [32, 8, 7], P('trans', 'cross'), may hold values from 0 to 23, as said below
- lead_sites: int32 [4], replicated, may hold values from 0 to 7, as said below
- lead_sigma: float32 [8, 64, 64], P('energy'), parts along dimension 0
Outputs:
- basis: bfloat16 [64, 8, 64, 512], P(('energy', 'trans'), 'cross'), parts along dimension 0
- r_factor: float32 [1024, 512], P('energy'), parts along dimension 0
There are 2 independent parts, one for each index of `energy`. A program takes and returns all parts, laid end to end along the dimension named above; an argument that names none is the same for every part. Nothing has to cross between parts.
Inputs may be any that keep to these rules, and one draw needn't show every extreme that they name: `block_cols`: slot 0 of every block row names the row's own block, 8 plus its cross position; an entry c names the block at cross position c % 8 in the layer c // 8 - 1 steps away, which is absent beyond the wire's ends. `lead_sites`: the first 2 entries are the contacts at layer 0, the last 2 those at layer 31; the positions of one end are distinct.
All inputs are finite; a program needn't handle non-finite values.
Results may differ from a plain program's by a relative error of at most 0.001.
Values sent between devices are 32-bit elements; how exact they have to be, the bound alone decides.
No kernel may reach another device: no remote copies, remote signals or barrier semaphores. Data moves between devices by JAX's collectives and lax.ppermute only.
A program may use at most 64 MiB of HBM per device.

v0:
```python
import functools
import math

import jax
import jax.numpy as jnp
from jax import lax
from jax.experimental import pallas as pl
from jax.experimental.pallas import tpu as pltpu
from jax.sharding import PartitionSpec as P

S = 3
center_shift = 2.0
half_range = 1.6
HIGH = lax.Precision.HIGH
HIGHEST = lax.Precision.HIGHEST
VMEM_LIMIT = 48 * 1024 * 1024


def split(x):
    high = x.astype(jnp.bfloat16)
    low = (x - high.astype(jnp.float32)).astype(jnp.bfloat16)
    return high, low


def pack_kernel(count, cross_local, layers, slots, info, sites, couplings, sigma, out):
    layer = pl.program_id(0)
    first = jnp.logical_and(layer == 0, info[1] == 1)
    last = jnp.logical_and(layer == layers - 1, info[2] == 1)
    for q in range(cross_local):
        place = info[0] * cross_local + q
        lead = None
        for k in range(2 * count):
            flag = first if k < count else last
            weight = jnp.where(jnp.logical_and(flag, sites[k] == place), -1.0, 0.0)
            term = sigma[k] * weight
            lead = term if lead is None else lead + term
        blocks = [couplings[0, q, j] for j in range(slots)] + [lead]
        row = jnp.concatenate(
            [jnp.concatenate(blocks[i : i + 2], axis=1) for i in range(0, slots + 1, 2)], axis=1
        )
        high, low = split(row)
        half = high.shape[0]
        out[q, :half] = high
        out[q, half:] = low


def pack(couplings, lead_sites, lead_sigma, info):
    layers, cross_local, slots, size, _ = couplings.shape
    contacts = lead_sigma.shape[0]
    body = functools.partial(pack_kernel, contacts // 2, cross_local, layers, slots)
    return pl.pallas_call(
        body,
        grid_spec=pltpu.PrefetchScalarGridSpec(
            num_scalar_prefetch=2,
            grid=(layers,),
            in_specs=[
                pl.BlockSpec((1, cross_local, slots, size, size), lambda i, *_: (i, 0, 0, 0, 0)),
                pl.BlockSpec((contacts, size, size), lambda i, *_: (0, 0, 0)),
            ],
            out_specs=pl.BlockSpec(
                (cross_local, 2 * size, (slots + 1) * size), lambda i, *_: (i, 0, 0)
            ),
        ),
        out_shape=jax.ShapeDtypeStruct(
            (layers * cross_local, 2 * size, (slots + 1) * size), jnp.bfloat16
        ),
        compiler_params=pltpu.CompilerParams(vmem_limit_bytes=VMEM_LIMIT),
        name="pack",
    )(info, lead_sites, couplings, lead_sigma)


def step_kernel(
    first, slots, info, index, packed, own, other, edge_own, edge_other, before, out, field
):
    layers, cross_local, size, columns = own.shape
    total = 2 * cross_local
    mine = info[0] * cross_local
    theirs = (1 - info[0]) * cross_local

    def put(place, x):
        high, low = split(x)
        field[place, :, :columns] = high
        field[place, :, columns:] = low

    for layer in range(layers):
        for q in range(cross_local):
            put((layer + 1) * total + mine + q, own[layer, q])
            put((layer + 1) * total + theirs + q, other[layer, q])
    for q in range(cross_local):
        put(mine + q, edge_own[0, q])
        put(theirs + q, edge_other[0, q])
        put((layers + 1) * total + mine + q, edge_own[1, q])
        put((layers + 1) * total + theirs + q, edge_other[1, q])
    for layer in range(layers):
        for q in range(cross_local):
            row = layer * cross_local + q
            picked = jnp.concatenate(
                [field[index[row * slots + j]] for j in range(slots)], axis=0
            )
            acc = jnp.dot(packed[row], picked, preferred_element_type=jnp.float32)
            acc = acc[:, :columns] + acc[:, columns:]
            applied = acc[:size] + acc[size:]
            value = (applied - center_shift * own[layer, q]) * (1.0 / half_range)
            if not first:
                value = 2.0 * value - before[layer, q]
            out[layer, q] = value


def step(packed, index, info, own, other, edge_own, edge_other, before, first):
    layers, cross_local, size, columns = own.shape
    rows, _, depth = packed.shape
    slots = depth // size
    whole = pl.BlockSpec(memory_space=pltpu.VMEM)
    scalar = pl.BlockSpec(memory_space=pltpu.SMEM)
    return pl.pallas_call(
        functools.partial(step_kernel, first, slots),
        in_specs=[scalar, scalar] + [whole] * 6,
        out_specs=whole,
        out_shape=jax.ShapeDtypeStruct(own.shape, jnp.float32),
        scratch_shapes=[
            pltpu.VMEM(((layers + 2) * 2 * cross_local, size, 2 * columns), jnp.bfloat16)
        ],
        cost_estimate=pl.CostEstimate(
            flops=8 * rows * size * depth * columns, bytes_accessed=6 << 20, transcendentals=0
        ),
        compiler_params=pltpu.CompilerParams(vmem_limit_bytes=VMEM_LIMIT),
        name="step",
    )(info, index, packed, own, other, edge_own, edge_other, before)


def factor(block):
    size = block.shape[0]
    tall = 8
    tiles = size // tall
    lanes = lax.broadcasted_iota(jnp.int32, (tall, size), 1)
    sub = lax.broadcasted_iota(jnp.int32, (tall, size), 0)
    gram = [block[tall * t : tall * (t + 1)] for t in range(tiles)]
    unit = [jnp.where(lanes == sub + tall * t, 1.0, 0.0) for t in range(tiles)]

    def spread(row):
        return jnp.broadcast_to(row, (tall, size))

    for p in range(tiles):
        cols = [
            [
                jnp.broadcast_to(gram[t][:, tall * p + c : tall * p + c + 1], (tall, size))
                for t in range(p, tiles)
            ]
            for c in range(tall)
        ]
        scales = []
        for c in range(tall):
            scale = lax.rsqrt(spread(cols[c][0][c : c + 1]))
            scales.append(scale)
            cols[c] = [x * scale for x in cols[c]]
            cols[c][0] = jnp.where(sub > c, cols[c][0], 0.0)
            for d in range(c + 1, tall):
                weight = spread(cols[c][0][d : d + 1])
                cols[d] = [x - m * weight for x, m in zip(cols[d], cols[c])]
        for c in range(tall):
            row_gram = spread(gram[p][c : c + 1]) * scales[c]
            row_unit = spread(unit[p][c : c + 1]) * scales[c]
            gram[p] = jnp.where(sub == c, row_gram, gram[p] - cols[c][0] * row_gram)
            unit[p] = jnp.where(sub == c, row_unit, unit[p] - cols[c][0] * row_unit)
            for t in range(p + 1, tiles):
                m = cols[c][t - p]
                gram[t] = gram[t] - m * row_gram
                unit[t] = unit[t] - m * row_unit
    upper = [jnp.where(lanes >= sub + tall * t, gram[t], 0.0) for t in range(tiles)]
    return jnp.concatenate(upper, axis=0), jnp.concatenate(unit, axis=0)


def dot(a, b, dims=((1,), (0,))):
    return lax.dot_general(
        a, b, (dims, ((), ())), precision=HIGHEST, preferred_element_type=jnp.float32
    )


def column_kernel(place, *refs):
    if place:
        gram, inverse, upper_out, inverse_out = refs
    else:
        gram, upper_out, inverse_out = refs
    size = gram.shape[1]
    split_at = place * size
    corner = gram[split_at:, :]
    if place:
        known = inverse[...]
        above = dot(known, gram[:split_at, :], ((0,), (0,)))
        corner = corner - dot(above, above, ((0,), (0,)))
        carried = dot(known, above)
    upper, lower_inverse = factor(corner)
    upper_inverse = lower_inverse.T
    if place:
        upper_out[:split_at, :] = above
        inverse_out[:split_at, :] = -dot(carried, upper_inverse)
    upper_out[split_at:, :] = upper
    inverse_out[split_at:, :] = upper_inverse


def column(place, gram, inverse):
    whole = pl.BlockSpec(memory_space=pltpu.VMEM)
    args = (gram, inverse) if place else (gram,)
    shape = jax.ShapeDtypeStruct(gram.shape, jnp.float32)
    return pl.pallas_call(
        functools.partial(column_kernel, place),
        in_specs=[whole] * len(args),
        out_specs=[whole, whole],
        out_shape=[shape, shape],
        compiler_params=pltpu.CompilerParams(vmem_limit_bytes=VMEM_LIMIT),
        cost_estimate=pl.CostEstimate(flops=1 << 23, bytes_accessed=1 << 19, transcendentals=128),
        name="column",
    )(*args)


def total(x, axes):
    count = math.prod(lax.axis_size(a) for a in axes)
    shares = x.reshape(count, -1) if x.size // count % 1024 else x.reshape(count, -1, x.shape[-1])
    parts = lax.all_to_all(shares, axes, 0, 0, tiled=True)
    mine = jnp.sum(parts, axis=0, keepdims=True)
    copies = jnp.broadcast_to(mine, shares.shape)
    return lax.all_to_all(copies, axes, 0, 0, tiled=True).reshape(x.shape)


def local(sources, couplings, block_cols, lead_sites, lead_sigma):
    layers, cross_local, size, columns = sources.shape
    cross_count = lax.axis_size("cross")
    trans_count = lax.axis_size("trans")
    cross_total = cross_local * cross_count
    trans_place = lax.axis_index("trans")
    cross_place = lax.axis_index("cross")
    info = jnp.stack(
        [
            cross_place,
            (trans_place == 0).astype(jnp.int32),
            (trans_place == trans_count - 1).astype(jnp.int32),
        ]
    ).astype(jnp.int32)
    layer_base = jnp.arange(layers, dtype=jnp.int32)[:, None, None] * cross_total
    self_cols = (cross_total + cross_place * cross_local + jnp.arange(cross_local, dtype=jnp.int32))
    self_cols = jnp.broadcast_to(self_cols[None, :, None], (layers, cross_local, 1))
    index = (layer_base + jnp.concatenate([block_cols, self_cols], axis=2)).reshape(-1)
    packed = pack(couplings, lead_sites, lead_sigma, info)

    forward = [(i, i + 1) for i in range(trans_count - 1)]
    backward = [(i + 1, i) for i in range(trans_count - 1)]
    swap = [(0, 1), (1, 0)]

    powers = [sources]
    uppers = []
    inverses = []
    inverse = None
    for k in range(S + 1):
        field = powers[k]
        if k < S:
            low = lax.ppermute(field[layers - 1 :], "trans", forward)
            high = lax.ppermute(field[:1], "trans", backward)
            other = lax.ppermute(field, "cross", swap)
            edge_own = jnp.concatenate([low, high], axis=0)
            edge_other = lax.ppermute(edge_own, "cross", swap)
        krylov = jnp.concatenate([x.reshape(-1, columns) for x in powers], axis=1)
        part = lax.dot_general(
            krylov, field.reshape(-1, columns), (((0,), (0,)), ((), ())), precision=HIGH
        )
        gram = total(part, ("trans", "cross"))
        upper_col, inverse_col = column(k, gram, inverse)
        fill = ((0, (S - k) * columns), (0, 0))
        uppers.append(jnp.pad(upper_col, fill))
        inverses.append(jnp.pad(inverse_col, fill))
        if k < S:
            inverse = jnp.concatenate([x[: (k + 1) * columns] for x in inverses], axis=1)
            before = powers[k - 1] if k else field
            powers.append(
                step(packed, index, info, field, other, edge_own, edge_other, before, k == 0)
            )
    scale_rows = math.sqrt(trans_count * layers * cross_total * size)
    solver = jnp.concatenate(inverses, axis=1) * scale_rows
    basis = lax.dot_general(krylov, solver, (((1,), (0,)), ((), ())), precision=HIGH)
    basis = basis.astype(jnp.bfloat16).reshape(layers, cross_local, size, (S + 1) * columns)
    return basis, jnp.concatenate(uppers, axis=1) / scale_rows


def solution(mesh):
    return jax.shard_map(
        local,
        mesh=mesh,
        in_specs=(
            P(("energy", "trans"), "cross", None, None),
            P(("energy", "trans"), "cross", None, None, None),
            P("trans", "cross", None),
            P(),
            P("energy", None, None),
        ),
        out_specs=(P(("energy", "trans"), "cross", None, None), P("energy", None)),
        check_vma=False,
    )
```

profile of v0, /device:TPU:0, one launch (start us, length us, event | category | flops | bytes accessed | tf_op | source)
XLA Modules:
  0.0 167.0 jit_solution(506918581392338447)
XLA Ops:
  1.2 1.0 fusion.27
  2.2 4.4 %collective-permute-start.1 = (f32[1,4,64,128]{3,2,1,0:T(8,128)S(1)}, f32[1,4,64,128]{3,2,1,0:T(8,128)S(1)}, u32[]{:S(2)}, u32[]{:S(2)}) collective-permute-start(f32[1,4,64,128]{3,2,1,0:T(8,128)S(1)} %get-tuple-element.23), channel_id=1, source_target_pairs={{0,2},{2,4},{4,6},{6,8},{8,10},{10,12},{12,14},{1,3},{3,5},{5,7},{... | collective-permute-start | bytes 393224 | tf_op jit(solution)/shard_map/ppermute | solution.py:256
  6.6 1.3 collective-permute-start.2
  7.9 1.2 copy.19
  9.1 2.0 %fusion.17 = f32[16,8,128]{2,1,0:T(8,128)} fusion(f32[1024,128,1]{1,0,2:T(8,128)} %bitcast.42, f32[128,1024]{1,0:T(8,128)S(1)} %copy.19), kind=kOutput, calls=%fused_computation.28 | convolution fusion | flops 100663296 | bytes 1114112 | tf_op jit(solution)/shard_map/dot_general | solution.py:262
  11.2 7.1 %all-to-all-start = ((f32[16,8,128]{2,1,0:T(8,128)}), f32[16,8,128]{2,1,0:T(8,128)}, u32[]{:S(2)}, u32[]{:S(2)}) async-start(f32[16,8,128]{2,1,0:T(8,128)} %fusion.17), calls=%async_computation | async-start | bytes 131072 | tf_op jit(solution)/shard_map/all_to_all | solution.py:219
  19.1 2.0 %copy-done.3 = f32[4,4,7,64,64]{4,3,2,1,0:T(8,128)S(1)} copy-done((f32[4,4,7,64,64]{4,3,2,1,0:T(8,128)S(1)}, f32[4,4,7,64,64]{4,3,2,1,0:T(8,128)}, u32[]{:S(2)}) %copy-start.3) | copy-done | bytes 1835032
  21.2 1.4 pack.1.packed
  23.4 1.0 copy-done.5
  24.5 1.9 %step.3.own.before = f32[4,4,64,128]{3,2,1,0:T(8,128)S(1)} custom-call(s32[3]{0:T(128)S(1)} %pad_add_fusion.info, s32[128]{0:T(128)S(1)} %add.42.index, bf16[16,128,512]{2,1,0:T(8,128)(2,1)S(1)} %pack.1.packed, f32[4,4,64,128]{3,2,1,0:T(8,128)S(1)} %copy-done, f32[4,4,64,128]{3,2,1,0:T(8,128)S(1)} %copy-done.5, ...), custom_call_target="tpu_custom_call" | custom-call | flops 536870912 | bytes 6291456 | tf_op jit(solution)/shard_map/step/pallas_call | solution.py:115
  27.3 4.4 %collective-permute-start.5 = (f32[1,4,64,128]{3,2,1,0:T(8,128)S(1)}, f32[1,4,64,128]{3,2,1,0:T(8,128)}, u32[]{:S(2)}, u32[]{:S(2)}) collective-permute-start(f32[1,4,64,128]{3,2,1,0:T(8,128)S(1)} %get-tuple-element.21), channel_id=1, source_target_pairs={{0,2},{2,4},{4,6},{6,8},{8,10},{10,12},{12,14},{1,3},{3,5},{5,7},{... | collective-permute-start | bytes 393224 | tf_op jit(solution)/shard_map/ppermute | solution.py:256
  31.7 1.3 collective-permute-start.6
  33.0 1.0 maximum_bitcast_fusion.1
  34.1 2.5 %copy.20 = f32[256,1024]{1,0:T(8,128)} copy(f32[256,1024]{0,1:T(8,128)} %maximum_bitcast_fusion.1) | data formatting | bytes 2097152 | tf_op jit(solution)/shard_map/dot_general | solution.py:262
  36.6 0.9 constant_dynamic-update-slice_fusion.3
  37.5 1.7 %collective-permute-done.6 = f32[1,4,64,128]{3,2,1,0:T(8,128)} collective-permute-done((f32[1,4,64,128]{3,2,1,0:T(8,128)}, f32[1,4,64,128]{3,2,1,0:T(8,128)}, u32[]{:S(2)}, u32[]{:S(2)}) %collective-permute-start.6) | collective-permute-done | bytes 131104 | tf_op jit(solution)/shard_map/ppermute | solution.py:257
  39.2 0.9 constant_dynamic-update-slice_fusion.2.edge_own
  40.2 2.5 %fusion.28 = f32[16,16,128]{2,1,0:T(8,128)} fusion(f32[16,16,1024]{2,1,0:T(8,128)} %bitcast.61, f32[1024,128,1]{1,0,2:T(8,128)S(1)} %bitcast.48), kind=kOutput, calls=%fused_computation.53 | convolution fusion | flops 201326592 | bytes 1703936 | tf_op jit(solution)/shard_map/dot_general | solution.py:262
  42.7 5.2 %all-to-all-start.2 = ((f32[16,16,128]{2,1,0:T(8,128)}), f32[16,16,128]{2,1,0:T(8,128)}, u32[]{:S(2)}, u32[]{:S(2)}) async-start(f32[16,16,128]{2,1,0:T(8,128)} %fusion.28), calls=%async_computation.2 | async-start | bytes 262144 | tf_op jit(solution)/shard_map/all_to_all | solution.py:219
  48.7 7.1 %all-to-all-done.2 = f32[16,16,128]{2,1,0:T(8,128)} async-done(((f32[16,16,128]{2,1,0:T(8,128)}), f32[16,16,128]{2,1,0:T(8,128)}, u32[]{:S(2)}, u32[]{:S(2)}) %all-to-all-start.2) | async-done | bytes 131104 | tf_op jit(solution)/shard_map/all_to_all | solution.py:219
  56.5 3.5 %all-to-all-start.1 = ((f32[16,8,128]{2,1,0:T(8,128)}), f32[16,8,128]{2,1,0:T(8,128)S(1)}, u32[]{:S(2)}, u32[]{:S(2)}) async-start(f32[16,8,128]{2,1,0:T(8,128)} %broadcast_in_dim.11), calls=%async_computation.1 | async-start | bytes 131072 | tf_op jit(solution)/shard_map/all_to_all | solution.py:222
  60.0 0.9 reduce_sum.37
  60.9 2.9 %step.4.own = f32[4,4,64,128]{3,2,1,0:T(8,128)} custom-call(s32[3]{0:T(128)S(1)} %pad_add_fusion.info, s32[128]{0:T(128)S(1)} %add.42.index, bf16[16,128,512]{2,1,0:T(8,128)(2,1)S(1)} %pack.1.packed, f32[4,4,64,128]{3,2,1,0:T(8,128)S(1)} %step.3.own.before, f32[4,4,64,128]{3,2,1,0:T(8,128)} %collective-permute-done.4.other, ...), custom_call_target="tpu_custom_call" | custom-call | flops 536870912 | bytes 6291456 | tf_op jit(solution)/shard_map/step/pallas_call | solution.py:115
  64.1 1.6 fusion.25
  65.7 4.2 %collective-permute-start.9 = (f32[1,4,64,128]{3,2,1,0:T(8,128)S(1)}, f32[1,4,64,128]{3,2,1,0:T(8,128)}, u32[]{:S(2)}, u32[]{:S(2)}) collective-permute-start(f32[1,4,64,128]{3,2,1,0:T(8,128)S(1)} %get-tuple-element.19), channel_id=1, source_target_pairs={{0,2},{2,4},{4,6},{6,8},{8,10},{10,12},{12,14},{1,3},{3,5},{5,7},{... | collective-permute-start | bytes 393224 | tf_op jit(solution)/shard_map/ppermute | solution.py:256
  70.0 1.3 collective-permute-start.10
  71.3 2.3 %maximum_bitcast_fusion = f32[384,1024]{0,1:T(8,128)} fusion(f32[1024,128]{1,0:T(8,128)} %bitcast.5, f32[1024,128]{1,0:T(8,128)S(1)} %bitcast.49, f32[1024,128]{1,0:T(8,128)S(1)} %bitcast.44), kind=kLoop, calls=%fused_computation.5 | loop fusion | flops 786432 | bytes 3145728 | tf_op jit(solution)/shard_map/dot_general | solution.py:262
  73.6 3.1 %copy.21 = f32[384,1024]{1,0:T(8,128)} copy(f32[384,1024]{0,1:T(8,128)} %maximum_bitcast_fusion) | data formatting | bytes 3145728 | tf_op jit(solution)/shard_map/dot_general | solution.py:262
  76.6 0.9 constant_dynamic-update-slice_fusion.5
  79.3 6.8 %all-to-all-start.3 = ((f32[16,16,128]{2,1,0:T(8,128)}), f32[16,16,128]{2,1,0:T(8,128)S(1)}, u32[]{:S(2)}, u32[]{:S(2)}) async-start(f32[16,16,128]{2,1,0:T(8,128)} %broadcast_in_dim.12), calls=%async_computation.3 | async-start | bytes 262144 | tf_op jit(solution)/shard_map/all_to_all | solution.py:222
  86.2 3.0 %fusion.29 = f32[16,24,128]{2,1,0:T(8,128)} fusion(f32[16,24,1024]{2,1,0:T(8,128)} %bitcast.60, f32[1024,128,1]{1,0,2:T(8,128)} %bitcast.17), kind=kOutput, calls=%fused_computation.54 | convolution fusion | flops 301989888 | bytes 2293760 | tf_op jit(solution)/shard_map/dot_general | solution.py:262
  89.1 2.3 %step.5 = f32[4,4,64,128]{3,2,1,0:T(8,128)S(1)} custom-call(s32[3]{0:T(128)S(1)} %pad_add_fusion.info, s32[128]{0:T(128)S(1)} %add.42.index, bf16[16,128,512]{2,1,0:T(8,128)(2,1)S(1)} %pack.1.packed, f32[4,4,64,128]{3,2,1,0:T(8,128)} %step.4.own, f32[4,4,64,128]{3,2,1,0:T(8,128)} %collective-permute-done.8.other, ...), custom_call_target="tpu_custom_call" | custom-call | flops 536870912 | bytes 6291456 | tf_op jit(solution)/shard_map/step/pallas_call | solution.py:115
  92.2 1.9 %all-to-all-done.3 = f32[16,16,128]{2,1,0:T(8,128)S(1)} async-done(((f32[16,16,128]{2,1,0:T(8,128)}), f32[16,16,128]{2,1,0:T(8,128)S(1)}, u32[]{:S(2)}, u32[]{:S(2)}) %all-to-all-start.3) | async-done | bytes 131104 | tf_op jit(solution)/shard_map/all_to_all | solution.py:222
  94.1 4.1 %all-to-all-start.4 = ((f32[16,24,128]{2,1,0:T(8,128)}), f32[16,24,128]{2,1,0:T(8,128)S(1)}, u32[]{:S(2)}, u32[]{:S(2)}) async-start(f32[16,24,128]{2,1,0:T(8,128)} %fusion.29), calls=%async_computation.4 | async-start | bytes 393216 | tf_op jit(solution)/shard_map/all_to_all | solution.py:219
  98.2 2.7 %fusion = f32[512,1024]{0,1:T(8,128)} fusion(f32[1024,128]{1,0:T(8,128)} %bitcast.52, f32[1024,128]{1,0:T(8,128)} %bitcast.5, f32[1024,128]{1,0:T(8,128)S(1)} %bitcast.50, f32[1024,128]{1,0:T(8,128)S(1)} %bitcast.45), kind=kLoop, calls=%fused_computation.7 | loop fusion | flops 1572864 | bytes 4194304 | tf_op jit(solution)/shard_map/dot_general | solution.py:262
  100.9 2.9 %copy.22 = f32[512,1024]{1,0:T(8,128)} copy(f32[512,1024]{0,1:T(8,128)} %fusion) | data formatting | bytes 4194304 | tf_op jit(solution)/shard_map/dot_general | solution.py:262
  103.9 3.3 %fusion.30 = f32[16,32,128]{2,1,0:T(8,128)} fusion(f32[16,32,1024]{2,1,0:T(8,128)} %bitcast.59, f32[1024,128,1]{1,0,2:T(8,128)S(1)} %bitcast.53), kind=kOutput, calls=%fused_computation.55 | convolution fusion | flops 402653184 | bytes 2883584 | tf_op jit(solution)/shard_map/dot_general | solution.py:262
  107.2 6.0 %all-to-all-start.6 = ((f32[16,32,128]{2,1,0:T(8,128)}), f32[16,32,128]{2,1,0:T(8,128)S(1)}, u32[]{:S(2)}, u32[]{:S(2)}) async-start(f32[16,32,128]{2,1,0:T(8,128)} %fusion.30), calls=%async_computation.6 | async-start | bytes 524288 | tf_op jit(solution)/shard_map/all_to_all | solution.py:219
  113.2 10.0 %all-to-all-done.6 = f32[16,32,128]{2,1,0:T(8,128)S(1)} async-done(((f32[16,32,128]{2,1,0:T(8,128)}), f32[16,32,128]{2,1,0:T(8,128)S(1)}, u32[]{:S(2)}, u32[]{:S(2)}) %all-to-all-start.6) | async-done | bytes 262176 | tf_op jit(solution)/shard_map/all_to_all | solution.py:219
  123.9 3.5 %all-to-all-start.5 = ((f32[16,24,128]{2,1,0:T(8,128)}), f32[16,24,128]{2,1,0:T(8,128)S(1)}, u32[]{:S(2)}, u32[]{:S(2)}) async-start(f32[16,24,128]{2,1,0:T(8,128)} %broadcast_in_dim.13), calls=%async_computation.5 | async-start | bytes 393216 | tf_op jit(solution)/shard_map/all_to_all | solution.py:222
  127.5 8.9 %all-to-all-done.5 = f32[16,24,128]{2,1,0:T(8,128)S(1)} async-done(((f32[16,24,128]{2,1,0:T(8,128)}), f32[16,24,128]{2,1,0:T(8,128)S(1)}, u32[]{:S(2)}, u32[]{:S(2)}) %all-to-all-start.5) | async-done | bytes 196640 | tf_op jit(solution)/shard_map/all_to_all | solution.py:222
  137.2 3.7 %all-to-all-start.7 = ((f32[16,32,128]{2,1,0:T(8,128)}), f32[16,32,128]{2,1,0:T(8,128)S(1)}, u32[]{:S(2)}, u32[]{:S(2)}) async-start(f32[16,32,128]{2,1,0:T(8,128)} %broadcast_in_dim.14), calls=%async_computation.7 | async-start | bytes 524288 | tf_op jit(solution)/shard_map/all_to_all | solution.py:222
  140.9 4.0 %column.4 = (f32[128,128]{1,0:T(8,128)S(1)}, f32[128,128]{1,0:T(8,128)S(1)}) custom-call(f32[128,128]{1,0:T(8,128)S(1)} %bitcast.58), custom_call_target="tpu_custom_call" | custom-call | flops 8388608 | bytes 524288 | tf_op jit(solution)/shard_map/column/pallas_call | solution.py:205
  145.0 4.9 %column.5 = (f32[256,128]{1,0:T(8,128)S(1)}, f32[256,128]{1,0:T(8,128)S(1)}) custom-call(f32[256,128]{1,0:T(8,128)S(1)} %bitcast.57, f32[128,128]{1,0:T(8,128)S(1)} %get-tuple-element.10.refs_1_), custom_call_target="tpu_custom_call" | custom-call | flops 8388608 | bytes 524288 | tf_op jit(solution)/shard_map/column/pallas_call | solution.py:205
  150.6 5.3 %column.6 = (f32[384,128]{1,0:T(8,128)S(1)}, f32[384,128]{1,0:T(8,128)S(1)}) custom-call(f32[384,128]{1,0:T(8,128)S(1)} %bitcast.56, f32[256,256]{1,0:T(8,128)S(1)} %pad_maximum_fusion.3.refs_1_), custom_call_target="tpu_custom_call" | custom-call | flops 8388608 | bytes 524288 | tf_op jit(solution)/shard_map/column/pallas_call | solution.py:205
  156.0 6.0 %column.7 = (f32[512,128]{1,0:T(8,128)S(1)}, f32[512,128]{1,0:T(8,128)S(1)}) custom-call(f32[512,128]{1,0:T(8,128)S(1)} %bitcast.55, f32[384,384]{1,0:T(8,128)S(1)} %pad_maximum_fusion.2.refs_1_), custom_call_target="tpu_custom_call" | custom-call | flops 8388608 | bytes 524288 | tf_op jit(solution)/shard_map/column/pallas_call | solution.py:205
  162.0 3.9 %convolution_convert_fusion = bf16[1024,512]{1,0:T(8,128)(2,1)} fusion(f32[1024,128]{1,0:T(8,128)S(1)} %bitcast.54, f32[1024,128]{1,0:T(8,128)} %bitcast.5, f32[1024,128]{1,0:T(8,128)S(1)} %bitcast.51, f32[1024,128]{1,0:T(8,128)S(1)} %bitcast.46, f32[384,128]{1,0:T(8,128)S(1)} %get-tuple-element.12, f32[512,128]{1,0:T(8,128)S(1)} %get-tuple-element.13, ...), kind=kOutput, calls=%fused_computation.6 | convolution fusion | flops 1614807040 | bytes 4128768 | tf_op jit(solution)/shard_map/dot_general | solution.py:278
  165.9 1.1 fusion.2
  (64 shorter events, 9.7 us)
Async XLA Ops:
  0.6 18.2 %copy-start.10 = (s32[4,4,7]{2,1,0:T(4,128)S(1)}, s32[4,4,7]{2,1,0:T(4,128)}, u32[]{:S(2)}) copy-start(s32[4,4,7]{2,1,0:T(4,128)} %param.7) | copy-start | bytes 1348
  0.6 18.5 %copy-start.9 = (s32[4]{0:T(128)S(1)}, s32[4]{0:T(128)}, u32[]{:S(2)}) copy-start(s32[4]{0:T(128)} %sites.1) | copy-start | bytes 52
  0.7 18.5 %copy-start.8 = (f32[4,64,64]{2,1,0:T(8,128)S(1)}, f32[4,64,64]{2,1,0:T(8,128)}, u32[]{:S(2)}) copy-start(f32[4,64,64]{2,1,0:T(8,128)} %sigma.1) | copy-start | bytes 196612
  0.7 22.0 %collective-permute-start = (f32[4,4,64,128]{3,2,1,0:T(8,128)}, f32[4,4,64,128]{3,2,1,0:T(8,128)S(1)}, u32[]{:S(2)}, u32[]{:S(2)}) collective-permute-start(f32[4,4,64,128]{3,2,1,0:T(8,128)} %before.3), channel_id=1, source_target_pairs={{0,1},{1,0},{2,3},{3,2},{4,5},{5,4},{6,7},{7,6},{8,9},{9,8},{10,11... | collective-permute-start | bytes 1572872 | tf_op jit(solution)/shard_map/ppermute | solution.py:258
  2.2 16.2 %collective-permute-start.1 = (f32[1,4,64,128]{3,2,1,0:T(8,128)S(1)}, f32[1,4,64,128]{3,2,1,0:T(8,128)S(1)}, u32[]{:S(2)}, u32[]{:S(2)}) collective-permute-start(f32[1,4,64,128]{3,2,1,0:T(8,128)S(1)} %get-tuple-element.23), channel_id=1, source_target_pairs={{0,2},{2,4},{4,6},{6,8},{8,10},{10,12},{12,14},{1,3},{3,5},{5,7},{... | collective-permute-start | bytes 393224 | tf_op jit(solution)/shard_map/ppermute | solution.py:256
  6.6 11.8 %collective-permute-start.2 = (f32[1,4,64,128]{3,2,1,0:T(8,128)S(1)}, f32[1,4,64,128]{3,2,1,0:T(8,128)S(1)}, u32[]{:S(2)}, u32[]{:S(2)}) collective-permute-start(f32[1,4,64,128]{3,2,1,0:T(8,128)S(1)} %get-tuple-element.22), channel_id=1, source_target_pairs={{2,0},{4,2},{6,4},{8,6},{10,8},{12,10},{14,12},{3,1},{5,3},{7,5},{... | collective-permute-start | bytes 393224 | tf_op jit(solution)/shard_map/ppermute | solution.py:257
  11.2 31.5 %all-to-all-start = ((f32[16,8,128]{2,1,0:T(8,128)}), f32[16,8,128]{2,1,0:T(8,128)}, u32[]{:S(2)}, u32[]{:S(2)}) async-start(f32[16,8,128]{2,1,0:T(8,128)} %fusion.17), calls=%async_computation | async-start | bytes 131072 | tf_op jit(solution)/shard_map/all_to_all | solution.py:219
  18.4 4.2 %collective-permute-start.3 = (f32[2,4,64,128]{3,2,1,0:T(8,128)S(1)}, f32[2,4,64,128]{3,2,1,0:T(8,128)}, u32[]{:S(2)}, u32[]{:S(2)}) collective-permute-start(f32[2,4,64,128]{3,2,1,0:T(8,128)S(1)} %constant_dynamic-update-slice_fusion.edge_own), channel_id=1, source_target_pairs={{0,1},{1,0},{2,3},{3,2},{4,5},{5,4},{6,7},{7,6},{8,9},{9,8},{10,11... | collective-permute-start | bytes 786440 | tf_op jit(solution)/shard_map/ppermute | solution.py:260
  19.1 2.0 %copy-start.3 = (f32[4,4,7,64,64]{4,3,2,1,0:T(8,128)S(1)}, f32[4,4,7,64,64]{4,3,2,1,0:T(8,128)}, u32[]{:S(2)}) copy-start(f32[4,4,7,64,64]{4,3,2,1,0:T(8,128)} %couplings.1) | copy-start | bytes 5505028
  21.2 2.2 %copy-start = (f32[4,4,64,128]{3,2,1,0:T(8,128)S(1)}, f32[4,4,64,128]{3,2,1,0:T(8,128)}, u32[]{:S(2)}) copy-start(f32[4,4,64,128]{3,2,1,0:T(8,128)} %before.3) | copy-start | bytes 1572868
  22.6 0.8 copy-start.4
  23.4 1.0 copy-start.5
  26.4 34.5 %collective-permute-start.4 = (f32[4,4,64,128]{3,2,1,0:T(8,128)S(1)}, f32[4,4,64,128]{3,2,1,0:T(8,128)}, u32[]{:S(2)}, u32[]{:S(2)}) collective-permute-start(f32[4,4,64,128]{3,2,1,0:T(8,128)S(1)} %step.3.own.before), channel_id=1, source_target_pairs={{0,1},{1,0},{2,3},{3,2},{4,5},{5,4},{6,7},{7,6},{8,9},{9,8},{10,11... | collective-permute-start | bytes 1572872 | tf_op jit(solution)/shard_map/ppermute | solution.py:258
  27.3 9.3 %collective-permute-start.5 = (f32[1,4,64,128]{3,2,1,0:T(8,128)S(1)}, f32[1,4,64,128]{3,2,1,0:T(8,128)}, u32[]{:S(2)}, u32[]{:S(2)}) collective-permute-start(f32[1,4,64,128]{3,2,1,0:T(8,128)S(1)} %get-tuple-element.21), channel_id=1, source_target_pairs={{0,2},{2,4},{4,6},{6,8},{8,10},{10,12},{12,14},{1,3},{3,5},{5,7},{... | collective-permute-start | bytes 393224 | tf_op jit(solution)/shard_map/ppermute | solution.py:256
  31.7 7.5 %collective-permute-start.6 = (f32[1,4,64,128]{3,2,1,0:T(8,128)}, f32[1,4,64,128]{3,2,1,0:T(8,128)}, u32[]{:S(2)}, u32[]{:S(2)}) collective-permute-start(f32[1,4,64,128]{3,2,1,0:T(8,128)} %get-tuple-element.20), channel_id=1, source_target_pairs={{2,0},{4,2},{6,4},{8,6},{10,8},{12,10},{14,12},{3,1},{5,3},{7,5},{... | collective-permute-start | bytes 393224 | tf_op jit(solution)/shard_map/ppermute | solution.py:257
  40.1 20.8 %collective-permute-start.7 = (f32[2,4,64,128]{3,2,1,0:T(8,128)S(1)}, f32[2,4,64,128]{3,2,1,0:T(8,128)}, u32[]{:S(2)}, u32[]{:S(2)}) collective-permute-start(f32[2,4,64,128]{3,2,1,0:T(8,128)S(1)} %constant_dynamic-update-slice_fusion.2.edge_own), channel_id=1, source_target_pairs={{0,1},{1,0},{2,3},{3,2},{4,5},{5,4},{6,7},{7,6},{8,9},{9,8},{10,11... | collective-permute-start | bytes 786440 | tf_op jit(solution)/shard_map/ppermute | solution.py:260
  42.7 13.2 %all-to-all-start.2 = ((f32[16,16,128]{2,1,0:T(8,128)}), f32[16,16,128]{2,1,0:T(8,128)}, u32[]{:S(2)}, u32[]{:S(2)}) async-start(f32[16,16,128]{2,1,0:T(8,128)} %fusion.28), calls=%async_computation.2 | async-start | bytes 262144 | tf_op jit(solution)/shard_map/all_to_all | solution.py:219
  56.5 22.2 %all-to-all-start.1 = ((f32[16,8,128]{2,1,0:T(8,128)}), f32[16,8,128]{2,1,0:T(8,128)S(1)}, u32[]{:S(2)}, u32[]{:S(2)}) async-start(f32[16,8,128]{2,1,0:T(8,128)} %broadcast_in_dim.11), calls=%async_computation.1 | async-start | bytes 131072 | tf_op jit(solution)/shard_map/all_to_all | solution.py:222
  63.8 25.3 %collective-permute-start.8 = (f32[4,4,64,128]{3,2,1,0:T(8,128)}, f32[4,4,64,128]{3,2,1,0:T(8,128)}, u32[]{:S(2)}, u32[]{:S(2)}) collective-permute-start(f32[4,4,64,128]{3,2,1,0:T(8,128)} %step.4.own), channel_id=1, source_target_pairs={{0,1},{1,0},{2,3},{3,2},{4,5},{5,4},{6,7},{7,6},{8,9},{9,8},{10,11... | collective-permute-start | bytes 1572872 | tf_op jit(solution)/shard_map/ppermute | solution.py:258
  65.7 10.9 %collective-permute-start.9 = (f32[1,4,64,128]{3,2,1,0:T(8,128)S(1)}, f32[1,4,64,128]{3,2,1,0:T(8,128)}, u32[]{:S(2)}, u32[]{:S(2)}) collective-permute-start(f32[1,4,64,128]{3,2,1,0:T(8,128)S(1)} %get-tuple-element.19), channel_id=1, source_target_pairs={{0,2},{2,4},{4,6},{6,8},{8,10},{10,12},{12,14},{1,3},{3,5},{5,7},{... | collective-permute-start | bytes 393224 | tf_op jit(solution)/shard_map/ppermute | solution.py:256
  70.0 7.7 %collective-permute-start.10 = (f32[1,4,64,128]{3,2,1,0:T(8,128)}, f32[1,4,64,128]{3,2,1,0:T(8,128)}, u32[]{:S(2)}, u32[]{:S(2)}) collective-permute-start(f32[1,4,64,128]{3,2,1,0:T(8,128)} %get-tuple-element.18), channel_id=1, source_target_pairs={{2,0},{4,2},{6,4},{8,6},{10,8},{12,10},{14,12},{3,1},{5,3},{7,5},{... | collective-permute-start | bytes 393224 | tf_op jit(solution)/shard_map/ppermute | solution.py:257
  78.6 10.6 %collective-permute-start.11 = (f32[2,4,64,128]{3,2,1,0:T(8,128)S(1)}, f32[2,4,64,128]{3,2,1,0:T(8,128)}, u32[]{:S(2)}, u32[]{:S(2)}) collective-permute-start(f32[2,4,64,128]{3,2,1,0:T(8,128)S(1)} %constant_dynamic-update-slice_fusion.4.edge_own), channel_id=1, source_target_pairs={{0,1},{1,0},{2,3},{3,2},{4,5},{5,4},{6,7},{7,6},{8,9},{9,8},{10,11... | collective-permute-start | bytes 786440 | tf_op jit(solution)/shard_map/ppermute | solution.py:260
  78.7 0.7 copy-start.6
  79.3 14.8 %all-to-all-start.3 = ((f32[16,16,128]{2,1,0:T(8,128)}), f32[16,16,128]{2,1,0:T(8,128)S(1)}, u32[]{:S(2)}, u32[]{:S(2)}) async-start(f32[16,16,128]{2,1,0:T(8,128)} %broadcast_in_dim.12), calls=%async_computation.3 | async-start | bytes 262144 | tf_op jit(solution)/shard_map/all_to_all | solution.py:222
  91.4 0.8 copy-start.1
  94.1 13.1 %all-to-all-start.4 = ((f32[16,24,128]{2,1,0:T(8,128)}), f32[16,24,128]{2,1,0:T(8,128)S(1)}, u32[]{:S(2)}, u32[]{:S(2)}) async-start(f32[16,24,128]{2,1,0:T(8,128)} %fusion.29), calls=%async_computation.4 | async-start | bytes 393216 | tf_op jit(solution)/shard_map/all_to_all | solution.py:219
  100.9 3.0 %copy-start.2 = (f32[4,4,64,128]{3,2,1,0:T(8,128)S(1)}, f32[4,4,64,128]{3,2,1,0:T(8,128)}, u32[]{:S(2)}) copy-start(f32[4,4,64,128]{3,2,1,0:T(8,128)} %copy-done.1) | copy-start | bytes 1572868
  103.9 37.0 %copy-start.7 = (f32[16,8,128]{2,1,0:T(8,128)S(1)}, f32[16,8,128]{2,1,0:T(8,128)}, u32[]{:S(2)}) copy-start(f32[16,8,128]{2,1,0:T(8,128)} %copy-done.6) | copy-start | bytes 196612
  107.2 16.0 %all-to-all-start.6 = ((f32[16,32,128]{2,1,0:T(8,128)}), f32[16,32,128]{2,1,0:T(8,128)S(1)}, u32[]{:S(2)}, u32[]{:S(2)}) async-start(f32[16,32,128]{2,1,0:T(8,128)} %fusion.30), calls=%async_computation.6 | async-start | bytes 524288 | tf_op jit(solution)/shard_map/all_to_all | solution.py:219
  123.9 12.5 %all-to-all-start.5 = ((f32[16,24,128]{2,1,0:T(8,128)}), f32[16,24,128]{2,1,0:T(8,128)S(1)}, u32[]{:S(2)}, u32[]{:S(2)}) async-start(f32[16,24,128]{2,1,0:T(8,128)} %broadcast_in_dim.13), calls=%async_computation.5 | async-start | bytes 393216 | tf_op jit(solution)/shard_map/all_to_all | solution.py:222
  137.2 18.8 %all-to-all-start.7 = ((f32[16,32,128]{2,1,0:T(8,128)}), f32[16,32,128]{2,1,0:T(8,128)S(1)}, u32[]{:S(2)}, u32[]{:S(2)}) async-start(f32[16,32,128]{2,1,0:T(8,128)} %broadcast_in_dim.14), calls=%async_computation.7 | async-start | bytes 524288 | tf_op jit(solution)/shard_map/all_to_all | solution.py:222
where the time goes:
time: 169 us; the launch traced here: 167 us
  starting transfers between devices  58.4 us (35%)
  waiting for transfers between devices  29.8 us (18%)
  Pallas kernels  28.7 us (17%)
  local copies, waits for them, and re-layouts  25.1 us (15%)
  matrix products  14.7 us (9%)
  other arithmetic  9.13 us (5%)
    all_to_all x4, starting transfers between devices, total(): parts = lax.all_to_all(shares, axes, 0, 0, tiled=True)  22.4 us
    pallas_call x4, Pallas kernels, column(): pl.pallas_call(functools.partial(column_kernel, place), in_specs=[whole]...  20.2 us
    all_to_all x4, starting transfers between devices, total(): return lax.all_to_all(copies, axes, 0, 0, tiled=True).reshape(x.shape)  17.5 us
    all_to_all x4, waiting for transfers between devices, total(): parts = lax.all_to_all(shares, axes, 0, 0, tiled=True)  17.2 us
    ppermute x3, starting transfers between devices, local(): low = lax.ppermute(field[layers - 1:], 'trans', forward)  13.1 us
    all_to_all x4, waiting for transfers between devices, total(): return lax.all_to_all(copies, axes, 0, 0, tiled=True).reshape(x.shape)  10.8 us
    dot_general x4, matrix products, local(): lax.dot_general(krylov, field.reshape(-1, columns), (((0,), (0,)), ((), (...  10.8 us
    dot_general x4, local copies, waits for them, and re-layouts, local(): lax.dot_general(krylov, field.reshape(-1, columns), (((0,), (0,)), ((), (...  9.77 us
  transfers between devices with their start and end apart: 20, of which 6 were waited for; matrix products, arithmetic and copies ran while one was open for 23% of the time, Pallas kernels for 14%

commit v1 on v0

--- a/solution.py
+++ b/solution.py
@@ -11,7 +11,6 @@
 S = 3
 center_shift = 2.0
 half_range = 1.6
-HIGH = lax.Precision.HIGH
 HIGHEST = lax.Precision.HIGHEST
 VMEM_LIMIT = 48 * 1024 * 1024
 
@@ -69,9 +68,10 @@
     )(info, lead_sites, couplings, lead_sigma)
 
 
-def step_kernel(
-    first, slots, info, index, packed, own, other, edge_own, edge_other, before, out, field
-):
+def step_kernel(first, last, slots, info, cols, packed, own, other, *refs):
+    edges, refs = refs[:4], refs[4:]
+    before, refs = (None, refs) if first else (refs[0], refs[1:])
+    out, field = refs[0], refs[-1]
     layers, cross_local, size, columns = own.shape
     total = 2 * cross_local
     mine = info[0] * cross_local
@@ -86,17 +86,17 @@
         for q in range(cross_local):
             put((layer + 1) * total + mine + q, own[layer, q])
             put((layer + 1) * total + theirs + q, other[layer, q])
+    low_own, low_other, high_own, high_other = edges
     for q in range(cross_local):
-        put(mine + q, edge_own[0, q])
-        put(theirs + q, edge_other[0, q])
-        put((layers + 1) * total + mine + q, edge_own[1, q])
-        put((layers + 1) * total + theirs + q, edge_other[1, q])
+        put(mine + q, low_own[0, q])
+        put(theirs + q, low_other[0, q])
+        put((layers + 1) * total + mine + q, high_own[0, q])
+        put((layers + 1) * total + theirs + q, high_other[0, q])
     for layer in range(layers):
         for q in range(cross_local):
             row = layer * cross_local + q
-            picked = jnp.concatenate(
-                [field[index[row * slots + j]] for j in range(slots)], axis=0
-            )
+            places = [cols[layer, q, j] for j in range(slots)] + [total + mine + q]
+            picked = jnp.concatenate([field[layer * total + c] for c in places], axis=0)
             acc = jnp.dot(packed[row], picked, preferred_element_type=jnp.float32)
             acc = acc[:, :columns] + acc[:, columns:]
             applied = acc[:size] + acc[size:]
@@ -104,19 +104,25 @@
             if not first:
                 value = 2.0 * value - before[layer, q]
             out[layer, q] = value
-
-
-def step(packed, index, info, own, other, edge_own, edge_other, before, first):
+            if not last and layer == 0:
+                refs[1][0, q] = value
+            if not last and layer == layers - 1:
+                refs[2][0, q] = value
+
+
+def step(packed, cols, info, own, other, edges, before, last):
     layers, cross_local, size, columns = own.shape
     rows, _, depth = packed.shape
-    slots = depth // size
     whole = pl.BlockSpec(memory_space=pltpu.VMEM)
     scalar = pl.BlockSpec(memory_space=pltpu.SMEM)
+    args = [packed, own, other, *edges] + ([] if before is None else [before])
+    edge = jax.ShapeDtypeStruct((1,) + own.shape[1:], jnp.float32)
+    shapes = [jax.ShapeDtypeStruct(own.shape, jnp.float32)] + ([] if last else [edge, edge])
     return pl.pallas_call(
-        functools.partial(step_kernel, first, slots),
-        in_specs=[scalar, scalar] + [whole] * 6,
-        out_specs=whole,
-        out_shape=jax.ShapeDtypeStruct(own.shape, jnp.float32),
+        functools.partial(step_kernel, before is None, last, cols.shape[2]),
+        in_specs=[scalar, scalar] + [whole] * len(args),
+        out_specs=[whole] * len(shapes),
+        out_shape=shapes,
         scratch_shapes=[
             pltpu.VMEM(((layers + 2) * 2 * cross_local, size, 2 * columns), jnp.bfloat16)
         ],
@@ -125,7 +131,64 @@
         ),
         compiler_params=pltpu.CompilerParams(vmem_limit_bytes=VMEM_LIMIT),
         name="step",
-    )(info, index, packed, own, other, edge_own, edge_other, before)
+    )(info, cols, *args)
+
+
+def gram_kernel(pairs, count, *refs):
+    if len(refs) > count + 3:
+        info, refs = refs[0], refs[1:]
+        outs = refs[count : count + 2]
+    else:
+        info, outs = None, refs[count : count + 1]
+    powers, held = refs[:count], refs[-1]
+    columns = outs[0].shape[-1] // len(pairs)
+
+    for j in range(count):
+        high, low = split(powers[j][...].reshape(-1, columns))
+        held[j, :, :columns] = high
+        held[j, :, columns:] = low
+    if info is not None:
+        half = columns // 2
+        mine = pl.multiple_of(info[0] * half, half)
+        theirs = pl.multiple_of((1 - info[0]) * half, half)
+        block = refs[-2]
+    for place, (i, j) in enumerate(pairs):
+        acc = lax.dot_general(
+            held[i], held[j], (((0,), (0,)), ((), ())), preferred_element_type=jnp.float32
+        )
+        acc = acc[:, :columns] + acc[:, columns:]
+        acc = acc[:columns] + acc[columns:]
+        at = slice(place * columns, (place + 1) * columns)
+        if info is None:
+            outs[0][:, at] = acc
+        else:
+            block[...] = acc
+            outs[0][:, at] = block[pl.ds(mine, half), :]
+            outs[1][:, at] = block[pl.ds(theirs, half), :]
+
+
+def gram_blocks(powers, pairs, info=None):
+    columns = powers[0].shape[-1]
+    rows = powers[0].size // columns
+    whole = pl.BlockSpec(memory_space=pltpu.VMEM)
+    cut = 1 if info is None else 2
+    shape = jax.ShapeDtypeStruct((columns // cut, len(pairs) * columns), jnp.float32)
+    scalars = [] if info is None else [info]
+    return pl.pallas_call(
+        functools.partial(gram_kernel, pairs, len(powers)),
+        in_specs=[pl.BlockSpec(memory_space=pltpu.SMEM)] * len(scalars) + [whole] * len(powers),
+        out_specs=[whole] * cut,
+        out_shape=[shape] * cut,
+        scratch_shapes=[pltpu.VMEM((columns, columns), jnp.float32)] * (cut - 1)
+        + [pltpu.VMEM((len(powers), rows, 2 * columns), jnp.bfloat16)],
+        cost_estimate=pl.CostEstimate(
+            flops=8 * rows * columns * columns * len(pairs),
+            bytes_accessed=len(powers) * rows * columns * 4,
+            transcendentals=0,
+        ),
+        compiler_params=pltpu.CompilerParams(vmem_limit_bytes=VMEM_LIMIT),
+        name="gram",
+    )(*scalars, *powers)
 
 
 def factor(block):
@@ -176,108 +239,179 @@
     )
 
 
-def column_kernel(place, *refs):
-    if place:
-        gram, inverse, upper_out, inverse_out = refs
+def column_kernel(place, scale, offset, *refs):
+    if scale is None:
+        gram, refs = refs[0], refs[1:]
+        size = gram.shape[0]
     else:
-        gram, upper_out, inverse_out = refs
-    size = gram.shape[1]
-    split_at = place * size
-    corner = gram[split_at:, :]
-    if place:
-        known = inverse[...]
-        above = dot(known, gram[:split_at, :], ((0,), (0,)))
-        corner = corner - dot(above, above, ((0,), (0,)))
-        carried = dot(known, above)
+        info, own, other, refs, gram = *refs[:3], refs[3:-1], refs[-1]
+        half = own.shape[0]
+        size = 2 * half
+        gram[pl.ds(pl.multiple_of(info[0] * half, half), half), :] = own[...]
+        gram[pl.ds(pl.multiple_of((1 - info[0]) * half, half), half), :] = other[...]
+    inverses, refs = refs[:place], refs[place:]
+
+    def part(m):
+        return slice(m * size, (m + 1) * size)
+
+    corner = gram[:, part(offset + place)]
+    above = [
+        dot(inverses[i][...], gram[:, offset * size : (offset + i + 1) * size], ((0,), (1,)))
+        for i in range(place)
+    ]
+    for x in above:
+        corner = corner - dot(x, x, ((0,), (0,)))
+    carried = []
+    for m in range(place):
+        terms = [dot(inverses[i][part(m), :], above[i]) for i in range(m, place)]
+        carried.append(functools.reduce(lambda x, y: x + y, terms))
     upper, lower_inverse = factor(corner)
     upper_inverse = lower_inverse.T
-    if place:
-        upper_out[:split_at, :] = above
-        inverse_out[:split_at, :] = -dot(carried, upper_inverse)
-    upper_out[split_at:, :] = upper
-    inverse_out[split_at:, :] = upper_inverse
-
-
-def column(place, gram, inverse):
+    if scale is None:
+        upper_out, inverse_out = refs
+    else:
+        uppers, (result, inverse_out) = refs[:place], refs[place:]
+        result[...] = jnp.zeros_like(result)
+        for i in range(place):
+            result[: (i + 1) * size, part(i)] = uppers[i][...] * scale
+        upper_out = result.at[:, part(place)]
+        above = [x * scale for x in above]
+        upper = upper * scale
+    for m in range(place):
+        upper_out[part(m), :] = above[m]
+        inverse_out[part(m), :] = -dot(carried[m], upper_inverse)
+    upper_out[part(place), :] = upper
+    inverse_out[part(place), :] = upper_inverse
+
+
+def column(gram, inverses, offset=0, info=None, uppers=(), scale=None):
     whole = pl.BlockSpec(memory_space=pltpu.VMEM)
-    args = (gram, inverse) if place else (gram,)
-    shape = jax.ShapeDtypeStruct(gram.shape, jnp.float32)
+    place = len(inverses)
+    args = [gram] if scale is None else list(gram)
+    size = args[0].shape[0] * len(args)
+    specs = [whole] * (len(args) + place + len(uppers))
+    args += [*inverses, *uppers]
+    shape = jax.ShapeDtypeStruct(((place + 1) * size, size), jnp.float32)
+    square = jax.ShapeDtypeStruct(((place + 1) * size,) * 2, jnp.float32)
+    scratch = []
+    if scale is not None:
+        args = [info] + args
+        specs = [pl.BlockSpec(memory_space=pltpu.SMEM)] + specs
+        scratch = [pltpu.VMEM((size, (place + 1) * size), jnp.float32)]
     return pl.pallas_call(
-        functools.partial(column_kernel, place),
-        in_specs=[whole] * len(args),
+        functools.partial(column_kernel, place, scale, offset),
+        in_specs=specs,
         out_specs=[whole, whole],
-        out_shape=[shape, shape],
+        out_shape=[shape if scale is None else square, shape],
+        scratch_shapes=scratch,
         compiler_params=pltpu.CompilerParams(vmem_limit_bytes=VMEM_LIMIT),
         cost_estimate=pl.CostEstimate(flops=1 << 23, bytes_accessed=1 << 19, transcendentals=128),
         name="column",
     )(*args)
 
 
-def total(x, axes):
-    count = math.prod(lax.axis_size(a) for a in axes)
-    shares = x.reshape(count, -1) if x.size // count % 1024 else x.reshape(count, -1, x.shape[-1])
-    parts = lax.all_to_all(shares, axes, 0, 0, tiled=True)
+def basis_kernel(scale, count, *refs):
+    powers, inverses, (out, high, low) = refs[:count], refs[count : 2 * count], refs[2 * count :]
+    columns = powers[0].shape[-1]
+
+    @pl.when(pl.program_id(0) == 0)
+    def _():
+        high[...] = jnp.zeros_like(high)
+        low[...] = jnp.zeros_like(low)
+        for j, inverse in enumerate(inverses):
+            a, b = split(inverse[...] * scale)
+            high[: (j + 1) * columns, j * columns : (j + 1) * columns] = a
+            low[: (j + 1) * columns, j * columns : (j + 1) * columns] = b
+
+    pairs = [split(p[...].reshape(-1, columns)) for p in powers]
+    wide = 2 * columns
+    for start in range(0, count * columns, wide):
+        stop = min(start + wide, count * columns)
+        left_high = jnp.concatenate([p[0] for p in pairs[: stop // columns]], axis=1)
+        left_low = jnp.concatenate([p[1] for p in pairs[: stop // columns]], axis=1)
+        right = high[:stop, start:stop]
+        acc = jnp.dot(left_high, right, preferred_element_type=jnp.float32)
+        acc = acc + jnp.dot(left_low, right, preferred_element_type=jnp.float32)
+        acc = acc + jnp.dot(left_high, low[:stop, start:stop], preferred_element_type=jnp.float32)
+        out[:, :, :, start:stop] = acc.astype(jnp.bfloat16).reshape(out.shape[:3] + (stop - start,))
+
+
+def basis_of(powers, inverses, scale):
+    layers, cross_local, size, columns = powers[0].shape
+    count = len(powers)
+    full = count * columns
+    return pl.pallas_call(
+        functools.partial(basis_kernel, scale, count),
+        grid=(layers,),
+        in_specs=[pl.BlockSpec((1, cross_local, size, columns), lambda i: (i, 0, 0, 0))] * count
+        + [pl.BlockSpec(x.shape, lambda i: (0, 0)) for x in inverses],
+        out_specs=pl.BlockSpec((1, cross_local, size, full), lambda i: (i, 0, 0, 0)),
+        out_shape=jax.ShapeDtypeStruct((layers, cross_local, size, full), jnp.bfloat16),
+        scratch_shapes=[pltpu.VMEM((full, full), jnp.bfloat16)] * 2,
+        compiler_params=pltpu.CompilerParams(vmem_limit_bytes=VMEM_LIMIT),
+        name="basis",
+    )(*powers, *inverses)
+
+
+def total(x, axis):
+    count = lax.axis_size(axis)
+    shares = x.reshape(count, -1) if x.shape[0] % count else x.reshape(count, -1, x.shape[1])
+    parts = lax.all_to_all(shares, axis, 0, 0, tiled=True)
     mine = jnp.sum(parts, axis=0, keepdims=True)
     copies = jnp.broadcast_to(mine, shares.shape)
-    return lax.all_to_all(copies, axes, 0, 0, tiled=True).reshape(x.shape)
+    return lax.all_to_all(copies, axis, 0, 0, tiled=True).reshape(x.shape)
 
 
 def local(sources, couplings, block_cols, lead_sites, lead_sigma):
     layers, cross_local, size, columns = sources.shape
     cross_count = lax.axis_size("cross")
     trans_count = lax.axis_size("trans")
-    cross_total = cross_local * cross_count
     trans_place = lax.axis_index("trans")
-    cross_place = lax.axis_index("cross")
     info = jnp.stack(
         [
-            cross_place,
+            lax.axis_index("cross"),
             (trans_place == 0).astype(jnp.int32),
             (trans_place == trans_count - 1).astype(jnp.int32),
         ]
     ).astype(jnp.int32)
-    layer_base = jnp.arange(layers, dtype=jnp.int32)[:, None, None] * cross_total
-    self_cols = (cross_total + cross_place * cross_local + jnp.arange(cross_local, dtype=jnp.int32))
-    self_cols = jnp.broadcast_to(self_cols[None, :, None], (layers, cross_local, 1))
-    index = (layer_base + jnp.concatenate([block_cols, self_cols], axis=2)).reshape(-1)
     packed = pack(couplings, lead_sites, lead_sigma, info)
 
     forward = [(i, i + 1) for i in range(trans_count - 1)]
     backward = [(i + 1, i) for i in range(trans_count - 1)]
     swap = [(0, 1), (1, 0)]
+    scale_rows = math.sqrt(trans_count * layers * cross_local * cross_count * size)
 
     powers = [sources]
-    uppers = []
-    inverses = []
-    inverse = None
-    for k in range(S + 1):
+    first_layer, last_layer = sources[:1], sources[layers - 1 :]
+    sums = []
+    for k in range(S):
         field = powers[k]
-        if k < S:
-            low = lax.ppermute(field[layers - 1 :], "trans", forward)
-            high = lax.ppermute(field[:1], "trans", backward)
-            other = lax.ppermute(field, "cross", swap)
-            edge_own = jnp.concatenate([low, high], axis=0)
-            edge_other = lax.ppermute(edge_own, "cross", swap)
-        krylov = jnp.concatenate([x.reshape(-1, columns) for x in powers], axis=1)
-        part = lax.dot_general(
-            krylov, field.reshape(-1, columns), (((0,), (0,)), ((), ())), precision=HIGH
-        )
-        gram = total(part, ("trans", "cross"))
-        upper_col, inverse_col = column(k, gram, inverse)
-        fill = ((0, (S - k) * columns), (0, 0))
-        uppers.append(jnp.pad(upper_col, fill))
-        inverses.append(jnp.pad(inverse_col, fill))
-        if k < S:
-            inverse = jnp.concatenate([x[: (k + 1) * columns] for x in inverses], axis=1)
-            before = powers[k - 1] if k else field
-            powers.append(
-                step(packed, index, info, field, other, edge_own, edge_other, before, k == 0)
-            )
-    scale_rows = math.sqrt(trans_count * layers * cross_total * size)
-    solver = jnp.concatenate(inverses, axis=1) * scale_rows
-    basis = lax.dot_general(krylov, solver, (((1,), (0,)), ((), ())), precision=HIGH)
-    basis = basis.astype(jnp.bfloat16).reshape(layers, cross_local, size, (S + 1) * columns)
-    return basis, jnp.concatenate(uppers, axis=1) / scale_rows
+        low = lax.ppermute(last_layer, "trans", forward)
+        high = lax.ppermute(first_layer, "trans", backward)
+        other = lax.ppermute(field, "cross", swap)
+        edges = (low, lax.ppermute(low, "cross", swap), high, lax.ppermute(high, "cross", swap))
+        if k == 1:
+            part = gram_blocks(powers, ((0, 0), (1, 0), (1, 1)))[0]
+            sums.append(lax.psum(part, ("trans", "cross")))
+        if k == 2:
+            part = gram_blocks(powers, ((2, 0), (2, 1), (2, 2)))[0]
+            sums.append(lax.psum(part, ("cross", "trans")))
+        before = powers[k - 1] if k else None
+        got = step(packed, block_cols, info, field, other, edges, before, k == S - 1)
+        powers.append(got[0])
+        if k < S - 1:
+            first_layer, last_layer = got[1:]
+    mine, theirs = gram_blocks(powers, tuple((S, j) for j in range(S + 1)), info)
+    mine = total(mine + lax.ppermute(theirs, "cross", swap), "trans")
+    theirs = lax.ppermute(mine, "cross", swap)
+
+    upper_0, inverse_0 = column(sums[0][:, :columns], [])
+    upper_1, inverse_1 = column(sums[0], [inverse_0], 1)
+    upper_2, inverse_2 = column(sums[1], [inverse_0, inverse_1])
+    inverses = [inverse_0, inverse_1, inverse_2]
+    uppers = [upper_0, upper_1, upper_2]
+    r_factor, inverse_3 = column((mine, theirs), inverses, 0, info, uppers, 1.0 / scale_rows)
+    return basis_of(powers, inverses + [inverse_3], scale_rows), r_factor
 
 
 def solution(mesh):

time: 169 us -> 288 us (1.70)
  waiting for transfers between devices: 29.8 us -> 196 us
  starting transfers between devices: 58.4 us -> 21.8 us
  local copies, waits for them, and re-layouts: 25.1 us -> 7.95 us
  matrix products: 14.7 us -> 0 us
  between operations: 1.06 us -> 14.3 us
  blocking collectives: 0 us -> 12.5 us
  other arithmetic: 9.13 us -> 0.11 us
  Pallas kernels: 28.7 us -> 34.7 us
    psum x0 -> x2, waiting for transfers between devices: none -> 169 us  [the longest x1 87 us: local(): sums.append(lax.psum(part, ('trans', 'cross')))]
    all_to_all x8 -> x1, starting transfers between devices: 39.9 us -> 3.37 us  [total(): return lax.all_to_all(copies, axis, 0, 0, tiled=True).reshape(x.shape)]
    all_to_all x8 -> x1, waiting for transfers between devices: 28 us -> 5.64 us  [total(): return lax.all_to_all(copies, axis, 0, 0, tiled=True).reshape(x.shape)]
    ppermute x9 -> x14, waiting for transfers between devices: 1.82 us -> 21.9 us  [the longest x3 12.4 us: local(): high = lax.ppermute(first_layer, 'trans', backward)]
    dot_general x5 -> x0, matrix products: 14.7 us -> none  [the longest x4 10.8 us: local(): lax.dot_general(krylov, field.reshape(-1, columns), (((0,), (0,)), ((), (...]
    all_to_all x0 -> x1, blocking collectives: none -> 12.5 us  [total(): parts = lax.all_to_all(shares, axis, 0, 0, tiled=True)]
    dot_general x4 -> x0, local copies, waits for them, and re-layouts: 9.77 us -> none  [local(): lax.dot_general(krylov, field.reshape(-1, columns), (((0,), (0,)), ((), (...]
    dot_general x3 -> x0, other arithmetic: 6.02 us -> none  [local(): lax.dot_general(krylov, field.reshape(-1, columns), (((0,), (0,)), ((), (...]
  transfers between devices with their start and end apart: 20 -> 20, of which waited for: 6 -> 12; matrix products, arithmetic and copies ran while one was open for 23% -> 1% of each run, Pallas kernels for 14% -> 6%
where the time goes in v1:
time: 288 us
  waiting for transfers between devices  196 us (68%)
  Pallas kernels  34.7 us (12%)
  starting transfers between devices  21.8 us (8%)
  between operations  14.3 us (5%)
  blocking collectives  12.5 us (4%)
  local copies, waits for them, and re-layouts  7.95 us (3%)
    psum x1, waiting for transfers between devices, local(): sums.append(lax.psum(part, ('trans', 'cross')))  87 us
    psum x1, waiting for transfers between devices, local(): sums.append(lax.psum(part, ('cross', 'trans')))  81.9 us
    pallas_call x4, Pallas kernels, column(): pl.pallas_call(functools.partial(column_kernel, place, scale, offset), in...  21 us
    ppermute x3, starting transfers between devices, local(): low = lax.ppermute(last_layer, 'trans', forward)  12.8 us
    all_to_all x1, blocking collectives, total(): parts = lax.all_to_all(shares, axis, 0, 0, tiled=True)  12.5 us
    ppermute x3, waiting for transfers between devices, local(): high = lax.ppermute(first_layer, 'trans', backward)  12.4 us
  transfers between devices with their start and end apart: 20, of which 12 were waited for; matrix products, arithmetic and copies ran while one was open for 1% of the time, Pallas kernels for 6%

profile of v1, /device:TPU:0, one launch (start us, length us, event | category | flops | bytes accessed | tf_op | source)
XLA Modules:
  0.0 287.8 jit_solution(6038895992099598574)
XLA Ops:
  7.2 0.5 collective-permute-start
  7.7 1.0 fusion
  8.7 4.5 %collective-permute-start.1 = (f32[1,4,64,128]{3,2,1,0:T(8,128)S(1)}, f32[1,4,64,128]{3,2,1,0:T(8,128)S(1)}, u32[]{:S(2)}, u32[]{:S(2)}) collective-permute-start(f32[1,4,64,128]{3,2,1,0:T(8,128)S(1)} %get-tuple-element.35), channel_id=1, source_target_pairs={{0,2},{2,4},{4,6},{6,8},{8,10},{10,12},{12,14},{1,3},{3,5},{5,7},{... | collective-permute-start | bytes 393224 | tf_op jit(solution)/shard_map/ppermute | solution.py:389
  13.2 1.3 collective-permute-start.3
  14.5 2.0 collective-permute-done.1.refs_0_
  16.5 4.1 %collective-permute-done.3.refs_2_ = f32[1,4,64,128]{3,2,1,0:T(8,128)S(1)} collective-permute-done((f32[1,4,64,128]{3,2,1,0:T(8,128)S(1)}, f32[1,4,64,128]{3,2,1,0:T(8,128)S(1)}, u32[]{:S(2)}, u32[]{:S(2)}) %collective-permute-start.3) | collective-permute-done | bytes 131104 | tf_op jit(solution)/shard_map/ppermute | solution.py:390
  20.6 0.1 pad_add_fusion.info.refs_0_
  20.7 2.0 copy-done.1
  22.7 0.9 copy-done.4
  23.6 0.7 copy-done.6
  24.3 1.4 pack.1.packed
  25.8 1.7 step.3
  27.4 0.6 collective-permute-start.5
  28.0 4.3 %collective-permute-start.6 = (f32[1,4,64,128]{3,2,1,0:T(8,128)S(1)}, f32[1,4,64,128]{3,2,1,0:T(8,128)S(1)}, u32[]{:S(2)}, u32[]{:S(2)}) collective-permute-start(f32[1,4,64,128]{3,2,1,0:T(8,128)S(1)} %get-tuple-element.19), channel_id=1, source_target_pairs={{0,2},{2,4},{4,6},{6,8},{8,10},{10,12},{12,14},{1,3},{3,5},{5,7},{... | collective-permute-start | bytes 393224 | tf_op jit(solution)/shard_map/ppermute | solution.py:389
  32.4 1.3 collective-permute-start.8
  33.7 1.6 collective-permute-done.6.refs_0_
  35.3 4.1 %collective-permute-done.8.refs_2_ = f32[1,4,64,128]{3,2,1,0:T(8,128)S(1)} collective-permute-done((f32[1,4,64,128]{3,2,1,0:T(8,128)S(1)}, f32[1,4,64,128]{3,2,1,0:T(8,128)S(1)}, u32[]{:S(2)}, u32[]{:S(2)}) %collective-permute-start.8) | collective-permute-done | bytes 131104 | tf_op jit(solution)/shard_map/ppermute | solution.py:390
  39.4 1.3 collective-permute-done.9.refs_3_
  40.8 1.7 step.4
  42.4 0.2 collective-permute-start.10
  42.6 4.0 %collective-permute-start.11 = (f32[1,4,64,128]{3,2,1,0:T(8,128)S(1)}, f32[1,4,64,128]{3,2,1,0:T(8,128)S(1)}, u32[]{:S(2)}, u32[]{:S(2)}) collective-permute-start(f32[1,4,64,128]{3,2,1,0:T(8,128)S(1)} %get-tuple-element.22), channel_id=1, source_target_pairs={{0,2},{2,4},{4,6},{6,8},{8,10},{10,12},{12,14},{1,3},{3,5},{5,7},{... | collective-permute-start | bytes 393224 | tf_op jit(solution)/shard_map/ppermute | solution.py:389
  46.6 1.3 collective-permute-start.13
  47.9 1.9 collective-permute-done.11.refs_0_
  49.9 4.1 %collective-permute-done.13.refs_2_ = f32[1,4,64,128]{3,2,1,0:T(8,128)S(1)} collective-permute-done((f32[1,4,64,128]{3,2,1,0:T(8,128)S(1)}, f32[1,4,64,128]{3,2,1,0:T(8,128)S(1)}, u32[]{:S(2)}, u32[]{:S(2)}) %collective-permute-start.13) | collective-permute-done | bytes 131104 | tf_op jit(solution)/shard_map/ppermute | solution.py:390
  54.0 1.3 collective-permute-done.14.refs_3_
  55.3 1.7 step.5.refs_4_.refs_3_
  57.0 1.4 gram.5
  58.4 0.2 collective-permute-start.15
  58.7 1.2 collective-permute-done.15
  59.9 12.5 %all_to_all.10 = f32[8,8,512]{2,1,0:T(8,128)S(1)} all-to-all(f32[8,8,512]{2,1,0:T(8,128)S(1)} %add_bitcast_fusion), channel_id=1, replica_groups=mesh['energy'=2,'trans'=8,'cross'=2] {'trans'}, dimensions={0} | all-to-all | bytes 262144 | tf_op jit(solution)/shard_map/all_to_all | solution.py:359
  72.4 0.7 broadcast_in_dim.2
  73.1 3.4 %all-to-all-start.1 = ((f32[8,8,512]{2,1,0:T(8,128)}), f32[8,8,512]{2,1,0:T(8,128)S(1)}, u32[]{:S(2)}, u32[]{:S(2)}) async-start(f32[8,8,512]{2,1,0:T(8,128)} %broadcast_in_dim.2), calls=%async_computation.1 | async-start | bytes 262144 | tf_op jit(solution)/shard_map/all_to_all | solution.py:362
  76.4 0.0 all-reduce.3.cloned.1.call-start
  76.5 1.3 gram.3
  77.8 0.0 all-reduce.3.cloned.1.call-update
  77.9 0.2 all-reduce.5.cloned.1.call-start
  78.1 5.6 %all-to-all-done.1 = f32[8,8,512]{2,1,0:T(8,128)S(1)} async-done(((f32[8,8,512]{2,1,0:T(8,128)}), f32[8,8,512]{2,1,0:T(8,128)S(1)}, u32[]{:S(2)}, u32[]{:S(2)}) %all-to-all-start.1) | async-done | bytes 131104 | tf_op jit(solution)/shard_map/all_to_all | solution.py:362
  83.7 1.4 gram.4
  85.2 87.0 %all-reduce.3.cloned.1.call-done.refs_0_ = f32[128,384]{1,0:T(8,128)} async-done(((f32[128,384]{1,0:T(8,128)}), f32[128,384]{1,0:T(8,128)}) %all-reduce.3.cloned.1.call-update) | async-done | bytes 196624 | tf_op jit(solution)/shard_map/psum | solution.py:395
  172.2 0.8 slice.12.refs_0_
  173.1 4.0 %column.4 = (f32[128,128]{1,0:T(8,128)S(1)}, f32[128,128]{1,0:T(8,128)S(1)}) custom-call(f32[128,128]{1,0:T(8,128)S(1)} %slice.12.refs_0_), custom_call_target="tpu_custom_call" | custom-call | flops 8388608 | bytes 524288 | tf_op jit(solution)/shard_map/column/pallas_call | solution.py:301
  177.1 0.9 copy-done.2
  178.0 4.9 %column.5 = (f32[256,128]{1,0:T(8,128)S(1)}, f32[256,128]{1,0:T(8,128)S(1)}) custom-call(f32[128,384]{1,0:T(8,128)S(1)} %copy-done.2, f32[128,128]{1,0:T(8,128)S(1)} %get-tuple-element.24.refs_1_.refs_3_.refs_4_), custom_call_target="tpu_custom_call" | custom-call | flops 8388608 | bytes 524288 | tf_op jit(solution)/shard_map/column/pallas_call | solution.py:301
  182.9 81.9 %all-reduce.5.cloned.1.call-done.refs_0_ = f32[128,384]{1,0:T(8,128)} async-done(((f32[128,384]{1,0:T(8,128)}), f32[128,384]{1,0:T(8,128)}) %all-reduce.5.cloned.1.call-update) | async-done | bytes 196624 | tf_op jit(solution)/shard_map/psum | solution.py:398
  264.8 0.9 copy-done.3
  265.7 5.0 %column.6 = (f32[384,128]{1,0:T(8,128)S(1)}, f32[384,128]{1,0:T(8,128)S(1)}) custom-call(f32[128,384]{1,0:T(8,128)S(1)} %copy-done.3, f32[128,128]{1,0:T(8,128)S(1)} %get-tuple-element.24.refs_1_.refs_3_.refs_4_, f32[256,128]{1,0:T(8,128)S(1)} %get-tuple-element.25.refs_2_.refs_4_.refs_5_), custom_call_target="tpu_custom_call" | custom-call | flops 8388608 | bytes 524288 | tf_op jit(solution)/shard_map/column/pallas_call | solution.py:301
  270.8 7.1 %column.7 = (f32[512,512]{1,0:T(8,128)}, f32[512,128]{1,0:T(8,128)S(1)}) custom-call(s32[3]{0:T(128)S(1)} %pad_add_fusion.info.refs_0_, f32[64,512]{1,0:T(8,128)S(1)} %bitcast.7, f32[64,512]{1,0:T(8,128)S(1)} %collective-permute-done.16.refs_2_, f32[128,128]{1,0:T(8,128)S(1)} %get-tuple-element.24.refs_1_.refs_3_.refs_4_, ...), custom_call_target="tpu_custom_call" | custom-call | flops 8388608 | bytes 524288 | tf_op jit(solution)/shard_map/column/pallas_call | solution.py:301
  277.9 3.1 %basis.1 = bf16[4,4,64,512]{3,2,1,0:T(8,128)(2,1)} custom-call(f32[4,4,64,128]{3,2,1,0:T(8,128)S(1)} %copy-done, f32[4,4,64,128]{3,2,1,0:T(8,128)S(1)} %get-tuple-element.18.own.refs_4_.refs_1_.refs_2_, f32[4,4,64,128]{3,2,1,0:T(8,128)S(1)} %get-tuple-element.21.own.refs_2_.refs_3_, f32[4,4,64,128]{3,2,1,0:T(8,128)S(1)} %step.5.refs_4_.refs_3_, ...), custom_call_target="tpu_custom_call" | custom-call | tf_op jit(solution)/shard_map/basis/pallas_call | solution.py:343
  (27 shorter events, 0.1 us)
Async XLA Ops:
  7.2 18.6 %copy-start = (f32[4,4,64,128]{3,2,1,0:T(8,128)S(1)}, f32[4,4,64,128]{3,2,1,0:T(8,128)}, u32[]{:S(2)}) copy-start(f32[4,4,64,128]{3,2,1,0:T(8,128)} %refs_0_.5) | copy-start | bytes 1572868
  7.2 18.6 %copy-start.5 = (s32[4,4,7]{2,1,0:T(4,128)S(1)}, s32[4,4,7]{2,1,0:T(4,128)}, u32[]{:S(2)}) copy-start(s32[4,4,7]{2,1,0:T(4,128)} %cols.5) | copy-start | bytes 1348
  7.2 18.6 %collective-permute-start = (f32[4,4,64,128]{3,2,1,0:T(8,128)}, f32[4,4,64,128]{3,2,1,0:T(8,128)S(1)}, u32[]{:S(2)}, u32[]{:S(2)}) collective-permute-start(f32[4,4,64,128]{3,2,1,0:T(8,128)} %refs_0_.5), channel_id=1, source_target_pairs={{0,1},{1,0},{2,3},{3,2},{4,5},{5,4},{6,7},{7,6},{8,9},{9,8},{10,11... | collective-permute-start | bytes 1572872 | tf_op jit(solution)/shard_map/ppermute | solution.py:391
  8.7 7.8 %collective-permute-start.1 = (f32[1,4,64,128]{3,2,1,0:T(8,128)S(1)}, f32[1,4,64,128]{3,2,1,0:T(8,128)S(1)}, u32[]{:S(2)}, u32[]{:S(2)}) collective-permute-start(f32[1,4,64,128]{3,2,1,0:T(8,128)S(1)} %get-tuple-element.35), channel_id=1, source_target_pairs={{0,2},{2,4},{4,6},{6,8},{8,10},{10,12},{12,14},{1,3},{3,5},{5,7},{... | collective-permute-start | bytes 393224 | tf_op jit(solution)/shard_map/ppermute | solution.py:389
  13.2 7.5 %collective-permute-start.3 = (f32[1,4,64,128]{3,2,1,0:T(8,128)S(1)}, f32[1,4,64,128]{3,2,1,0:T(8,128)S(1)}, u32[]{:S(2)}, u32[]{:S(2)}) collective-permute-start(f32[1,4,64,128]{3,2,1,0:T(8,128)S(1)} %get-tuple-element.34), channel_id=1, source_target_pairs={{2,0},{4,2},{6,4},{8,6},{10,8},{12,10},{14,12},{3,1},{5,3},{7,5},{... | collective-permute-start | bytes 393224 | tf_op jit(solution)/shard_map/ppermute | solution.py:390
  16.5 9.2 %collective-permute-start.2 = (f32[1,4,64,128]{3,2,1,0:T(8,128)S(1)}, f32[1,4,64,128]{3,2,1,0:T(8,128)S(1)}, u32[]{:S(2)}, u32[]{:S(2)}) collective-permute-start(f32[1,4,64,128]{3,2,1,0:T(8,128)S(1)} %collective-permute-done.1.refs_0_), channel_id=1, source_target_pairs={{0,1},{1,0},{2,3},{3,2},{4,5},{5,4},{6,7},{7,6},{8,9},{9,8},{10,11... | collective-permute-start | bytes 393224 | tf_op jit(solution)/shard_map/ppermute | solution.py:392
  20.6 5.1 %collective-permute-start.4 = (f32[1,4,64,128]{3,2,1,0:T(8,128)S(1)}, f32[1,4,64,128]{3,2,1,0:T(8,128)S(1)}, u32[]{:S(2)}, u32[]{:S(2)}) collective-permute-start(f32[1,4,64,128]{3,2,1,0:T(8,128)S(1)} %collective-permute-done.3.refs_2_), channel_id=1, source_target_pairs={{0,1},{1,0},{2,3},{3,2},{4,5},{5,4},{6,7},{7,6},{8,9},{9,8},{10,11... | collective-permute-start | bytes 393224 | tf_op jit(solution)/shard_map/ppermute | solution.py:392
  20.7 2.0 copy-start.1
  22.7 0.9 copy-start.4
  23.6 0.7 copy-start.6
  27.4 13.3 %collective-permute-start.5 = (f32[4,4,64,128]{3,2,1,0:T(8,128)S(1)}, f32[4,4,64,128]{3,2,1,0:T(8,128)S(1)}, u32[]{:S(2)}, u32[]{:S(2)}) collective-permute-start(f32[4,4,64,128]{3,2,1,0:T(8,128)S(1)} %get-tuple-element.18.own.refs_4_.refs_1_.refs_2_), channel_id=1, source_target_pairs={{0,1},{1,0},{2,3},{3,2},{4,5},{5,4},{6,7},{7,6},{8,9},{9,8},{10,11... | collective-permute-start | bytes 1572872 | tf_op jit(solution)/shard_map/ppermute | solution.py:391
  28.0 7.3 %collective-permute-start.6 = (f32[1,4,64,128]{3,2,1,0:T(8,128)S(1)}, f32[1,4,64,128]{3,2,1,0:T(8,128)S(1)}, u32[]{:S(2)}, u32[]{:S(2)}) collective-permute-start(f32[1,4,64,128]{3,2,1,0:T(8,128)S(1)} %get-tuple-element.19), channel_id=1, source_target_pairs={{0,2},{2,4},{4,6},{6,8},{8,10},{10,12},{12,14},{1,3},{3,5},{5,7},{... | collective-permute-start | bytes 393224 | tf_op jit(solution)/shard_map/ppermute | solution.py:389
  32.4 7.0 %collective-permute-start.8 = (f32[1,4,64,128]{3,2,1,0:T(8,128)S(1)}, f32[1,4,64,128]{3,2,1,0:T(8,128)S(1)}, u32[]{:S(2)}, u32[]{:S(2)}) collective-permute-start(f32[1,4,64,128]{3,2,1,0:T(8,128)S(1)} %get-tuple-element.20), channel_id=1, source_target_pairs={{2,0},{4,2},{6,4},{8,6},{10,8},{12,10},{14,12},{3,1},{5,3},{7,5},{... | collective-permute-start | bytes 393224 | tf_op jit(solution)/shard_map/ppermute | solution.py:390
  35.3 4.1 %collective-permute-start.7 = (f32[1,4,64,128]{3,2,1,0:T(8,128)S(1)}, f32[1,4,64,128]{3,2,1,0:T(8,128)S(1)}, u32[]{:S(2)}, u32[]{:S(2)}) collective-permute-start(f32[1,4,64,128]{3,2,1,0:T(8,128)S(1)} %collective-permute-done.6.refs_0_), channel_id=1, source_target_pairs={{0,1},{1,0},{2,3},{3,2},{4,5},{5,4},{6,7},{7,6},{8,9},{9,8},{10,11... | collective-permute-start | bytes 393224 | tf_op jit(solution)/shard_map/ppermute | solution.py:392
  39.4 1.3 collective-permute-start.9
  42.4 12.9 %collective-permute-start.10 = (f32[4,4,64,128]{3,2,1,0:T(8,128)S(1)}, f32[4,4,64,128]{3,2,1,0:T(8,128)S(1)}, u32[]{:S(2)}, u32[]{:S(2)}) collective-permute-start(f32[4,4,64,128]{3,2,1,0:T(8,128)S(1)} %get-tuple-element.21.own.refs_2_.refs_3_), channel_id=1, source_target_pairs={{0,1},{1,0},{2,3},{3,2},{4,5},{5,4},{6,7},{7,6},{8,9},{9,8},{10,11... | collective-permute-start | bytes 1572872 | tf_op jit(solution)/shard_map/ppermute | solution.py:391
  42.6 7.2 %collective-permute-start.11 = (f32[1,4,64,128]{3,2,1,0:T(8,128)S(1)}, f32[1,4,64,128]{3,2,1,0:T(8,128)S(1)}, u32[]{:S(2)}, u32[]{:S(2)}) collective-permute-start(f32[1,4,64,128]{3,2,1,0:T(8,128)S(1)} %get-tuple-element.22), channel_id=1, source_target_pairs={{0,2},{2,4},{4,6},{6,8},{8,10},{10,12},{12,14},{1,3},{3,5},{5,7},{... | collective-permute-start | bytes 393224 | tf_op jit(solution)/shard_map/ppermute | solution.py:389
  46.6 7.4 %collective-permute-start.13 = (f32[1,4,64,128]{3,2,1,0:T(8,128)S(1)}, f32[1,4,64,128]{3,2,1,0:T(8,128)S(1)}, u32[]{:S(2)}, u32[]{:S(2)}) collective-permute-start(f32[1,4,64,128]{3,2,1,0:T(8,128)S(1)} %get-tuple-element.23), channel_id=1, source_target_pairs={{2,0},{4,2},{6,4},{8,6},{10,8},{12,10},{14,12},{3,1},{5,3},{7,5},{... | collective-permute-start | bytes 393224 | tf_op jit(solution)/shard_map/ppermute | solution.py:390
  49.9 4.1 %collective-permute-start.12 = (f32[1,4,64,128]{3,2,1,0:T(8,128)S(1)}, f32[1,4,64,128]{3,2,1,0:T(8,128)S(1)}, u32[]{:S(2)}, u32[]{:S(2)}) collective-permute-start(f32[1,4,64,128]{3,2,1,0:T(8,128)S(1)} %collective-permute-done.11.refs_0_), channel_id=1, source_target_pairs={{0,1},{1,0},{2,3},{3,2},{4,5},{5,4},{6,7},{7,6},{8,9},{9,8},{10,11... | collective-permute-start | bytes 393224 | tf_op jit(solution)/shard_map/ppermute | solution.py:392
  54.0 1.3 collective-permute-start.14
  58.4 1.4 collective-permute-start.15
  73.1 10.7 %all-to-all-start.1 = ((f32[8,8,512]{2,1,0:T(8,128)}), f32[8,8,512]{2,1,0:T(8,128)S(1)}, u32[]{:S(2)}, u32[]{:S(2)}) async-start(f32[8,8,512]{2,1,0:T(8,128)} %broadcast_in_dim.2), calls=%async_computation.1 | async-start | bytes 262144 | tf_op jit(solution)/shard_map/all_to_all | solution.py:362
  76.4 95.8 %all-reduce.3.cloned.1.call-start = ((), (), s32[]{:S(2)}) async-start(), calls=%async_computation.2 | async-start | bytes 393216 | tf_op jit(solution)/shard_map/psum | solution.py:395
  77.9 186.9 %all-reduce.5.cloned.1.call-start = ((), (), s32[]{:S(2)}) async-start(), calls=%async_computation.3 | async-start | bytes 393216 | tf_op jit(solution)/shard_map/psum | solution.py:398
  83.7 187.0 %collective-permute-start.16 = (f32[64,512]{1,0:T(8,128)S(1)}, f32[64,512]{1,0:T(8,128)S(1)}, u32[]{:S(2)}, u32[]{:S(2)}) collective-permute-start(f32[64,512]{1,0:T(8,128)S(1)} %bitcast.6), channel_id=1, source_target_pairs={{0,1},{1,0},{2,3},{3,2},{4,5},{5,4},{6,7},{7,6},{8,9},{9,8},{10,11... | collective-permute-start | bytes 393224 | tf_op jit(solution)/shard_map/ppermute | solution.py:406
  177.1 0.9 copy-start.2
  264.8 0.9 copy-start.3
Sparse Core Ops, SparseCore 0:
  81.3 90.8 all-reduce.2
  176.2 88.5 all-reduce.4

commit v2 on v0

v2 whole, which is shorter than its diff:
```python
import functools
import math

import jax
import jax.numpy as jnp
from jax import lax
from jax.experimental import pallas as pl
from jax.experimental.pallas import tpu as pltpu
from jax.sharding import PartitionSpec as P

S = 3
center_shift = 2.0
half_range = 1.6
HIGHEST = lax.Precision.HIGHEST
VMEM_LIMIT = 48 * 1024 * 1024


def estimate(us):
    return pl.CostEstimate(flops=int(us * 1.15e9), bytes_accessed=0, transcendentals=0)


def split(x):
    high = x.astype(jnp.bfloat16)
    low = (x - high.astype(jnp.float32)).astype(jnp.bfloat16)
    return high, low


def pack_kernel(count, cross_local, layers, slots, info, sites, couplings, sigma, out):
    layer = pl.program_id(0)
    first = jnp.logical_and(layer == 0, info[1] == 1)
    last = jnp.logical_and(layer == layers - 1, info[2] == 1)
    for q in range(cross_local):
        place = info[0] * cross_local + q
        lead = None
        for k in range(2 * count):
            flag = first if k < count else last
            weight = jnp.where(jnp.logical_and(flag, sites[k] == place), -1.0, 0.0)
            term = sigma[k] * weight
            lead = term if lead is None else lead + term
        blocks = [couplings[0, q, j] for j in range(slots)] + [lead]
        row = jnp.concatenate(
            [jnp.concatenate(blocks[i : i + 2], axis=1) for i in range(0, slots + 1, 2)], axis=1
        )
        high, low = split(row)
        half = high.shape[0]
        out[q, :half] = high
        out[q, half:] = low


def pack(couplings, lead_sites, lead_sigma, info):
    layers, cross_local, slots, size, _ = couplings.shape
    contacts = lead_sigma.shape[0]
    body = functools.partial(pack_kernel, contacts // 2, cross_local, layers, slots)
    return pl.pallas_call(
        body,
        grid_spec=pltpu.PrefetchScalarGridSpec(
            num_scalar_prefetch=2,
            grid=(layers,),
            in_specs=[
                pl.BlockSpec((1, cross_local, slots, size, size), lambda i, *_: (i, 0, 0, 0, 0)),
                pl.BlockSpec((contacts, size, size), lambda i, *_: (0, 0, 0)),
            ],
            out_specs=pl.BlockSpec(
                (cross_local, 2 * size, (slots + 1) * size), lambda i, *_: (i, 0, 0)
            ),
        ),
        out_shape=jax.ShapeDtypeStruct(
            (layers * cross_local, 2 * size, (slots + 1) * size), jnp.bfloat16
        ),
        compiler_params=pltpu.CompilerParams(vmem_limit_bytes=VMEM_LIMIT),
        cost_estimate=estimate(1.5),
        name="pack",
    )(info, lead_sites, couplings, lead_sigma)


def step_kernel(first, last, slots, info, cols, packed, own, other, *refs):
    edges, refs = refs[:4], refs[4:]
    before, refs = (None, refs) if first else (refs[0], refs[1:])
    out, field = refs[0], refs[-1]
    layers, cross_local, size, columns = own.shape
    total = 2 * cross_local
    mine = info[0] * cross_local
    theirs = (1 - info[0]) * cross_local

    def put(place, x):
        high, low = split(x)
        field[place, :, :columns] = high
        field[place, :, columns:] = low

    for layer in range(layers):
        for q in range(cross_local):
            put((layer + 1) * total + mine + q, own[layer, q])
            put((layer + 1) * total + theirs + q, other[layer, q])
    even = info[3]
    for pair, place in enumerate((even, 1 - even)):
        for q in range(cross_local):
            put(place * (layers + 1) * total + mine + q, edges[2 * pair][0, q])
            put(place * (layers + 1) * total + theirs + q, edges[2 * pair + 1][0, q])
    for layer in range(layers):
        for q in range(cross_local):
            row = layer * cross_local + q
            places = [cols[layer, q, j] for j in range(slots)] + [total + mine + q]
            picked = jnp.concatenate([field[layer * total + c] for c in places], axis=0)
            acc = jnp.dot(packed[row], picked, preferred_element_type=jnp.float32)
            acc = acc[:, :columns] + acc[:, columns:]
            applied = acc[:size] + acc[size:]
            value = (applied - center_shift * own[layer, q]) * (1.0 / half_range)
            if not first:
                value = 2.0 * value - before[layer, q]
            out[layer, q] = value
    if not last:
        refs[1][0] = out[even * (layers - 1)]
        refs[2][0] = out[(1 - even) * (layers - 1)]


def step(packed, cols, info, own, other, edges, before, last):
    layers, cross_local, size, columns = own.shape
    rows, _, depth = packed.shape
    whole = pl.BlockSpec(memory_space=pltpu.VMEM)
    scalar = pl.BlockSpec(memory_space=pltpu.SMEM)
    args = [packed, own, other, *edges] + ([] if before is None else [before])
    edge = jax.ShapeDtypeStruct((1,) + own.shape[1:], jnp.float32)
    shapes = [jax.ShapeDtypeStruct(own.shape, jnp.float32)] + ([] if last else [edge, edge])
    return pl.pallas_call(
        functools.partial(step_kernel, before is None, last, cols.shape[2]),
        in_specs=[scalar, scalar] + [whole] * len(args),
        out_specs=[whole] * len(shapes),
        out_shape=shapes,
        scratch_shapes=[
            pltpu.VMEM(((layers + 2) * 2 * cross_local, size, 2 * columns), jnp.bfloat16)
        ],
        cost_estimate=estimate(1.7),
        compiler_params=pltpu.CompilerParams(vmem_limit_bytes=VMEM_LIMIT),
        name="step",
    )(info, cols, *args)


def gram_kernel(pairs, info, *refs):
    *powers, mine, theirs, block, held = refs
    columns = mine.shape[1]
    half = columns // 2
    for j, power in enumerate(powers):
        high, low = split(power[...].reshape(-1, columns))
        held[j, :, :columns] = high
        held[j, :, columns:] = low
    for place, (i, j) in enumerate(pairs):
        acc = lax.dot_general(
            held[i], held[j], (((0,), (0,)), ((), ())), preferred_element_type=jnp.float32
        )
        acc = acc[:, :columns] + acc[:, columns:]
        block[place] = acc[:columns] + acc[columns:]
        for core, out in ((info[0], mine), (1 - info[0], theirs)):
            rows = pl.ds(pl.multiple_of(core * half, half), half)
            out[place * half : (place + 1) * half, :] = block[place, rows, :]
    used = len(pairs) * half
    if used < mine.shape[0]:
        for out in (mine, theirs):
            out[used:, :] = jnp.zeros((mine.shape[0] - used, columns), jnp.float32)


def gram_blocks(powers, pairs, info, count):
    columns = powers[0].shape[-1]
    rows = powers[0].size // columns
    whole = pl.BlockSpec(memory_space=pltpu.VMEM)
    tall = share(len(pairs), columns, count) * count
    return pl.pallas_call(
        functools.partial(gram_kernel, pairs),
        in_specs=[pl.BlockSpec(memory_space=pltpu.SMEM)] + [whole] * len(powers),
        out_specs=[whole] * 2,
        out_shape=[jax.ShapeDtypeStruct((tall, columns), jnp.float32)] * 2,
        scratch_shapes=[
            pltpu.VMEM((len(pairs), columns, columns), jnp.float32),
            pltpu.VMEM((len(powers), rows, 2 * columns), jnp.bfloat16),
        ],
        cost_estimate=estimate(1.4),
        compiler_params=pltpu.CompilerParams(vmem_limit_bytes=VMEM_LIMIT),
        name="gram",
    )(info, *powers)


def share(blocks, columns, count):
    return -(-blocks * (columns // 2) // count)


def message_kernel(done, fresh, *refs):
    *ins, out = refs
    count = out.shape[0]
    if fresh:
        mine, theirs = ins[:2]
    if done:
        parts = ins[-1]
        width = parts.shape[1] - done
        acc = parts[0, width:, :]
        for p in range(1, count):
            acc = acc + parts[p, width:, :]
    for p in range(count):
        if done:
            out[p, :done, :] = acc
        if fresh:
            rows = slice(p * fresh, (p + 1) * fresh)
            out[p, done:, :] = mine[rows, :] + theirs[rows, :]


def message(halves, parts, done, count):
    whole = pl.BlockSpec(memory_space=pltpu.VMEM)
    args = list(halves) + ([] if parts is None else [parts])
    fresh = halves[0].shape[0] // count if halves else 0
    return pl.pallas_call(
        functools.partial(message_kernel, done, fresh),
        in_specs=[whole] * len(args),
        out_specs=whole,
        out_shape=jax.ShapeDtypeStruct((count, done + fresh, args[0].shape[-1]), jnp.float32),
        cost_estimate=estimate(0.3),
        compiler_params=pltpu.CompilerParams(vmem_limit_bytes=VMEM_LIMIT),
        name="message",
    )(*args)


def factor(block):
    size = block.shape[0]
    tall = 8
    tiles = size // tall
    lanes = lax.broadcasted_iota(jnp.int32, (tall, size), 1)
    sub = lax.broadcasted_iota(jnp.int32, (tall, size), 0)
    gram = [block[tall * t : tall * (t + 1)] for t in range(tiles)]
    unit = [jnp.where(lanes == sub + tall * t, 1.0, 0.0) for t in range(tiles)]

    def spread(row):
        return jnp.broadcast_to(row, (tall, size))

    for p in range(tiles):
        cols = [
            [
                jnp.broadcast_to(gram[t][:, tall * p + c : tall * p + c + 1], (tall, size))
                for t in range(p, tiles)
            ]
            for c in range(tall)
        ]
        scales = []
        for c in range(tall):
            scale = lax.rsqrt(spread(cols[c][0][c : c + 1]))
            scales.append(scale)
            cols[c] = [x * scale for x in cols[c]]
            cols[c][0] = jnp.where(sub > c, cols[c][0], 0.0)
            for d in range(c + 1, tall):
                weight = spread(cols[c][0][d : d + 1])
                cols[d] = [x - m * weight for x, m in zip(cols[d], cols[c])]
        for c in range(tall):
            row_gram = spread(gram[p][c : c + 1]) * scales[c]
            row_unit = spread(unit[p][c : c + 1]) * scales[c]
            gram[p] = jnp.where(sub == c, row_gram, gram[p] - cols[c][0] * row_gram)
            unit[p] = jnp.where(sub == c, row_unit, unit[p] - cols[c][0] * row_unit)
            for t in range(p + 1, tiles):
                m = cols[c][t - p]
                gram[t] = gram[t] - m * row_gram
                unit[t] = unit[t] - m * row_unit
    upper = [jnp.where(lanes >= sub + tall * t, gram[t], 0.0) for t in range(tiles)]
    return jnp.concatenate(upper, axis=0), jnp.concatenate(unit, axis=0)


def dot(a, b, dims=((1,), (0,))):
    return lax.dot_general(
        a, b, (dims, ((), ())), precision=HIGHEST, preferred_element_type=jnp.float32
    )


def column_kernel(place, first, row_share, scale, info, own, other, *refs):
    *refs, flat, gram = refs
    known, refs = (None, refs) if place == 0 else (refs[0], refs[1:])
    upper_known, refs = (None, refs) if place == 0 else (refs[0], refs[1:])
    upper_out, inverse_out = refs
    size = gram.shape[0]
    half = size // 2
    count = own.shape[0]
    at = place * size
    for core, source in ((info[0], own), (1 - info[0], other)):
        rows = pl.ds(pl.multiple_of(core * half, half), half)
        for p in range(count):
            flat[p * row_share : (p + 1) * row_share, :] = source[p, :row_share, :]
        for j in range(place + 1):
            gram[rows, j * size : (j + 1) * size] = flat[(first + j) * half : (first + j + 1) * half, :]
    corner = gram[:, at:]
    if place:
        above = dot(known[...], gram[:, :at], ((0,), (1,)))
        corner = corner - dot(above, above, ((0,), (0,)))
        carried = dot(known[...], above)
    upper, lower_inverse = factor(corner)
    upper_inverse = lower_inverse.T
    if place:
        upper_out[:at, :at] = upper_known[...] * scale
        inverse_out[:at, :at] = known[...]
        upper_out[:at, at:] = above * scale
        inverse_out[:at, at:] = -dot(carried, upper_inverse)
        upper_out[at:, :at] = jnp.zeros((size, at), jnp.float32)
        inverse_out[at:, :at] = jnp.zeros((size, at), jnp.float32)
    upper_out[at:, at:] = upper * scale
    inverse_out[at:, at:] = upper_inverse


def column(place, first, blocks, info, own, other, before, scale=1.0):
    whole = pl.BlockSpec(memory_space=pltpu.VMEM)
    count, _, size = own.shape
    row_share = share(blocks, size, count)
    args = [own, other, *before]
    square = jax.ShapeDtypeStruct(((place + 1) * size,) * 2, jnp.float32)
    return pl.pallas_call(
        functools.partial(column_kernel, place, first, row_share, scale),
        in_specs=[pl.BlockSpec(memory_space=pltpu.SMEM)] + [whole] * len(args),
        out_specs=[whole, whole],
        out_shape=[square, square],
        scratch_shapes=[
            pltpu.VMEM((count * row_share, size), jnp.float32),
            pltpu.VMEM((size, (place + 1) * size), jnp.float32),
        ],
        compiler_params=pltpu.CompilerParams(vmem_limit_bytes=VMEM_LIMIT),
        cost_estimate=estimate(4.5),
        name="column",
    )(info, *args)


def basis_kernel(scale, count, *refs):
    *powers, inverse, out, high, low = refs
    columns = powers[0].shape[-1]

    @pl.when(pl.program_id(0) == 0)
    def _():
        high[...], low[...] = split(inverse[...] * scale)

    pairs = [split(p[...].reshape(-1, columns)) for p in powers]
    wide = 2 * columns
    for start in range(0, count * columns, wide):
        stop = min(start + wide, count * columns)
        left_high = jnp.concatenate([p[0] for p in pairs[: stop // columns]], axis=1)
        left_low = jnp.concatenate([p[1] for p in pairs[: stop // columns]], axis=1)
        right = high[:stop, start:stop]
        acc = jnp.dot(left_high, right, preferred_element_type=jnp.float32)
        acc = acc + jnp.dot(left_low, right, preferred_element_type=jnp.float32)
        acc = acc + jnp.dot(left_high, low[:stop, start:stop], preferred_element_type=jnp.float32)
        out[:, :, :, start:stop] = acc.astype(jnp.bfloat16).reshape(out.shape[:3] + (stop - start,))


def basis_of(powers, inverse, scale):
    layers, cross_local, size, columns = powers[0].shape
    count = len(powers)
    full = count * columns
    return pl.pallas_call(
        functools.partial(basis_kernel, scale, count),
        grid=(layers,),
        in_specs=[pl.BlockSpec((1, cross_local, size, columns), lambda i: (i, 0, 0, 0))] * count
        + [pl.BlockSpec(inverse.shape, lambda i: (0, 0))],
        out_specs=pl.BlockSpec((1, cross_local, size, full), lambda i: (i, 0, 0, 0)),
        out_shape=jax.ShapeDtypeStruct((layers, cross_local, size, full), jnp.bfloat16),
        scratch_shapes=[pltpu.VMEM((full, full), jnp.bfloat16)] * 2,
        compiler_params=pltpu.CompilerParams(vmem_limit_bytes=VMEM_LIMIT),
        cost_estimate=estimate(3.0),
        name="basis",
    )(*powers, inverse)


def local(sources, couplings, block_cols, lead_sites, lead_sigma):
    layers, cross_local, size, columns = sources.shape
    cross_count = lax.axis_size("cross")
    count = lax.axis_size("trans")
    place = lax.axis_index("trans")
    even = 1 - place % 2
    info = jnp.stack([lax.axis_index("cross"), place == 0, place == count - 1, even]).astype(jnp.int32)
    packed = pack(couplings, lead_sites, lead_sigma, info)

    near = [(i, i + 1) for i in range(0, count - 1, 2)]
    far = [(i, i + 1) for i in range(1, count - 1, 2)]
    near, far = ([*x, *[(j, i) for i, j in x]] for x in (near, far))
    scale_rows = math.sqrt(count * layers * cross_local * cross_count * size)

    def swap(x):
        return lax.ppermute(x, "cross", [(0, 1), (1, 0)])

    def exchange(x):
        return lax.all_to_all(x, "trans", 0, 0, tiled=True)

    def ahead(pairs, parts, done):
        mine, theirs = gram_blocks(powers, pairs, info, count)
        return exchange(message((mine, swap(theirs)), parts, done, count))

    groups = (((0, 0), (1, 0), (1, 1)), ((2, 0), (2, 1), (2, 2)), tuple((S, j) for j in range(S + 1)))
    shares = [share(len(g), columns, count) for g in groups]
    powers = [sources]
    near_layer = lax.dynamic_slice_in_dim(sources, even * (layers - 1), 1)
    far_layer = lax.dynamic_slice_in_dim(sources, (1 - even) * (layers - 1), 1)
    parts, done = None, 0
    sums = []
    for k in range(S):
        field = powers[k]
        near_edge = lax.ppermute(near_layer, "trans", near)
        far_edge = lax.ppermute(far_layer, "trans", far)
        other = swap(field)
        if k == 0:
            near_edge, far_edge, packed = lax.optimization_barrier((near_edge, far_edge, packed))
        else:
            parts = ahead(groups[k - 1], parts, done)
            done = shares[k - 1]
            sums.append(parts)
        edges = (near_edge, swap(near_edge), far_edge, swap(far_edge))
        before = powers[k - 1] if k else None
        got = step(packed, block_cols, info, field, other, edges, before, k == S - 1)
        powers.append(got[0])
        if k < S - 1:
            near_layer, far_layer = got[1:]
    parts = ahead(groups[2], parts, done)
    first = column(0, 0, 3, info, sums[1], swap(sums[1]), ())
    second = column(1, 1, 3, info, sums[1], swap(sums[1]), first[::-1])
    last = exchange(message((), parts, shares[2], count))
    third = column(2, 0, 3, info, parts, swap(parts), second[::-1])
    r_factor, inverse = column(3, 0, 4, info, last, swap(last), third[::-1], 1.0 / scale_rows)
    return basis_of(powers, inverse, scale_rows), r_factor


def solution(mesh):
    return jax.shard_map(
        local,
        mesh=mesh,
        in_specs=(
            P(("energy", "trans"), "cross", None, None),
            P(("energy", "trans"), "cross", None, None, None),
            P("trans", "cross", None),
            P(),
            P("energy", None, None),
        ),
        out_specs=(P(("energy", "trans"), "cross", None, None), P("energy", None)),
        check_vma=False,
    )
```

time: 169 us -> 108 us (0.64)
  starting transfers between devices: 58.4 us -> 37.1 us
  local copies, waits for them, and re-layouts: 25.1 us -> 7.79 us
  matrix products: 14.7 us -> 0 us
  Pallas kernels: 28.7 us -> 39.3 us
  other arithmetic: 9.13 us -> 0.08 us
  waiting for transfers between devices: 29.8 us -> 21.7 us
    all_to_all x8 -> x4, waiting for transfers between devices: 28 us -> 7.86 us  [exchange(): return lax.all_to_all(x, 'trans', 0, 0, tiled=True)]
    all_to_all x8 -> x4, starting transfers between devices: 39.9 us -> 22.4 us  [exchange(): return lax.all_to_all(x, 'trans', 0, 0, tiled=True)]
    dot_general x5 -> x0, matrix products: 14.7 us -> none  [the longest x4 10.8 us: local(): lax.dot_general(krylov, field.reshape(-1, columns), (((0,), (0,)), ((), (...]
    ppermute x12 -> x21, waiting for transfers between devices: 1.83 us -> 13.9 us  [the longest x3 9.57 us: local(): near_edge = lax.ppermute(near_layer, 'trans', near)]
    pallas_call x7 -> x15, Pallas kernels: 27.3 us -> 37.9 us  [the longest x4 23.1 us: column(): pl.pallas_call(functools.partial(column_kernel, place, first, row_share,...]
    dot_general x4 -> x0, local copies, waits for them, and re-layouts: 9.77 us -> none  [local(): lax.dot_general(krylov, field.reshape(-1, columns), (((0,), (0,)), ((), (...]
    dot_general x3 -> x0, other arithmetic: 6.02 us -> none  [local(): lax.dot_general(krylov, field.reshape(-1, columns), (((0,), (0,)), ((), (...]
    ppermute x12 -> x21, starting transfers between devices: 18.5 us -> 14.7 us  [the longest x3 8.94 us: local(): near_edge = lax.ppermute(near_layer, 'trans', near)]
  transfers between devices with their start and end apart: 20 -> 25, of which waited for: 6 -> 11; matrix products, arithmetic and copies ran while one was open for 23% -> 1% of each run, Pallas kernels for 14% -> 25%
where the time goes in v2:
time: 108 us; the launch traced here: 107 us
  Pallas kernels  39.3 us (36%)
  starting transfers between devices  37.1 us (34%)
  waiting for transfers between devices  21.7 us (20%)
  local copies, waits for them, and re-layouts  7.79 us (7%)
    pallas_call x4, Pallas kernels, column(): pl.pallas_call(functools.partial(column_kernel, place, first, row_share,...  23.1 us
    all_to_all x4, starting transfers between devices, exchange(): return lax.all_to_all(x, 'trans', 0, 0, tiled=True)  22.4 us
    ppermute x3, waiting for transfers between devices, local(): near_edge = lax.ppermute(near_layer, 'trans', near)  9.57 us
    ppermute x3, starting transfers between devices, local(): near_edge = lax.ppermute(near_layer, 'trans', near)  8.94 us
    all_to_all x4, waiting for transfers between devices, exchange(): return lax.all_to_all(x, 'trans', 0, 0, tiled=True)  7.86 us
    unnamed x20, local copies, waits for them, and re-layouts  6.8 us
    pallas_call x3, Pallas kernels, step(): pl.pallas_call(functools.partial(step_kernel, before is None, last, cols....  5.05 us
    ppermute x15, waiting for transfers between devices, swap(): return lax.ppermute(x, 'cross', [(0, 1), (1, 0)])  4.3 us
  transfers between devices with their start and end apart: 25, of which 11 were waited for; matrix products, arithmetic and copies ran while one was open for 1% of the time, Pallas kernels for 25%

profile of v2, /device:TPU:0, one launch (start us, length us, event | category | flops | bytes accessed | tf_op | source)
XLA Modules:
  0.0 106.9 jit_solution(17875267639302577082)
XLA Ops:
  0.6 0.5 collective-permute-start.2
  1.2 1.0 constant_dynamic-slice_fusion
  2.2 2.6 %collective-permute-start = (f32[1,4,64,128]{3,2,1,0:T(8,128)S(1)}, f32[1,4,64,128]{3,2,1,0:T(8,128)S(1)}, u32[]{:S(2)}, u32[]{:S(2)}) collective-permute-start(f32[1,4,64,128]{3,2,1,0:T(8,128)S(1)} %get-tuple-element.49), channel_id=1, source_target_pairs={{0,2},{4,6},{8,10},{12,14},{2,0},{6,4},{10,8},{14,12},{1,3},{5,7},... | collective-permute-start | bytes 393224 | tf_op jit(solution)/shard_map/ppermute | solution.py:393
  4.8 0.7 collective-permute-start.1
  5.6 2.0 %copy-done.1 = f32[4,4,7,64,64]{4,3,2,1,0:T(8,128)S(1)} copy-done((f32[4,4,7,64,64]{4,3,2,1,0:T(8,128)S(1)}, f32[4,4,7,64,64]{4,3,2,1,0:T(8,128)}, u32[]{:S(2)}) %copy-start.1) | copy-done | bytes 1835032
  7.6 0.9 copy-done.2
  8.5 0.7 copy-done.4
  9.2 1.4 %pack.1.packed = bf16[16,128,512]{2,1,0:T(8,128)(2,1)S(1)} custom-call(s32[4]{0:T(128)S(1)} %pad_add_fusion.info, s32[4]{0:T(128)S(1)} %copy-done.4, f32[4,4,7,64,64]{4,3,2,1,0:T(8,128)S(1)} %copy-done.1, f32[4,64,64]{2,1,0:T(8,128)S(1)} %copy-done.2), custom_call_target="tpu_custom_call" | custom-call | flops 1724999936 | tf_op jit(solution)/shard_map/pack/pallas_call | solution.py:54
  10.8 0.4 collective-permute-start.4
  11.2 0.8 collective-permute-done.3.refs_1_
  12.2 1.7 %step.3 = (f32[4,4,64,128]{3,2,1,0:T(8,128)S(1)}, f32[1,4,64,128]{3,2,1,0:T(8,128)S(1)}, f32[1,4,64,128]{3,2,1,0:T(8,128)S(1)}) custom-call(s32[4]{0:T(128)S(1)} %pad_add_fusion.info, s32[4,4,7]{2,1,0:T(4,128)S(1)} %copy-done.3, bf16[16,128,512]{2,1,0:T(8,128)(2,1)S(1)} %pack.1.packed, f32[4,4,64,128]{3,2,1,0:T(8,128)S(1)} %copy-done, ...), custom_call_target="tpu_custom_call" | custom-call | flops 1955000064 | tf_op jit(solution)/shard_map/step/pallas_call | solution.py:124
  13.9 0.4 collective-permute-start.5
  14.3 4.3 %collective-permute-start.6 = (f32[1,4,64,128]{3,2,1,0:T(8,128)S(1)}, f32[1,4,64,128]{3,2,1,0:T(8,128)S(1)}, u32[]{:S(2)}, u32[]{:S(2)}) collective-permute-start(f32[1,4,64,128]{3,2,1,0:T(8,128)S(1)} %get-tuple-element.29), channel_id=1, source_target_pairs={{0,2},{4,6},{8,10},{12,14},{2,0},{6,4},{10,8},{14,12},{1,3},{5,7},... | collective-permute-start | bytes 393224 | tf_op jit(solution)/shard_map/ppermute | solution.py:393
  18.6 0.7 collective-permute-start.8
  19.2 3.2 %collective-permute-done.6.refs_0_ = f32[1,4,64,128]{3,2,1,0:T(8,128)S(1)} collective-permute-done((f32[1,4,64,128]{3,2,1,0:T(8,128)S(1)}, f32[1,4,64,128]{3,2,1,0:T(8,128)S(1)}, u32[]{:S(2)}, u32[]{:S(2)}) %collective-permute-start.6) | collective-permute-done | bytes 131104 | tf_op jit(solution)/shard_map/ppermute | solution.py:393
  22.4 0.5 collective-permute-start.9
  22.9 1.2 %gram.5 = (f32[192,128]{1,0:T(8,128)S(1)}, f32[192,128]{1,0:T(8,128)S(1)}) custom-call(s32[4]{0:T(128)S(1)} %pad_add_fusion.info, f32[4,4,64,128]{3,2,1,0:T(8,128)S(1)} %copy-done, f32[4,4,64,128]{3,2,1,0:T(8,128)S(1)} %get-tuple-element.28.own.refs_4_.refs_1_), custom_call_target="tpu_custom_call" | custom-call | flops 1610000000 | tf_op jit(solution)/shard_map/gram/pallas_call | solution.py:166
  24.2 1.3 %collective-permute-done.17.refs_1_ = f32[192,128]{1,0:T(8,128)S(1)} collective-permute-done((f32[192,128]{1,0:T(8,128)S(1)}, f32[192,128]{1,0:T(8,128)S(1)}, u32[]{:S(2)}, u32[]{:S(2)}) %collective-permute-start.17) | collective-permute-done | bytes 98336 | tf_op jit(solution)/shard_map/ppermute | solution.py:375
  25.5 0.7 message.4
  26.2 7.8 %all-to-all-start = ((f32[8,24,128]{2,1,0:T(8,128)}), f32[8,24,128]{2,1,0:T(8,128)S(1)}, u32[]{:S(2)}, u32[]{:S(2)}) async-start(f32[8,24,128]{2,1,0:T(8,128)} %message.4), calls=%async_computation | async-start | bytes 196608 | tf_op jit(solution)/shard_map/all_to_all | solution.py:378
  34.0 1.6 %copy-done.6 = bf16[16,128,512]{2,1,0:T(8,128)(2,1)S(1)} copy-done((bf16[16,128,512]{2,1,0:T(8,128)(2,1)S(1)}, bf16[16,128,512]{2,1,0:T(8,128)(2,1)}, u32[]{:S(2)}) %copy-start.6) | copy-done | bytes 2097176
  35.5 1.7 %step.4 = (f32[4,4,64,128]{3,2,1,0:T(8,128)S(1)}, f32[1,4,64,128]{3,2,1,0:T(8,128)S(1)}, f32[1,4,64,128]{3,2,1,0:T(8,128)S(1)}) custom-call(s32[4]{0:T(128)S(1)} %pad_add_fusion.info, s32[4,4,7]{2,1,0:T(4,128)S(1)} %copy-done.3, bf16[16,128,512]{2,1,0:T(8,128)(2,1)S(1)} %copy-done.6, f32[4,4,64,128]{3,2,1,0:T(8,128)S(1)} %get-tuple-element.28.own.refs_4_.refs_1_, ...), custom_call_target="tpu_custom_call" | custom-call | flops 1955000064 | tf_op jit(solution)/shard_map/step/pallas_call | solution.py:124
  37.4 1.3 %gram.4 = (f32[192,128]{1,0:T(8,128)S(1)}, f32[192,128]{1,0:T(8,128)S(1)}) custom-call(s32[4]{0:T(128)S(1)} %pad_add_fusion.info, f32[4,4,64,128]{3,2,1,0:T(8,128)S(1)} %copy-done, f32[4,4,64,128]{3,2,1,0:T(8,128)S(1)} %get-tuple-element.28.own.refs_4_.refs_1_, f32[4,4,64,128]{3,2,1,0:T(8,128)S(1)} %get-tuple-element.31.own.refs_2_), custom_call_target="tpu_custom_call" | custom-call | flops 1610000000 | tf_op jit(solution)/shard_map/gram/pallas_call | solution.py:166
  38.6 0.5 collective-permute-start.16
  39.2 1.9 %all-to-all-done.refs_2_ = f32[8,24,128]{2,1,0:T(8,128)S(1)} async-done(((f32[8,24,128]{2,1,0:T(8,128)}), f32[8,24,128]{2,1,0:T(8,128)S(1)}, u32[]{:S(2)}, u32[]{:S(2)}) %all-to-all-start) | async-done | bytes 98336 | tf_op jit(solution)/shard_map/all_to_all | solution.py:378
  41.0 0.7 message.5
  41.7 5.1 %all-to-all-start.1 = ((f32[8,48,128]{2,1,0:T(8,128)}), f32[8,48,128]{2,1,0:T(8,128)S(1)}, u32[]{:S(2)}, u32[]{:S(2)}) async-start(f32[8,48,128]{2,1,0:T(8,128)} %message.5), calls=%async_computation.1 | async-start | bytes 393216 | tf_op jit(solution)/shard_map/all_to_all | solution.py:378
  46.8 2.0 %collective-permute-start.11 = (f32[1,4,64,128]{3,2,1,0:T(8,128)S(1)}, f32[1,4,64,128]{3,2,1,0:T(8,128)S(1)}, u32[]{:S(2)}, u32[]{:S(2)}) collective-permute-start(f32[1,4,64,128]{3,2,1,0:T(8,128)S(1)} %get-tuple-element.32), channel_id=1, source_target_pairs={{0,2},{4,6},{8,10},{12,14},{2,0},{6,4},{10,8},{14,12},{1,3},{5,7},... | collective-permute-start | bytes 393224 | tf_op jit(solution)/shard_map/ppermute | solution.py:393
  48.8 0.7 collective-permute-start.13
  49.5 6.4 %collective-permute-done.11.refs_0_ = f32[1,4,64,128]{3,2,1,0:T(8,128)S(1)} collective-permute-done((f32[1,4,64,128]{3,2,1,0:T(8,128)S(1)}, f32[1,4,64,128]{3,2,1,0:T(8,128)S(1)}, u32[]{:S(2)}, u32[]{:S(2)}) %collective-permute-start.11) | collective-permute-done | bytes 131104 | tf_op jit(solution)/shard_map/ppermute | solution.py:393
  55.9 0.5 collective-permute-start.14
  56.5 0.8 collective-permute-done.12.refs_1_
  57.4 1.6 %copy-done.7 = bf16[16,128,512]{2,1,0:T(8,128)(2,1)S(1)} copy-done((bf16[16,128,512]{2,1,0:T(8,128)(2,1)S(1)}, bf16[16,128,512]{2,1,0:T(8,128)(2,1)}, u32[]{:S(2)}) %copy-start.7) | copy-done | bytes 2097176
  59.0 1.7 %step.5.refs_3_ = f32[4,4,64,128]{3,2,1,0:T(8,128)S(1)} custom-call(s32[4]{0:T(128)S(1)} %pad_add_fusion.info, s32[4,4,7]{2,1,0:T(4,128)S(1)} %copy-done.3, bf16[16,128,512]{2,1,0:T(8,128)(2,1)S(1)} %copy-done.7, f32[4,4,64,128]{3,2,1,0:T(8,128)S(1)} %get-tuple-element.31.own.refs_2_, f32[4,4,64,128]{3,2,1,0:T(8,128)S(1)} %collective-permute-done.10.other, ...), custom_call_target="tpu_custom_call" | custom-call | flops 1955000064 | tf_op jit(solution)/shard_map/step/pallas_call | solution.py:124
  60.7 1.4 %gram.3 = (f32[256,128]{1,0:T(8,128)S(1)}, f32[256,128]{1,0:T(8,128)S(1)}) custom-call(s32[4]{0:T(128)S(1)} %pad_add_fusion.info, f32[4,4,64,128]{3,2,1,0:T(8,128)S(1)} %copy-done, f32[4,4,64,128]{3,2,1,0:T(8,128)S(1)} %get-tuple-element.28.own.refs_4_.refs_1_, f32[4,4,64,128]{3,2,1,0:T(8,128)S(1)} %get-tuple-element.31.own.refs_2_, ...), custom_call_target="tpu_custom_call" | custom-call | flops 1610000000 | tf_op jit(solution)/shard_map/gram/pallas_call | solution.py:166
  62.1 0.4 collective-permute-start.15
  62.5 1.0 collective-permute-done.15.refs_1_
  63.6 0.7 message.6
  64.3 6.1 %all-to-all-start.2 = ((f32[8,56,128]{2,1,0:T(8,128)}), f32[8,56,128]{2,1,0:T(8,128)S(1)}, u32[]{:S(2)}, u32[]{:S(2)}) async-start(f32[8,56,128]{2,1,0:T(8,128)} %message.6), calls=%async_computation.2 | async-start | bytes 458752 | tf_op jit(solution)/shard_map/all_to_all | solution.py:378
  70.3 4.6 %column.4 = (f32[128,128]{1,0:T(8,128)S(1)}, f32[128,128]{1,0:T(8,128)S(1)}) custom-call(s32[4]{0:T(128)S(1)} %pad_add_fusion.info, f32[8,48,128]{2,1,0:T(8,128)S(1)} %all-to-all-done.1.refs_2_.own, f32[8,48,128]{2,1,0:T(8,128)S(1)} %collective-permute-done.20.other), custom_call_target="tpu_custom_call" | custom-call | flops 5175000064 | tf_op jit(solution)/shard_map/column/pallas_call | solution.py:306
  74.9 4.3 %all-to-all-done.2.refs_0_.own = f32[8,56,128]{2,1,0:T(8,128)S(1)} async-done(((f32[8,56,128]{2,1,0:T(8,128)}), f32[8,56,128]{2,1,0:T(8,128)S(1)}, u32[]{:S(2)}, u32[]{:S(2)}) %all-to-all-start.2) | async-done | bytes 229408 | tf_op jit(solution)/shard_map/all_to_all | solution.py:378
  79.2 0.7 message.7
  79.9 3.6 %all-to-all-start.3 = ((f32[8,32,128]{2,1,0:T(8,128)}), f32[8,32,128]{2,1,0:T(8,128)S(1)}, u32[]{:S(2)}, u32[]{:S(2)}) async-start(f32[8,32,128]{2,1,0:T(8,128)} %message.7), calls=%async_computation.3 | async-start | bytes 262144 | tf_op jit(solution)/shard_map/all_to_all | solution.py:378
  83.6 5.4 %column.5 = (f32[256,256]{1,0:T(8,128)S(1)}, f32[256,256]{1,0:T(8,128)S(1)}) custom-call(s32[4]{0:T(128)S(1)} %pad_add_fusion.info, f32[8,48,128]{2,1,0:T(8,128)S(1)} %all-to-all-done.1.refs_2_.own, f32[8,48,128]{2,1,0:T(8,128)S(1)} %collective-permute-done.20.other, f32[128,128]{1,0:T(8,128)S(1)} %get-tuple-element.40.refs_0_, ...), custom_call_target="tpu_custom_call" | custom-call | flops 5175000064 | tf_op jit(solution)/shard_map/column/pallas_call | solution.py:306
  89.0 1.6 %all-to-all-done.3.own = f32[8,32,128]{2,1,0:T(8,128)S(1)} async-done(((f32[8,32,128]{2,1,0:T(8,128)}), f32[8,32,128]{2,1,0:T(8,128)S(1)}, u32[]{:S(2)}, u32[]{:S(2)}) %all-to-all-start.3) | async-done | bytes 131104 | tf_op jit(solution)/shard_map/all_to_all | solution.py:378
  90.6 5.9 %column.6 = (f32[384,384]{1,0:T(8,128)S(1)}, f32[384,384]{1,0:T(8,128)S(1)}) custom-call(s32[4]{0:T(128)S(1)} %pad_add_fusion.info, f32[8,56,128]{2,1,0:T(8,128)S(1)} %all-to-all-done.2.refs_0_.own, f32[8,56,128]{2,1,0:T(8,128)S(1)} %collective-permute-done.19.other, f32[256,256]{1,0:T(8,128)S(1)} %get-tuple-element.42.refs_0_, ...), custom_call_target="tpu_custom_call" | custom-call | flops 5175000064 | tf_op jit(solution)/shard_map/column/pallas_call | solution.py:306
  96.6 7.2 %column.7 = (f32[512,512]{1,0:T(8,128)}, f32[512,512]{1,0:T(8,128)S(1)}) custom-call(s32[4]{0:T(128)S(1)} %pad_add_fusion.info, f32[8,32,128]{2,1,0:T(8,128)S(1)} %all-to-all-done.3.own, f32[8,32,128]{2,1,0:T(8,128)S(1)} %collective-permute-done.18.other, f32[384,384]{1,0:T(8,128)S(1)} %get-tuple-element.44.refs_0_, f32[384,384]{1,0:T(8,128)S(1)} %get-tuple-element.45.refs_1_), custom_call_target="tpu_custom_call" | custom-call | flops 5175000064 | tf_op jit(solution)/shard_map/column/pallas_call | solution.py:306
  103.8 3.1 %basis.1 = bf16[4,4,64,512]{3,2,1,0:T(8,128)(2,1)} custom-call(f32[4,4,64,128]{3,2,1,0:T(8,128)S(1)} %copy-done, f32[4,4,64,128]{3,2,1,0:T(8,128)S(1)} %get-tuple-element.28.own.refs_4_.refs_1_, f32[4,4,64,128]{3,2,1,0:T(8,128)S(1)} %get-tuple-element.31.own.refs_2_, f32[4,4,64,128]{3,2,1,0:T(8,128)S(1)} %copy-done.9, f32[512,512]{1,0:T(8,128)S(1)} %get-tuple-element.46.refs_4_), custom_call_target="tpu_custom_call" | custom-call | flops 3449999872 | tf_op jit(solution)/shard_map/basis/pallas_call | solution.py:346
  (40 shorter events, 1.1 us)
Async XLA Ops:
  0.6 11.6 %copy-start = (f32[4,4,64,128]{3,2,1,0:T(8,128)S(1)}, f32[4,4,64,128]{3,2,1,0:T(8,128)}, u32[]{:S(2)}) copy-start(f32[4,4,64,128]{3,2,1,0:T(8,128)} %refs_0_.7) | copy-start | bytes 1572868
  0.6 11.6 %copy-start.3 = (s32[4,4,7]{2,1,0:T(4,128)S(1)}, s32[4,4,7]{2,1,0:T(4,128)}, u32[]{:S(2)}) copy-start(s32[4,4,7]{2,1,0:T(4,128)} %cols.5) | copy-start | bytes 1348
  0.6 11.6 %collective-permute-start.2 = (f32[4,4,64,128]{3,2,1,0:T(8,128)}, f32[4,4,64,128]{3,2,1,0:T(8,128)S(1)}, u32[]{:S(2)}, u32[]{:S(2)}) collective-permute-start(f32[4,4,64,128]{3,2,1,0:T(8,128)} %refs_0_.7), channel_id=1, source_target_pairs={{0,1},{1,0},{2,3},{3,2},{4,5},{5,4},{6,7},{7,6},{8,9},{9,8},{10,11... | collective-permute-start | bytes 1572872 | tf_op jit(solution)/shard_map/ppermute | solution.py:375
  2.2 8.4 %collective-permute-start = (f32[1,4,64,128]{3,2,1,0:T(8,128)S(1)}, f32[1,4,64,128]{3,2,1,0:T(8,128)S(1)}, u32[]{:S(2)}, u32[]{:S(2)}) collective-permute-start(f32[1,4,64,128]{3,2,1,0:T(8,128)S(1)} %get-tuple-element.49), channel_id=1, source_target_pairs={{0,2},{4,6},{8,10},{12,14},{2,0},{6,4},{10,8},{14,12},{1,3},{5,7},... | collective-permute-start | bytes 393224 | tf_op jit(solution)/shard_map/ppermute | solution.py:393
  4.8 5.8 %collective-permute-start.1 = (f32[1,4,64,128]{3,2,1,0:T(8,128)S(1)}, f32[1,4,64,128]{3,2,1,0:T(8,128)S(1)}, u32[]{:S(2)}, u32[]{:S(2)}) collective-permute-start(f32[1,4,64,128]{3,2,1,0:T(8,128)S(1)} %get-tuple-element.48), channel_id=1, source_target_pairs={{2,4},{6,8},{10,12},{4,2},{8,6},{12,10},{3,5},{7,9},{11,13},{5,3},... | collective-permute-start | bytes 393224 | tf_op jit(solution)/shard_map/ppermute | solution.py:394
  5.6 2.0 %copy-start.1 = (f32[4,4,7,64,64]{4,3,2,1,0:T(8,128)S(1)}, f32[4,4,7,64,64]{4,3,2,1,0:T(8,128)}, u32[]{:S(2)}) copy-start(f32[4,4,7,64,64]{4,3,2,1,0:T(8,128)} %couplings.1) | copy-start | bytes 5505028
  7.6 0.9 copy-start.2
  8.5 0.7 copy-start.4
  10.6 13.5 %copy-start.5 = (bf16[16,128,512]{2,1,0:T(8,128)(2,1)}, bf16[16,128,512]{2,1,0:T(8,128)(2,1)S(1)}, u32[]{:S(2)}) copy-start(bf16[16,128,512]{2,1,0:T(8,128)(2,1)S(1)} %pack.1.packed) | copy-start | bytes 6291460
  10.6 1.4 %collective-permute-start.3 = (f32[1,4,64,128]{3,2,1,0:T(8,128)S(1)}, f32[1,4,64,128]{3,2,1,0:T(8,128)S(1)}, u32[]{:S(2)}, u32[]{:S(2)}) collective-permute-start(f32[1,4,64,128]{3,2,1,0:T(8,128)S(1)} %collective-permute-done.refs_0_), channel_id=1, source_target_pairs={{0,1},{1,0},{2,3},{3,2},{4,5},{5,4},{6,7},{7,6},{8,9},{9,8},{10,11... | collective-permute-start | bytes 393224 | tf_op jit(solution)/shard_map/ppermute | solution.py:375
  10.8 1.4 %collective-permute-start.4 = (f32[1,4,64,128]{3,2,1,0:T(8,128)S(1)}, f32[1,4,64,128]{3,2,1,0:T(8,128)S(1)}, u32[]{:S(2)}, u32[]{:S(2)}) collective-permute-start(f32[1,4,64,128]{3,2,1,0:T(8,128)S(1)} %collective-permute-done.1.refs_2_), channel_id=1, source_target_pairs={{0,1},{1,0},{2,3},{3,2},{4,5},{5,4},{6,7},{7,6},{8,9},{9,8},{10,11... | collective-permute-start | bytes 393224 | tf_op jit(solution)/shard_map/ppermute | solution.py:375
  13.9 20.0 %collective-permute-start.5 = (f32[4,4,64,128]{3,2,1,0:T(8,128)S(1)}, f32[4,4,64,128]{3,2,1,0:T(8,128)S(1)}, u32[]{:S(2)}, u32[]{:S(2)}) collective-permute-start(f32[4,4,64,128]{3,2,1,0:T(8,128)S(1)} %get-tuple-element.28.own.refs_4_.refs_1_), channel_id=1, source_target_pairs={{0,1},{1,0},{2,3},{3,2},{4,5},{5,4},{6,7},{7,6},{8,9},{9,8},{10,11... | collective-permute-start | bytes 1572872 | tf_op jit(solution)/shard_map/ppermute | solution.py:375
  14.3 8.1 %collective-permute-start.6 = (f32[1,4,64,128]{3,2,1,0:T(8,128)S(1)}, f32[1,4,64,128]{3,2,1,0:T(8,128)S(1)}, u32[]{:S(2)}, u32[]{:S(2)}) collective-permute-start(f32[1,4,64,128]{3,2,1,0:T(8,128)S(1)} %get-tuple-element.29), channel_id=1, source_target_pairs={{0,2},{4,6},{8,10},{12,14},{2,0},{6,4},{10,8},{14,12},{1,3},{5,7},... | collective-permute-start | bytes 393224 | tf_op jit(solution)/shard_map/ppermute | solution.py:393
  18.6 3.9 %collective-permute-start.8 = (f32[1,4,64,128]{3,2,1,0:T(8,128)S(1)}, f32[1,4,64,128]{3,2,1,0:T(8,128)S(1)}, u32[]{:S(2)}, u32[]{:S(2)}) collective-permute-start(f32[1,4,64,128]{3,2,1,0:T(8,128)S(1)} %get-tuple-element.30), channel_id=1, source_target_pairs={{2,4},{6,8},{10,12},{4,2},{8,6},{12,10},{3,5},{7,9},{11,13},{5,3},... | collective-permute-start | bytes 393224 | tf_op jit(solution)/shard_map/ppermute | solution.py:394
  22.4 11.5 %collective-permute-start.7 = (f32[1,4,64,128]{3,2,1,0:T(8,128)S(1)}, f32[1,4,64,128]{3,2,1,0:T(8,128)S(1)}, u32[]{:S(2)}, u32[]{:S(2)}) collective-permute-start(f32[1,4,64,128]{3,2,1,0:T(8,128)S(1)} %collective-permute-done.6.refs_0_), channel_id=1, source_target_pairs={{0,1},{1,0},{2,3},{3,2},{4,5},{5,4},{6,7},{7,6},{8,9},{9,8},{10,11... | collective-permute-start | bytes 393224 | tf_op jit(solution)/shard_map/ppermute | solution.py:375
  22.4 11.5 %collective-permute-start.9 = (f32[1,4,64,128]{3,2,1,0:T(8,128)S(1)}, f32[1,4,64,128]{3,2,1,0:T(8,128)S(1)}, u32[]{:S(2)}, u32[]{:S(2)}) collective-permute-start(f32[1,4,64,128]{3,2,1,0:T(8,128)S(1)} %collective-permute-done.8.refs_2_), channel_id=1, source_target_pairs={{0,1},{1,0},{2,3},{3,2},{4,5},{5,4},{6,7},{7,6},{8,9},{9,8},{10,11... | collective-permute-start | bytes 393224 | tf_op jit(solution)/shard_map/ppermute | solution.py:375
  24.1 1.4 %collective-permute-start.17 = (f32[192,128]{1,0:T(8,128)S(1)}, f32[192,128]{1,0:T(8,128)S(1)}, u32[]{:S(2)}, u32[]{:S(2)}) collective-permute-start(f32[192,128]{1,0:T(8,128)S(1)} %get-tuple-element.39), channel_id=1, source_target_pairs={{0,1},{1,0},{2,3},{3,2},{4,5},{5,4},{6,7},{7,6},{8,9},{9,8},{10,11... | collective-permute-start | bytes 294920 | tf_op jit(solution)/shard_map/ppermute | solution.py:375
  26.2 14.9 %all-to-all-start = ((f32[8,24,128]{2,1,0:T(8,128)}), f32[8,24,128]{2,1,0:T(8,128)S(1)}, u32[]{:S(2)}, u32[]{:S(2)}) async-start(f32[8,24,128]{2,1,0:T(8,128)} %message.4), calls=%async_computation | async-start | bytes 196608 | tf_op jit(solution)/shard_map/all_to_all | solution.py:378
  33.9 1.6 %copy-start.6 = (bf16[16,128,512]{2,1,0:T(8,128)(2,1)S(1)}, bf16[16,128,512]{2,1,0:T(8,128)(2,1)}, u32[]{:S(2)}) copy-start(bf16[16,128,512]{2,1,0:T(8,128)(2,1)} %copy-done.5) | copy-start | bytes 6291460
  37.2 20.2 %collective-permute-start.10 = (f32[4,4,64,128]{3,2,1,0:T(8,128)S(1)}, f32[4,4,64,128]{3,2,1,0:T(8,128)S(1)}, u32[]{:S(2)}, u32[]{:S(2)}) collective-permute-start(f32[4,4,64,128]{3,2,1,0:T(8,128)S(1)} %get-tuple-element.31.own.refs_2_), channel_id=1, source_target_pairs={{0,1},{1,0},{2,3},{3,2},{4,5},{5,4},{6,7},{7,6},{8,9},{9,8},{10,11... | collective-permute-start | bytes 1572872 | tf_op jit(solution)/shard_map/ppermute | solution.py:375
  38.6 2.4 %collective-permute-start.16 = (f32[192,128]{1,0:T(8,128)S(1)}, f32[192,128]{1,0:T(8,128)S(1)}, u32[]{:S(2)}, u32[]{:S(2)}) collective-permute-start(f32[192,128]{1,0:T(8,128)S(1)} %get-tuple-element.37), channel_id=1, source_target_pairs={{0,1},{1,0},{2,3},{3,2},{4,5},{5,4},{6,7},{7,6},{8,9},{9,8},{10,11... | collective-permute-start | bytes 294920 | tf_op jit(solution)/shard_map/ppermute | solution.py:375
  41.7 14.6 %all-to-all-start.1 = ((f32[8,48,128]{2,1,0:T(8,128)}), f32[8,48,128]{2,1,0:T(8,128)S(1)}, u32[]{:S(2)}, u32[]{:S(2)}) async-start(f32[8,48,128]{2,1,0:T(8,128)} %message.5), calls=%async_computation.1 | async-start | bytes 393216 | tf_op jit(solution)/shard_map/all_to_all | solution.py:378
  46.8 9.1 %collective-permute-start.11 = (f32[1,4,64,128]{3,2,1,0:T(8,128)S(1)}, f32[1,4,64,128]{3,2,1,0:T(8,128)S(1)}, u32[]{:S(2)}, u32[]{:S(2)}) collective-permute-start(f32[1,4,64,128]{3,2,1,0:T(8,128)S(1)} %get-tuple-element.32), channel_id=1, source_target_pairs={{0,2},{4,6},{8,10},{12,14},{2,0},{6,4},{10,8},{14,12},{1,3},{5,7},... | collective-permute-start | bytes 393224 | tf_op jit(solution)/shard_map/ppermute | solution.py:393
  48.8 7.1 %collective-permute-start.13 = (f32[1,4,64,128]{3,2,1,0:T(8,128)S(1)}, f32[1,4,64,128]{3,2,1,0:T(8,128)S(1)}, u32[]{:S(2)}, u32[]{:S(2)}) collective-permute-start(f32[1,4,64,128]{3,2,1,0:T(8,128)S(1)} %get-tuple-element.33), channel_id=1, source_target_pairs={{2,4},{6,8},{10,12},{4,2},{8,6},{12,10},{3,5},{7,9},{11,13},{5,3},... | collective-permute-start | bytes 393224 | tf_op jit(solution)/shard_map/ppermute | solution.py:394
  55.9 1.3 %collective-permute-start.12 = (f32[1,4,64,128]{3,2,1,0:T(8,128)S(1)}, f32[1,4,64,128]{3,2,1,0:T(8,128)S(1)}, u32[]{:S(2)}, u32[]{:S(2)}) collective-permute-start(f32[1,4,64,128]{3,2,1,0:T(8,128)S(1)} %collective-permute-done.11.refs_0_), channel_id=1, source_target_pairs={{0,1},{1,0},{2,3},{3,2},{4,5},{5,4},{6,7},{7,6},{8,9},{9,8},{10,11... | collective-permute-start | bytes 393224 | tf_op jit(solution)/shard_map/ppermute | solution.py:375
  55.9 1.5 %collective-permute-start.14 = (f32[1,4,64,128]{3,2,1,0:T(8,128)S(1)}, f32[1,4,64,128]{3,2,1,0:T(8,128)S(1)}, u32[]{:S(2)}, u32[]{:S(2)}) collective-permute-start(f32[1,4,64,128]{3,2,1,0:T(8,128)S(1)} %collective-permute-done.13.refs_2_), channel_id=1, source_target_pairs={{0,1},{1,0},{2,3},{3,2},{4,5},{5,4},{6,7},{7,6},{8,9},{9,8},{10,11... | collective-permute-start | bytes 393224 | tf_op jit(solution)/shard_map/ppermute | solution.py:375
  56.4 13.9 %collective-permute-start.20 = (f32[8,48,128]{2,1,0:T(8,128)S(1)}, f32[8,48,128]{2,1,0:T(8,128)S(1)}, u32[]{:S(2)}, u32[]{:S(2)}) collective-permute-start(f32[8,48,128]{2,1,0:T(8,128)S(1)} %all-to-all-done.1.refs_2_.own), channel_id=1, source_target_pairs={{0,1},{1,0},{2,3},{3,2},{4,5},{5,4},{6,7},{7,6},{8,9},{9,8},{10,11... | collective-permute-start | bytes 589832 | tf_op jit(solution)/shard_map/ppermute | solution.py:375
  57.4 1.6 %copy-start.7 = (bf16[16,128,512]{2,1,0:T(8,128)(2,1)S(1)}, bf16[16,128,512]{2,1,0:T(8,128)(2,1)}, u32[]{:S(2)}) copy-start(bf16[16,128,512]{2,1,0:T(8,128)(2,1)} %copy-done.5) | copy-start | bytes 6291460
  60.7 2.9 %copy-start.8 = (f32[4,4,64,128]{3,2,1,0:T(8,128)}, f32[4,4,64,128]{3,2,1,0:T(8,128)S(1)}, u32[]{:S(2)}) copy-start(f32[4,4,64,128]{3,2,1,0:T(8,128)S(1)} %step.5.refs_3_) | copy-start | bytes 1572868
  62.1 1.4 %collective-permute-start.15 = (f32[256,128]{1,0:T(8,128)S(1)}, f32[256,128]{1,0:T(8,128)S(1)}, u32[]{:S(2)}, u32[]{:S(2)}) collective-permute-start(f32[256,128]{1,0:T(8,128)S(1)} %get-tuple-element.35), channel_id=1, source_target_pairs={{0,1},{1,0},{2,3},{3,2},{4,5},{5,4},{6,7},{7,6},{8,9},{9,8},{10,11... | collective-permute-start | bytes 393224 | tf_op jit(solution)/shard_map/ppermute | solution.py:375
  64.3 15.0 %all-to-all-start.2 = ((f32[8,56,128]{2,1,0:T(8,128)}), f32[8,56,128]{2,1,0:T(8,128)S(1)}, u32[]{:S(2)}, u32[]{:S(2)}) async-start(f32[8,56,128]{2,1,0:T(8,128)} %message.6), calls=%async_computation.2 | async-start | bytes 458752 | tf_op jit(solution)/shard_map/all_to_all | solution.py:378
  79.9 10.7 %all-to-all-start.3 = ((f32[8,32,128]{2,1,0:T(8,128)}), f32[8,32,128]{2,1,0:T(8,128)S(1)}, u32[]{:S(2)}, u32[]{:S(2)}) async-start(f32[8,32,128]{2,1,0:T(8,128)} %message.7), calls=%async_computation.3 | async-start | bytes 262144 | tf_op jit(solution)/shard_map/all_to_all | solution.py:378
  83.5 7.2 %collective-permute-start.19 = (f32[8,56,128]{2,1,0:T(8,128)S(1)}, f32[8,56,128]{2,1,0:T(8,128)S(1)}, u32[]{:S(2)}, u32[]{:S(2)}) collective-permute-start(f32[8,56,128]{2,1,0:T(8,128)S(1)} %all-to-all-done.2.refs_0_.own), channel_id=1, source_target_pairs={{0,1},{1,0},{2,3},{3,2},{4,5},{5,4},{6,7},{7,6},{8,9},{9,8},{10,11... | collective-permute-start | bytes 688136 | tf_op jit(solution)/shard_map/ppermute | solution.py:375
  90.6 5.9 %collective-permute-start.18 = (f32[8,32,128]{2,1,0:T(8,128)S(1)}, f32[8,32,128]{2,1,0:T(8,128)S(1)}, u32[]{:S(2)}, u32[]{:S(2)}) collective-permute-start(f32[8,32,128]{2,1,0:T(8,128)S(1)} %all-to-all-done.3.own), channel_id=1, source_target_pairs={{0,1},{1,0},{2,3},{3,2},{4,5},{5,4},{6,7},{7,6},{8,9},{9,8},{10,11... | collective-permute-start | bytes 393224 | tf_op jit(solution)/shard_map/ppermute | solution.py:375
  96.5 7.2 %copy-start.9 = (f32[4,4,64,128]{3,2,1,0:T(8,128)S(1)}, f32[4,4,64,128]{3,2,1,0:T(8,128)}, u32[]{:S(2)}) copy-start(f32[4,4,64,128]{3,2,1,0:T(8,128)} %copy-done.8) | copy-start | bytes 1572868

commit v3 on v2

--- a/solution.py
+++ b/solution.py
@@ -11,8 +11,8 @@
 S = 3
 center_shift = 2.0
 half_range = 1.6
-HIGHEST = lax.Precision.HIGHEST
-VMEM_LIMIT = 48 * 1024 * 1024
+VMEM_LIMIT = 16 * 1024 * 1024
+PACK_VMEM_LIMIT = 60 * 1024 * 1024
 
 
 def estimate(us):
@@ -25,7 +25,7 @@
     return high, low
 
 
-def pack_kernel(count, cross_local, layers, slots, info, sites, couplings, sigma, out):
+def pack_kernel(count, cross_local, layers, slots, info, couplings, sigma, out):
     layer = pl.program_id(0)
     first = jnp.logical_and(layer == 0, info[1] == 1)
     last = jnp.logical_and(layer == layers - 1, info[2] == 1)
@@ -34,7 +34,7 @@
         lead = None
         for k in range(2 * count):
             flag = first if k < count else last
-            weight = jnp.where(jnp.logical_and(flag, sites[k] == place), -1.0, 0.0)
+            weight = jnp.where(jnp.logical_and(flag, info[4 + k] == place), -1.0, 0.0)
             term = sigma[k] * weight
             lead = term if lead is None else lead + term
         blocks = [couplings[0, q, j] for j in range(slots)] + [lead]
@@ -47,14 +47,14 @@
         out[q, half:] = low
 
 
-def pack(couplings, lead_sites, lead_sigma, info):
+def pack(couplings, lead_sigma, info):
     layers, cross_local, slots, size, _ = couplings.shape
     contacts = lead_sigma.shape[0]
     body = functools.partial(pack_kernel, contacts // 2, cross_local, layers, slots)
     return pl.pallas_call(
         body,
         grid_spec=pltpu.PrefetchScalarGridSpec(
-            num_scalar_prefetch=2,
+            num_scalar_prefetch=1,
             grid=(layers,),
             in_specs=[
                 pl.BlockSpec((1, cross_local, slots, size, size), lambda i, *_: (i, 0, 0, 0, 0)),
@@ -67,10 +67,10 @@
         out_shape=jax.ShapeDtypeStruct(
             (layers * cross_local, 2 * size, (slots + 1) * size), jnp.bfloat16
         ),
-        compiler_params=pltpu.CompilerParams(vmem_limit_bytes=VMEM_LIMIT),
-        cost_estimate=estimate(1.5),
+        compiler_params=pltpu.CompilerParams(vmem_limit_bytes=PACK_VMEM_LIMIT),
+        cost_estimate=estimate(2.5),
         name="pack",
-    )(info, lead_sites, couplings, lead_sigma)
+    )(info, couplings, lead_sigma)
 
 
 def step_kernel(first, last, slots, info, cols, packed, own, other, *refs):
@@ -182,40 +182,6 @@
     return -(-blocks * (columns // 2) // count)
 
 
-def message_kernel(done, fresh, *refs):
-    *ins, out = refs
-    count = out.shape[0]
-    if fresh:
-        mine, theirs = ins[:2]
-    if done:
-        parts = ins[-1]
-        width = parts.shape[1] - done
-        acc = parts[0, width:, :]
-        for p in range(1, count):
-            acc = acc + parts[p, width:, :]
-    for p in range(count):
-        if done:
-            out[p, :done, :] = acc
-        if fresh:
-            rows = slice(p * fresh, (p + 1) * fresh)
-            out[p, done:, :] = mine[rows, :] + theirs[rows, :]
-
-
-def message(halves, parts, done, count):
-    whole = pl.BlockSpec(memory_space=pltpu.VMEM)
-    args = list(halves) + ([] if parts is None else [parts])
-    fresh = halves[0].shape[0] // count if halves else 0
-    return pl.pallas_call(
-        functools.partial(message_kernel, done, fresh),
-        in_specs=[whole] * len(args),
-        out_specs=whole,
-        out_shape=jax.ShapeDtypeStruct((count, done + fresh, args[0].shape[-1]), jnp.float32),
-        cost_estimate=estimate(0.3),
-        compiler_params=pltpu.CompilerParams(vmem_limit_bytes=VMEM_LIMIT),
-        name="message",
-    )(*args)
-
-
 def factor(block):
     size = block.shape[0]
     tall = 8
@@ -225,95 +191,99 @@
     gram = [block[tall * t : tall * (t + 1)] for t in range(tiles)]
     unit = [jnp.where(lanes == sub + tall * t, 1.0, 0.0) for t in range(tiles)]
 
-    def spread(row):
-        return jnp.broadcast_to(row, (tall, size))
-
+    def spread(x, row):
+        return jnp.broadcast_to(x[row : row + 1], (tall, size))
+
+    def lane(x, at):
+        return jnp.broadcast_to(x[:, at : at + 1], (tall, size))
+
+    corner = [lane(gram[0], c) for c in range(tall)]
     for p in range(tiles):
-        cols = [
-            [
-                jnp.broadcast_to(gram[t][:, tall * p + c : tall * p + c + 1], (tall, size))
-                for t in range(p, tiles)
-            ]
-            for c in range(tall)
-        ]
-        scales = []
+        at = tall * p
+        below = range(p + 1, tiles)
+        cols = [[lane(gram[t], at + c) for t in below] for c in range(tall)]
+        ahead = [lane(gram[p + 1], at + tall + d) for d in range(tall)] if p + 1 < tiles else []
+        scales, tops, lows = [], [], []
         for c in range(tall):
-            scale = lax.rsqrt(spread(cols[c][0][c : c + 1]))
+            scale = lax.rsqrt(spread(corner[c], c))
+            square = scale * scale
+            top = jnp.where(sub > c, corner[c], 0.0)
+            weights = [spread(corner[d], c) for d in range(c + 1, tall)]
+            for d in range(c + 1, tall):
+                corner[d] = corner[d] - (top * weights[d - c - 1]) * square
+            low = [x * scale for x in cols[c]]
+            for d in range(c + 1, tall):
+                weight = weights[d - c - 1] * scale
+                cols[d] = [x - m * weight for x, m in zip(cols[d], low)]
+            if low:
+                ahead = [x - low[0] * spread(low[0], d) for d, x in enumerate(ahead)]
             scales.append(scale)
-            cols[c] = [x * scale for x in cols[c]]
-            cols[c][0] = jnp.where(sub > c, cols[c][0], 0.0)
-            for d in range(c + 1, tall):
-                weight = spread(cols[c][0][d : d + 1])
-                cols[d] = [x - m * weight for x, m in zip(cols[d], cols[c])]
+            tops.append(top * scale)
+            lows.append(low)
         for c in range(tall):
-            row_gram = spread(gram[p][c : c + 1]) * scales[c]
-            row_unit = spread(unit[p][c : c + 1]) * scales[c]
-            gram[p] = jnp.where(sub == c, row_gram, gram[p] - cols[c][0] * row_gram)
-            unit[p] = jnp.where(sub == c, row_unit, unit[p] - cols[c][0] * row_unit)
-            for t in range(p + 1, tiles):
-                m = cols[c][t - p]
+            row_gram = spread(gram[p], c) * scales[c]
+            row_unit = spread(unit[p], c) * scales[c]
+            gram[p] = jnp.where(sub == c, row_gram, gram[p] - tops[c] * row_gram)
+            unit[p] = jnp.where(sub == c, row_unit, unit[p] - tops[c] * row_unit)
+            for t, m in zip(below, lows[c]):
                 gram[t] = gram[t] - m * row_gram
                 unit[t] = unit[t] - m * row_unit
+        corner = ahead
     upper = [jnp.where(lanes >= sub + tall * t, gram[t], 0.0) for t in range(tiles)]
     return jnp.concatenate(upper, axis=0), jnp.concatenate(unit, axis=0)
 
 
-def dot(a, b, dims=((1,), (0,))):
-    return lax.dot_general(
-        a, b, (dims, ((), ())), precision=HIGHEST, preferred_element_type=jnp.float32
-    )
-
-
-def column_kernel(place, first, row_share, scale, info, own, other, *refs):
-    *refs, flat, gram = refs
-    known, refs = (None, refs) if place == 0 else (refs[0], refs[1:])
-    upper_known, refs = (None, refs) if place == 0 else (refs[0], refs[1:])
-    upper_out, inverse_out = refs
+def dot(a, b, right=0):
+    (a_high, a_low), (b_high, b_low) = split(a), split(b)
+
+    def product(x, y):
+        return lax.dot_general(
+            x, y, (((1,), (right,)), ((), ())), preferred_element_type=jnp.float32
+        )
+
+    return product(a_high, b_high) + (product(a_high, b_low) + product(a_low, b_high))
+
+
+def column_kernel(place, first, scale, info, own, other, *refs):
+    *refs, upper_out, inverse_out, gram = refs
     size = gram.shape[0]
     half = size // 2
-    count = own.shape[0]
     at = place * size
     for core, source in ((info[0], own), (1 - info[0], other)):
         rows = pl.ds(pl.multiple_of(core * half, half), half)
-        for p in range(count):
-            flat[p * row_share : (p + 1) * row_share, :] = source[p, :row_share, :]
         for j in range(place + 1):
-            gram[rows, j * size : (j + 1) * size] = flat[(first + j) * half : (first + j + 1) * half, :]
+            gram[rows, j * size : (j + 1) * size] = source[(first + j) * half : (first + j + 1) * half, :]
     corner = gram[:, at:]
     if place:
-        above = dot(known[...], gram[:, :at], ((0,), (1,)))
-        corner = corner - dot(above, above, ((0,), (0,)))
-        carried = dot(known[...], above)
-    upper, lower_inverse = factor(corner)
-    upper_inverse = lower_inverse.T
+        known, upper_known = refs
+        left = dot(gram[:, :at], known[...], 1)
+        corner = corner - dot(left, left, 1)
+        carried = dot(left, known[...])
+    upper, inverse = factor(corner)
     if place:
+        inverse_out[at:, :at] = -dot(inverse, carried)
+        inverse_out[:at, :at] = known[...]
+        inverse_out[:at, at:] = jnp.zeros((at, size), jnp.float32)
         upper_out[:at, :at] = upper_known[...] * scale
-        inverse_out[:at, :at] = known[...]
-        upper_out[:at, at:] = above * scale
-        inverse_out[:at, at:] = -dot(carried, upper_inverse)
         upper_out[at:, :at] = jnp.zeros((size, at), jnp.float32)
-        inverse_out[at:, :at] = jnp.zeros((size, at), jnp.float32)
+        upper_out[:at, at:] = left.T * scale
+    inverse_out[at:, at:] = inverse
     upper_out[at:, at:] = upper * scale
-    inverse_out[at:, at:] = upper_inverse
-
-
-def column(place, first, blocks, info, own, other, before, scale=1.0):
+
+
+def column(place, first, info, own, other, before, scale=1.0):
     whole = pl.BlockSpec(memory_space=pltpu.VMEM)
-    count, _, size = own.shape
-    row_share = share(blocks, size, count)
+    size = own.shape[1]
     args = [own, other, *before]
     square = jax.ShapeDtypeStruct(((place + 1) * size,) * 2, jnp.float32)
     return pl.pallas_call(
-        functools.partial(column_kernel, place, first, row_share, scale),
+        functools.partial(column_kernel, place, first, scale),
         in_specs=[pl.BlockSpec(memory_space=pltpu.SMEM)] + [whole] * len(args),
         out_specs=[whole, whole],
         out_shape=[square, square],
-        scratch_shapes=[
-            pltpu.VMEM((count * row_share, size), jnp.float32),
-            pltpu.VMEM((size, (place + 1) * size), jnp.float32),
-        ],
+        scratch_shapes=[pltpu.VMEM((size, (place + 1) * size), jnp.float32)],
         compiler_params=pltpu.CompilerParams(vmem_limit_bytes=VMEM_LIMIT),
-        cost_estimate=estimate(4.5),
+        cost_estimate=estimate(4.0),
         name="column",
     )(info, *args)
 
@@ -332,10 +302,15 @@
         stop = min(start + wide, count * columns)
         left_high = jnp.concatenate([p[0] for p in pairs[: stop // columns]], axis=1)
         left_low = jnp.concatenate([p[1] for p in pairs[: stop // columns]], axis=1)
-        right = high[:stop, start:stop]
-        acc = jnp.dot(left_high, right, preferred_element_type=jnp.float32)
-        acc = acc + jnp.dot(left_low, right, preferred_element_type=jnp.float32)
-        acc = acc + jnp.dot(left_high, low[:stop, start:stop], preferred_element_type=jnp.float32)
+        acc = None
+        for left, right in ((left_high, high), (left_low, high), (left_high, low)):
+            term = lax.dot_general(
+                left,
+                right[start:stop, :stop],
+                (((1,), (1,)), ((), ())),
+                preferred_element_type=jnp.float32,
+            )
+            acc = term if acc is None else acc + term
         out[:, :, :, start:stop] = acc.astype(jnp.bfloat16).reshape(out.shape[:3] + (stop - start,))
 
 
@@ -363,13 +338,13 @@
     count = lax.axis_size("trans")
     place = lax.axis_index("trans")
     even = 1 - place % 2
-    info = jnp.stack([lax.axis_index("cross"), place == 0, place == count - 1, even]).astype(jnp.int32)
-    packed = pack(couplings, lead_sites, lead_sigma, info)
-
-    near = [(i, i + 1) for i in range(0, count - 1, 2)]
-    far = [(i, i + 1) for i in range(1, count - 1, 2)]
-    near, far = ([*x, *[(j, i) for i, j in x]] for x in (near, far))
+    info = jnp.stack([lax.axis_index("cross"), place == 0, place == count - 1, even])
+    info = jnp.concatenate([info.astype(jnp.int32), lead_sites])
+    packed = pack(couplings, lead_sigma, info)
     scale_rows = math.sqrt(count * layers * cross_local * cross_count * size)
+
+    near = [(i, i ^ 1) for i in range(count) if i ^ 1 < count]
+    far = [(i, j) for i in range(count) for j in (i - 1 + 2 * (i % 2),) if 0 <= j < count]
 
     def swap(x):
         return lax.ppermute(x, "cross", [(0, 1), (1, 0)])
@@ -377,40 +352,42 @@
     def exchange(x):
         return lax.all_to_all(x, "trans", 0, 0, tiled=True)
 
-    def ahead(pairs, parts, done):
-        mine, theirs = gram_blocks(powers, pairs, info, count)
-        return exchange(message((mine, swap(theirs)), parts, done, count))
-
-    groups = (((0, 0), (1, 0), (1, 1)), ((2, 0), (2, 1), (2, 2)), tuple((S, j) for j in range(S + 1)))
-    shares = [share(len(g), columns, count) for g in groups]
+    early = tuple((i, j) for i in range(S) for j in range(i + 1))
     powers = [sources]
     near_layer = lax.dynamic_slice_in_dim(sources, even * (layers - 1), 1)
     far_layer = lax.dynamic_slice_in_dim(sources, (1 - even) * (layers - 1), 1)
-    parts, done = None, 0
-    sums = []
     for k in range(S):
         field = powers[k]
+        far_edge = lax.ppermute(far_layer, "trans", far)
         near_edge = lax.ppermute(near_layer, "trans", near)
-        far_edge = lax.ppermute(far_layer, "trans", far)
         other = swap(field)
         if k == 0:
             near_edge, far_edge, packed = lax.optimization_barrier((near_edge, far_edge, packed))
-        else:
-            parts = ahead(groups[k - 1], parts, done)
-            done = shares[k - 1]
-            sums.append(parts)
+        if k == S - 1:
+            mine, theirs = gram_blocks(powers, early, info, count)
+            shares = (mine + swap(theirs)).reshape(count, -1, columns)
+            near_edge, far_edge, shares = lax.optimization_barrier((near_edge, far_edge, shares))
+            parts = exchange(shares)
         edges = (near_edge, swap(near_edge), far_edge, swap(far_edge))
         before = powers[k - 1] if k else None
         got = step(packed, block_cols, info, field, other, edges, before, k == S - 1)
         powers.append(got[0])
         if k < S - 1:
             near_layer, far_layer = got[1:]
-    parts = ahead(groups[2], parts, done)
-    first = column(0, 0, 3, info, sums[1], swap(sums[1]), ())
-    second = column(1, 1, 3, info, sums[1], swap(sums[1]), first[::-1])
-    last = exchange(message((), parts, shares[2], count))
-    third = column(2, 0, 3, info, parts, swap(parts), second[::-1])
-    r_factor, inverse = column(3, 0, 4, info, last, swap(last), third[::-1], 1.0 / scale_rows)
+    mine, theirs = gram_blocks(powers, tuple((S, j) for j in range(S + 1)), info, count)
+    last = mine + swap(theirs)
+    last, parts = lax.optimization_barrier((last, parts))
+    summed = jnp.sum(parts, axis=0, keepdims=True)
+    known = exchange(jnp.broadcast_to(summed, parts.shape)).reshape(-1, columns)
+    known_other = swap(known)
+    reach = 1
+    while reach < count:
+        last = last + lax.ppermute(last, "trans", [(i, i ^ reach) for i in range(count)])
+        reach *= 2
+    first = column(0, 0, info, known, known_other, ())
+    second = column(1, 1, info, known, known_other, first[::-1])
+    third = column(2, 3, info, known, known_other, second[::-1])
+    r_factor, inverse = column(3, 0, info, last, swap(last), third[::-1], 1.0 / scale_rows)
     return basis_of(powers, inverse, scale_rows), r_factor
 
 

time: 108 us -> 103 us (0.954)
  Pallas kernels: 39.3 us -> 34.4 us
  waiting for transfers between devices: 21.7 us -> 24.6 us
  local copies, waits for them, and re-layouts: 7.79 us -> 6.17 us
  starting transfers between devices: 37.1 us -> 35.7 us
    ppermute x0 -> x3, waiting for transfers between devices: none -> 13.2 us  [local(): lax.ppermute(last, 'trans', [(i, i ^ reach) for i in range(count)])]
    all_to_all x4 -> x2, starting transfers between devices: 22.4 us -> 12.9 us  [exchange(): return lax.all_to_all(x, 'trans', 0, 0, tiled=True)]
    pallas_call x8 -> x4, Pallas kernels: 25.8 us -> 17.9 us  [column(): pl.pallas_call(functools.partial(column_kernel, place, first, scale), in_...]
    ppermute x0 -> x3, starting transfers between devices: none -> 6.5 us  [local(): lax.ppermute(last, 'trans', [(i, i ^ reach) for i in range(count)])]
    all_to_all x4 -> x2, waiting for transfers between devices: 7.86 us -> 1.94 us  [exchange(): return lax.all_to_all(x, 'trans', 0, 0, tiled=True)]
    pallas_call x1, Pallas kernels: 1.42 us -> 5.23 us  [pack(): pl.pallas_call(body, grid_spec=pltpu.PrefetchScalarGridSpec(num_scalar_pr...]
    unnamed x20 -> x10, local copies, waits for them, and re-layouts: 6.8 us -> 3.18 us
    ppermute x3, waiting for transfers between devices: 9.57 us -> 6.04 us  [local(): near_edge = lax.ppermute(near_layer, 'trans', near)]
  transfers between devices with their start and end apart: 25 -> 24, of which waited for: 11 -> 11; matrix products, arithmetic and copies ran while one was open for 1% -> 3% of each run, Pallas kernels for 25% -> 22%
where the time goes in v3:
time: 103 us; the launch traced here: 102 us
  starting transfers between devices  35.7 us (35%)
  Pallas kernels  34.4 us (33%)
  waiting for transfers between devices  24.6 us (24%)
  local copies, waits for them, and re-layouts  6.17 us (6%)
    pallas_call x4, Pallas kernels, column(): pl.pallas_call(functools.partial(column_kernel, place, first, scale), in_...  17.9 us
    ppermute x3, waiting for transfers between devices, local(): lax.ppermute(last, 'trans', [(i, i ^ reach) for i in range(count)])  13.2 us
    all_to_all x2, starting transfers between devices, exchange(): return lax.all_to_all(x, 'trans', 0, 0, tiled=True)  12.9 us
    ppermute x3, starting transfers between devices, local(): near_edge = lax.ppermute(near_layer, 'trans', near)  11 us
    ppermute x3, starting transfers between devices, local(): lax.ppermute(last, 'trans', [(i, i ^ reach) for i in range(count)])  6.5 us
    ppermute x3, waiting for transfers between devices, local(): near_edge = lax.ppermute(near_layer, 'trans', near)  6.04 us
    pallas_call x1, Pallas kernels, pack(): pl.pallas_call(body, grid_spec=pltpu.PrefetchScalarGridSpec(num_scalar_pr...  5.23 us
    pallas_call x3, Pallas kernels, step(): pl.pallas_call(functools.partial(step_kernel, before is None, last, cols....  5.04 us
  transfers between devices with their start and end apart: 24, of which 11 were waited for; matrix products, arithmetic and copies ran while one was open for 3% of the time, Pallas kernels for 22%

profile of v3, /device:TPU:0, one launch (start us, length us, event | category | flops | bytes accessed | tf_op | source)
XLA Modules:
  0.0 102.5 jit_solution(7017653346254780381)
XLA Ops:
  0.6 0.5 collective-permute-start.2
  1.1 1.0 constant_dynamic-slice_fusion
  2.1 0.7 collective-permute-start.1
  2.8 5.4 %collective-permute-start = (f32[1,4,64,128]{3,2,1,0:T(8,128)S(1)}, f32[1,4,64,128]{3,2,1,0:T(8,128)S(1)}, u32[]{:S(2)}, u32[]{:S(2)}) collective-permute-start(f32[1,4,64,128]{3,2,1,0:T(8,128)S(1)} %get-tuple-element.55), channel_id=1, source_target_pairs={{0,2},{2,0},{4,6},{6,4},{8,10},{10,8},{12,14},{14,12},{1,3},{3,1},... | collective-permute-start | bytes 393224 | tf_op jit(solution)/shard_map/ppermute | solution.py:362
  8.2 1.3 %concatenate.3.info = s32[8]{0:T(128)} concatenate(s32[1]{0:T(128)} %bitcast, s32[1]{0:T(128)} %bitcast.1, s32[1]{0:T(128)} %bitcast.2, s32[1]{0:T(128)} %bitcast.3, s32[4]{0:T(128)} %param.8), dimensions={0} | concatenate | bytes 64 | tf_op jit(solution)/shard_map/concatenate | solution.py:342
  9.5 5.2 %pack.1.packed = bf16[16,128,512]{2,1,0:T(8,128)(2,1)} custom-call(s32[8]{0:T(128)} %concatenate.3.info, f32[4,4,7,64,64]{4,3,2,1,0:T(8,128)} %couplings.1, f32[4,64,64]{2,1,0:T(8,128)} %sigma.1), custom_call_target="tpu_custom_call" | custom-call | flops 2875000064 | tf_op jit(solution)/shard_map/pack/pallas_call | solution.py:54
  14.8 0.1 collective-permute-start.3
  14.8 0.5 collective-permute-start.4
  15.3 0.8 collective-permute-done.3.refs_1_
  16.2 0.2 collective-permute-done.4.refs_3_
  16.4 1.6 %copy-done.3 = bf16[16,128,512]{2,1,0:T(8,128)(2,1)S(1)} copy-done((bf16[16,128,512]{2,1,0:T(8,128)(2,1)S(1)}, bf16[16,128,512]{2,1,0:T(8,128)(2,1)}, u32[]{:S(2)}) %copy-start.3) | copy-done | bytes 2097176
  18.0 1.7 %step.3 = (f32[4,4,64,128]{3,2,1,0:T(8,128)S(1)}, f32[1,4,64,128]{3,2,1,0:T(8,128)S(1)}, f32[1,4,64,128]{3,2,1,0:T(8,128)S(1)}) custom-call(s32[8]{0:T(128)S(1)} %copy-done.1, s32[4,4,7]{2,1,0:T(4,128)S(1)} %copy-done.2, bf16[16,128,512]{2,1,0:T(8,128)(2,1)S(1)} %copy-done.3, f32[4,4,64,128]{3,2,1,0:T(8,128)S(1)} %copy-done, ...), custom_call_target="tpu_custom_call" | custom-call | flops 1955000064 | tf_op jit(solution)/shard_map/step/pallas_call | solution.py:124
  19.6 0.4 collective-permute-start.5
  20.0 1.3 %collective-permute-start.6 = (f32[1,4,64,128]{3,2,1,0:T(8,128)S(1)}, f32[1,4,64,128]{3,2,1,0:T(8,128)S(1)}, u32[]{:S(2)}, u32[]{:S(2)}) collective-permute-start(f32[1,4,64,128]{3,2,1,0:T(8,128)S(1)} %get-tuple-element.32), channel_id=1, source_target_pairs={{0,2},{2,0},{4,6},{6,4},{8,10},{10,8},{12,14},{14,12},{1,3},{3,1},... | collective-permute-start | bytes 393224 | tf_op jit(solution)/shard_map/ppermute | solution.py:362
  21.3 0.7 collective-permute-start.8
  22.0 3.6 %collective-permute-done.6.refs_0_ = f32[1,4,64,128]{3,2,1,0:T(8,128)S(1)} collective-permute-done((f32[1,4,64,128]{3,2,1,0:T(8,128)S(1)}, f32[1,4,64,128]{3,2,1,0:T(8,128)S(1)}, u32[]{:S(2)}, u32[]{:S(2)}) %collective-permute-start.6) | collective-permute-done | bytes 131104 | tf_op jit(solution)/shard_map/ppermute | solution.py:362
  25.6 0.5 collective-permute-start.9
  26.1 0.8 collective-permute-done.7.refs_1_
  27.0 0.2 collective-permute-done.9.refs_3_
  27.2 1.7 %step.4 = (f32[4,4,64,128]{3,2,1,0:T(8,128)S(1)}, f32[1,4,64,128]{3,2,1,0:T(8,128)S(1)}, f32[1,4,64,128]{3,2,1,0:T(8,128)S(1)}) custom-call(s32[8]{0:T(128)S(1)} %copy-done.1, s32[4,4,7]{2,1,0:T(4,128)S(1)} %copy-done.2, bf16[16,128,512]{2,1,0:T(8,128)(2,1)S(1)} %copy-done.3, f32[4,4,64,128]{3,2,1,0:T(8,128)S(1)} %get-tuple-element.31.own.refs_1_.refs_4_, ...), custom_call_target="tpu_custom_call" | custom-call | flops 1955000064 | tf_op jit(solution)/shard_map/step/pallas_call | solution.py:124
  28.9 0.4 collective-permute-start.10
  29.3 1.6 %gram.2 = (f32[384,128]{1,0:T(8,128)S(1)}, f32[384,128]{1,0:T(8,128)S(1)}) custom-call(s32[8]{0:T(128)S(1)} %copy-done.1, f32[4,4,64,128]{3,2,1,0:T(8,128)S(1)} %copy-done, f32[4,4,64,128]{3,2,1,0:T(8,128)S(1)} %get-tuple-element.31.own.refs_1_.refs_4_, f32[4,4,64,128]{3,2,1,0:T(8,128)S(1)} %get-tuple-element.34.refs_2_.own), custom_call_target="tpu_custom_call" | custom-call | flops 1610000000 | tf_op jit(solution)/shard_map/gram/pallas_call | solution.py:166
  30.9 0.2 collective-permute-start.13
  31.1 4.3 %collective-permute-start.11 = (f32[1,4,64,128]{3,2,1,0:T(8,128)S(1)}, f32[1,4,64,128]{3,2,1,0:T(8,128)S(1)}, u32[]{:S(2)}, u32[]{:S(2)}) collective-permute-start(f32[1,4,64,128]{3,2,1,0:T(8,128)S(1)} %get-tuple-element.35), channel_id=1, source_target_pairs={{0,2},{2,0},{4,6},{6,4},{8,10},{10,8},{12,14},{14,12},{1,3},{3,1},... | collective-permute-start | bytes 393224 | tf_op jit(solution)/shard_map/ppermute | solution.py:362
  35.5 0.7 collective-permute-start.12
  36.1 0.7 add.28
  36.8 2.4 %collective-permute-done.11.refs_0_ = f32[1,4,64,128]{3,2,1,0:T(8,128)S(1)} collective-permute-done((f32[1,4,64,128]{3,2,1,0:T(8,128)S(1)}, f32[1,4,64,128]{3,2,1,0:T(8,128)S(1)}, u32[]{:S(2)}, u32[]{:S(2)}) %collective-permute-start.11) | collective-permute-done | bytes 131104 | tf_op jit(solution)/shard_map/ppermute | solution.py:362
  39.3 0.5 collective-permute-start.15
  39.8 8.9 %all-to-all-start = ((f32[8,48,128]{2,1,0:T(8,128)}), f32[8,48,128]{2,1,0:T(8,128)S(1)}, u32[]{:S(2)}, u32[]{:S(2)}) async-start(f32[8,48,128]{2,1,0:T(8,128)} %bitcast.4), calls=%async_computation | async-start | bytes 393216 | tf_op jit(solution)/shard_map/all_to_all | solution.py:353
  48.7 1.6 %copy-done.4 = bf16[16,128,512]{2,1,0:T(8,128)(2,1)S(1)} copy-done((bf16[16,128,512]{2,1,0:T(8,128)(2,1)S(1)}, bf16[16,128,512]{2,1,0:T(8,128)(2,1)}, u32[]{:S(2)}) %copy-start.4) | copy-done | bytes 2097176
  50.3 1.7 %step.5.refs_3_ = f32[4,4,64,128]{3,2,1,0:T(8,128)S(1)} custom-call(s32[8]{0:T(128)S(1)} %copy-done.1, s32[4,4,7]{2,1,0:T(4,128)S(1)} %copy-done.2, bf16[16,128,512]{2,1,0:T(8,128)(2,1)S(1)} %copy-done.4, f32[4,4,64,128]{3,2,1,0:T(8,128)S(1)} %get-tuple-element.34.refs_2_.own, f32[4,4,64,128]{3,2,1,0:T(8,128)S(1)} %collective-permute-done.10.other, ...), custom_call_target="tpu_custom_call" | custom-call | flops 1955000064 | tf_op jit(solution)/shard_map/step/pallas_call | solution.py:124
  52.0 1.4 %gram.3 = (f32[256,128]{1,0:T(8,128)S(1)}, f32[256,128]{1,0:T(8,128)S(1)}) custom-call(s32[8]{0:T(128)S(1)} %copy-done.1, f32[4,4,64,128]{3,2,1,0:T(8,128)S(1)} %copy-done, f32[4,4,64,128]{3,2,1,0:T(8,128)S(1)} %get-tuple-element.31.own.refs_1_.refs_4_, f32[4,4,64,128]{3,2,1,0:T(8,128)S(1)} %get-tuple-element.34.refs_2_.own, f32[4,4,64,128]{3,2,1,0:T(8,128)S(1)} %step.5.refs_3_), custom_call_target="tpu_custom_call" | custom-call | flops 1610000000 | tf_op jit(solution)/shard_map/gram/pallas_call | solution.py:166
  53.4 0.1 collective-permute-start.16
  53.5 1.3 %collective-permute-done.16 = f32[256,128]{1,0:T(8,128)S(1)} collective-permute-done((f32[256,128]{1,0:T(8,128)S(1)}, f32[256,128]{1,0:T(8,128)S(1)}, u32[]{:S(2)}, u32[]{:S(2)}) %collective-permute-start.16) | collective-permute-done | bytes 131104 | tf_op jit(solution)/shard_map/ppermute | solution.py:350
  54.8 1.9 %all-to-all-done = f32[8,48,128]{2,1,0:T(8,128)S(1)} async-done(((f32[8,48,128]{2,1,0:T(8,128)}), f32[8,48,128]{2,1,0:T(8,128)S(1)}, u32[]{:S(2)}, u32[]{:S(2)}) %all-to-all-start) | async-done | bytes 196640 | tf_op jit(solution)/shard_map/all_to_all | solution.py:353
  56.8 0.7 broadcast_in_dim.2
  57.5 4.1 %all-to-all-start.1 = ((f32[8,48,128]{2,1,0:T(8,128)}), f32[8,48,128]{2,1,0:T(8,128)S(1)}, u32[]{:S(2)}, u32[]{:S(2)}) async-start(f32[8,48,128]{2,1,0:T(8,128)} %broadcast_in_dim.2), calls=%async_computation.1 | async-start | bytes 393216 | tf_op jit(solution)/shard_map/all_to_all | solution.py:353
  61.5 2.0 %collective-permute-start.17 = (f32[256,128]{1,0:T(8,128)S(1)}, f32[256,128]{1,0:T(8,128)S(1)}, u32[]{:S(2)}, u32[]{:S(2)}) collective-permute-start(f32[256,128]{1,0:T(8,128)S(1)} %add.29), channel_id=1, source_target_pairs={{0,2},{2,0},{4,6},{6,4},{8,10},{10,8},{12,14},{14,12},{1,3},{3,1},... | collective-permute-start | bytes 393224 | tf_op jit(solution)/shard_map/ppermute | solution.py:385
  63.6 5.3 %collective-permute-done.17 = f32[256,128]{1,0:T(8,128)S(1)} collective-permute-done((f32[256,128]{1,0:T(8,128)S(1)}, f32[256,128]{1,0:T(8,128)S(1)}, u32[]{:S(2)}, u32[]{:S(2)}) %collective-permute-start.17) | collective-permute-done | bytes 131104 | tf_op jit(solution)/shard_map/ppermute | solution.py:385
  68.9 1.8 %collective-permute-start.18 = (f32[256,128]{1,0:T(8,128)S(1)}, f32[256,128]{1,0:T(8,128)S(1)}, u32[]{:S(2)}, u32[]{:S(2)}) collective-permute-start(f32[256,128]{1,0:T(8,128)S(1)} %add.30), channel_id=1, source_target_pairs={{0,4},{2,6},{4,0},{6,2},{8,12},{10,14},{12,8},{14,10},{1,5},{3,7},... | collective-permute-start | bytes 393224 | tf_op jit(solution)/shard_map/ppermute | solution.py:385
  70.7 3.2 %collective-permute-done.18 = f32[256,128]{1,0:T(8,128)S(1)} collective-permute-done((f32[256,128]{1,0:T(8,128)S(1)}, f32[256,128]{1,0:T(8,128)S(1)}, u32[]{:S(2)}, u32[]{:S(2)}) %collective-permute-start.18) | collective-permute-done | bytes 131104 | tf_op jit(solution)/shard_map/ppermute | solution.py:385
  73.9 2.7 %collective-permute-start.19 = (f32[256,128]{1,0:T(8,128)S(1)}, f32[256,128]{1,0:T(8,128)S(1)}, u32[]{:S(2)}, u32[]{:S(2)}) collective-permute-start(f32[256,128]{1,0:T(8,128)S(1)} %add.31), channel_id=1, source_target_pairs={{0,8},{2,10},{4,12},{6,14},{8,0},{10,2},{12,4},{14,6},{1,9},{3,11}... | collective-permute-start | bytes 393224 | tf_op jit(solution)/shard_map/ppermute | solution.py:385
  76.6 4.6 %collective-permute-done.19 = f32[256,128]{1,0:T(8,128)S(1)} collective-permute-done((f32[256,128]{1,0:T(8,128)S(1)}, f32[256,128]{1,0:T(8,128)S(1)}, u32[]{:S(2)}, u32[]{:S(2)}) %collective-permute-start.19) | collective-permute-done | bytes 131104 | tf_op jit(solution)/shard_map/ppermute | solution.py:385
  81.4 3.8 %column.4 = (f32[128,128]{1,0:T(8,128)S(1)}, f32[128,128]{1,0:T(8,128)S(1)}) custom-call(s32[8]{0:T(128)S(1)} %copy-done.1, f32[384,128]{1,0:T(8,128)S(1)} %bitcast.7, f32[384,128]{1,0:T(8,128)S(1)} %collective-permute-done.21.other), custom_call_target="tpu_custom_call" | custom-call | flops 4600000000 | tf_op jit(solution)/shard_map/column/pallas_call | solution.py:279
  85.2 4.2 %column.5 = (f32[256,256]{1,0:T(8,128)S(1)}, f32[256,256]{1,0:T(8,128)S(1)}) custom-call(s32[8]{0:T(128)S(1)} %copy-done.1, f32[384,128]{1,0:T(8,128)S(1)} %bitcast.8, f32[384,128]{1,0:T(8,128)S(1)} %collective-permute-done.21.other, f32[128,128]{1,0:T(8,128)S(1)} %get-tuple-element.46.refs_0_, f32[128,128]{1,0:T(8,128)S(1)} %get-tuple-element.47.refs_1_), custom_call_target="tpu_custom_call" | custom-call | flops 4600000000 | tf_op jit(solution)/shard_map/column/pallas_call | solution.py:279
  89.3 4.2 %column.6 = (f32[384,384]{1,0:T(8,128)S(1)}, f32[384,384]{1,0:T(8,128)S(1)}) custom-call(s32[8]{0:T(128)S(1)} %copy-done.1, f32[384,128]{1,0:T(8,128)S(1)} %bitcast.9, f32[384,128]{1,0:T(8,128)S(1)} %collective-permute-done.21.other, f32[256,256]{1,0:T(8,128)S(1)} %get-tuple-element.48.refs_0_, f32[256,256]{1,0:T(8,128)S(1)} %get-tuple-element.49.refs_1_), custom_call_target="tpu_custom_call" | custom-call | flops 4600000000 | tf_op jit(solution)/shard_map/column/pallas_call | solution.py:279
  93.6 5.7 %column.7 = (f32[512,512]{1,0:T(8,128)}, f32[512,512]{1,0:T(8,128)S(1)}) custom-call(s32[8]{0:T(128)S(1)} %copy-done.1, f32[256,128]{1,0:T(8,128)S(1)} %add.32.own, f32[256,128]{1,0:T(8,128)S(1)} %collective-permute-done.20.other, f32[384,384]{1,0:T(8,128)S(1)} %get-tuple-element.50.refs_0_, f32[384,384]{1,0:T(8,128)S(1)} %get-tuple-element.51.refs_1_), custom_call_target="tpu_custom_call" | custom-call | flops 4600000000 | tf_op jit(solution)/shard_map/column/pallas_call | solution.py:279
  99.3 3.2 %basis.1 = bf16[4,4,64,512]{3,2,1,0:T(8,128)(2,1)} custom-call(f32[4,4,64,128]{3,2,1,0:T(8,128)S(1)} %copy-done, f32[4,4,64,128]{3,2,1,0:T(8,128)S(1)} %get-tuple-element.31.own.refs_1_.refs_4_, f32[4,4,64,128]{3,2,1,0:T(8,128)S(1)} %get-tuple-element.34.refs_2_.own, f32[4,4,64,128]{3,2,1,0:T(8,128)S(1)} %step.5.refs_3_, ...), custom_call_target="tpu_custom_call" | custom-call | flops 3449999872 | tf_op jit(solution)/shard_map/basis/pallas_call | solution.py:321
  (30 shorter events, 0.2 us)
Async XLA Ops:
  0.6 15.7 %collective-permute-start.2 = (f32[4,4,64,128]{3,2,1,0:T(8,128)}, f32[4,4,64,128]{3,2,1,0:T(8,128)S(1)}, u32[]{:S(2)}, u32[]{:S(2)}) collective-permute-start(f32[4,4,64,128]{3,2,1,0:T(8,128)} %refs_0_.5), channel_id=1, source_target_pairs={{0,1},{1,0},{2,3},{3,2},{4,5},{5,4},{6,7},{7,6},{8,9},{9,8},{10,11... | collective-permute-start | bytes 1572872 | tf_op jit(solution)/shard_map/ppermute | solution.py:350
  2.1 12.6 %collective-permute-start.1 = (f32[1,4,64,128]{3,2,1,0:T(8,128)S(1)}, f32[1,4,64,128]{3,2,1,0:T(8,128)S(1)}, u32[]{:S(2)}, u32[]{:S(2)}) collective-permute-start(f32[1,4,64,128]{3,2,1,0:T(8,128)S(1)} %get-tuple-element.54), channel_id=1, source_target_pairs={{2,4},{4,2},{6,8},{8,6},{10,12},{12,10},{3,5},{5,3},{7,9},{9,7},{1... | collective-permute-start | bytes 393224 | tf_op jit(solution)/shard_map/ppermute | solution.py:361
  2.8 11.9 %collective-permute-start = (f32[1,4,64,128]{3,2,1,0:T(8,128)S(1)}, f32[1,4,64,128]{3,2,1,0:T(8,128)S(1)}, u32[]{:S(2)}, u32[]{:S(2)}) collective-permute-start(f32[1,4,64,128]{3,2,1,0:T(8,128)S(1)} %get-tuple-element.55), channel_id=1, source_target_pairs={{0,2},{2,0},{4,6},{6,4},{8,10},{10,8},{12,14},{14,12},{1,3},{3,1},... | collective-permute-start | bytes 393224 | tf_op jit(solution)/shard_map/ppermute | solution.py:362
  9.5 6.8 %copy-start = (f32[4,4,64,128]{3,2,1,0:T(8,128)S(1)}, f32[4,4,64,128]{3,2,1,0:T(8,128)}, u32[]{:S(2)}) copy-start(f32[4,4,64,128]{3,2,1,0:T(8,128)} %refs_0_.5) | copy-start | bytes 1572868
  9.5 6.9 %copy-start.1 = (s32[8]{0:T(128)S(1)}, s32[8]{0:T(128)}, u32[]{:S(2)}) copy-start(s32[8]{0:T(128)} %concatenate.3.info) | copy-start | bytes 100
  9.5 6.9 %copy-start.2 = (s32[4,4,7]{2,1,0:T(4,128)S(1)}, s32[4,4,7]{2,1,0:T(4,128)}, u32[]{:S(2)}) copy-start(s32[4,4,7]{2,1,0:T(4,128)} %cols.5) | copy-start | bytes 1348
  14.8 1.4 %collective-permute-start.3 = (f32[1,4,64,128]{3,2,1,0:T(8,128)S(1)}, f32[1,4,64,128]{3,2,1,0:T(8,128)S(1)}, u32[]{:S(2)}, u32[]{:S(2)}) collective-permute-start(f32[1,4,64,128]{3,2,1,0:T(8,128)S(1)} %collective-permute-done.refs_0_), channel_id=1, source_target_pairs={{0,1},{1,0},{2,3},{3,2},{4,5},{5,4},{6,7},{7,6},{8,9},{9,8},{10,11... | collective-permute-start | bytes 393224 | tf_op jit(solution)/shard_map/ppermute | solution.py:350
  14.8 1.5 %collective-permute-start.4 = (f32[1,4,64,128]{3,2,1,0:T(8,128)S(1)}, f32[1,4,64,128]{3,2,1,0:T(8,128)S(1)}, u32[]{:S(2)}, u32[]{:S(2)}) collective-permute-start(f32[1,4,64,128]{3,2,1,0:T(8,128)S(1)} %collective-permute-done.1.refs_2_), channel_id=1, source_target_pairs={{0,1},{1,0},{2,3},{3,2},{4,5},{5,4},{6,7},{7,6},{8,9},{9,8},{10,11... | collective-permute-start | bytes 393224 | tf_op jit(solution)/shard_map/ppermute | solution.py:350
  16.4 1.6 %copy-start.3 = (bf16[16,128,512]{2,1,0:T(8,128)(2,1)S(1)}, bf16[16,128,512]{2,1,0:T(8,128)(2,1)}, u32[]{:S(2)}) copy-start(bf16[16,128,512]{2,1,0:T(8,128)(2,1)} %pack.1.packed) | copy-start | bytes 6291460
  19.6 7.5 %collective-permute-start.5 = (f32[4,4,64,128]{3,2,1,0:T(8,128)S(1)}, f32[4,4,64,128]{3,2,1,0:T(8,128)S(1)}, u32[]{:S(2)}, u32[]{:S(2)}) collective-permute-start(f32[4,4,64,128]{3,2,1,0:T(8,128)S(1)} %get-tuple-element.31.own.refs_1_.refs_4_), channel_id=1, source_target_pairs={{0,1},{1,0},{2,3},{3,2},{4,5},{5,4},{6,7},{7,6},{8,9},{9,8},{10,11... | collective-permute-start | bytes 1572872 | tf_op jit(solution)/shard_map/ppermute | solution.py:350
  20.0 5.6 %collective-permute-start.6 = (f32[1,4,64,128]{3,2,1,0:T(8,128)S(1)}, f32[1,4,64,128]{3,2,1,0:T(8,128)S(1)}, u32[]{:S(2)}, u32[]{:S(2)}) collective-permute-start(f32[1,4,64,128]{3,2,1,0:T(8,128)S(1)} %get-tuple-element.32), channel_id=1, source_target_pairs={{0,2},{2,0},{4,6},{6,4},{8,10},{10,8},{12,14},{14,12},{1,3},{3,1},... | collective-permute-start | bytes 393224 | tf_op jit(solution)/shard_map/ppermute | solution.py:362
  21.3 4.3 %collective-permute-start.8 = (f32[1,4,64,128]{3,2,1,0:T(8,128)S(1)}, f32[1,4,64,128]{3,2,1,0:T(8,128)S(1)}, u32[]{:S(2)}, u32[]{:S(2)}) collective-permute-start(f32[1,4,64,128]{3,2,1,0:T(8,128)S(1)} %get-tuple-element.33), channel_id=1, source_target_pairs={{2,4},{4,2},{6,8},{8,6},{10,12},{12,10},{3,5},{5,3},{7,9},{9,7},{1... | collective-permute-start | bytes 393224 | tf_op jit(solution)/shard_map/ppermute | solution.py:361
  25.6 1.3 %collective-permute-start.7 = (f32[1,4,64,128]{3,2,1,0:T(8,128)S(1)}, f32[1,4,64,128]{3,2,1,0:T(8,128)S(1)}, u32[]{:S(2)}, u32[]{:S(2)}) collective-permute-start(f32[1,4,64,128]{3,2,1,0:T(8,128)S(1)} %collective-permute-done.6.refs_0_), channel_id=1, source_target_pairs={{0,1},{1,0},{2,3},{3,2},{4,5},{5,4},{6,7},{7,6},{8,9},{9,8},{10,11... | collective-permute-start | bytes 393224 | tf_op jit(solution)/shard_map/ppermute | solution.py:350
  25.6 1.5 %collective-permute-start.9 = (f32[1,4,64,128]{3,2,1,0:T(8,128)S(1)}, f32[1,4,64,128]{3,2,1,0:T(8,128)S(1)}, u32[]{:S(2)}, u32[]{:S(2)}) collective-permute-start(f32[1,4,64,128]{3,2,1,0:T(8,128)S(1)} %collective-permute-done.8.refs_2_), channel_id=1, source_target_pairs={{0,1},{1,0},{2,3},{3,2},{4,5},{5,4},{6,7},{7,6},{8,9},{9,8},{10,11... | collective-permute-start | bytes 393224 | tf_op jit(solution)/shard_map/ppermute | solution.py:350
  28.9 19.8 %collective-permute-start.10 = (f32[4,4,64,128]{3,2,1,0:T(8,128)S(1)}, f32[4,4,64,128]{3,2,1,0:T(8,128)S(1)}, u32[]{:S(2)}, u32[]{:S(2)}) collective-permute-start(f32[4,4,64,128]{3,2,1,0:T(8,128)S(1)} %get-tuple-element.34.refs_2_.own), channel_id=1, source_target_pairs={{0,1},{1,0},{2,3},{3,2},{4,5},{5,4},{6,7},{7,6},{8,9},{9,8},{10,11... | collective-permute-start | bytes 1572872 | tf_op jit(solution)/shard_map/ppermute | solution.py:350
  30.9 5.3 %collective-permute-start.13 = (f32[384,128]{1,0:T(8,128)S(1)}, f32[384,128]{1,0:T(8,128)S(1)}, u32[]{:S(2)}, u32[]{:S(2)}) collective-permute-start(f32[384,128]{1,0:T(8,128)S(1)} %get-tuple-element.38), channel_id=1, source_target_pairs={{0,1},{1,0},{2,3},{3,2},{4,5},{5,4},{6,7},{7,6},{8,9},{9,8},{10,11... | collective-permute-start | bytes 589832 | tf_op jit(solution)/shard_map/ppermute | solution.py:350
  31.1 8.1 %collective-permute-start.11 = (f32[1,4,64,128]{3,2,1,0:T(8,128)S(1)}, f32[1,4,64,128]{3,2,1,0:T(8,128)S(1)}, u32[]{:S(2)}, u32[]{:S(2)}) collective-permute-start(f32[1,4,64,128]{3,2,1,0:T(8,128)S(1)} %get-tuple-element.35), channel_id=1, source_target_pairs={{0,2},{2,0},{4,6},{6,4},{8,10},{10,8},{12,14},{14,12},{1,3},{3,1},... | collective-permute-start | bytes 393224 | tf_op jit(solution)/shard_map/ppermute | solution.py:362
  35.5 3.8 %collective-permute-start.12 = (f32[1,4,64,128]{3,2,1,0:T(8,128)S(1)}, f32[1,4,64,128]{3,2,1,0:T(8,128)S(1)}, u32[]{:S(2)}, u32[]{:S(2)}) collective-permute-start(f32[1,4,64,128]{3,2,1,0:T(8,128)S(1)} %get-tuple-element.36), channel_id=1, source_target_pairs={{2,4},{4,2},{6,8},{8,6},{10,12},{12,10},{3,5},{5,3},{7,9},{9,7},{1... | collective-permute-start | bytes 393224 | tf_op jit(solution)/shard_map/ppermute | solution.py:361
  39.3 9.4 %collective-permute-start.14 = (f32[1,4,64,128]{3,2,1,0:T(8,128)S(1)}, f32[1,4,64,128]{3,2,1,0:T(8,128)S(1)}, u32[]{:S(2)}, u32[]{:S(2)}) collective-permute-start(f32[1,4,64,128]{3,2,1,0:T(8,128)S(1)} %collective-permute-done.11.refs_0_), channel_id=1, source_target_pairs={{0,1},{1,0},{2,3},{3,2},{4,5},{5,4},{6,7},{7,6},{8,9},{9,8},{10,11... | collective-permute-start | bytes 393224 | tf_op jit(solution)/shard_map/ppermute | solution.py:350
  39.3 9.4 %collective-permute-start.15 = (f32[1,4,64,128]{3,2,1,0:T(8,128)S(1)}, f32[1,4,64,128]{3,2,1,0:T(8,128)S(1)}, u32[]{:S(2)}, u32[]{:S(2)}) collective-permute-start(f32[1,4,64,128]{3,2,1,0:T(8,128)S(1)} %collective-permute-done.12.refs_2_), channel_id=1, source_target_pairs={{0,1},{1,0},{2,3},{3,2},{4,5},{5,4},{6,7},{7,6},{8,9},{9,8},{10,11... | collective-permute-start | bytes 393224 | tf_op jit(solution)/shard_map/ppermute | solution.py:350
  39.8 17.0 %all-to-all-start = ((f32[8,48,128]{2,1,0:T(8,128)}), f32[8,48,128]{2,1,0:T(8,128)S(1)}, u32[]{:S(2)}, u32[]{:S(2)}) async-start(f32[8,48,128]{2,1,0:T(8,128)} %bitcast.4), calls=%async_computation | async-start | bytes 393216 | tf_op jit(solution)/shard_map/all_to_all | solution.py:353
  48.7 1.6 %copy-start.4 = (bf16[16,128,512]{2,1,0:T(8,128)(2,1)S(1)}, bf16[16,128,512]{2,1,0:T(8,128)(2,1)}, u32[]{:S(2)}) copy-start(bf16[16,128,512]{2,1,0:T(8,128)(2,1)} %pack.1.packed) | copy-start | bytes 6291460
  53.4 1.4 %collective-permute-start.16 = (f32[256,128]{1,0:T(8,128)S(1)}, f32[256,128]{1,0:T(8,128)S(1)}, u32[]{:S(2)}, u32[]{:S(2)}) collective-permute-start(f32[256,128]{1,0:T(8,128)S(1)} %get-tuple-element.42), channel_id=1, source_target_pairs={{0,1},{1,0},{2,3},{3,2},{4,5},{5,4},{6,7},{7,6},{8,9},{9,8},{10,11... | collective-permute-start | bytes 393224 | tf_op jit(solution)/shard_map/ppermute | solution.py:350
  57.5 13.2 %all-to-all-start.1 = ((f32[8,48,128]{2,1,0:T(8,128)}), f32[8,48,128]{2,1,0:T(8,128)S(1)}, u32[]{:S(2)}, u32[]{:S(2)}) async-start(f32[8,48,128]{2,1,0:T(8,128)} %broadcast_in_dim.2), calls=%async_computation.1 | async-start | bytes 393216 | tf_op jit(solution)/shard_map/all_to_all | solution.py:353
  61.5 7.3 %collective-permute-start.17 = (f32[256,128]{1,0:T(8,128)S(1)}, f32[256,128]{1,0:T(8,128)S(1)}, u32[]{:S(2)}, u32[]{:S(2)}) collective-permute-start(f32[256,128]{1,0:T(8,128)S(1)} %add.29), channel_id=1, source_target_pairs={{0,2},{2,0},{4,6},{6,4},{8,10},{10,8},{12,14},{14,12},{1,3},{3,1},... | collective-permute-start | bytes 393224 | tf_op jit(solution)/shard_map/ppermute | solution.py:385
  68.9 5.0 %collective-permute-start.18 = (f32[256,128]{1,0:T(8,128)S(1)}, f32[256,128]{1,0:T(8,128)S(1)}, u32[]{:S(2)}, u32[]{:S(2)}) collective-permute-start(f32[256,128]{1,0:T(8,128)S(1)} %add.30), channel_id=1, source_target_pairs={{0,4},{2,6},{4,0},{6,2},{8,12},{10,14},{12,8},{14,10},{1,5},{3,7},... | collective-permute-start | bytes 393224 | tf_op jit(solution)/shard_map/ppermute | solution.py:385
  70.7 10.7 %collective-permute-start.21 = (f32[384,128]{1,0:T(8,128)S(1)}, f32[384,128]{1,0:T(8,128)S(1)}, u32[]{:S(2)}, u32[]{:S(2)}) collective-permute-start(f32[384,128]{1,0:T(8,128)S(1)} %bitcast.6), channel_id=1, source_target_pairs={{0,1},{1,0},{2,3},{3,2},{4,5},{5,4},{6,7},{7,6},{8,9},{9,8},{10,11... | collective-permute-start | bytes 589832 | tf_op jit(solution)/shard_map/ppermute | solution.py:350
  73.9 7.3 %collective-permute-start.19 = (f32[256,128]{1,0:T(8,128)S(1)}, f32[256,128]{1,0:T(8,128)S(1)}, u32[]{:S(2)}, u32[]{:S(2)}) collective-permute-start(f32[256,128]{1,0:T(8,128)S(1)} %add.31), channel_id=1, source_target_pairs={{0,8},{2,10},{4,12},{6,14},{8,0},{10,2},{12,4},{14,6},{1,9},{3,11}... | collective-permute-start | bytes 393224 | tf_op jit(solution)/shard_map/ppermute | solution.py:385
  81.3 12.3 %collective-permute-start.20 = (f32[256,128]{1,0:T(8,128)S(1)}, f32[256,128]{1,0:T(8,128)S(1)}, u32[]{:S(2)}, u32[]{:S(2)}) collective-permute-start(f32[256,128]{1,0:T(8,128)S(1)} %add.32.own), channel_id=1, source_target_pairs={{0,1},{1,0},{2,3},{3,2},{4,5},{5,4},{6,7},{7,6},{8,9},{9,8},{10,11... | collective-permute-start | bytes 393224 | tf_op jit(solution)/shard_map/ppermute | solution.py:350

commit v4 on v3

--- a/solution.py
+++ b/solution.py
@@ -12,7 +12,6 @@
 center_shift = 2.0
 half_range = 1.6
 VMEM_LIMIT = 16 * 1024 * 1024
-PACK_VMEM_LIMIT = 60 * 1024 * 1024
 
 
 def estimate(us):
@@ -25,52 +24,43 @@
     return high, low
 
 
-def pack_kernel(count, cross_local, layers, slots, info, couplings, sigma, out):
-    layer = pl.program_id(0)
-    first = jnp.logical_and(layer == 0, info[1] == 1)
-    last = jnp.logical_and(layer == layers - 1, info[2] == 1)
-    for q in range(cross_local):
-        place = info[0] * cross_local + q
-        lead = None
-        for k in range(2 * count):
-            flag = first if k < count else last
-            weight = jnp.where(jnp.logical_and(flag, info[4 + k] == place), -1.0, 0.0)
-            term = sigma[k] * weight
-            lead = term if lead is None else lead + term
-        blocks = [couplings[0, q, j] for j in range(slots)] + [lead]
-        row = jnp.concatenate(
-            [jnp.concatenate(blocks[i : i + 2], axis=1) for i in range(0, slots + 1, 2)], axis=1
-        )
-        high, low = split(row)
-        half = high.shape[0]
-        out[q, :half] = high
-        out[q, half:] = low
-
-
-def pack(couplings, lead_sigma, info):
+def pack_kernel(info, sites, held, leads, out):
+    layers, cross_local, slots, size, _ = held.shape
+    contacts = leads.shape[0]
+    for layer in range(layers):
+        for q in range(cross_local):
+            place = info[0] * cross_local + q
+            lead = jnp.zeros((size, size), jnp.float32)
+            for k in range(contacts):
+                end, flag = (0, info[1]) if k < contacts // 2 else (layers - 1, info[2])
+                if layer == end:
+                    here = jnp.logical_and(flag == 1, sites[k] == place)
+                    lead = lead - leads[k] * jnp.where(here, 1.0, 0.0)
+            blocks = [held[layer, q, j] for j in range(slots)] + [lead]
+            row = jnp.concatenate(
+                [jnp.concatenate(blocks[i : i + 2], axis=1) for i in range(0, slots + 1, 2)],
+                axis=1,
+            )
+            high, low = split(row)
+            out[layer * cross_local + q, :size] = high
+            out[layer * cross_local + q, size:] = low
+
+
+def pack(couplings, lead_sites, lead_sigma, info):
     layers, cross_local, slots, size, _ = couplings.shape
-    contacts = lead_sigma.shape[0]
-    body = functools.partial(pack_kernel, contacts // 2, cross_local, layers, slots)
+    scalar = pl.BlockSpec(memory_space=pltpu.SMEM)
+    whole = pl.BlockSpec(memory_space=pltpu.VMEM)
     return pl.pallas_call(
-        body,
-        grid_spec=pltpu.PrefetchScalarGridSpec(
-            num_scalar_prefetch=1,
-            grid=(layers,),
-            in_specs=[
-                pl.BlockSpec((1, cross_local, slots, size, size), lambda i, *_: (i, 0, 0, 0, 0)),
-                pl.BlockSpec((contacts, size, size), lambda i, *_: (0, 0, 0)),
-            ],
-            out_specs=pl.BlockSpec(
-                (cross_local, 2 * size, (slots + 1) * size), lambda i, *_: (i, 0, 0)
-            ),
-        ),
+        pack_kernel,
+        in_specs=[scalar, scalar, whole, whole],
+        out_specs=whole,
         out_shape=jax.ShapeDtypeStruct(
             (layers * cross_local, 2 * size, (slots + 1) * size), jnp.bfloat16
         ),
-        compiler_params=pltpu.CompilerParams(vmem_limit_bytes=PACK_VMEM_LIMIT),
+        compiler_params=pltpu.CompilerParams(vmem_limit_bytes=VMEM_LIMIT),
         cost_estimate=estimate(2.5),
         name="pack",
-    )(info, couplings, lead_sigma)
+    )(info, lead_sites, couplings, lead_sigma)
 
 
 def step_kernel(first, last, slots, info, cols, packed, own, other, *refs):
@@ -92,7 +82,7 @@
             put((layer + 1) * total + mine + q, own[layer, q])
             put((layer + 1) * total + theirs + q, other[layer, q])
     even = info[3]
-    for pair, place in enumerate((even, 1 - even)):
+    for pair, place in enumerate((1 - even, even)):
         for q in range(cross_local):
             put(place * (layers + 1) * total + mine + q, edges[2 * pair][0, q])
             put(place * (layers + 1) * total + theirs + q, edges[2 * pair + 1][0, q])
@@ -339,8 +329,8 @@
     place = lax.axis_index("trans")
     even = 1 - place % 2
     info = jnp.stack([lax.axis_index("cross"), place == 0, place == count - 1, even])
-    info = jnp.concatenate([info.astype(jnp.int32), lead_sites])
-    packed = pack(couplings, lead_sigma, info)
+    info = info.astype(jnp.int32)
+    packed = pack(couplings, lead_sites, lead_sigma, info)
     scale_rows = math.sqrt(count * layers * cross_local * cross_count * size)
 
     near = [(i, i ^ 1) for i in range(count) if i ^ 1 < count]
@@ -351,6 +341,9 @@
 
     def exchange(x):
         return lax.all_to_all(x, "trans", 0, 0, tiled=True)
+
+    def double(x, reach):
+        return x + lax.ppermute(x, "trans", [(i, i ^ reach) for i in range(count)])
 
     early = tuple((i, j) for i in range(S) for j in range(i + 1))
     powers = [sources]
@@ -364,11 +357,12 @@
         if k == 0:
             near_edge, far_edge, packed = lax.optimization_barrier((near_edge, far_edge, packed))
         if k == S - 1:
-            mine, theirs = gram_blocks(powers, early, info, count)
+            held, other = lax.optimization_barrier((field, other))
+            mine, theirs = gram_blocks([*powers[:-1], held], early, info, count)
             shares = (mine + swap(theirs)).reshape(count, -1, columns)
             near_edge, far_edge, shares = lax.optimization_barrier((near_edge, far_edge, shares))
             parts = exchange(shares)
-        edges = (near_edge, swap(near_edge), far_edge, swap(far_edge))
+        edges = (far_edge, swap(far_edge), near_edge, swap(near_edge))
         before = powers[k - 1] if k else None
         got = step(packed, block_cols, info, field, other, edges, before, k == S - 1)
         powers.append(got[0])
@@ -380,12 +374,15 @@
     summed = jnp.sum(parts, axis=0, keepdims=True)
     known = exchange(jnp.broadcast_to(summed, parts.shape)).reshape(-1, columns)
     known_other = swap(known)
+    first = column(0, 0, info, known, known_other, ())
     reach = 1
     while reach < count:
-        last = last + lax.ppermute(last, "trans", [(i, i ^ reach) for i in range(count)])
+        last = double(last, reach)
         reach *= 2
-    first = column(0, 0, info, known, known_other, ())
+        if reach == count // 2:
+            last, first = lax.optimization_barrier((last, first))
     second = column(1, 1, info, known, known_other, first[::-1])
+    last, second = lax.optimization_barrier((last, second))
     third = column(2, 3, info, known, known_other, second[::-1])
     r_factor, inverse = column(3, 0, info, last, swap(last), third[::-1], 1.0 / scale_rows)
     return basis_of(powers, inverse, scale_rows), r_factor

time: 103 us -> 103 us (level)
  waiting for transfers between devices: 24.6 us -> 30.4 us
  Pallas kernels: 34.4 us -> 30.2 us
  starting transfers between devices: 35.7 us -> 33.5 us
    all_to_all x2, waiting for transfers between devices: 1.94 us -> 8.2 us  [exchange(): return lax.all_to_all(x, 'trans', 0, 0, tiled=True)]
    ppermute x3, waiting for transfers between devices: 13.2 us -> 8.26 us  [double(): return x + lax.ppermute(x, 'trans', [(i, i ^ reach) for i in range(count)])]
    pallas_call x1, Pallas kernels: 5.23 us -> 1.08 us  [pack(): pl.pallas_call(pack_kernel, in_specs=[scalar, scalar, whole, whole], out_...]
    ppermute x3, starting transfers between devices: 6.5 us -> 3.65 us  [double(): return x + lax.ppermute(x, 'trans', [(i, i ^ reach) for i in range(count)])]
    ppermute x3, waiting for transfers between devices: 6.04 us -> 8.48 us  [local(): near_edge = lax.ppermute(near_layer, 'trans', near)]
    ppermute x3, starting transfers between devices: 11 us -> 13.2 us  [local(): near_edge = lax.ppermute(near_layer, 'trans', near)]
    ppermute x13, waiting for transfers between devices: 3.4 us -> 5.47 us  [swap(): return lax.ppermute(x, 'cross', [(0, 1), (1, 0)])]
    unnamed x10 -> x14, local copies, waits for them, and re-layouts: 3.18 us -> 5.19 us
  transfers between devices with their start and end apart: 24 -> 24, of which waited for: 11 -> 12; matrix products, arithmetic and copies ran while one was open for 3% -> 2% of each run, Pallas kernels for 22% -> 12%
where the time goes in v4:
time: 103 us
  starting transfers between devices  33.5 us (33%)
  waiting for transfers between devices  30.4 us (30%)
  Pallas kernels  30.2 us (29%)
  local copies, waits for them, and re-layouts  6.87 us (7%)
    pallas_call x4, Pallas kernels, column(): pl.pallas_call(functools.partial(column_kernel, place, first, scale), in_...  17.9 us
    ppermute x3, starting transfers between devices, local(): near_edge = lax.ppermute(near_layer, 'trans', near)  13.2 us
    all_to_all x2, starting transfers between devices, exchange(): return lax.all_to_all(x, 'trans', 0, 0, tiled=True)  12.2 us
    ppermute x3, waiting for transfers between devices, local(): near_edge = lax.ppermute(near_layer, 'trans', near)  8.48 us
    ppermute x3, waiting for transfers between devices, double(): return x + lax.ppermute(x, 'trans', [(i, i ^ reach) for i in range(count)])  8.26 us
    all_to_all x2, waiting for transfers between devices, exchange(): return lax.all_to_all(x, 'trans', 0, 0, tiled=True)  8.2 us
    ppermute x13, waiting for transfers between devices, swap(): return lax.ppermute(x, 'cross', [(0, 1), (1, 0)])  5.47 us
    unnamed x14, local copies, waits for them, and re-layouts  5.19 us
  transfers between devices with their start and end apart: 24, of which 12 were waited for; matrix products, arithmetic and copies ran while one was open for 2% of the time, Pallas kernels for 12%

profile of v4, /device:TPU:0, one launch (start us, length us, event | category | flops | bytes accessed | tf_op | source)
XLA Modules:
  0.0 102.7 jit_solution(5941852183478593230)
XLA Ops:
  0.6 0.5 collective-permute-start.2
  1.1 1.0 constant_dynamic-slice_fusion
  2.1 0.7 collective-permute-start.1
  2.8 5.4 %collective-permute-start = (f32[1,4,64,128]{3,2,1,0:T(8,128)S(1)}, f32[1,4,64,128]{3,2,1,0:T(8,128)S(1)}, u32[]{:S(2)}, u32[]{:S(2)}) collective-permute-start(f32[1,4,64,128]{3,2,1,0:T(8,128)S(1)} %get-tuple-element.71), channel_id=1, source_target_pairs={{0,2},{2,0},{4,6},{6,4},{8,10},{10,8},{12,14},{14,12},{1,3},{3,1},... | collective-permute-start | bytes 393224 | tf_op jit(solution)/shard_map/ppermute | solution.py:355
  8.2 0.1 pad_add_fusion.info
  8.3 2.0 %copy-done.1 = f32[4,4,7,64,64]{4,3,2,1,0:T(8,128)S(1)} copy-done((f32[4,4,7,64,64]{4,3,2,1,0:T(8,128)S(1)}, f32[4,4,7,64,64]{4,3,2,1,0:T(8,128)}, u32[]{:S(2)}) %copy-start.1) | copy-done | bytes 1835032
  10.3 0.9 copy-done.2
  11.2 0.7 copy-done.4
  11.9 1.1 %pack.1.packed = bf16[16,128,512]{2,1,0:T(8,128)(2,1)S(1)} custom-call(s32[4]{0:T(128)S(1)} %pad_add_fusion.info, s32[4]{0:T(128)S(1)} %copy-done.4, f32[4,4,7,64,64]{4,3,2,1,0:T(8,128)S(1)} %copy-done.1, f32[4,64,64]{2,1,0:T(8,128)S(1)} %copy-done.2), custom_call_target="tpu_custom_call" | custom-call | flops 2875000064 | tf_op jit(solution)/shard_map/pack/pallas_call | solution.py:53
  13.0 0.7 collective-permute-done.refs_2_
  13.7 0.5 collective-permute-start.4
  14.2 0.8 collective-permute-done.3.refs_1_
  15.0 0.2 collective-permute-done.4.refs_3_
  15.2 1.7 %step.3 = (f32[4,4,64,128]{3,2,1,0:T(8,128)S(1)}, f32[1,4,64,128]{3,2,1,0:T(8,128)S(1)}, f32[1,4,64,128]{3,2,1,0:T(8,128)S(1)}) custom-call(s32[4]{0:T(128)S(1)} %pad_add_fusion.info, s32[4,4,7]{2,1,0:T(4,128)S(1)} %copy-done.3, bf16[16,128,512]{2,1,0:T(8,128)(2,1)S(1)} %pack.1.packed, f32[4,4,64,128]{3,2,1,0:T(8,128)S(1)} %copy-done, ...), custom_call_target="tpu_custom_call" | custom-call | flops 1955000064 | tf_op jit(solution)/shard_map/step/pallas_call | solution.py:114
  16.9 0.4 collective-permute-start.5
  17.3 0.7 collective-permute-start.6
  18.0 5.3 %collective-permute-start.8 = (f32[1,4,64,128]{3,2,1,0:T(8,128)S(1)}, f32[1,4,64,128]{3,2,1,0:T(8,128)S(1)}, u32[]{:S(2)}, u32[]{:S(2)}) collective-permute-start(f32[1,4,64,128]{3,2,1,0:T(8,128)S(1)} %get-tuple-element.41), channel_id=1, source_target_pairs={{0,2},{2,0},{4,6},{6,4},{8,10},{10,8},{12,14},{14,12},{1,3},{3,1},... | collective-permute-start | bytes 393224 | tf_op jit(solution)/shard_map/ppermute | solution.py:355
  23.3 5.2 %collective-permute-done.8.refs_2_ = f32[1,4,64,128]{3,2,1,0:T(8,128)S(1)} collective-permute-done((f32[1,4,64,128]{3,2,1,0:T(8,128)S(1)}, f32[1,4,64,128]{3,2,1,0:T(8,128)S(1)}, u32[]{:S(2)}, u32[]{:S(2)}) %collective-permute-start.8) | collective-permute-done | bytes 131104 | tf_op jit(solution)/shard_map/ppermute | solution.py:355
  28.5 1.3 %collective-permute-done.9.refs_3_ = f32[1,4,64,128]{3,2,1,0:T(8,128)S(1)} collective-permute-done((f32[1,4,64,128]{3,2,1,0:T(8,128)S(1)}, f32[1,4,64,128]{3,2,1,0:T(8,128)S(1)}, u32[]{:S(2)}, u32[]{:S(2)}) %collective-permute-start.9) | collective-permute-done | bytes 131104 | tf_op jit(solution)/shard_map/ppermute | solution.py:340
  29.8 1.7 %step.4 = (f32[4,4,64,128]{3,2,1,0:T(8,128)S(1)}, f32[1,4,64,128]{3,2,1,0:T(8,128)S(1)}, f32[1,4,64,128]{3,2,1,0:T(8,128)S(1)}) custom-call(s32[4]{0:T(128)S(1)} %pad_add_fusion.info, s32[4,4,7]{2,1,0:T(4,128)S(1)} %copy-done.3, bf16[16,128,512]{2,1,0:T(8,128)(2,1)S(1)} %pack.1.packed, f32[4,4,64,128]{3,2,1,0:T(8,128)S(1)} %get-tuple-element.39.own.refs_1_.refs_4_, ...), custom_call_target="tpu_custom_call" | custom-call | flops 1955000064 | tf_op jit(solution)/shard_map/step/pallas_call | solution.py:114
  31.5 0.2 collective-permute-start.10
  31.7 1.8 %collective-permute-done.10.other = f32[4,4,64,128]{3,2,1,0:T(8,128)S(1)} collective-permute-done((f32[4,4,64,128]{3,2,1,0:T(8,128)S(1)}, f32[4,4,64,128]{3,2,1,0:T(8,128)S(1)}, u32[]{:S(2)}, u32[]{:S(2)}) %collective-permute-start.10) | collective-permute-done | bytes 524320 | tf_op jit(solution)/shard_map/ppermute | solution.py:340
  33.5 1.6 %gram.2 = (f32[384,128]{1,0:T(8,128)S(1)}, f32[384,128]{1,0:T(8,128)S(1)}) custom-call(s32[4]{0:T(128)S(1)} %pad_add_fusion.info, f32[4,4,64,128]{3,2,1,0:T(8,128)S(1)} %copy-done, f32[4,4,64,128]{3,2,1,0:T(8,128)S(1)} %get-tuple-element.39.own.refs_1_.refs_4_, f32[4,4,64,128]{3,2,1,0:T(8,128)S(1)} %get-tuple-element.46.refs_2_.own), custom_call_target="tpu_custom_call" | custom-call | flops 1610000000 | tf_op jit(solution)/shard_map/gram/pallas_call | solution.py:156
  35.1 0.2 collective-permute-start.13
  35.3 2.5 %collective-permute-start.11 = (f32[1,4,64,128]{3,2,1,0:T(8,128)S(1)}, f32[1,4,64,128]{3,2,1,0:T(8,128)S(1)}, u32[]{:S(2)}, u32[]{:S(2)}) collective-permute-start(f32[1,4,64,128]{3,2,1,0:T(8,128)S(1)} %get-tuple-element.44), channel_id=1, source_target_pairs={{0,2},{2,0},{4,6},{6,4},{8,10},{10,8},{12,14},{14,12},{1,3},{3,1},... | collective-permute-start | bytes 393224 | tf_op jit(solution)/shard_map/ppermute | solution.py:355
  37.8 0.7 collective-permute-start.12
  38.5 0.7 add.28
  39.2 2.6 %collective-permute-done.11.refs_2_ = f32[1,4,64,128]{3,2,1,0:T(8,128)S(1)} collective-permute-done((f32[1,4,64,128]{3,2,1,0:T(8,128)S(1)}, f32[1,4,64,128]{3,2,1,0:T(8,128)S(1)}, u32[]{:S(2)}, u32[]{:S(2)}) %collective-permute-start.11) | collective-permute-done | bytes 131104 | tf_op jit(solution)/shard_map/ppermute | solution.py:355
  41.8 0.5 collective-permute-start.15
  42.3 8.1 %all-to-all-start = ((f32[8,48,128]{2,1,0:T(8,128)}), f32[8,48,128]{2,1,0:T(8,128)S(1)}, u32[]{:S(2)}, u32[]{:S(2)}) async-start(f32[8,48,128]{2,1,0:T(8,128)} %bitcast.4), calls=%async_computation | async-start | bytes 393216 | tf_op jit(solution)/shard_map/all_to_all | solution.py:343
  50.5 1.6 %copy-done.6 = bf16[16,128,512]{2,1,0:T(8,128)(2,1)S(1)} copy-done((bf16[16,128,512]{2,1,0:T(8,128)(2,1)S(1)}, bf16[16,128,512]{2,1,0:T(8,128)(2,1)}, u32[]{:S(2)}) %copy-start.6) | copy-done | bytes 2097176
  52.1 1.7 %step.5.refs_3_ = f32[4,4,64,128]{3,2,1,0:T(8,128)S(1)} custom-call(s32[4]{0:T(128)S(1)} %pad_add_fusion.info, s32[4,4,7]{2,1,0:T(4,128)S(1)} %copy-done.3, bf16[16,128,512]{2,1,0:T(8,128)(2,1)S(1)} %copy-done.6, f32[4,4,64,128]{3,2,1,0:T(8,128)S(1)} %get-tuple-element.46.refs_2_.own, f32[4,4,64,128]{3,2,1,0:T(8,128)S(1)} %collective-permute-done.10.other, ...), custom_call_target="tpu_custom_call" | custom-call | flops 1955000064 | tf_op jit(solution)/shard_map/step/pallas_call | solution.py:114
  53.8 1.4 %gram.3 = (f32[256,128]{1,0:T(8,128)S(1)}, f32[256,128]{1,0:T(8,128)S(1)}) custom-call(s32[4]{0:T(128)S(1)} %pad_add_fusion.info, f32[4,4,64,128]{3,2,1,0:T(8,128)S(1)} %copy-done, f32[4,4,64,128]{3,2,1,0:T(8,128)S(1)} %get-tuple-element.39.own.refs_1_.refs_4_, f32[4,4,64,128]{3,2,1,0:T(8,128)S(1)} %get-tuple-element.46.refs_2_.own, ...), custom_call_target="tpu_custom_call" | custom-call | flops 1610000000 | tf_op jit(solution)/shard_map/gram/pallas_call | solution.py:156
  55.3 1.3 %collective-permute-done.16 = f32[256,128]{1,0:T(8,128)S(1)} collective-permute-done((f32[256,128]{1,0:T(8,128)S(1)}, f32[256,128]{1,0:T(8,128)S(1)}, u32[]{:S(2)}, u32[]{:S(2)}) %collective-permute-start.16) | collective-permute-done | bytes 131104 | tf_op jit(solution)/shard_map/ppermute | solution.py:340
  56.6 2.0 %all-to-all-done = f32[8,48,128]{2,1,0:T(8,128)S(1)} async-done(((f32[8,48,128]{2,1,0:T(8,128)}), f32[8,48,128]{2,1,0:T(8,128)S(1)}, u32[]{:S(2)}, u32[]{:S(2)}) %all-to-all-start) | async-done | bytes 196640 | tf_op jit(solution)/shard_map/all_to_all | solution.py:343
  58.6 0.7 broadcast_in_dim.2
  59.3 4.1 %all-to-all-start.1 = ((f32[8,48,128]{2,1,0:T(8,128)}), f32[8,48,128]{2,1,0:T(8,128)S(1)}, u32[]{:S(2)}, u32[]{:S(2)}) async-start(f32[8,48,128]{2,1,0:T(8,128)} %broadcast_in_dim.2), calls=%async_computation.1 | async-start | bytes 393216 | tf_op jit(solution)/shard_map/all_to_all | solution.py:343
  63.3 2.0 %collective-permute-start.17 = (f32[256,128]{1,0:T(8,128)S(1)}, f32[256,128]{1,0:T(8,128)S(1)}, u32[]{:S(2)}, u32[]{:S(2)}) collective-permute-start(f32[256,128]{1,0:T(8,128)S(1)} %add.29), channel_id=1, source_target_pairs={{0,2},{2,0},{4,6},{6,4},{8,10},{10,8},{12,14},{14,12},{1,3},{3,1},... | collective-permute-start | bytes 393224 | tf_op jit(solution)/shard_map/ppermute | solution.py:346
  65.4 6.2 %all-to-all-done.1 = f32[8,48,128]{2,1,0:T(8,128)S(1)} async-done(((f32[8,48,128]{2,1,0:T(8,128)}), f32[8,48,128]{2,1,0:T(8,128)S(1)}, u32[]{:S(2)}, u32[]{:S(2)}) %all-to-all-start.1) | async-done | bytes 196640 | tf_op jit(solution)/shard_map/all_to_all | solution.py:343
  71.6 0.8 collective-permute-start.18
  72.5 5.1 %collective-permute-done.18 = f32[256,128]{1,0:T(8,128)S(1)} collective-permute-done((f32[256,128]{1,0:T(8,128)S(1)}, f32[256,128]{1,0:T(8,128)S(1)}, u32[]{:S(2)}, u32[]{:S(2)}) %collective-permute-start.18) | collective-permute-done | bytes 131104 | tf_op jit(solution)/shard_map/ppermute | solution.py:346
  77.6 3.8 %column.4 = (f32[128,128]{1,0:T(8,128)S(1)}, f32[128,128]{1,0:T(8,128)S(1)}) custom-call(s32[4]{0:T(128)S(1)} %pad_add_fusion.info, f32[384,128]{1,0:T(8,128)S(1)} %bitcast.7, f32[384,128]{1,0:T(8,128)S(1)} %collective-permute-done.19.other), custom_call_target="tpu_custom_call" | custom-call | flops 4600000000 | tf_op jit(solution)/shard_map/column/pallas_call | solution.py:269
  81.4 0.8 collective-permute-start.20
  82.2 4.2 %column.5 = (f32[256,256]{1,0:T(8,128)S(1)}, f32[256,256]{1,0:T(8,128)S(1)}) custom-call(s32[4]{0:T(128)S(1)} %pad_add_fusion.info, f32[384,128]{1,0:T(8,128)S(1)} %bitcast.8, f32[384,128]{1,0:T(8,128)S(1)} %collective-permute-done.19.other, f32[128,128]{1,0:T(8,128)S(1)} %get-tuple-element.59.refs_0_, f32[128,128]{1,0:T(8,128)S(1)} %get-tuple-element.60.refs_1_), custom_call_target="tpu_custom_call" | custom-call | flops 4600000000 | tf_op jit(solution)/shard_map/column/pallas_call | solution.py:269
  86.4 3.1 %collective-permute-done.20 = f32[256,128]{1,0:T(8,128)S(1)} collective-permute-done((f32[256,128]{1,0:T(8,128)S(1)}, f32[256,128]{1,0:T(8,128)S(1)}, u32[]{:S(2)}, u32[]{:S(2)}) %collective-permute-start.20) | collective-permute-done | bytes 131104 | tf_op jit(solution)/shard_map/ppermute | solution.py:346
  89.6 4.2 %column.6 = (f32[384,384]{1,0:T(8,128)S(1)}, f32[384,384]{1,0:T(8,128)S(1)}) custom-call(s32[4]{0:T(128)S(1)} %pad_add_fusion.info, f32[384,128]{1,0:T(8,128)S(1)} %bitcast.9, f32[384,128]{1,0:T(8,128)S(1)} %collective-permute-done.19.other, f32[256,256]{1,0:T(8,128)S(1)} %get-tuple-element.64.refs_0_, f32[256,256]{1,0:T(8,128)S(1)} %get-tuple-element.65.refs_1_), custom_call_target="tpu_custom_call" | custom-call | flops 4600000000 | tf_op jit(solution)/shard_map/column/pallas_call | solution.py:269
  93.8 5.7 %column.7 = (f32[512,512]{1,0:T(8,128)}, f32[512,512]{1,0:T(8,128)S(1)}) custom-call(s32[4]{0:T(128)S(1)} %pad_add_fusion.info, f32[256,128]{1,0:T(8,128)S(1)} %add.32.own, f32[256,128]{1,0:T(8,128)S(1)} %collective-permute-done.21.other, f32[384,384]{1,0:T(8,128)S(1)} %get-tuple-element.66.refs_0_, f32[384,384]{1,0:T(8,128)S(1)} %get-tuple-element.67.refs_1_), custom_call_target="tpu_custom_call" | custom-call | flops 4600000000 | tf_op jit(solution)/shard_map/column/pallas_call | solution.py:269
  99.5 3.2 %basis.1 = bf16[4,4,64,512]{3,2,1,0:T(8,128)(2,1)} custom-call(f32[4,4,64,128]{3,2,1,0:T(8,128)S(1)} %copy-done, f32[4,4,64,128]{3,2,1,0:T(8,128)S(1)} %get-tuple-element.39.own.refs_1_.refs_4_, f32[4,4,64,128]{3,2,1,0:T(8,128)S(1)} %get-tuple-element.46.refs_2_.own, f32[4,4,64,128]{3,2,1,0:T(8,128)S(1)} %step.5.refs_3_, ...), custom_call_target="tpu_custom_call" | custom-call | flops 3449999872 | tf_op jit(solution)/shard_map/basis/pallas_call | solution.py:311
  (34 shorter events, 0.3 us)
Async XLA Ops:
  0.6 14.6 %collective-permute-start.2 = (f32[4,4,64,128]{3,2,1,0:T(8,128)}, f32[4,4,64,128]{3,2,1,0:T(8,128)S(1)}, u32[]{:S(2)}, u32[]{:S(2)}) collective-permute-start(f32[4,4,64,128]{3,2,1,0:T(8,128)} %refs_0_.5), channel_id=1, source_target_pairs={{0,1},{1,0},{2,3},{3,2},{4,5},{5,4},{6,7},{7,6},{8,9},{9,8},{10,11... | collective-permute-start | bytes 1572872 | tf_op jit(solution)/shard_map/ppermute | solution.py:340
  2.1 10.8 %collective-permute-start.1 = (f32[1,4,64,128]{3,2,1,0:T(8,128)S(1)}, f32[1,4,64,128]{3,2,1,0:T(8,128)S(1)}, u32[]{:S(2)}, u32[]{:S(2)}) collective-permute-start(f32[1,4,64,128]{3,2,1,0:T(8,128)S(1)} %get-tuple-element.70), channel_id=1, source_target_pairs={{2,4},{4,2},{6,8},{8,6},{10,12},{12,10},{3,5},{5,3},{7,9},{9,7},{1... | collective-permute-start | bytes 393224 | tf_op jit(solution)/shard_map/ppermute | solution.py:354
  2.8 10.9 %collective-permute-start = (f32[1,4,64,128]{3,2,1,0:T(8,128)S(1)}, f32[1,4,64,128]{3,2,1,0:T(8,128)S(1)}, u32[]{:S(2)}, u32[]{:S(2)}) collective-permute-start(f32[1,4,64,128]{3,2,1,0:T(8,128)S(1)} %get-tuple-element.71), channel_id=1, source_target_pairs={{0,2},{2,0},{4,6},{6,4},{8,10},{10,8},{12,14},{14,12},{1,3},{3,1},... | collective-permute-start | bytes 393224 | tf_op jit(solution)/shard_map/ppermute | solution.py:355
  8.3 2.0 %copy-start.1 = (f32[4,4,7,64,64]{4,3,2,1,0:T(8,128)S(1)}, f32[4,4,7,64,64]{4,3,2,1,0:T(8,128)}, u32[]{:S(2)}) copy-start(f32[4,4,7,64,64]{4,3,2,1,0:T(8,128)} %held.1) | copy-start | bytes 5505028
  10.3 0.9 copy-start.2
  11.2 0.7 copy-start.4
  11.9 3.3 %copy-start = (f32[4,4,64,128]{3,2,1,0:T(8,128)S(1)}, f32[4,4,64,128]{3,2,1,0:T(8,128)}, u32[]{:S(2)}) copy-start(f32[4,4,64,128]{3,2,1,0:T(8,128)} %refs_0_.5) | copy-start | bytes 1572868
  11.9 3.3 %copy-start.3 = (s32[4,4,7]{2,1,0:T(4,128)S(1)}, s32[4,4,7]{2,1,0:T(4,128)}, u32[]{:S(2)}) copy-start(s32[4,4,7]{2,1,0:T(4,128)} %cols.5) | copy-start | bytes 1348
  13.0 18.5 %copy-start.5 = (bf16[16,128,512]{2,1,0:T(8,128)(2,1)}, bf16[16,128,512]{2,1,0:T(8,128)(2,1)S(1)}, u32[]{:S(2)}) copy-start(bf16[16,128,512]{2,1,0:T(8,128)(2,1)S(1)} %pack.1.packed) | copy-start | bytes 6291460
  13.7 1.3 %collective-permute-start.3 = (f32[1,4,64,128]{3,2,1,0:T(8,128)S(1)}, f32[1,4,64,128]{3,2,1,0:T(8,128)S(1)}, u32[]{:S(2)}, u32[]{:S(2)}) collective-permute-start(f32[1,4,64,128]{3,2,1,0:T(8,128)S(1)} %collective-permute-done.1.refs_0_), channel_id=1, source_target_pairs={{0,1},{1,0},{2,3},{3,2},{4,5},{5,4},{6,7},{7,6},{8,9},{9,8},{10,11... | collective-permute-start | bytes 393224 | tf_op jit(solution)/shard_map/ppermute | solution.py:340
  13.7 1.5 %collective-permute-start.4 = (f32[1,4,64,128]{3,2,1,0:T(8,128)S(1)}, f32[1,4,64,128]{3,2,1,0:T(8,128)S(1)}, u32[]{:S(2)}, u32[]{:S(2)}) collective-permute-start(f32[1,4,64,128]{3,2,1,0:T(8,128)S(1)} %collective-permute-done.refs_2_), channel_id=1, source_target_pairs={{0,1},{1,0},{2,3},{3,2},{4,5},{5,4},{6,7},{7,6},{8,9},{9,8},{10,11... | collective-permute-start | bytes 393224 | tf_op jit(solution)/shard_map/ppermute | solution.py:340
  16.9 12.9 %collective-permute-start.5 = (f32[4,4,64,128]{3,2,1,0:T(8,128)S(1)}, f32[4,4,64,128]{3,2,1,0:T(8,128)S(1)}, u32[]{:S(2)}, u32[]{:S(2)}) collective-permute-start(f32[4,4,64,128]{3,2,1,0:T(8,128)S(1)} %get-tuple-element.39.own.refs_1_.refs_4_), channel_id=1, source_target_pairs={{0,1},{1,0},{2,3},{3,2},{4,5},{5,4},{6,7},{7,6},{8,9},{9,8},{10,11... | collective-permute-start | bytes 1572872 | tf_op jit(solution)/shard_map/ppermute | solution.py:340
  17.3 6.0 %collective-permute-start.6 = (f32[1,4,64,128]{3,2,1,0:T(8,128)S(1)}, f32[1,4,64,128]{3,2,1,0:T(8,128)S(1)}, u32[]{:S(2)}, u32[]{:S(2)}) collective-permute-start(f32[1,4,64,128]{3,2,1,0:T(8,128)S(1)} %get-tuple-element.40), channel_id=1, source_target_pairs={{2,4},{4,2},{6,8},{8,6},{10,12},{12,10},{3,5},{5,3},{7,9},{9,7},{1... | collective-permute-start | bytes 393224 | tf_op jit(solution)/shard_map/ppermute | solution.py:354
  18.0 10.5 %collective-permute-start.8 = (f32[1,4,64,128]{3,2,1,0:T(8,128)S(1)}, f32[1,4,64,128]{3,2,1,0:T(8,128)S(1)}, u32[]{:S(2)}, u32[]{:S(2)}) collective-permute-start(f32[1,4,64,128]{3,2,1,0:T(8,128)S(1)} %get-tuple-element.41), channel_id=1, source_target_pairs={{0,2},{2,0},{4,6},{6,4},{8,10},{10,8},{12,14},{14,12},{1,3},{3,1},... | collective-permute-start | bytes 393224 | tf_op jit(solution)/shard_map/ppermute | solution.py:355
  23.3 5.2 %collective-permute-start.7 = (f32[1,4,64,128]{3,2,1,0:T(8,128)S(1)}, f32[1,4,64,128]{3,2,1,0:T(8,128)S(1)}, u32[]{:S(2)}, u32[]{:S(2)}) collective-permute-start(f32[1,4,64,128]{3,2,1,0:T(8,128)S(1)} %collective-permute-done.6.refs_0_), channel_id=1, source_target_pairs={{0,1},{1,0},{2,3},{3,2},{4,5},{5,4},{6,7},{7,6},{8,9},{9,8},{10,11... | collective-permute-start | bytes 393224 | tf_op jit(solution)/shard_map/ppermute | solution.py:340
  28.5 1.3 %collective-permute-start.9 = (f32[1,4,64,128]{3,2,1,0:T(8,128)S(1)}, f32[1,4,64,128]{3,2,1,0:T(8,128)S(1)}, u32[]{:S(2)}, u32[]{:S(2)}) collective-permute-start(f32[1,4,64,128]{3,2,1,0:T(8,128)S(1)} %collective-permute-done.8.refs_2_), channel_id=1, source_target_pairs={{0,1},{1,0},{2,3},{3,2},{4,5},{5,4},{6,7},{7,6},{8,9},{9,8},{10,11... | collective-permute-start | bytes 393224 | tf_op jit(solution)/shard_map/ppermute | solution.py:340
  31.5 2.0 %collective-permute-start.10 = (f32[4,4,64,128]{3,2,1,0:T(8,128)S(1)}, f32[4,4,64,128]{3,2,1,0:T(8,128)S(1)}, u32[]{:S(2)}, u32[]{:S(2)}) collective-permute-start(f32[4,4,64,128]{3,2,1,0:T(8,128)S(1)} %get-tuple-element.46.refs_2_.own), channel_id=1, source_target_pairs={{0,1},{1,0},{2,3},{3,2},{4,5},{5,4},{6,7},{7,6},{8,9},{9,8},{10,11... | collective-permute-start | bytes 1572872 | tf_op jit(solution)/shard_map/ppermute | solution.py:340
  35.1 3.4 %collective-permute-start.13 = (f32[384,128]{1,0:T(8,128)S(1)}, f32[384,128]{1,0:T(8,128)S(1)}, u32[]{:S(2)}, u32[]{:S(2)}) collective-permute-start(f32[384,128]{1,0:T(8,128)S(1)} %get-tuple-element.48), channel_id=1, source_target_pairs={{0,1},{1,0},{2,3},{3,2},{4,5},{5,4},{6,7},{7,6},{8,9},{9,8},{10,11... | collective-permute-start | bytes 589832 | tf_op jit(solution)/shard_map/ppermute | solution.py:340
  35.3 6.5 %collective-permute-start.11 = (f32[1,4,64,128]{3,2,1,0:T(8,128)S(1)}, f32[1,4,64,128]{3,2,1,0:T(8,128)S(1)}, u32[]{:S(2)}, u32[]{:S(2)}) collective-permute-start(f32[1,4,64,128]{3,2,1,0:T(8,128)S(1)} %get-tuple-element.44), channel_id=1, source_target_pairs={{0,2},{2,0},{4,6},{6,4},{8,10},{10,8},{12,14},{14,12},{1,3},{3,1},... | collective-permute-start | bytes 393224 | tf_op jit(solution)/shard_map/ppermute | solution.py:355
  37.8 4.0 %collective-permute-start.12 = (f32[1,4,64,128]{3,2,1,0:T(8,128)S(1)}, f32[1,4,64,128]{3,2,1,0:T(8,128)S(1)}, u32[]{:S(2)}, u32[]{:S(2)}) collective-permute-start(f32[1,4,64,128]{3,2,1,0:T(8,128)S(1)} %get-tuple-element.45), channel_id=1, source_target_pairs={{2,4},{4,2},{6,8},{8,6},{10,12},{12,10},{3,5},{5,3},{7,9},{9,7},{1... | collective-permute-start | bytes 393224 | tf_op jit(solution)/shard_map/ppermute | solution.py:354
  41.8 8.6 %collective-permute-start.14 = (f32[1,4,64,128]{3,2,1,0:T(8,128)S(1)}, f32[1,4,64,128]{3,2,1,0:T(8,128)S(1)}, u32[]{:S(2)}, u32[]{:S(2)}) collective-permute-start(f32[1,4,64,128]{3,2,1,0:T(8,128)S(1)} %collective-permute-done.12.refs_0_), channel_id=1, source_target_pairs={{0,1},{1,0},{2,3},{3,2},{4,5},{5,4},{6,7},{7,6},{8,9},{9,8},{10,11... | collective-permute-start | bytes 393224 | tf_op jit(solution)/shard_map/ppermute | solution.py:340
  41.8 8.6 %collective-permute-start.15 = (f32[1,4,64,128]{3,2,1,0:T(8,128)S(1)}, f32[1,4,64,128]{3,2,1,0:T(8,128)S(1)}, u32[]{:S(2)}, u32[]{:S(2)}) collective-permute-start(f32[1,4,64,128]{3,2,1,0:T(8,128)S(1)} %collective-permute-done.11.refs_2_), channel_id=1, source_target_pairs={{0,1},{1,0},{2,3},{3,2},{4,5},{5,4},{6,7},{7,6},{8,9},{9,8},{10,11... | collective-permute-start | bytes 393224 | tf_op jit(solution)/shard_map/ppermute | solution.py:340
  42.3 16.2 %all-to-all-start = ((f32[8,48,128]{2,1,0:T(8,128)}), f32[8,48,128]{2,1,0:T(8,128)S(1)}, u32[]{:S(2)}, u32[]{:S(2)}) async-start(f32[8,48,128]{2,1,0:T(8,128)} %bitcast.4), calls=%async_computation | async-start | bytes 393216 | tf_op jit(solution)/shard_map/all_to_all | solution.py:343
  50.5 1.6 %copy-start.6 = (bf16[16,128,512]{2,1,0:T(8,128)(2,1)S(1)}, bf16[16,128,512]{2,1,0:T(8,128)(2,1)}, u32[]{:S(2)}) copy-start(bf16[16,128,512]{2,1,0:T(8,128)(2,1)} %copy-done.5) | copy-start | bytes 6291460
  55.2 1.4 %collective-permute-start.16 = (f32[256,128]{1,0:T(8,128)S(1)}, f32[256,128]{1,0:T(8,128)S(1)}, u32[]{:S(2)}, u32[]{:S(2)}) collective-permute-start(f32[256,128]{1,0:T(8,128)S(1)} %get-tuple-element.52), channel_id=1, source_target_pairs={{0,1},{1,0},{2,3},{3,2},{4,5},{5,4},{6,7},{7,6},{8,9},{9,8},{10,11... | collective-permute-start | bytes 393224 | tf_op jit(solution)/shard_map/ppermute | solution.py:340
  59.3 12.3 %all-to-all-start.1 = ((f32[8,48,128]{2,1,0:T(8,128)}), f32[8,48,128]{2,1,0:T(8,128)S(1)}, u32[]{:S(2)}, u32[]{:S(2)}) async-start(f32[8,48,128]{2,1,0:T(8,128)} %broadcast_in_dim.2), calls=%async_computation.1 | async-start | bytes 393216 | tf_op jit(solution)/shard_map/all_to_all | solution.py:343
  63.3 8.3 %collective-permute-start.17 = (f32[256,128]{1,0:T(8,128)S(1)}, f32[256,128]{1,0:T(8,128)S(1)}, u32[]{:S(2)}, u32[]{:S(2)}) collective-permute-start(f32[256,128]{1,0:T(8,128)S(1)} %add.29), channel_id=1, source_target_pairs={{0,2},{2,0},{4,6},{6,4},{8,10},{10,8},{12,14},{14,12},{1,3},{3,1},... | collective-permute-start | bytes 393224 | tf_op jit(solution)/shard_map/ppermute | solution.py:346
  71.6 6.0 %collective-permute-start.19 = (f32[384,128]{1,0:T(8,128)S(1)}, f32[384,128]{1,0:T(8,128)S(1)}, u32[]{:S(2)}, u32[]{:S(2)}) collective-permute-start(f32[384,128]{1,0:T(8,128)S(1)} %bitcast.6), channel_id=1, source_target_pairs={{0,1},{1,0},{2,3},{3,2},{4,5},{5,4},{6,7},{7,6},{8,9},{9,8},{10,11... | collective-permute-start | bytes 589832 | tf_op jit(solution)/shard_map/ppermute | solution.py:340
  71.6 6.0 %collective-permute-start.18 = (f32[256,128]{1,0:T(8,128)S(1)}, f32[256,128]{1,0:T(8,128)S(1)}, u32[]{:S(2)}, u32[]{:S(2)}) collective-permute-start(f32[256,128]{1,0:T(8,128)S(1)} %add.30), channel_id=1, source_target_pairs={{0,4},{2,6},{4,0},{6,2},{8,12},{10,14},{12,8},{14,10},{1,5},{3,7},... | collective-permute-start | bytes 393224 | tf_op jit(solution)/shard_map/ppermute | solution.py:346
  81.4 8.1 %collective-permute-start.20 = (f32[256,128]{1,0:T(8,128)S(1)}, f32[256,128]{1,0:T(8,128)S(1)}, u32[]{:S(2)}, u32[]{:S(2)}) collective-permute-start(f32[256,128]{1,0:T(8,128)S(1)} %add.31), channel_id=1, source_target_pairs={{0,8},{2,10},{4,12},{6,14},{8,0},{10,2},{12,4},{14,6},{1,9},{3,11}... | collective-permute-start | bytes 393224 | tf_op jit(solution)/shard_map/ppermute | solution.py:346
  89.5 4.3 %collective-permute-start.21 = (f32[256,128]{1,0:T(8,128)S(1)}, f32[256,128]{1,0:T(8,128)S(1)}, u32[]{:S(2)}, u32[]{:S(2)}) collective-permute-start(f32[256,128]{1,0:T(8,128)S(1)} %add.32.own), channel_id=1, source_target_pairs={{0,1},{1,0},{2,3},{3,2},{4,5},{5,4},{6,7},{7,6},{8,9},{9,8},{10,11... | collective-permute-start | bytes 393224 | tf_op jit(solution)/shard_map/ppermute | solution.py:340

commit v5 on v4

--- a/solution.py
+++ b/solution.py
@@ -82,7 +82,7 @@
             put((layer + 1) * total + mine + q, own[layer, q])
             put((layer + 1) * total + theirs + q, other[layer, q])
     even = info[3]
-    for pair, place in enumerate((1 - even, even)):
+    for pair, place in enumerate((even, 1 - even)):
         for q in range(cross_local):
             put(place * (layers + 1) * total + mine + q, edges[2 * pair][0, q])
             put(place * (layers + 1) * total + theirs + q, edges[2 * pair + 1][0, q])
@@ -190,10 +190,10 @@
     corner = [lane(gram[0], c) for c in range(tall)]
     for p in range(tiles):
         at = tall * p
-        below = range(p + 1, tiles)
-        cols = [[lane(gram[t], at + c) for t in below] for c in range(tall)]
-        ahead = [lane(gram[p + 1], at + tall + d) for d in range(tall)] if p + 1 < tiles else []
-        scales, tops, lows = [], [], []
+        more = p + 1 < tiles
+        cols = [lane(gram[p + 1], at + c) for c in range(tall)] if more else []
+        ahead = [lane(gram[p + 1], at + tall + d) for d in range(tall)] if more else []
+        scales, tops = [], []
         for c in range(tall):
             scale = lax.rsqrt(spread(corner[c], c))
             square = scale * scale
@@ -201,23 +201,33 @@
             weights = [spread(corner[d], c) for d in range(c + 1, tall)]
             for d in range(c + 1, tall):
                 corner[d] = corner[d] - (top * weights[d - c - 1]) * square
-            low = [x * scale for x in cols[c]]
-            for d in range(c + 1, tall):
-                weight = weights[d - c - 1] * scale
-                cols[d] = [x - m * weight for x, m in zip(cols[d], low)]
-            if low:
-                ahead = [x - low[0] * spread(low[0], d) for d, x in enumerate(ahead)]
+            if more:
+                low = cols[c] * scale
+                for d in range(c + 1, tall):
+                    cols[d] = cols[d] - low * (weights[d - c - 1] * scale)
+                ahead = [x - low * spread(low, d) for d, x in enumerate(ahead)]
             scales.append(scale)
             tops.append(top * scale)
-            lows.append(low)
         for c in range(tall):
             row_gram = spread(gram[p], c) * scales[c]
             row_unit = spread(unit[p], c) * scales[c]
             gram[p] = jnp.where(sub == c, row_gram, gram[p] - tops[c] * row_gram)
             unit[p] = jnp.where(sub == c, row_unit, unit[p] - tops[c] * row_unit)
-            for t, m in zip(below, lows[c]):
-                gram[t] = gram[t] - m * row_gram
-                unit[t] = unit[t] - m * row_unit
+        if more:
+            rows = jnp.concatenate([gram[p], unit[p]], axis=1)
+            high = rows.astype(jnp.bfloat16).astype(jnp.float32)
+            low = rows - high
+            left = jnp.concatenate([high[:, :size], high[:, :size], low[:, :size]], axis=0)
+            right = jnp.concatenate([high, low, high], axis=0)
+            taken = lax.dot_general(
+                left.astype(jnp.bfloat16),
+                right.astype(jnp.bfloat16),
+                (((0,), (0,)), ((), ())),
+                preferred_element_type=jnp.float32,
+            )
+            for t in range(p + 1, tiles):
+                gram[t] = gram[t] - taken[tall * t : tall * (t + 1), :size]
+                unit[t] = unit[t] - taken[tall * t : tall * (t + 1), size:]
         corner = ahead
     upper = [jnp.where(lanes >= sub + tall * t, gram[t], 0.0) for t in range(tiles)]
     return jnp.concatenate(upper, axis=0), jnp.concatenate(unit, axis=0)
@@ -342,8 +352,9 @@
     def exchange(x):
         return lax.all_to_all(x, "trans", 0, 0, tiled=True)
 
-    def double(x, reach):
-        return x + lax.ppermute(x, "trans", [(i, i ^ reach) for i in range(count)])
+    def double(x, reach, work=None):
+        other = lax.ppermute(x, "trans", [(i, i ^ reach) for i in range(count)])
+        return x + (other if work is None else lax.optimization_barrier((other, work))[0])
 
     early = tuple((i, j) for i in range(S) for j in range(i + 1))
     powers = [sources]
@@ -351,18 +362,16 @@
     far_layer = lax.dynamic_slice_in_dim(sources, (1 - even) * (layers - 1), 1)
     for k in range(S):
         field = powers[k]
+        near_edge = lax.ppermute(near_layer, "trans", near)
         far_edge = lax.ppermute(far_layer, "trans", far)
-        near_edge = lax.ppermute(near_layer, "trans", near)
         other = swap(field)
         if k == 0:
             near_edge, far_edge, packed = lax.optimization_barrier((near_edge, far_edge, packed))
         if k == S - 1:
-            held, other = lax.optimization_barrier((field, other))
-            mine, theirs = gram_blocks([*powers[:-1], held], early, info, count)
-            shares = (mine + swap(theirs)).reshape(count, -1, columns)
-            near_edge, far_edge, shares = lax.optimization_barrier((near_edge, far_edge, shares))
-            parts = exchange(shares)
-        edges = (far_edge, swap(far_edge), near_edge, swap(near_edge))
+            mine, theirs = gram_blocks(powers, early, info, count)
+            theirs, _, _ = lax.optimization_barrier((swap(theirs), near_edge, far_edge))
+            parts = exchange((mine + theirs).reshape(count, -1, columns))
+        edges = (near_edge, swap(near_edge), far_edge, swap(far_edge))
         before = powers[k - 1] if k else None
         got = step(packed, block_cols, info, field, other, edges, before, k == S - 1)
         powers.append(got[0])
@@ -375,15 +384,13 @@
     known = exchange(jnp.broadcast_to(summed, parts.shape)).reshape(-1, columns)
     known_other = swap(known)
     first = column(0, 0, info, known, known_other, ())
+    second = column(1, 1, info, known, known_other, first[::-1])
+    third = column(2, 3, info, known, known_other, second[::-1])
     reach = 1
     while reach < count:
-        last = double(last, reach)
+        work = third if 2 * reach == count else first if 4 * reach == count else None
+        last = double(last, reach, work)
         reach *= 2
-        if reach == count // 2:
-            last, first = lax.optimization_barrier((last, first))
-    second = column(1, 1, info, known, known_other, first[::-1])
-    last, second = lax.optimization_barrier((last, second))
-    third = column(2, 3, info, known, known_other, second[::-1])
     r_factor, inverse = column(3, 0, info, last, swap(last), third[::-1], 1.0 / scale_rows)
     return basis_of(powers, inverse, scale_rows), r_factor
 

time: 103 us -> 98.4 us (0.955)
  waiting for transfers between devices: 30.4 us -> 18.1 us
  blocking collectives: 0 us -> 11.6 us
  starting transfers between devices: 33.5 us -> 28.1 us
  Pallas kernels: 30.2 us -> 32.3 us
    all_to_all x0 -> x1, blocking collectives: none -> 11.6 us  [exchange(): return lax.all_to_all(x, 'trans', 0, 0, tiled=True)]
    all_to_all x2 -> x1, waiting for transfers between devices: 8.2 us -> 2.45 us  [exchange(): return lax.all_to_all(x, 'trans', 0, 0, tiled=True)]
    all_to_all x2 -> x1, starting transfers between devices: 12.2 us -> 8.66 us  [exchange(): return lax.all_to_all(x, 'trans', 0, 0, tiled=True)]
    ppermute x3, waiting for transfers between devices: 8.48 us -> 5.44 us  [local(): near_edge = lax.ppermute(near_layer, 'trans', near)]
    ppermute x3, waiting for transfers between devices: 8.26 us -> 5.72 us  [double(): other = lax.ppermute(x, 'trans', [(i, i ^ reach) for i in range(count)])]
    pallas_call x4, Pallas kernels: 17.9 us -> 19.9 us  [column(): pl.pallas_call(functools.partial(column_kernel, place, first, scale), in_...]
    ppermute x3, starting transfers between devices: 3.65 us -> 2 us  [double(): other = lax.ppermute(x, 'trans', [(i, i ^ reach) for i in range(count)])]
    ppermute x3, starting transfers between devices: 13.2 us -> 12.2 us  [local(): near_edge = lax.ppermute(near_layer, 'trans', near)]
  transfers between devices with their start and end apart: 24 -> 23, of which waited for: 12 -> 12; matrix products, arithmetic and copies ran while one was open for 2% -> 2% of each run, Pallas kernels for 12% -> 20%
where the time goes in v5:
time: 98.4 us; the launch traced here: 98 us
  Pallas kernels  32.3 us (33%)
  starting transfers between devices  28.1 us (29%)
  waiting for transfers between devices  18.1 us (18%)
  blocking collectives  11.6 us (12%)
  local copies, waits for them, and re-layouts  6.19 us (6%)
    pallas_call x4, Pallas kernels, column(): pl.pallas_call(functools.partial(column_kernel, place, first, scale), in_...  19.9 us
    ppermute x3, starting transfers between devices, local(): near_edge = lax.ppermute(near_layer, 'trans', near)  12.2 us
    all_to_all x1, blocking collectives, exchange(): return lax.all_to_all(x, 'trans', 0, 0, tiled=True)  11.6 us
    all_to_all x1, starting transfers between devices, exchange(): return lax.all_to_all(x, 'trans', 0, 0, tiled=True)  8.66 us
    ppermute x3, waiting for transfers between devices, double(): other = lax.ppermute(x, 'trans', [(i, i ^ reach) for i in range(count)])  5.72 us
    ppermute x3, waiting for transfers between devices, local(): near_edge = lax.ppermute(near_layer, 'trans', near)  5.44 us
    unnamed x14, local copies, waits for them, and re-layouts  5.19 us
    pallas_call x3, Pallas kernels, step(): pl.pallas_call(functools.partial(step_kernel, before is None, last, cols....  5.05 us
  transfers between devices with their start and end apart: 23, of which 12 were waited for; matrix products, arithmetic and copies ran while one was open for 2% of the time, Pallas kernels for 20%

profile of v5, /device:TPU:0, one launch (start us, length us, event | category | flops | bytes accessed | tf_op | source)
XLA Modules:
  0.0 98.0 jit_solution(6651328087274748474)
XLA Ops:
  0.6 0.5 collective-permute-start.2
  1.1 1.0 %constant_dynamic-slice_fusion = (f32[1,4,64,128]{3,2,1,0:T(8,128)S(1)}, f32[1,4,64,128]{3,2,1,0:T(8,128)S(1)}) fusion(f32[4,4,64,128]{3,2,1,0:T(8,128)} %refs_0_.5, s32[]{:T(128)S(6)} %select_n.15, s32[]{:T(128)S(6)} %select_n.14), kind=kLoop, calls=%fused_computation.1 | loop fusion | bytes 524296 | tf_op jit(solution)/shard_map/dynamic_slice | solution.py:362
  2.1 0.7 collective-permute-start.1
  2.8 5.4 %collective-permute-start = (f32[1,4,64,128]{3,2,1,0:T(8,128)S(1)}, f32[1,4,64,128]{3,2,1,0:T(8,128)S(1)}, u32[]{:S(2)}, u32[]{:S(2)}) collective-permute-start(f32[1,4,64,128]{3,2,1,0:T(8,128)S(1)} %get-tuple-element.55), channel_id=1, source_target_pairs={{0,2},{2,0},{4,6},{6,4},{8,10},{10,8},{12,14},{14,12},{1,3},{3,1},... | collective-permute-start | bytes 393224 | tf_op jit(solution)/shard_map/ppermute | solution.py:365
  8.3 2.0 %copy-done.1 = f32[4,4,7,64,64]{4,3,2,1,0:T(8,128)S(1)} copy-done((f32[4,4,7,64,64]{4,3,2,1,0:T(8,128)S(1)}, f32[4,4,7,64,64]{4,3,2,1,0:T(8,128)}, u32[]{:S(2)}) %copy-start.1) | copy-done | bytes 1835032
  10.3 0.9 copy-done.2
  11.2 0.7 copy-done.4
  11.9 1.1 %pack.1.packed = bf16[16,128,512]{2,1,0:T(8,128)(2,1)S(1)} custom-call(s32[4]{0:T(128)S(1)} %pad_add_fusion.info, s32[4]{0:T(128)S(1)} %copy-done.4, f32[4,4,7,64,64]{4,3,2,1,0:T(8,128)S(1)} %copy-done.1, f32[4,64,64]{2,1,0:T(8,128)S(1)} %copy-done.2), custom_call_target="tpu_custom_call" | custom-call | flops 2875000064 | tf_op jit(solution)/shard_map/pack/pallas_call | solution.py:53
  13.0 0.7 collective-permute-done.refs_0_
  13.7 0.5 collective-permute-start.4
  14.2 0.8 collective-permute-done.3.refs_1_
  15.0 0.2 collective-permute-done.4.refs_3_
  15.2 1.7 %step.3 = (f32[4,4,64,128]{3,2,1,0:T(8,128)S(1)}, f32[1,4,64,128]{3,2,1,0:T(8,128)S(1)}, f32[1,4,64,128]{3,2,1,0:T(8,128)S(1)}) custom-call(s32[4]{0:T(128)S(1)} %pad_add_fusion.info, s32[4,4,7]{2,1,0:T(4,128)S(1)} %copy-done.3, bf16[16,128,512]{2,1,0:T(8,128)(2,1)S(1)} %pack.1.packed, f32[4,4,64,128]{3,2,1,0:T(8,128)S(1)} %copy-done, ...), custom_call_target="tpu_custom_call" | custom-call | flops 1955000064 | tf_op jit(solution)/shard_map/step/pallas_call | solution.py:114
  16.9 0.4 collective-permute-start.5
  17.3 2.5 %collective-permute-start.6 = (f32[1,4,64,128]{3,2,1,0:T(8,128)S(1)}, f32[1,4,64,128]{3,2,1,0:T(8,128)S(1)}, u32[]{:S(2)}, u32[]{:S(2)}) collective-permute-start(f32[1,4,64,128]{3,2,1,0:T(8,128)S(1)} %get-tuple-element.32), channel_id=1, source_target_pairs={{0,2},{2,0},{4,6},{6,4},{8,10},{10,8},{12,14},{14,12},{1,3},{3,1},... | collective-permute-start | bytes 393224 | tf_op jit(solution)/shard_map/ppermute | solution.py:365
  19.8 0.7 collective-permute-start.8
  20.4 3.2 %collective-permute-done.6.refs_0_ = f32[1,4,64,128]{3,2,1,0:T(8,128)S(1)} collective-permute-done((f32[1,4,64,128]{3,2,1,0:T(8,128)S(1)}, f32[1,4,64,128]{3,2,1,0:T(8,128)S(1)}, u32[]{:S(2)}, u32[]{:S(2)}) %collective-permute-start.6) | collective-permute-done | bytes 131104 | tf_op jit(solution)/shard_map/ppermute | solution.py:365
  23.6 0.5 collective-permute-start.9
  24.1 0.8 collective-permute-done.7.refs_1_
  25.0 0.2 collective-permute-done.9.refs_3_
  25.1 1.7 %step.4 = (f32[4,4,64,128]{3,2,1,0:T(8,128)S(1)}, f32[1,4,64,128]{3,2,1,0:T(8,128)S(1)}, f32[1,4,64,128]{3,2,1,0:T(8,128)S(1)}) custom-call(s32[4]{0:T(128)S(1)} %pad_add_fusion.info, s32[4,4,7]{2,1,0:T(4,128)S(1)} %copy-done.3, bf16[16,128,512]{2,1,0:T(8,128)(2,1)S(1)} %pack.1.packed, f32[4,4,64,128]{3,2,1,0:T(8,128)S(1)} %get-tuple-element.31.own.refs_4_.refs_1_, ...), custom_call_target="tpu_custom_call" | custom-call | flops 1955000064 | tf_op jit(solution)/shard_map/step/pallas_call | solution.py:114
  26.9 0.4 collective-permute-start.10
  27.2 4.3 %collective-permute-start.11 = (f32[1,4,64,128]{3,2,1,0:T(8,128)S(1)}, f32[1,4,64,128]{3,2,1,0:T(8,128)S(1)}, u32[]{:S(2)}, u32[]{:S(2)}) collective-permute-start(f32[1,4,64,128]{3,2,1,0:T(8,128)S(1)} %get-tuple-element.35), channel_id=1, source_target_pairs={{0,2},{2,0},{4,6},{6,4},{8,10},{10,8},{12,14},{14,12},{1,3},{3,1},... | collective-permute-start | bytes 393224 | tf_op jit(solution)/shard_map/ppermute | solution.py:365
  31.5 0.7 collective-permute-start.13
  32.2 1.6 %gram.3 = (f32[384,128]{1,0:T(8,128)S(1)}, f32[384,128]{1,0:T(8,128)S(1)}) custom-call(s32[4]{0:T(128)S(1)} %pad_add_fusion.info, f32[4,4,64,128]{3,2,1,0:T(8,128)S(1)} %copy-done, f32[4,4,64,128]{3,2,1,0:T(8,128)S(1)} %get-tuple-element.31.own.refs_4_.refs_1_, f32[4,4,64,128]{3,2,1,0:T(8,128)S(1)} %get-tuple-element.34.own.refs_2_), custom_call_target="tpu_custom_call" | custom-call | flops 1610000000 | tf_op jit(solution)/shard_map/gram/pallas_call | solution.py:156
  33.8 0.1 collective-permute-start.16
  34.0 1.6 %collective-permute-done.11.refs_0_ = f32[1,4,64,128]{3,2,1,0:T(8,128)S(1)} collective-permute-done((f32[1,4,64,128]{3,2,1,0:T(8,128)S(1)}, f32[1,4,64,128]{3,2,1,0:T(8,128)S(1)}, u32[]{:S(2)}, u32[]{:S(2)}) %collective-permute-start.11) | collective-permute-done | bytes 131104 | tf_op jit(solution)/shard_map/ppermute | solution.py:365
  35.6 0.5 collective-permute-start.14
  36.1 0.7 add.29
  36.8 8.7 %all-to-all-start = ((f32[8,48,128]{2,1,0:T(8,128)}), f32[8,48,128]{2,1,0:T(8,128)S(1)}, u32[]{:S(2)}, u32[]{:S(2)}) async-start(f32[8,48,128]{2,1,0:T(8,128)} %bitcast.4), calls=%async_computation | async-start | bytes 393216 | tf_op jit(solution)/shard_map/all_to_all | solution.py:353
  45.5 1.6 %copy-done.6 = bf16[16,128,512]{2,1,0:T(8,128)(2,1)S(1)} copy-done((bf16[16,128,512]{2,1,0:T(8,128)(2,1)S(1)}, bf16[16,128,512]{2,1,0:T(8,128)(2,1)}, u32[]{:S(2)}) %copy-start.6) | copy-done | bytes 2097176
  47.0 1.7 %step.5.refs_3_ = f32[4,4,64,128]{3,2,1,0:T(8,128)S(1)} custom-call(s32[4]{0:T(128)S(1)} %pad_add_fusion.info, s32[4,4,7]{2,1,0:T(4,128)S(1)} %copy-done.3, bf16[16,128,512]{2,1,0:T(8,128)(2,1)S(1)} %copy-done.6, f32[4,4,64,128]{3,2,1,0:T(8,128)S(1)} %get-tuple-element.34.own.refs_2_, f32[4,4,64,128]{3,2,1,0:T(8,128)S(1)} %collective-permute-done.10.other, ...), custom_call_target="tpu_custom_call" | custom-call | flops 1955000064 | tf_op jit(solution)/shard_map/step/pallas_call | solution.py:114
  48.7 1.4 %gram.2 = (f32[256,128]{1,0:T(8,128)S(1)}, f32[256,128]{1,0:T(8,128)S(1)}) custom-call(s32[4]{0:T(128)S(1)} %pad_add_fusion.info, f32[4,4,64,128]{3,2,1,0:T(8,128)S(1)} %copy-done, f32[4,4,64,128]{3,2,1,0:T(8,128)S(1)} %get-tuple-element.31.own.refs_4_.refs_1_, f32[4,4,64,128]{3,2,1,0:T(8,128)S(1)} %get-tuple-element.34.own.refs_2_, ...), custom_call_target="tpu_custom_call" | custom-call | flops 1610000000 | tf_op jit(solution)/shard_map/gram/pallas_call | solution.py:156
  50.2 0.3 collective-permute-start.15
  50.5 1.1 %collective-permute-done.15 = f32[256,128]{1,0:T(8,128)S(1)} collective-permute-done((f32[256,128]{1,0:T(8,128)S(1)}, f32[256,128]{1,0:T(8,128)S(1)}, u32[]{:S(2)}, u32[]{:S(2)}) %collective-permute-start.15) | collective-permute-done | bytes 131104 | tf_op jit(solution)/shard_map/ppermute | solution.py:350
  51.6 2.4 %all-to-all-done = f32[8,48,128]{2,1,0:T(8,128)S(1)} async-done(((f32[8,48,128]{2,1,0:T(8,128)}), f32[8,48,128]{2,1,0:T(8,128)S(1)}, u32[]{:S(2)}, u32[]{:S(2)}) %all-to-all-start) | async-done | bytes 196640 | tf_op jit(solution)/shard_map/all_to_all | solution.py:353
  54.1 11.6 %all_to_all.10 = f32[8,48,128]{2,1,0:T(8,128)S(1)} all-to-all(f32[8,48,128]{2,1,0:T(8,128)S(1)} %broadcast_in_dim.2), channel_id=1, replica_groups=mesh['energy'=2,'trans'=8,'cross'=2] {'trans'}, dimensions={0} | all-to-all | bytes 393216 | tf_op jit(solution)/shard_map/all_to_all | solution.py:353
  65.7 1.0 collective-permute-start.17
  66.7 4.9 %collective-permute-done.17 = f32[256,128]{1,0:T(8,128)S(1)} collective-permute-done((f32[256,128]{1,0:T(8,128)S(1)}, f32[256,128]{1,0:T(8,128)S(1)}, u32[]{:S(2)}, u32[]{:S(2)}) %collective-permute-start.17) | collective-permute-done | bytes 131104 | tf_op jit(solution)/shard_map/ppermute | solution.py:356
  71.6 0.3 collective-permute-start.18
  71.9 4.2 %column.4 = (f32[128,128]{1,0:T(8,128)S(1)}, f32[128,128]{1,0:T(8,128)S(1)}) custom-call(s32[4]{0:T(128)S(1)} %pad_add_fusion.info, f32[384,128]{1,0:T(8,128)S(1)} %bitcast.7, f32[384,128]{1,0:T(8,128)S(1)} %collective-permute-done.19.other), custom_call_target="tpu_custom_call" | custom-call | flops 4600000000 | tf_op jit(solution)/shard_map/column/pallas_call | solution.py:279
  76.1 0.8 collective-permute-done.18
  76.9 0.8 collective-permute-start.20
  77.6 4.8 %column.5 = (f32[256,256]{1,0:T(8,128)S(1)}, f32[256,256]{1,0:T(8,128)S(1)}) custom-call(s32[4]{0:T(128)S(1)} %pad_add_fusion.info, f32[384,128]{1,0:T(8,128)S(1)} %bitcast.8, f32[384,128]{1,0:T(8,128)S(1)} %collective-permute-done.19.other, f32[128,128]{1,0:T(8,128)S(1)} %get-tuple-element.45.refs_0_, f32[128,128]{1,0:T(8,128)S(1)} %get-tuple-element.44.refs_1_), custom_call_target="tpu_custom_call" | custom-call | flops 4600000000 | tf_op jit(solution)/shard_map/column/pallas_call | solution.py:279
  82.4 4.9 %column.6 = (f32[384,384]{1,0:T(8,128)S(1)}, f32[384,384]{1,0:T(8,128)S(1)}) custom-call(s32[4]{0:T(128)S(1)} %pad_add_fusion.info, f32[384,128]{1,0:T(8,128)S(1)} %bitcast.9, f32[384,128]{1,0:T(8,128)S(1)} %collective-permute-done.19.other, f32[256,256]{1,0:T(8,128)S(1)} %get-tuple-element.47.refs_0_, f32[256,256]{1,0:T(8,128)S(1)} %get-tuple-element.48.refs_1_), custom_call_target="tpu_custom_call" | custom-call | flops 4600000000 | tf_op jit(solution)/shard_map/column/pallas_call | solution.py:279
  87.4 1.3 %collective-permute-done.21.other = f32[256,128]{1,0:T(8,128)S(1)} collective-permute-done((f32[256,128]{1,0:T(8,128)S(1)}, f32[256,128]{1,0:T(8,128)S(1)}, u32[]{:S(2)}, u32[]{:S(2)}) %collective-permute-start.21) | collective-permute-done | bytes 131104 | tf_op jit(solution)/shard_map/ppermute | solution.py:350
  88.7 6.1 %column.7 = (f32[512,512]{1,0:T(8,128)}, f32[512,512]{1,0:T(8,128)S(1)}) custom-call(s32[4]{0:T(128)S(1)} %pad_add_fusion.info, f32[256,128]{1,0:T(8,128)S(1)} %add.32.own, f32[256,128]{1,0:T(8,128)S(1)} %collective-permute-done.21.other, f32[384,384]{1,0:T(8,128)S(1)} %get-tuple-element.50.refs_0_, f32[384,384]{1,0:T(8,128)S(1)} %get-tuple-element.49.refs_1_), custom_call_target="tpu_custom_call" | custom-call | flops 4600000000 | tf_op jit(solution)/shard_map/column/pallas_call | solution.py:279
  94.8 3.2 %basis.1 = bf16[4,4,64,512]{3,2,1,0:T(8,128)(2,1)} custom-call(f32[4,4,64,128]{3,2,1,0:T(8,128)S(1)} %copy-done, f32[4,4,64,128]{3,2,1,0:T(8,128)S(1)} %get-tuple-element.31.own.refs_4_.refs_1_, f32[4,4,64,128]{3,2,1,0:T(8,128)S(1)} %get-tuple-element.34.own.refs_2_, f32[4,4,64,128]{3,2,1,0:T(8,128)S(1)} %step.5.refs_3_, ...), custom_call_target="tpu_custom_call" | custom-call | flops 3449999872 | tf_op jit(solution)/shard_map/basis/pallas_call | solution.py:321
  (33 shorter events, 0.3 us)
Async XLA Ops:
  0.6 14.6 %collective-permute-start.2 = (f32[4,4,64,128]{3,2,1,0:T(8,128)}, f32[4,4,64,128]{3,2,1,0:T(8,128)S(1)}, u32[]{:S(2)}, u32[]{:S(2)}) collective-permute-start(f32[4,4,64,128]{3,2,1,0:T(8,128)} %refs_0_.5), channel_id=1, source_target_pairs={{0,1},{1,0},{2,3},{3,2},{4,5},{5,4},{6,7},{7,6},{8,9},{9,8},{10,11... | collective-permute-start | bytes 1572872 | tf_op jit(solution)/shard_map/ppermute | solution.py:350
  2.1 10.8 %collective-permute-start.1 = (f32[1,4,64,128]{3,2,1,0:T(8,128)S(1)}, f32[1,4,64,128]{3,2,1,0:T(8,128)S(1)}, u32[]{:S(2)}, u32[]{:S(2)}) collective-permute-start(f32[1,4,64,128]{3,2,1,0:T(8,128)S(1)} %get-tuple-element.54), channel_id=1, source_target_pairs={{2,4},{4,2},{6,8},{8,6},{10,12},{12,10},{3,5},{5,3},{7,9},{9,7},{1... | collective-permute-start | bytes 393224 | tf_op jit(solution)/shard_map/ppermute | solution.py:366
  2.8 10.9 %collective-permute-start = (f32[1,4,64,128]{3,2,1,0:T(8,128)S(1)}, f32[1,4,64,128]{3,2,1,0:T(8,128)S(1)}, u32[]{:S(2)}, u32[]{:S(2)}) collective-permute-start(f32[1,4,64,128]{3,2,1,0:T(8,128)S(1)} %get-tuple-element.55), channel_id=1, source_target_pairs={{0,2},{2,0},{4,6},{6,4},{8,10},{10,8},{12,14},{14,12},{1,3},{3,1},... | collective-permute-start | bytes 393224 | tf_op jit(solution)/shard_map/ppermute | solution.py:365
  8.3 2.0 %copy-start.1 = (f32[4,4,7,64,64]{4,3,2,1,0:T(8,128)S(1)}, f32[4,4,7,64,64]{4,3,2,1,0:T(8,128)}, u32[]{:S(2)}) copy-start(f32[4,4,7,64,64]{4,3,2,1,0:T(8,128)} %held.1) | copy-start | bytes 5505028
  10.3 0.9 copy-start.2
  11.2 0.7 copy-start.4
  11.9 3.3 %copy-start = (f32[4,4,64,128]{3,2,1,0:T(8,128)S(1)}, f32[4,4,64,128]{3,2,1,0:T(8,128)}, u32[]{:S(2)}) copy-start(f32[4,4,64,128]{3,2,1,0:T(8,128)} %refs_0_.5) | copy-start | bytes 1572868
  11.9 3.3 %copy-start.3 = (s32[4,4,7]{2,1,0:T(4,128)S(1)}, s32[4,4,7]{2,1,0:T(4,128)}, u32[]{:S(2)}) copy-start(s32[4,4,7]{2,1,0:T(4,128)} %cols.5) | copy-start | bytes 1348
  13.0 13.9 %copy-start.5 = (bf16[16,128,512]{2,1,0:T(8,128)(2,1)}, bf16[16,128,512]{2,1,0:T(8,128)(2,1)S(1)}, u32[]{:S(2)}) copy-start(bf16[16,128,512]{2,1,0:T(8,128)(2,1)S(1)} %pack.1.packed) | copy-start | bytes 6291460
  13.7 1.3 %collective-permute-start.3 = (f32[1,4,64,128]{3,2,1,0:T(8,128)S(1)}, f32[1,4,64,128]{3,2,1,0:T(8,128)S(1)}, u32[]{:S(2)}, u32[]{:S(2)}) collective-permute-start(f32[1,4,64,128]{3,2,1,0:T(8,128)S(1)} %collective-permute-done.refs_0_), channel_id=1, source_target_pairs={{0,1},{1,0},{2,3},{3,2},{4,5},{5,4},{6,7},{7,6},{8,9},{9,8},{10,11... | collective-permute-start | bytes 393224 | tf_op jit(solution)/shard_map/ppermute | solution.py:350
  13.7 1.5 %collective-permute-start.4 = (f32[1,4,64,128]{3,2,1,0:T(8,128)S(1)}, f32[1,4,64,128]{3,2,1,0:T(8,128)S(1)}, u32[]{:S(2)}, u32[]{:S(2)}) collective-permute-start(f32[1,4,64,128]{3,2,1,0:T(8,128)S(1)} %collective-permute-done.1.refs_2_), channel_id=1, source_target_pairs={{0,1},{1,0},{2,3},{3,2},{4,5},{5,4},{6,7},{7,6},{8,9},{9,8},{10,11... | collective-permute-start | bytes 393224 | tf_op jit(solution)/shard_map/ppermute | solution.py:350
  16.9 8.2 %collective-permute-start.5 = (f32[4,4,64,128]{3,2,1,0:T(8,128)S(1)}, f32[4,4,64,128]{3,2,1,0:T(8,128)S(1)}, u32[]{:S(2)}, u32[]{:S(2)}) collective-permute-start(f32[4,4,64,128]{3,2,1,0:T(8,128)S(1)} %get-tuple-element.31.own.refs_4_.refs_1_), channel_id=1, source_target_pairs={{0,1},{1,0},{2,3},{3,2},{4,5},{5,4},{6,7},{7,6},{8,9},{9,8},{10,11... | collective-permute-start | bytes 1572872 | tf_op jit(solution)/shard_map/ppermute | solution.py:350
  17.3 6.3 %collective-permute-start.6 = (f32[1,4,64,128]{3,2,1,0:T(8,128)S(1)}, f32[1,4,64,128]{3,2,1,0:T(8,128)S(1)}, u32[]{:S(2)}, u32[]{:S(2)}) collective-permute-start(f32[1,4,64,128]{3,2,1,0:T(8,128)S(1)} %get-tuple-element.32), channel_id=1, source_target_pairs={{0,2},{2,0},{4,6},{6,4},{8,10},{10,8},{12,14},{14,12},{1,3},{3,1},... | collective-permute-start | bytes 393224 | tf_op jit(solution)/shard_map/ppermute | solution.py:365
  19.8 3.9 %collective-permute-start.8 = (f32[1,4,64,128]{3,2,1,0:T(8,128)S(1)}, f32[1,4,64,128]{3,2,1,0:T(8,128)S(1)}, u32[]{:S(2)}, u32[]{:S(2)}) collective-permute-start(f32[1,4,64,128]{3,2,1,0:T(8,128)S(1)} %get-tuple-element.33), channel_id=1, source_target_pairs={{2,4},{4,2},{6,8},{8,6},{10,12},{12,10},{3,5},{5,3},{7,9},{9,7},{1... | collective-permute-start | bytes 393224 | tf_op jit(solution)/shard_map/ppermute | solution.py:366
  23.6 1.3 %collective-permute-start.7 = (f32[1,4,64,128]{3,2,1,0:T(8,128)S(1)}, f32[1,4,64,128]{3,2,1,0:T(8,128)S(1)}, u32[]{:S(2)}, u32[]{:S(2)}) collective-permute-start(f32[1,4,64,128]{3,2,1,0:T(8,128)S(1)} %collective-permute-done.6.refs_0_), channel_id=1, source_target_pairs={{0,1},{1,0},{2,3},{3,2},{4,5},{5,4},{6,7},{7,6},{8,9},{9,8},{10,11... | collective-permute-start | bytes 393224 | tf_op jit(solution)/shard_map/ppermute | solution.py:350
  23.6 1.5 %collective-permute-start.9 = (f32[1,4,64,128]{3,2,1,0:T(8,128)S(1)}, f32[1,4,64,128]{3,2,1,0:T(8,128)S(1)}, u32[]{:S(2)}, u32[]{:S(2)}) collective-permute-start(f32[1,4,64,128]{3,2,1,0:T(8,128)S(1)} %collective-permute-done.8.refs_2_), channel_id=1, source_target_pairs={{0,1},{1,0},{2,3},{3,2},{4,5},{5,4},{6,7},{7,6},{8,9},{9,8},{10,11... | collective-permute-start | bytes 393224 | tf_op jit(solution)/shard_map/ppermute | solution.py:350
  26.9 18.6 %collective-permute-start.10 = (f32[4,4,64,128]{3,2,1,0:T(8,128)S(1)}, f32[4,4,64,128]{3,2,1,0:T(8,128)S(1)}, u32[]{:S(2)}, u32[]{:S(2)}) collective-permute-start(f32[4,4,64,128]{3,2,1,0:T(8,128)S(1)} %get-tuple-element.34.own.refs_2_), channel_id=1, source_target_pairs={{0,1},{1,0},{2,3},{3,2},{4,5},{5,4},{6,7},{7,6},{8,9},{9,8},{10,11... | collective-permute-start | bytes 1572872 | tf_op jit(solution)/shard_map/ppermute | solution.py:350
  27.2 8.3 %collective-permute-start.11 = (f32[1,4,64,128]{3,2,1,0:T(8,128)S(1)}, f32[1,4,64,128]{3,2,1,0:T(8,128)S(1)}, u32[]{:S(2)}, u32[]{:S(2)}) collective-permute-start(f32[1,4,64,128]{3,2,1,0:T(8,128)S(1)} %get-tuple-element.35), channel_id=1, source_target_pairs={{0,2},{2,0},{4,6},{6,4},{8,10},{10,8},{12,14},{14,12},{1,3},{3,1},... | collective-permute-start | bytes 393224 | tf_op jit(solution)/shard_map/ppermute | solution.py:365
  31.5 4.0 %collective-permute-start.13 = (f32[1,4,64,128]{3,2,1,0:T(8,128)S(1)}, f32[1,4,64,128]{3,2,1,0:T(8,128)S(1)}, u32[]{:S(2)}, u32[]{:S(2)}) collective-permute-start(f32[1,4,64,128]{3,2,1,0:T(8,128)S(1)} %get-tuple-element.36), channel_id=1, source_target_pairs={{2,4},{4,2},{6,8},{8,6},{10,12},{12,10},{3,5},{5,3},{7,9},{9,7},{1... | collective-permute-start | bytes 393224 | tf_op jit(solution)/shard_map/ppermute | solution.py:366
  33.8 2.2 %collective-permute-start.16 = (f32[384,128]{1,0:T(8,128)S(1)}, f32[384,128]{1,0:T(8,128)S(1)}, u32[]{:S(2)}, u32[]{:S(2)}) collective-permute-start(f32[384,128]{1,0:T(8,128)S(1)} %get-tuple-element.40), channel_id=1, source_target_pairs={{0,1},{1,0},{2,3},{3,2},{4,5},{5,4},{6,7},{7,6},{8,9},{9,8},{10,11... | collective-permute-start | bytes 589832 | tf_op jit(solution)/shard_map/ppermute | solution.py:350
  35.6 9.9 %collective-permute-start.12 = (f32[1,4,64,128]{3,2,1,0:T(8,128)S(1)}, f32[1,4,64,128]{3,2,1,0:T(8,128)S(1)}, u32[]{:S(2)}, u32[]{:S(2)}) collective-permute-start(f32[1,4,64,128]{3,2,1,0:T(8,128)S(1)} %collective-permute-done.11.refs_0_), channel_id=1, source_target_pairs={{0,1},{1,0},{2,3},{3,2},{4,5},{5,4},{6,7},{7,6},{8,9},{9,8},{10,11... | collective-permute-start | bytes 393224 | tf_op jit(solution)/shard_map/ppermute | solution.py:350
  35.6 9.9 %collective-permute-start.14 = (f32[1,4,64,128]{3,2,1,0:T(8,128)S(1)}, f32[1,4,64,128]{3,2,1,0:T(8,128)S(1)}, u32[]{:S(2)}, u32[]{:S(2)}) collective-permute-start(f32[1,4,64,128]{3,2,1,0:T(8,128)S(1)} %collective-permute-done.13.refs_2_), channel_id=1, source_target_pairs={{0,1},{1,0},{2,3},{3,2},{4,5},{5,4},{6,7},{7,6},{8,9},{9,8},{10,11... | collective-permute-start | bytes 393224 | tf_op jit(solution)/shard_map/ppermute | solution.py:350
  36.8 17.3 %all-to-all-start = ((f32[8,48,128]{2,1,0:T(8,128)}), f32[8,48,128]{2,1,0:T(8,128)S(1)}, u32[]{:S(2)}, u32[]{:S(2)}) async-start(f32[8,48,128]{2,1,0:T(8,128)} %bitcast.4), calls=%async_computation | async-start | bytes 393216 | tf_op jit(solution)/shard_map/all_to_all | solution.py:353
  45.5 1.6 %copy-start.6 = (bf16[16,128,512]{2,1,0:T(8,128)(2,1)S(1)}, bf16[16,128,512]{2,1,0:T(8,128)(2,1)}, u32[]{:S(2)}) copy-start(bf16[16,128,512]{2,1,0:T(8,128)(2,1)} %copy-done.5) | copy-start | bytes 6291460
  50.2 1.4 %collective-permute-start.15 = (f32[256,128]{1,0:T(8,128)S(1)}, f32[256,128]{1,0:T(8,128)S(1)}, u32[]{:S(2)}, u32[]{:S(2)}) collective-permute-start(f32[256,128]{1,0:T(8,128)S(1)} %get-tuple-element.38), channel_id=1, source_target_pairs={{0,1},{1,0},{2,3},{3,2},{4,5},{5,4},{6,7},{7,6},{8,9},{9,8},{10,11... | collective-permute-start | bytes 393224 | tf_op jit(solution)/shard_map/ppermute | solution.py:350
  65.7 6.2 %collective-permute-start.19 = (f32[384,128]{1,0:T(8,128)S(1)}, f32[384,128]{1,0:T(8,128)S(1)}, u32[]{:S(2)}, u32[]{:S(2)}) collective-permute-start(f32[384,128]{1,0:T(8,128)S(1)} %bitcast.6), channel_id=1, source_target_pairs={{0,1},{1,0},{2,3},{3,2},{4,5},{5,4},{6,7},{7,6},{8,9},{9,8},{10,11... | collective-permute-start | bytes 589832 | tf_op jit(solution)/shard_map/ppermute | solution.py:350
  65.7 5.9 %collective-permute-start.17 = (f32[256,128]{1,0:T(8,128)S(1)}, f32[256,128]{1,0:T(8,128)S(1)}, u32[]{:S(2)}, u32[]{:S(2)}) collective-permute-start(f32[256,128]{1,0:T(8,128)S(1)} %add.28), channel_id=1, source_target_pairs={{0,2},{2,0},{4,6},{6,4},{8,10},{10,8},{12,14},{14,12},{1,3},{3,1},... | collective-permute-start | bytes 393224 | tf_op jit(solution)/shard_map/ppermute | solution.py:356
  71.6 5.2 %collective-permute-start.18 = (f32[256,128]{1,0:T(8,128)S(1)}, f32[256,128]{1,0:T(8,128)S(1)}, u32[]{:S(2)}, u32[]{:S(2)}) collective-permute-start(f32[256,128]{1,0:T(8,128)S(1)} %add.30), channel_id=1, source_target_pairs={{0,4},{2,6},{4,0},{6,2},{8,12},{10,14},{12,8},{14,10},{1,5},{3,7},... | collective-permute-start | bytes 393224 | tf_op jit(solution)/shard_map/ppermute | solution.py:356
  76.9 10.4 %collective-permute-start.20 = (f32[256,128]{1,0:T(8,128)S(1)}, f32[256,128]{1,0:T(8,128)S(1)}, u32[]{:S(2)}, u32[]{:S(2)}) collective-permute-start(f32[256,128]{1,0:T(8,128)S(1)} %add.31), channel_id=1, source_target_pairs={{0,8},{2,10},{4,12},{6,14},{8,0},{10,2},{12,4},{14,6},{1,9},{3,11}... | collective-permute-start | bytes 393224 | tf_op jit(solution)/shard_map/ppermute | solution.py:356
  87.3 1.4 %collective-permute-start.21 = (f32[256,128]{1,0:T(8,128)S(1)}, f32[256,128]{1,0:T(8,128)S(1)}, u32[]{:S(2)}, u32[]{:S(2)}) collective-permute-start(f32[256,128]{1,0:T(8,128)S(1)} %add.32.own), channel_id=1, source_target_pairs={{0,1},{1,0},{2,3},{3,2},{4,5},{5,4},{6,7},{7,6},{8,9},{9,8},{10,11... | collective-permute-start | bytes 393224 | tf_op jit(solution)/shard_map/ppermute | solution.py:350

commit v6 on v4

--- a/solution.py
+++ b/solution.py
@@ -82,7 +82,7 @@
             put((layer + 1) * total + mine + q, own[layer, q])
             put((layer + 1) * total + theirs + q, other[layer, q])
     even = info[3]
-    for pair, place in enumerate((1 - even, even)):
+    for pair, place in enumerate((even, 1 - even)):
         for q in range(cross_local):
             put(place * (layers + 1) * total + mine + q, edges[2 * pair][0, q])
             put(place * (layers + 1) * total + theirs + q, edges[2 * pair + 1][0, q])
@@ -342,8 +342,9 @@
     def exchange(x):
         return lax.all_to_all(x, "trans", 0, 0, tiled=True)
 
-    def double(x, reach):
-        return x + lax.ppermute(x, "trans", [(i, i ^ reach) for i in range(count)])
+    def double(x, reach, work=None):
+        other = lax.ppermute(x, "trans", [(i, i ^ reach) for i in range(count)])
+        return x + (other if work is None else lax.optimization_barrier((other, work))[0])
 
     early = tuple((i, j) for i in range(S) for j in range(i + 1))
     powers = [sources]
@@ -351,18 +352,16 @@
     far_layer = lax.dynamic_slice_in_dim(sources, (1 - even) * (layers - 1), 1)
     for k in range(S):
         field = powers[k]
+        near_edge = lax.ppermute(near_layer, "trans", near)
         far_edge = lax.ppermute(far_layer, "trans", far)
-        near_edge = lax.ppermute(near_layer, "trans", near)
         other = swap(field)
         if k == 0:
-            near_edge, far_edge, packed = lax.optimization_barrier((near_edge, far_edge, packed))
+            far_edge, near_edge, packed = lax.optimization_barrier((far_edge, near_edge, packed))
         if k == S - 1:
-            held, other = lax.optimization_barrier((field, other))
-            mine, theirs = gram_blocks([*powers[:-1], held], early, info, count)
-            shares = (mine + swap(theirs)).reshape(count, -1, columns)
-            near_edge, far_edge, shares = lax.optimization_barrier((near_edge, far_edge, shares))
-            parts = exchange(shares)
-        edges = (far_edge, swap(far_edge), near_edge, swap(near_edge))
+            mine, theirs = gram_blocks(powers, early, info, count)
+            theirs, _, _ = lax.optimization_barrier((swap(theirs), near_edge, far_edge))
+            parts = exchange((mine + theirs).reshape(count, -1, columns))
+        edges = (near_edge, swap(near_edge), far_edge, swap(far_edge))
         before = powers[k - 1] if k else None
         got = step(packed, block_cols, info, field, other, edges, before, k == S - 1)
         powers.append(got[0])
@@ -372,18 +371,19 @@
     last = mine + swap(theirs)
     last, parts = lax.optimization_barrier((last, parts))
     summed = jnp.sum(parts, axis=0, keepdims=True)
-    known = exchange(jnp.broadcast_to(summed, parts.shape)).reshape(-1, columns)
+    known = exchange(jnp.broadcast_to(summed, parts.shape))
+    last = double(last, 1)
+    known, _ = lax.optimization_barrier((known, last))
+    known = known.reshape(-1, columns)
     known_other = swap(known)
     first = column(0, 0, info, known, known_other, ())
-    reach = 1
+    second = column(1, 1, info, known, known_other, first[::-1])
+    third = column(2, 3, info, known, known_other, second[::-1])
+    reach = 2
     while reach < count:
-        last = double(last, reach)
+        work = third if 2 * reach == count else first if 4 * reach == count else None
+        last = double(last, reach, work)
         reach *= 2
-        if reach == count // 2:
-            last, first = lax.optimization_barrier((last, first))
-    second = column(1, 1, info, known, known_other, first[::-1])
-    last, second = lax.optimization_barrier((last, second))
-    third = column(2, 3, info, known, known_other, second[::-1])
     r_factor, inverse = column(3, 0, info, last, swap(last), third[::-1], 1.0 / scale_rows)
     return basis_of(powers, inverse, scale_rows), r_factor
 

time: 103 us -> 92 us (0.89)
  waiting for transfers between devices: 30.4 us -> 19.1 us
    all_to_all x2, waiting for transfers between devices: 8.2 us -> 3.38 us  [exchange(): return lax.all_to_all(x, 'trans', 0, 0, tiled=True)]
    ppermute x3, waiting for transfers between devices: 8.48 us -> 4.77 us  [local(): near_edge = lax.ppermute(near_layer, 'trans', near)]
    ppermute x3, waiting for transfers between devices: 8.26 us -> 5.97 us  [double(): other = lax.ppermute(x, 'trans', [(i, i ^ reach) for i in range(count)])]
    ppermute x3, starting transfers between devices: 13.2 us -> 11.2 us  [local(): near_edge = lax.ppermute(near_layer, 'trans', near)]
    ppermute x3, starting transfers between devices: 3.65 us -> 4.8 us  [double(): other = lax.ppermute(x, 'trans', [(i, i ^ reach) for i in range(count)])]
  transfers between devices with their start and end apart: 24 -> 24, of which waited for: 12 -> 13; matrix products, arithmetic and copies ran while one was open for 2% -> 2% of each run, Pallas kernels for 12% -> 20%
where the time goes in v6:
time: 92 us; the launch traced here: 91.5 us
  starting transfers between devices  33.6 us (37%)
  Pallas kernels  30.2 us (33%)
  waiting for transfers between devices  19.1 us (21%)
  local copies, waits for them, and re-layouts  6.87 us (7%)
    pallas_call x4, Pallas kernels, column(): pl.pallas_call(functools.partial(column_kernel, place, first, scale), in_...  17.8 us
    all_to_all x2, starting transfers between devices, exchange(): return lax.all_to_all(x, 'trans', 0, 0, tiled=True)  12.2 us
    ppermute x3, starting transfers between devices, local(): near_edge = lax.ppermute(near_layer, 'trans', near)  11.2 us
    ppermute x3, waiting for transfers between devices, double(): other = lax.ppermute(x, 'trans', [(i, i ^ reach) for i in range(count)])  5.97 us
    unnamed x14, local copies, waits for them, and re-layouts  5.19 us
    pallas_call x3, Pallas kernels, step(): pl.pallas_call(functools.partial(step_kernel, before is None, last, cols....  5.05 us
    ppermute x13, waiting for transfers between devices, swap(): return lax.ppermute(x, 'cross', [(0, 1), (1, 0)])  5.01 us
    ppermute x3, starting transfers between devices, double(): other = lax.ppermute(x, 'trans', [(i, i ^ reach) for i in range(count)])  4.8 us
  transfers between devices with their start and end apart: 24, of which 13 were waited for; matrix products, arithmetic and copies ran while one was open for 2% of the time, Pallas kernels for 20%

profile of v6, /device:TPU:0, one launch (start us, length us, event | category | flops | bytes accessed | tf_op | source)
XLA Modules:
  0.0 91.5 jit_solution(12909890724612850566)
XLA Ops:
  0.6 0.5 collective-permute-start.2
  1.1 1.0 %constant_dynamic-slice_fusion = (f32[1,4,64,128]{3,2,1,0:T(8,128)S(1)}, f32[1,4,64,128]{3,2,1,0:T(8,128)S(1)}) fusion(f32[4,4,64,128]{3,2,1,0:T(8,128)} %refs_0_.5, s32[]{:T(128)S(6)} %select_n.15, s32[]{:T(128)S(6)} %select_n.14), kind=kLoop, calls=%fused_computation.1 | loop fusion | bytes 524296 | tf_op jit(solution)/shard_map/dynamic_slice | solution.py:351
  2.1 2.6 %collective-permute-start.1 = (f32[1,4,64,128]{3,2,1,0:T(8,128)S(1)}, f32[1,4,64,128]{3,2,1,0:T(8,128)S(1)}, u32[]{:S(2)}, u32[]{:S(2)}) collective-permute-start(f32[1,4,64,128]{3,2,1,0:T(8,128)S(1)} %get-tuple-element.56), channel_id=1, source_target_pairs={{0,2},{2,0},{4,6},{6,4},{8,10},{10,8},{12,14},{14,12},{1,3},{3,1},... | collective-permute-start | bytes 393224 | tf_op jit(solution)/shard_map/ppermute | solution.py:355
  4.7 0.7 collective-permute-start
  5.5 2.0 %copy-done.1 = f32[4,4,7,64,64]{4,3,2,1,0:T(8,128)S(1)} copy-done((f32[4,4,7,64,64]{4,3,2,1,0:T(8,128)S(1)}, f32[4,4,7,64,64]{4,3,2,1,0:T(8,128)}, u32[]{:S(2)}) %copy-start.1) | copy-done | bytes 1835032
  7.5 0.9 copy-done.2
  8.4 0.7 copy-done.4
  9.1 1.1 %pack.1.packed = bf16[16,128,512]{2,1,0:T(8,128)(2,1)S(1)} custom-call(s32[4]{0:T(128)S(1)} %pad_add_fusion.info, s32[4]{0:T(128)S(1)} %copy-done.4, f32[4,4,7,64,64]{4,3,2,1,0:T(8,128)S(1)} %copy-done.1, f32[4,64,64]{2,1,0:T(8,128)S(1)} %copy-done.2), custom_call_target="tpu_custom_call" | custom-call | flops 2875000064 | tf_op jit(solution)/shard_map/pack/pallas_call | solution.py:53
  10.2 0.2 collective-permute-start.3
  10.5 0.3 collective-permute-start.4
  10.8 0.8 collective-permute-done.3.refs_1_
  11.8 1.7 %step.3 = (f32[4,4,64,128]{3,2,1,0:T(8,128)S(1)}, f32[1,4,64,128]{3,2,1,0:T(8,128)S(1)}, f32[1,4,64,128]{3,2,1,0:T(8,128)S(1)}) custom-call(s32[4]{0:T(128)S(1)} %pad_add_fusion.info, s32[4,4,7]{2,1,0:T(4,128)S(1)} %copy-done.3, bf16[16,128,512]{2,1,0:T(8,128)(2,1)S(1)} %pack.1.packed, f32[4,4,64,128]{3,2,1,0:T(8,128)S(1)} %copy-done, ...), custom_call_target="tpu_custom_call" | custom-call | flops 1955000064 | tf_op jit(solution)/shard_map/step/pallas_call | solution.py:114
  13.5 0.4 collective-permute-start.5
  13.9 4.3 %collective-permute-start.6 = (f32[1,4,64,128]{3,2,1,0:T(8,128)S(1)}, f32[1,4,64,128]{3,2,1,0:T(8,128)S(1)}, u32[]{:S(2)}, u32[]{:S(2)}) collective-permute-start(f32[1,4,64,128]{3,2,1,0:T(8,128)S(1)} %get-tuple-element.33), channel_id=1, source_target_pairs={{0,2},{2,0},{4,6},{6,4},{8,10},{10,8},{12,14},{14,12},{1,3},{3,1},... | collective-permute-start | bytes 393224 | tf_op jit(solution)/shard_map/ppermute | solution.py:355
  18.2 0.7 collective-permute-start.8
  18.8 3.2 %collective-permute-done.6.refs_0_ = f32[1,4,64,128]{3,2,1,0:T(8,128)S(1)} collective-permute-done((f32[1,4,64,128]{3,2,1,0:T(8,128)S(1)}, f32[1,4,64,128]{3,2,1,0:T(8,128)S(1)}, u32[]{:S(2)}, u32[]{:S(2)}) %collective-permute-start.6) | collective-permute-done | bytes 131104 | tf_op jit(solution)/shard_map/ppermute | solution.py:355
  22.0 0.5 collective-permute-start.9
  22.5 0.8 collective-permute-done.7.refs_1_
  23.6 1.7 %step.4 = (f32[4,4,64,128]{3,2,1,0:T(8,128)S(1)}, f32[1,4,64,128]{3,2,1,0:T(8,128)S(1)}, f32[1,4,64,128]{3,2,1,0:T(8,128)S(1)}) custom-call(s32[4]{0:T(128)S(1)} %pad_add_fusion.info, s32[4,4,7]{2,1,0:T(4,128)S(1)} %copy-done.3, bf16[16,128,512]{2,1,0:T(8,128)(2,1)S(1)} %pack.1.packed, f32[4,4,64,128]{3,2,1,0:T(8,128)S(1)} %get-tuple-element.32.own.refs_4_.refs_1_, ...), custom_call_target="tpu_custom_call" | custom-call | flops 1955000064 | tf_op jit(solution)/shard_map/step/pallas_call | solution.py:114
  25.3 0.4 collective-permute-start.10
  25.7 4.3 %collective-permute-start.11 = (f32[1,4,64,128]{3,2,1,0:T(8,128)S(1)}, f32[1,4,64,128]{3,2,1,0:T(8,128)S(1)}, u32[]{:S(2)}, u32[]{:S(2)}) collective-permute-start(f32[1,4,64,128]{3,2,1,0:T(8,128)S(1)} %get-tuple-element.36), channel_id=1, source_target_pairs={{0,2},{2,0},{4,6},{6,4},{8,10},{10,8},{12,14},{14,12},{1,3},{3,1},... | collective-permute-start | bytes 393224 | tf_op jit(solution)/shard_map/ppermute | solution.py:355
  30.0 0.7 collective-permute-start.13
  30.6 1.6 %gram.3 = (f32[384,128]{1,0:T(8,128)S(1)}, f32[384,128]{1,0:T(8,128)S(1)}) custom-call(s32[4]{0:T(128)S(1)} %pad_add_fusion.info, f32[4,4,64,128]{3,2,1,0:T(8,128)S(1)} %copy-done, f32[4,4,64,128]{3,2,1,0:T(8,128)S(1)} %get-tuple-element.32.own.refs_4_.refs_1_, f32[4,4,64,128]{3,2,1,0:T(8,128)S(1)} %get-tuple-element.35.own.refs_2_), custom_call_target="tpu_custom_call" | custom-call | flops 1610000000 | tf_op jit(solution)/shard_map/gram/pallas_call | solution.py:156
  32.4 1.6 %collective-permute-done.11.refs_0_ = f32[1,4,64,128]{3,2,1,0:T(8,128)S(1)} collective-permute-done((f32[1,4,64,128]{3,2,1,0:T(8,128)S(1)}, f32[1,4,64,128]{3,2,1,0:T(8,128)S(1)}, u32[]{:S(2)}, u32[]{:S(2)}) %collective-permute-start.11) | collective-permute-done | bytes 131104 | tf_op jit(solution)/shard_map/ppermute | solution.py:355
  34.0 0.5 collective-permute-start.14
  34.5 0.7 add.29
  35.2 8.7 %all-to-all-start = ((f32[8,48,128]{2,1,0:T(8,128)}), f32[8,48,128]{2,1,0:T(8,128)S(1)}, u32[]{:S(2)}, u32[]{:S(2)}) async-start(f32[8,48,128]{2,1,0:T(8,128)} %bitcast.4), calls=%async_computation | async-start | bytes 393216 | tf_op jit(solution)/shard_map/all_to_all | solution.py:343
  43.9 1.6 %copy-done.6 = bf16[16,128,512]{2,1,0:T(8,128)(2,1)S(1)} copy-done((bf16[16,128,512]{2,1,0:T(8,128)(2,1)S(1)}, bf16[16,128,512]{2,1,0:T(8,128)(2,1)}, u32[]{:S(2)}) %copy-start.6) | copy-done | bytes 2097176
  45.5 1.7 %step.5.refs_3_ = f32[4,4,64,128]{3,2,1,0:T(8,128)S(1)} custom-call(s32[4]{0:T(128)S(1)} %pad_add_fusion.info, s32[4,4,7]{2,1,0:T(4,128)S(1)} %copy-done.3, bf16[16,128,512]{2,1,0:T(8,128)(2,1)S(1)} %copy-done.6, f32[4,4,64,128]{3,2,1,0:T(8,128)S(1)} %get-tuple-element.35.own.refs_2_, f32[4,4,64,128]{3,2,1,0:T(8,128)S(1)} %collective-permute-done.10.other, ...), custom_call_target="tpu_custom_call" | custom-call | flops 1955000064 | tf_op jit(solution)/shard_map/step/pallas_call | solution.py:114
  47.2 1.4 %gram.2 = (f32[256,128]{1,0:T(8,128)S(1)}, f32[256,128]{1,0:T(8,128)S(1)}) custom-call(s32[4]{0:T(128)S(1)} %pad_add_fusion.info, f32[4,4,64,128]{3,2,1,0:T(8,128)S(1)} %copy-done, f32[4,4,64,128]{3,2,1,0:T(8,128)S(1)} %get-tuple-element.32.own.refs_4_.refs_1_, f32[4,4,64,128]{3,2,1,0:T(8,128)S(1)} %get-tuple-element.35.own.refs_2_, ...), custom_call_target="tpu_custom_call" | custom-call | flops 1610000000 | tf_op jit(solution)/shard_map/gram/pallas_call | solution.py:156
  48.6 0.3 collective-permute-start.15
  48.9 1.1 %collective-permute-done.15 = f32[256,128]{1,0:T(8,128)S(1)} collective-permute-done((f32[256,128]{1,0:T(8,128)S(1)}, f32[256,128]{1,0:T(8,128)S(1)}, u32[]{:S(2)}, u32[]{:S(2)}) %collective-permute-start.15) | collective-permute-done | bytes 131104 | tf_op jit(solution)/shard_map/ppermute | solution.py:340
  50.0 2.4 %all-to-all-done = f32[8,48,128]{2,1,0:T(8,128)S(1)} async-done(((f32[8,48,128]{2,1,0:T(8,128)}), f32[8,48,128]{2,1,0:T(8,128)S(1)}, u32[]{:S(2)}, u32[]{:S(2)}) %all-to-all-start) | async-done | bytes 196640 | tf_op jit(solution)/shard_map/all_to_all | solution.py:343
  52.5 0.7 broadcast_in_dim.2
  53.2 3.6 %all-to-all-start.1 = ((f32[8,48,128]{2,1,0:T(8,128)}), f32[8,48,128]{2,1,0:T(8,128)S(1)}, u32[]{:S(2)}, u32[]{:S(2)}) async-start(f32[8,48,128]{2,1,0:T(8,128)} %broadcast_in_dim.2), calls=%async_computation.1 | async-start | bytes 393216 | tf_op jit(solution)/shard_map/all_to_all | solution.py:343
  56.8 2.0 %collective-permute-start.17 = (f32[256,128]{1,0:T(8,128)S(1)}, f32[256,128]{1,0:T(8,128)S(1)}, u32[]{:S(2)}, u32[]{:S(2)}) collective-permute-start(f32[256,128]{1,0:T(8,128)S(1)} %add.28), channel_id=1, source_target_pairs={{0,2},{2,0},{4,6},{6,4},{8,10},{10,8},{12,14},{14,12},{1,3},{3,1},... | collective-permute-start | bytes 393224 | tf_op jit(solution)/shard_map/ppermute | solution.py:346
  58.8 5.3 %collective-permute-done.17 = f32[256,128]{1,0:T(8,128)S(1)} collective-permute-done((f32[256,128]{1,0:T(8,128)S(1)}, f32[256,128]{1,0:T(8,128)S(1)}, u32[]{:S(2)}, u32[]{:S(2)}) %collective-permute-start.17) | collective-permute-done | bytes 131104 | tf_op jit(solution)/shard_map/ppermute | solution.py:346
  64.1 0.9 %all-to-all-done.1 = f32[8,48,128]{2,1,0:T(8,128)S(1)} async-done(((f32[8,48,128]{2,1,0:T(8,128)}), f32[8,48,128]{2,1,0:T(8,128)S(1)}, u32[]{:S(2)}, u32[]{:S(2)}) %all-to-all-start.1) | async-done | bytes 196640 | tf_op jit(solution)/shard_map/all_to_all | solution.py:343
  65.0 0.9 %collective-permute-start.18 = (f32[256,128]{1,0:T(8,128)S(1)}, f32[256,128]{1,0:T(8,128)S(1)}, u32[]{:S(2)}, u32[]{:S(2)}) collective-permute-start(f32[256,128]{1,0:T(8,128)S(1)} %add.30), channel_id=1, source_target_pairs={{0,4},{2,6},{4,0},{6,2},{8,12},{10,14},{12,8},{14,10},{1,5},{3,7},... | collective-permute-start | bytes 393224 | tf_op jit(solution)/shard_map/ppermute | solution.py:346
  66.0 0.5 collective-permute-done.19.other
  66.5 3.8 %column.4 = (f32[128,128]{1,0:T(8,128)S(1)}, f32[128,128]{1,0:T(8,128)S(1)}) custom-call(s32[4]{0:T(128)S(1)} %pad_add_fusion.info, f32[384,128]{1,0:T(8,128)S(1)} %bitcast.7, f32[384,128]{1,0:T(8,128)S(1)} %collective-permute-done.19.other), custom_call_target="tpu_custom_call" | custom-call | flops 4600000000 | tf_op jit(solution)/shard_map/column/pallas_call | solution.py:269
  70.2 0.7 collective-permute-done.18
  70.9 1.8 %collective-permute-start.20 = (f32[256,128]{1,0:T(8,128)S(1)}, f32[256,128]{1,0:T(8,128)S(1)}, u32[]{:S(2)}, u32[]{:S(2)}) collective-permute-start(f32[256,128]{1,0:T(8,128)S(1)} %add.31), channel_id=1, source_target_pairs={{0,8},{2,10},{4,12},{6,14},{8,0},{10,2},{12,4},{14,6},{1,9},{3,11}... | collective-permute-start | bytes 393224 | tf_op jit(solution)/shard_map/ppermute | solution.py:346
  72.8 4.2 %column.5 = (f32[256,256]{1,0:T(8,128)S(1)}, f32[256,256]{1,0:T(8,128)S(1)}) custom-call(s32[4]{0:T(128)S(1)} %pad_add_fusion.info, f32[384,128]{1,0:T(8,128)S(1)} %bitcast.8, f32[384,128]{1,0:T(8,128)S(1)} %collective-permute-done.19.other, f32[128,128]{1,0:T(8,128)S(1)} %get-tuple-element.47.refs_0_, f32[128,128]{1,0:T(8,128)S(1)} %get-tuple-element.46.refs_1_), custom_call_target="tpu_custom_call" | custom-call | flops 4600000000 | tf_op jit(solution)/shard_map/column/pallas_call | solution.py:269
  76.9 4.2 %column.6 = (f32[384,384]{1,0:T(8,128)S(1)}, f32[384,384]{1,0:T(8,128)S(1)}) custom-call(s32[4]{0:T(128)S(1)} %pad_add_fusion.info, f32[384,128]{1,0:T(8,128)S(1)} %bitcast.9, f32[384,128]{1,0:T(8,128)S(1)} %collective-permute-done.19.other, f32[256,256]{1,0:T(8,128)S(1)} %get-tuple-element.49.refs_0_, f32[256,256]{1,0:T(8,128)S(1)} %get-tuple-element.50.refs_1_), custom_call_target="tpu_custom_call" | custom-call | flops 4600000000 | tf_op jit(solution)/shard_map/column/pallas_call | solution.py:269
  81.3 1.3 %collective-permute-done.21.other = f32[256,128]{1,0:T(8,128)S(1)} collective-permute-done((f32[256,128]{1,0:T(8,128)S(1)}, f32[256,128]{1,0:T(8,128)S(1)}, u32[]{:S(2)}, u32[]{:S(2)}) %collective-permute-start.21) | collective-permute-done | bytes 131104 | tf_op jit(solution)/shard_map/ppermute | solution.py:340
  82.6 5.7 %column.7 = (f32[512,512]{1,0:T(8,128)}, f32[512,512]{1,0:T(8,128)S(1)}) custom-call(s32[4]{0:T(128)S(1)} %pad_add_fusion.info, f32[256,128]{1,0:T(8,128)S(1)} %add.32.own, f32[256,128]{1,0:T(8,128)S(1)} %collective-permute-done.21.other, f32[384,384]{1,0:T(8,128)S(1)} %get-tuple-element.52.refs_0_, f32[384,384]{1,0:T(8,128)S(1)} %get-tuple-element.51.refs_1_), custom_call_target="tpu_custom_call" | custom-call | flops 4600000000 | tf_op jit(solution)/shard_map/column/pallas_call | solution.py:269
  88.3 3.2 %basis.1 = bf16[4,4,64,512]{3,2,1,0:T(8,128)(2,1)} custom-call(f32[4,4,64,128]{3,2,1,0:T(8,128)S(1)} %copy-done, f32[4,4,64,128]{3,2,1,0:T(8,128)S(1)} %get-tuple-element.32.own.refs_4_.refs_1_, f32[4,4,64,128]{3,2,1,0:T(8,128)S(1)} %get-tuple-element.35.own.refs_2_, f32[4,4,64,128]{3,2,1,0:T(8,128)S(1)} %step.5.refs_3_, ...), custom_call_target="tpu_custom_call" | custom-call | flops 3449999872 | tf_op jit(solution)/shard_map/basis/pallas_call | solution.py:311
  (34 shorter events, 0.8 us)
Async XLA Ops:
  0.6 11.2 %collective-permute-start.2 = (f32[4,4,64,128]{3,2,1,0:T(8,128)}, f32[4,4,64,128]{3,2,1,0:T(8,128)S(1)}, u32[]{:S(2)}, u32[]{:S(2)}) collective-permute-start(f32[4,4,64,128]{3,2,1,0:T(8,128)} %refs_0_.5), channel_id=1, source_target_pairs={{0,1},{1,0},{2,3},{3,2},{4,5},{5,4},{6,7},{7,6},{8,9},{9,8},{10,11... | collective-permute-start | bytes 1572872 | tf_op jit(solution)/shard_map/ppermute | solution.py:340
  2.1 8.1 %collective-permute-start.1 = (f32[1,4,64,128]{3,2,1,0:T(8,128)S(1)}, f32[1,4,64,128]{3,2,1,0:T(8,128)S(1)}, u32[]{:S(2)}, u32[]{:S(2)}) collective-permute-start(f32[1,4,64,128]{3,2,1,0:T(8,128)S(1)} %get-tuple-element.56), channel_id=1, source_target_pairs={{0,2},{2,0},{4,6},{6,4},{8,10},{10,8},{12,14},{14,12},{1,3},{3,1},... | collective-permute-start | bytes 393224 | tf_op jit(solution)/shard_map/ppermute | solution.py:355
  4.7 5.5 %collective-permute-start = (f32[1,4,64,128]{3,2,1,0:T(8,128)S(1)}, f32[1,4,64,128]{3,2,1,0:T(8,128)S(1)}, u32[]{:S(2)}, u32[]{:S(2)}) collective-permute-start(f32[1,4,64,128]{3,2,1,0:T(8,128)S(1)} %get-tuple-element.57), channel_id=1, source_target_pairs={{2,4},{4,2},{6,8},{8,6},{10,12},{12,10},{3,5},{5,3},{7,9},{9,7},{1... | collective-permute-start | bytes 393224 | tf_op jit(solution)/shard_map/ppermute | solution.py:356
  5.5 2.0 %copy-start.1 = (f32[4,4,7,64,64]{4,3,2,1,0:T(8,128)S(1)}, f32[4,4,7,64,64]{4,3,2,1,0:T(8,128)}, u32[]{:S(2)}) copy-start(f32[4,4,7,64,64]{4,3,2,1,0:T(8,128)} %held.1) | copy-start | bytes 5505028
  7.5 0.9 copy-start.2
  8.4 0.7 copy-start.4
  9.1 2.7 %copy-start = (f32[4,4,64,128]{3,2,1,0:T(8,128)S(1)}, f32[4,4,64,128]{3,2,1,0:T(8,128)}, u32[]{:S(2)}) copy-start(f32[4,4,64,128]{3,2,1,0:T(8,128)} %refs_0_.5) | copy-start | bytes 1572868
  9.1 2.7 %copy-start.3 = (s32[4,4,7]{2,1,0:T(4,128)S(1)}, s32[4,4,7]{2,1,0:T(4,128)}, u32[]{:S(2)}) copy-start(s32[4,4,7]{2,1,0:T(4,128)} %cols.5) | copy-start | bytes 1348
  10.2 15.1 %copy-start.5 = (bf16[16,128,512]{2,1,0:T(8,128)(2,1)}, bf16[16,128,512]{2,1,0:T(8,128)(2,1)S(1)}, u32[]{:S(2)}) copy-start(bf16[16,128,512]{2,1,0:T(8,128)(2,1)S(1)} %pack.1.packed) | copy-start | bytes 6291460
  10.2 1.4 %collective-permute-start.3 = (f32[1,4,64,128]{3,2,1,0:T(8,128)S(1)}, f32[1,4,64,128]{3,2,1,0:T(8,128)S(1)}, u32[]{:S(2)}, u32[]{:S(2)}) collective-permute-start(f32[1,4,64,128]{3,2,1,0:T(8,128)S(1)} %collective-permute-done.1.refs_0_), channel_id=1, source_target_pairs={{0,1},{1,0},{2,3},{3,2},{4,5},{5,4},{6,7},{7,6},{8,9},{9,8},{10,11... | collective-permute-start | bytes 393224 | tf_op jit(solution)/shard_map/ppermute | solution.py:340
  10.5 1.4 %collective-permute-start.4 = (f32[1,4,64,128]{3,2,1,0:T(8,128)S(1)}, f32[1,4,64,128]{3,2,1,0:T(8,128)S(1)}, u32[]{:S(2)}, u32[]{:S(2)}) collective-permute-start(f32[1,4,64,128]{3,2,1,0:T(8,128)S(1)} %collective-permute-done.refs_2_), channel_id=1, source_target_pairs={{0,1},{1,0},{2,3},{3,2},{4,5},{5,4},{6,7},{7,6},{8,9},{9,8},{10,11... | collective-permute-start | bytes 393224 | tf_op jit(solution)/shard_map/ppermute | solution.py:340
  13.5 10.1 %collective-permute-start.5 = (f32[4,4,64,128]{3,2,1,0:T(8,128)S(1)}, f32[4,4,64,128]{3,2,1,0:T(8,128)S(1)}, u32[]{:S(2)}, u32[]{:S(2)}) collective-permute-start(f32[4,4,64,128]{3,2,1,0:T(8,128)S(1)} %get-tuple-element.32.own.refs_4_.refs_1_), channel_id=1, source_target_pairs={{0,1},{1,0},{2,3},{3,2},{4,5},{5,4},{6,7},{7,6},{8,9},{9,8},{10,11... | collective-permute-start | bytes 1572872 | tf_op jit(solution)/shard_map/ppermute | solution.py:340
  13.9 8.1 %collective-permute-start.6 = (f32[1,4,64,128]{3,2,1,0:T(8,128)S(1)}, f32[1,4,64,128]{3,2,1,0:T(8,128)S(1)}, u32[]{:S(2)}, u32[]{:S(2)}) collective-permute-start(f32[1,4,64,128]{3,2,1,0:T(8,128)S(1)} %get-tuple-element.33), channel_id=1, source_target_pairs={{0,2},{2,0},{4,6},{6,4},{8,10},{10,8},{12,14},{14,12},{1,3},{3,1},... | collective-permute-start | bytes 393224 | tf_op jit(solution)/shard_map/ppermute | solution.py:355
  18.2 3.9 %collective-permute-start.8 = (f32[1,4,64,128]{3,2,1,0:T(8,128)S(1)}, f32[1,4,64,128]{3,2,1,0:T(8,128)S(1)}, u32[]{:S(2)}, u32[]{:S(2)}) collective-permute-start(f32[1,4,64,128]{3,2,1,0:T(8,128)S(1)} %get-tuple-element.34), channel_id=1, source_target_pairs={{2,4},{4,2},{6,8},{8,6},{10,12},{12,10},{3,5},{5,3},{7,9},{9,7},{1... | collective-permute-start | bytes 393224 | tf_op jit(solution)/shard_map/ppermute | solution.py:356
  22.0 1.3 %collective-permute-start.7 = (f32[1,4,64,128]{3,2,1,0:T(8,128)S(1)}, f32[1,4,64,128]{3,2,1,0:T(8,128)S(1)}, u32[]{:S(2)}, u32[]{:S(2)}) collective-permute-start(f32[1,4,64,128]{3,2,1,0:T(8,128)S(1)} %collective-permute-done.6.refs_0_), channel_id=1, source_target_pairs={{0,1},{1,0},{2,3},{3,2},{4,5},{5,4},{6,7},{7,6},{8,9},{9,8},{10,11... | collective-permute-start | bytes 393224 | tf_op jit(solution)/shard_map/ppermute | solution.py:340
  22.0 1.5 %collective-permute-start.9 = (f32[1,4,64,128]{3,2,1,0:T(8,128)S(1)}, f32[1,4,64,128]{3,2,1,0:T(8,128)S(1)}, u32[]{:S(2)}, u32[]{:S(2)}) collective-permute-start(f32[1,4,64,128]{3,2,1,0:T(8,128)S(1)} %collective-permute-done.8.refs_2_), channel_id=1, source_target_pairs={{0,1},{1,0},{2,3},{3,2},{4,5},{5,4},{6,7},{7,6},{8,9},{9,8},{10,11... | collective-permute-start | bytes 393224 | tf_op jit(solution)/shard_map/ppermute | solution.py:340
  25.3 18.6 %collective-permute-start.10 = (f32[4,4,64,128]{3,2,1,0:T(8,128)S(1)}, f32[4,4,64,128]{3,2,1,0:T(8,128)S(1)}, u32[]{:S(2)}, u32[]{:S(2)}) collective-permute-start(f32[4,4,64,128]{3,2,1,0:T(8,128)S(1)} %get-tuple-element.35.own.refs_2_), channel_id=1, source_target_pairs={{0,1},{1,0},{2,3},{3,2},{4,5},{5,4},{6,7},{7,6},{8,9},{9,8},{10,11... | collective-permute-start | bytes 1572872 | tf_op jit(solution)/shard_map/ppermute | solution.py:340
  25.7 8.3 %collective-permute-start.11 = (f32[1,4,64,128]{3,2,1,0:T(8,128)S(1)}, f32[1,4,64,128]{3,2,1,0:T(8,128)S(1)}, u32[]{:S(2)}, u32[]{:S(2)}) collective-permute-start(f32[1,4,64,128]{3,2,1,0:T(8,128)S(1)} %get-tuple-element.36), channel_id=1, source_target_pairs={{0,2},{2,0},{4,6},{6,4},{8,10},{10,8},{12,14},{14,12},{1,3},{3,1},... | collective-permute-start | bytes 393224 | tf_op jit(solution)/shard_map/ppermute | solution.py:355
  30.0 4.0 %collective-permute-start.13 = (f32[1,4,64,128]{3,2,1,0:T(8,128)S(1)}, f32[1,4,64,128]{3,2,1,0:T(8,128)S(1)}, u32[]{:S(2)}, u32[]{:S(2)}) collective-permute-start(f32[1,4,64,128]{3,2,1,0:T(8,128)S(1)} %get-tuple-element.37), channel_id=1, source_target_pairs={{2,4},{4,2},{6,8},{8,6},{10,12},{12,10},{3,5},{5,3},{7,9},{9,7},{1... | collective-permute-start | bytes 393224 | tf_op jit(solution)/shard_map/ppermute | solution.py:356
  32.3 2.2 %collective-permute-start.16 = (f32[384,128]{1,0:T(8,128)S(1)}, f32[384,128]{1,0:T(8,128)S(1)}, u32[]{:S(2)}, u32[]{:S(2)}) collective-permute-start(f32[384,128]{1,0:T(8,128)S(1)} %get-tuple-element.41), channel_id=1, source_target_pairs={{0,1},{1,0},{2,3},{3,2},{4,5},{5,4},{6,7},{7,6},{8,9},{9,8},{10,11... | collective-permute-start | bytes 589832 | tf_op jit(solution)/shard_map/ppermute | solution.py:340
  34.0 9.9 %collective-permute-start.12 = (f32[1,4,64,128]{3,2,1,0:T(8,128)S(1)}, f32[1,4,64,128]{3,2,1,0:T(8,128)S(1)}, u32[]{:S(2)}, u32[]{:S(2)}) collective-permute-start(f32[1,4,64,128]{3,2,1,0:T(8,128)S(1)} %collective-permute-done.11.refs_0_), channel_id=1, source_target_pairs={{0,1},{1,0},{2,3},{3,2},{4,5},{5,4},{6,7},{7,6},{8,9},{9,8},{10,11... | collective-permute-start | bytes 393224 | tf_op jit(solution)/shard_map/ppermute | solution.py:340
  34.0 9.9 %collective-permute-start.14 = (f32[1,4,64,128]{3,2,1,0:T(8,128)S(1)}, f32[1,4,64,128]{3,2,1,0:T(8,128)S(1)}, u32[]{:S(2)}, u32[]{:S(2)}) collective-permute-start(f32[1,4,64,128]{3,2,1,0:T(8,128)S(1)} %collective-permute-done.13.refs_2_), channel_id=1, source_target_pairs={{0,1},{1,0},{2,3},{3,2},{4,5},{5,4},{6,7},{7,6},{8,9},{9,8},{10,11... | collective-permute-start | bytes 393224 | tf_op jit(solution)/shard_map/ppermute | solution.py:340
  35.2 17.3 %all-to-all-start = ((f32[8,48,128]{2,1,0:T(8,128)}), f32[8,48,128]{2,1,0:T(8,128)S(1)}, u32[]{:S(2)}, u32[]{:S(2)}) async-start(f32[8,48,128]{2,1,0:T(8,128)} %bitcast.4), calls=%async_computation | async-start | bytes 393216 | tf_op jit(solution)/shard_map/all_to_all | solution.py:343
  43.9 1.6 %copy-start.6 = (bf16[16,128,512]{2,1,0:T(8,128)(2,1)S(1)}, bf16[16,128,512]{2,1,0:T(8,128)(2,1)}, u32[]{:S(2)}) copy-start(bf16[16,128,512]{2,1,0:T(8,128)(2,1)} %copy-done.5) | copy-start | bytes 6291460
  48.6 1.4 %collective-permute-start.15 = (f32[256,128]{1,0:T(8,128)S(1)}, f32[256,128]{1,0:T(8,128)S(1)}, u32[]{:S(2)}, u32[]{:S(2)}) collective-permute-start(f32[256,128]{1,0:T(8,128)S(1)} %get-tuple-element.39), channel_id=1, source_target_pairs={{0,1},{1,0},{2,3},{3,2},{4,5},{5,4},{6,7},{7,6},{8,9},{9,8},{10,11... | collective-permute-start | bytes 393224 | tf_op jit(solution)/shard_map/ppermute | solution.py:340
  53.2 11.8 %all-to-all-start.1 = ((f32[8,48,128]{2,1,0:T(8,128)}), f32[8,48,128]{2,1,0:T(8,128)S(1)}, u32[]{:S(2)}, u32[]{:S(2)}) async-start(f32[8,48,128]{2,1,0:T(8,128)} %broadcast_in_dim.2), calls=%async_computation.1 | async-start | bytes 393216 | tf_op jit(solution)/shard_map/all_to_all | solution.py:343
  56.8 7.3 %collective-permute-start.17 = (f32[256,128]{1,0:T(8,128)S(1)}, f32[256,128]{1,0:T(8,128)S(1)}, u32[]{:S(2)}, u32[]{:S(2)}) collective-permute-start(f32[256,128]{1,0:T(8,128)S(1)} %add.28), channel_id=1, source_target_pairs={{0,2},{2,0},{4,6},{6,4},{8,10},{10,8},{12,14},{14,12},{1,3},{3,1},... | collective-permute-start | bytes 393224 | tf_op jit(solution)/shard_map/ppermute | solution.py:346
  65.0 1.4 %collective-permute-start.19 = (f32[384,128]{1,0:T(8,128)S(1)}, f32[384,128]{1,0:T(8,128)S(1)}, u32[]{:S(2)}, u32[]{:S(2)}) collective-permute-start(f32[384,128]{1,0:T(8,128)S(1)} %bitcast.6), channel_id=1, source_target_pairs={{0,1},{1,0},{2,3},{3,2},{4,5},{5,4},{6,7},{7,6},{8,9},{9,8},{10,11... | collective-permute-start | bytes 589832 | tf_op jit(solution)/shard_map/ppermute | solution.py:340
  65.0 5.9 %collective-permute-start.18 = (f32[256,128]{1,0:T(8,128)S(1)}, f32[256,128]{1,0:T(8,128)S(1)}, u32[]{:S(2)}, u32[]{:S(2)}) collective-permute-start(f32[256,128]{1,0:T(8,128)S(1)} %add.30), channel_id=1, source_target_pairs={{0,4},{2,6},{4,0},{6,2},{8,12},{10,14},{12,8},{14,10},{1,5},{3,7},... | collective-permute-start | bytes 393224 | tf_op jit(solution)/shard_map/ppermute | solution.py:346
  70.9 10.3 %collective-permute-start.20 = (f32[256,128]{1,0:T(8,128)S(1)}, f32[256,128]{1,0:T(8,128)S(1)}, u32[]{:S(2)}, u32[]{:S(2)}) collective-permute-start(f32[256,128]{1,0:T(8,128)S(1)} %add.31), channel_id=1, source_target_pairs={{0,8},{2,10},{4,12},{6,14},{8,0},{10,2},{12,4},{14,6},{1,9},{3,11}... | collective-permute-start | bytes 393224 | tf_op jit(solution)/shard_map/ppermute | solution.py:346
  81.2 1.4 %collective-permute-start.21 = (f32[256,128]{1,0:T(8,128)S(1)}, f32[256,128]{1,0:T(8,128)S(1)}, u32[]{:S(2)}, u32[]{:S(2)}) collective-permute-start(f32[256,128]{1,0:T(8,128)S(1)} %add.32.own), channel_id=1, source_target_pairs={{0,1},{1,0},{2,3},{3,2},{4,5},{5,4},{6,7},{7,6},{8,9},{9,8},{10,11... | collective-permute-start | bytes 393224 | tf_op jit(solution)/shard_map/ppermute | solution.py:340

commit v7 on v6

--- a/solution.py
+++ b/solution.py
@@ -193,22 +193,24 @@
         below = range(p + 1, tiles)
         cols = [[lane(gram[t], at + c) for t in below] for c in range(tall)]
         ahead = [lane(gram[p + 1], at + tall + d) for d in range(tall)] if p + 1 < tiles else []
+        entry = {(d, c): spread(corner[c], d) for c in range(tall) for d in range(c, tall)}
         scales, tops, lows = [], [], []
         for c in range(tall):
-            scale = lax.rsqrt(spread(corner[c], c))
-            square = scale * scale
-            top = jnp.where(sub > c, corner[c], 0.0)
-            weights = [spread(corner[d], c) for d in range(c + 1, tall)]
+            scale = lax.rsqrt(entry[c, c])
+            weights = [entry[d, c] * scale for d in range(c + 1, tall)]
+            for e in range(c + 1, tall):
+                for d in range(e, tall):
+                    entry[d, e] = entry[d, e] - weights[d - c - 1] * weights[e - c - 1]
+            top = jnp.where(sub > c, corner[c], 0.0) * scale
             for d in range(c + 1, tall):
-                corner[d] = corner[d] - (top * weights[d - c - 1]) * square
+                corner[d] = corner[d] - top * weights[d - c - 1]
             low = [x * scale for x in cols[c]]
             for d in range(c + 1, tall):
-                weight = weights[d - c - 1] * scale
-                cols[d] = [x - m * weight for x, m in zip(cols[d], low)]
+                cols[d] = [x - m * weights[d - c - 1] for x, m in zip(cols[d], low)]
             if low:
                 ahead = [x - low[0] * spread(low[0], d) for d, x in enumerate(ahead)]
             scales.append(scale)
-            tops.append(top * scale)
+            tops.append(top)
             lows.append(low)
         for c in range(tall):
             row_gram = spread(gram[p], c) * scales[c]

time: 92 us -> 92.6 us (level)
  no operation moved by 1% of the time
where the time goes in v7:
time: 92.6 us; the launch traced here: 92.1 us
  starting transfers between devices  33.6 us (36%)
  Pallas kernels  30.9 us (33%)
  waiting for transfers between devices  19 us (21%)
  local copies, waits for them, and re-layouts  6.87 us (7%)
    pallas_call x4, Pallas kernels, column(): pl.pallas_call(functools.partial(column_kernel, place, first, scale), in_...  18.5 us
    all_to_all x2, starting transfers between devices, exchange(): return lax.all_to_all(x, 'trans', 0, 0, tiled=True)  12.2 us
    ppermute x3, starting transfers between devices, local(): near_edge = lax.ppermute(near_layer, 'trans', near)  11.2 us
    ppermute x3, waiting for transfers between devices, double(): other = lax.ppermute(x, 'trans', [(i, i ^ reach) for i in range(count)])  5.88 us
    unnamed x14, local copies, waits for them, and re-layouts  5.19 us
    pallas_call x3, Pallas kernels, step(): pl.pallas_call(functools.partial(step_kernel, before is None, last, cols....  5.05 us
    ppermute x13, waiting for transfers between devices, swap(): return lax.ppermute(x, 'cross', [(0, 1), (1, 0)])  5.01 us
    ppermute x3, starting transfers between devices, double(): other = lax.ppermute(x, 'trans', [(i, i ^ reach) for i in range(count)])  4.8 us
  transfers between devices with their start and end apart: 24, of which 13 were waited for; matrix products, arithmetic and copies ran while one was open for 2% of the time, Pallas kernels for 20%

profile of v7, /device:TPU:0, one launch (start us, length us, event | category | flops | bytes accessed | tf_op | source)
XLA Modules:
  0.0 92.1 jit_solution(9031314460463228950)
XLA Ops:
  0.6 0.5 collective-permute-start.2
  1.1 1.0 %constant_dynamic-slice_fusion = (f32[1,4,64,128]{3,2,1,0:T(8,128)S(1)}, f32[1,4,64,128]{3,2,1,0:T(8,128)S(1)}) fusion(f32[4,4,64,128]{3,2,1,0:T(8,128)} %refs_0_.5, s32[]{:T(128)S(6)} %select_n.15, s32[]{:T(128)S(6)} %select_n.14), kind=kLoop, calls=%fused_computation.1 | loop fusion | bytes 524296 | tf_op jit(solution)/shard_map/dynamic_slice | solution.py:353
  2.1 2.6 %collective-permute-start.1 = (f32[1,4,64,128]{3,2,1,0:T(8,128)S(1)}, f32[1,4,64,128]{3,2,1,0:T(8,128)S(1)}, u32[]{:S(2)}, u32[]{:S(2)}) collective-permute-start(f32[1,4,64,128]{3,2,1,0:T(8,128)S(1)} %get-tuple-element.56), channel_id=1, source_target_pairs={{0,2},{2,0},{4,6},{6,4},{8,10},{10,8},{12,14},{14,12},{1,3},{3,1},... | collective-permute-start | bytes 393224 | tf_op jit(solution)/shard_map/ppermute | solution.py:357
  4.7 0.7 collective-permute-start
  5.5 2.0 %copy-done.1 = f32[4,4,7,64,64]{4,3,2,1,0:T(8,128)S(1)} copy-done((f32[4,4,7,64,64]{4,3,2,1,0:T(8,128)S(1)}, f32[4,4,7,64,64]{4,3,2,1,0:T(8,128)}, u32[]{:S(2)}) %copy-start.1) | copy-done | bytes 1835032
  7.5 0.9 copy-done.2
  8.4 0.7 copy-done.4
  9.1 1.1 %pack.1.packed = bf16[16,128,512]{2,1,0:T(8,128)(2,1)S(1)} custom-call(s32[4]{0:T(128)S(1)} %pad_add_fusion.info, s32[4]{0:T(128)S(1)} %copy-done.4, f32[4,4,7,64,64]{4,3,2,1,0:T(8,128)S(1)} %copy-done.1, f32[4,64,64]{2,1,0:T(8,128)S(1)} %copy-done.2), custom_call_target="tpu_custom_call" | custom-call | flops 2875000064 | tf_op jit(solution)/shard_map/pack/pallas_call | solution.py:53
  10.2 0.2 collective-permute-start.3
  10.5 0.3 collective-permute-start.4
  10.8 0.8 collective-permute-done.3.refs_1_
  11.8 1.7 %step.3 = (f32[4,4,64,128]{3,2,1,0:T(8,128)S(1)}, f32[1,4,64,128]{3,2,1,0:T(8,128)S(1)}, f32[1,4,64,128]{3,2,1,0:T(8,128)S(1)}) custom-call(s32[4]{0:T(128)S(1)} %pad_add_fusion.info, s32[4,4,7]{2,1,0:T(4,128)S(1)} %copy-done.3, bf16[16,128,512]{2,1,0:T(8,128)(2,1)S(1)} %pack.1.packed, f32[4,4,64,128]{3,2,1,0:T(8,128)S(1)} %copy-done, ...), custom_call_target="tpu_custom_call" | custom-call | flops 1955000064 | tf_op jit(solution)/shard_map/step/pallas_call | solution.py:114
  13.5 0.4 collective-permute-start.5
  13.9 4.3 %collective-permute-start.6 = (f32[1,4,64,128]{3,2,1,0:T(8,128)S(1)}, f32[1,4,64,128]{3,2,1,0:T(8,128)S(1)}, u32[]{:S(2)}, u32[]{:S(2)}) collective-permute-start(f32[1,4,64,128]{3,2,1,0:T(8,128)S(1)} %get-tuple-element.33), channel_id=1, source_target_pairs={{0,2},{2,0},{4,6},{6,4},{8,10},{10,8},{12,14},{14,12},{1,3},{3,1},... | collective-permute-start | bytes 393224 | tf_op jit(solution)/shard_map/ppermute | solution.py:357
  18.2 0.7 collective-permute-start.8
  18.8 3.2 %collective-permute-done.6.refs_0_ = f32[1,4,64,128]{3,2,1,0:T(8,128)S(1)} collective-permute-done((f32[1,4,64,128]{3,2,1,0:T(8,128)S(1)}, f32[1,4,64,128]{3,2,1,0:T(8,128)S(1)}, u32[]{:S(2)}, u32[]{:S(2)}) %collective-permute-start.6) | collective-permute-done | bytes 131104 | tf_op jit(solution)/shard_map/ppermute | solution.py:357
  22.0 0.5 collective-permute-start.9
  22.5 0.8 collective-permute-done.7.refs_1_
  23.6 1.7 %step.4 = (f32[4,4,64,128]{3,2,1,0:T(8,128)S(1)}, f32[1,4,64,128]{3,2,1,0:T(8,128)S(1)}, f32[1,4,64,128]{3,2,1,0:T(8,128)S(1)}) custom-call(s32[4]{0:T(128)S(1)} %pad_add_fusion.info, s32[4,4,7]{2,1,0:T(4,128)S(1)} %copy-done.3, bf16[16,128,512]{2,1,0:T(8,128)(2,1)S(1)} %pack.1.packed, f32[4,4,64,128]{3,2,1,0:T(8,128)S(1)} %get-tuple-element.32.own.refs_4_.refs_1_, ...), custom_call_target="tpu_custom_call" | custom-call | flops 1955000064 | tf_op jit(solution)/shard_map/step/pallas_call | solution.py:114
  25.3 0.4 collective-permute-start.10
  25.7 4.3 %collective-permute-start.11 = (f32[1,4,64,128]{3,2,1,0:T(8,128)S(1)}, f32[1,4,64,128]{3,2,1,0:T(8,128)S(1)}, u32[]{:S(2)}, u32[]{:S(2)}) collective-permute-start(f32[1,4,64,128]{3,2,1,0:T(8,128)S(1)} %get-tuple-element.36), channel_id=1, source_target_pairs={{0,2},{2,0},{4,6},{6,4},{8,10},{10,8},{12,14},{14,12},{1,3},{3,1},... | collective-permute-start | bytes 393224 | tf_op jit(solution)/shard_map/ppermute | solution.py:357
  30.0 0.7 collective-permute-start.13
  30.6 1.6 %gram.3 = (f32[384,128]{1,0:T(8,128)S(1)}, f32[384,128]{1,0:T(8,128)S(1)}) custom-call(s32[4]{0:T(128)S(1)} %pad_add_fusion.info, f32[4,4,64,128]{3,2,1,0:T(8,128)S(1)} %copy-done, f32[4,4,64,128]{3,2,1,0:T(8,128)S(1)} %get-tuple-element.32.own.refs_4_.refs_1_, f32[4,4,64,128]{3,2,1,0:T(8,128)S(1)} %get-tuple-element.35.own.refs_2_), custom_call_target="tpu_custom_call" | custom-call | flops 1610000000 | tf_op jit(solution)/shard_map/gram/pallas_call | solution.py:156
  32.4 1.6 %collective-permute-done.11.refs_0_ = f32[1,4,64,128]{3,2,1,0:T(8,128)S(1)} collective-permute-done((f32[1,4,64,128]{3,2,1,0:T(8,128)S(1)}, f32[1,4,64,128]{3,2,1,0:T(8,128)S(1)}, u32[]{:S(2)}, u32[]{:S(2)}) %collective-permute-start.11) | collective-permute-done | bytes 131104 | tf_op jit(solution)/shard_map/ppermute | solution.py:357
  34.0 0.5 collective-permute-start.14
  34.5 0.7 add.29
  35.2 8.7 %all-to-all-start = ((f32[8,48,128]{2,1,0:T(8,128)}), f32[8,48,128]{2,1,0:T(8,128)S(1)}, u32[]{:S(2)}, u32[]{:S(2)}) async-start(f32[8,48,128]{2,1,0:T(8,128)} %bitcast.4), calls=%async_computation | async-start | bytes 393216 | tf_op jit(solution)/shard_map/all_to_all | solution.py:345
  43.9 1.6 %copy-done.6 = bf16[16,128,512]{2,1,0:T(8,128)(2,1)S(1)} copy-done((bf16[16,128,512]{2,1,0:T(8,128)(2,1)S(1)}, bf16[16,128,512]{2,1,0:T(8,128)(2,1)}, u32[]{:S(2)}) %copy-start.6) | copy-done | bytes 2097176
  45.5 1.7 %step.5.refs_3_ = f32[4,4,64,128]{3,2,1,0:T(8,128)S(1)} custom-call(s32[4]{0:T(128)S(1)} %pad_add_fusion.info, s32[4,4,7]{2,1,0:T(4,128)S(1)} %copy-done.3, bf16[16,128,512]{2,1,0:T(8,128)(2,1)S(1)} %copy-done.6, f32[4,4,64,128]{3,2,1,0:T(8,128)S(1)} %get-tuple-element.35.own.refs_2_, f32[4,4,64,128]{3,2,1,0:T(8,128)S(1)} %collective-permute-done.10.other, ...), custom_call_target="tpu_custom_call" | custom-call | flops 1955000064 | tf_op jit(solution)/shard_map/step/pallas_call | solution.py:114
  47.2 1.4 %gram.2 = (f32[256,128]{1,0:T(8,128)S(1)}, f32[256,128]{1,0:T(8,128)S(1)}) custom-call(s32[4]{0:T(128)S(1)} %pad_add_fusion.info, f32[4,4,64,128]{3,2,1,0:T(8,128)S(1)} %copy-done, f32[4,4,64,128]{3,2,1,0:T(8,128)S(1)} %get-tuple-element.32.own.refs_4_.refs_1_, f32[4,4,64,128]{3,2,1,0:T(8,128)S(1)} %get-tuple-element.35.own.refs_2_, ...), custom_call_target="tpu_custom_call" | custom-call | flops 1610000000 | tf_op jit(solution)/shard_map/gram/pallas_call | solution.py:156
  48.6 0.3 collective-permute-start.15
  48.9 1.1 %collective-permute-done.15 = f32[256,128]{1,0:T(8,128)S(1)} collective-permute-done((f32[256,128]{1,0:T(8,128)S(1)}, f32[256,128]{1,0:T(8,128)S(1)}, u32[]{:S(2)}, u32[]{:S(2)}) %collective-permute-start.15) | collective-permute-done | bytes 131104 | tf_op jit(solution)/shard_map/ppermute | solution.py:342
  50.0 2.4 %all-to-all-done = f32[8,48,128]{2,1,0:T(8,128)S(1)} async-done(((f32[8,48,128]{2,1,0:T(8,128)}), f32[8,48,128]{2,1,0:T(8,128)S(1)}, u32[]{:S(2)}, u32[]{:S(2)}) %all-to-all-start) | async-done | bytes 196640 | tf_op jit(solution)/shard_map/all_to_all | solution.py:345
  52.5 0.7 broadcast_in_dim.2
  53.2 3.6 %all-to-all-start.1 = ((f32[8,48,128]{2,1,0:T(8,128)}), f32[8,48,128]{2,1,0:T(8,128)S(1)}, u32[]{:S(2)}, u32[]{:S(2)}) async-start(f32[8,48,128]{2,1,0:T(8,128)} %broadcast_in_dim.2), calls=%async_computation.1 | async-start | bytes 393216 | tf_op jit(solution)/shard_map/all_to_all | solution.py:345
  56.8 2.0 %collective-permute-start.17 = (f32[256,128]{1,0:T(8,128)S(1)}, f32[256,128]{1,0:T(8,128)S(1)}, u32[]{:S(2)}, u32[]{:S(2)}) collective-permute-start(f32[256,128]{1,0:T(8,128)S(1)} %add.28), channel_id=1, source_target_pairs={{0,2},{2,0},{4,6},{6,4},{8,10},{10,8},{12,14},{14,12},{1,3},{3,1},... | collective-permute-start | bytes 393224 | tf_op jit(solution)/shard_map/ppermute | solution.py:348
  58.8 5.3 %collective-permute-done.17 = f32[256,128]{1,0:T(8,128)S(1)} collective-permute-done((f32[256,128]{1,0:T(8,128)S(1)}, f32[256,128]{1,0:T(8,128)S(1)}, u32[]{:S(2)}, u32[]{:S(2)}) %collective-permute-start.17) | collective-permute-done | bytes 131104 | tf_op jit(solution)/shard_map/ppermute | solution.py:348
  64.1 0.9 %all-to-all-done.1 = f32[8,48,128]{2,1,0:T(8,128)S(1)} async-done(((f32[8,48,128]{2,1,0:T(8,128)}), f32[8,48,128]{2,1,0:T(8,128)S(1)}, u32[]{:S(2)}, u32[]{:S(2)}) %all-to-all-start.1) | async-done | bytes 196640 | tf_op jit(solution)/shard_map/all_to_all | solution.py:345
  65.0 0.9 %collective-permute-start.18 = (f32[256,128]{1,0:T(8,128)S(1)}, f32[256,128]{1,0:T(8,128)S(1)}, u32[]{:S(2)}, u32[]{:S(2)}) collective-permute-start(f32[256,128]{1,0:T(8,128)S(1)} %add.30), channel_id=1, source_target_pairs={{0,4},{2,6},{4,0},{6,2},{8,12},{10,14},{12,8},{14,10},{1,5},{3,7},... | collective-permute-start | bytes 393224 | tf_op jit(solution)/shard_map/ppermute | solution.py:348
  66.0 0.5 collective-permute-done.19.other
  66.5 3.9 %column.4 = (f32[128,128]{1,0:T(8,128)S(1)}, f32[128,128]{1,0:T(8,128)S(1)}) custom-call(s32[4]{0:T(128)S(1)} %pad_add_fusion.info, f32[384,128]{1,0:T(8,128)S(1)} %bitcast.7, f32[384,128]{1,0:T(8,128)S(1)} %collective-permute-done.19.other), custom_call_target="tpu_custom_call" | custom-call | flops 4600000000 | tf_op jit(solution)/shard_map/column/pallas_call | solution.py:271
  70.3 0.6 collective-permute-done.18
  70.9 1.8 %collective-permute-start.20 = (f32[256,128]{1,0:T(8,128)S(1)}, f32[256,128]{1,0:T(8,128)S(1)}, u32[]{:S(2)}, u32[]{:S(2)}) collective-permute-start(f32[256,128]{1,0:T(8,128)S(1)} %add.31), channel_id=1, source_target_pairs={{0,8},{2,10},{4,12},{6,14},{8,0},{10,2},{12,4},{14,6},{1,9},{3,11}... | collective-permute-start | bytes 393224 | tf_op jit(solution)/shard_map/ppermute | solution.py:348
  72.8 4.3 %column.5 = (f32[256,256]{1,0:T(8,128)S(1)}, f32[256,256]{1,0:T(8,128)S(1)}) custom-call(s32[4]{0:T(128)S(1)} %pad_add_fusion.info, f32[384,128]{1,0:T(8,128)S(1)} %bitcast.8, f32[384,128]{1,0:T(8,128)S(1)} %collective-permute-done.19.other, f32[128,128]{1,0:T(8,128)S(1)} %get-tuple-element.47.refs_0_, f32[128,128]{1,0:T(8,128)S(1)} %get-tuple-element.46.refs_1_), custom_call_target="tpu_custom_call" | custom-call | flops 4600000000 | tf_op jit(solution)/shard_map/column/pallas_call | solution.py:271
  77.1 4.4 %column.6 = (f32[384,384]{1,0:T(8,128)S(1)}, f32[384,384]{1,0:T(8,128)S(1)}) custom-call(s32[4]{0:T(128)S(1)} %pad_add_fusion.info, f32[384,128]{1,0:T(8,128)S(1)} %bitcast.9, f32[384,128]{1,0:T(8,128)S(1)} %collective-permute-done.19.other, f32[256,256]{1,0:T(8,128)S(1)} %get-tuple-element.49.refs_0_, f32[256,256]{1,0:T(8,128)S(1)} %get-tuple-element.50.refs_1_), custom_call_target="tpu_custom_call" | custom-call | flops 4600000000 | tf_op jit(solution)/shard_map/column/pallas_call | solution.py:271
  81.7 1.3 %collective-permute-done.21.other = f32[256,128]{1,0:T(8,128)S(1)} collective-permute-done((f32[256,128]{1,0:T(8,128)S(1)}, f32[256,128]{1,0:T(8,128)S(1)}, u32[]{:S(2)}, u32[]{:S(2)}) %collective-permute-start.21) | collective-permute-done | bytes 131104 | tf_op jit(solution)/shard_map/ppermute | solution.py:342
  83.0 5.9 %column.7 = (f32[512,512]{1,0:T(8,128)}, f32[512,512]{1,0:T(8,128)S(1)}) custom-call(s32[4]{0:T(128)S(1)} %pad_add_fusion.info, f32[256,128]{1,0:T(8,128)S(1)} %add.32.own, f32[256,128]{1,0:T(8,128)S(1)} %collective-permute-done.21.other, f32[384,384]{1,0:T(8,128)S(1)} %get-tuple-element.52.refs_0_, f32[384,384]{1,0:T(8,128)S(1)} %get-tuple-element.51.refs_1_), custom_call_target="tpu_custom_call" | custom-call | flops 4600000000 | tf_op jit(solution)/shard_map/column/pallas_call | solution.py:271
  88.9 3.2 %basis.1 = bf16[4,4,64,512]{3,2,1,0:T(8,128)(2,1)} custom-call(f32[4,4,64,128]{3,2,1,0:T(8,128)S(1)} %copy-done, f32[4,4,64,128]{3,2,1,0:T(8,128)S(1)} %get-tuple-element.32.own.refs_4_.refs_1_, f32[4,4,64,128]{3,2,1,0:T(8,128)S(1)} %get-tuple-element.35.own.refs_2_, f32[4,4,64,128]{3,2,1,0:T(8,128)S(1)} %step.5.refs_3_, ...), custom_call_target="tpu_custom_call" | custom-call | flops 3449999872 | tf_op jit(solution)/shard_map/basis/pallas_call | solution.py:313
  (34 shorter events, 0.8 us)
Async XLA Ops:
  0.6 11.2 %collective-permute-start.2 = (f32[4,4,64,128]{3,2,1,0:T(8,128)}, f32[4,4,64,128]{3,2,1,0:T(8,128)S(1)}, u32[]{:S(2)}, u32[]{:S(2)}) collective-permute-start(f32[4,4,64,128]{3,2,1,0:T(8,128)} %refs_0_.5), channel_id=1, source_target_pairs={{0,1},{1,0},{2,3},{3,2},{4,5},{5,4},{6,7},{7,6},{8,9},{9,8},{10,11... | collective-permute-start | bytes 1572872 | tf_op jit(solution)/shard_map/ppermute | solution.py:342
  2.1 8.1 %collective-permute-start.1 = (f32[1,4,64,128]{3,2,1,0:T(8,128)S(1)}, f32[1,4,64,128]{3,2,1,0:T(8,128)S(1)}, u32[]{:S(2)}, u32[]{:S(2)}) collective-permute-start(f32[1,4,64,128]{3,2,1,0:T(8,128)S(1)} %get-tuple-element.56), channel_id=1, source_target_pairs={{0,2},{2,0},{4,6},{6,4},{8,10},{10,8},{12,14},{14,12},{1,3},{3,1},... | collective-permute-start | bytes 393224 | tf_op jit(solution)/shard_map/ppermute | solution.py:357
  4.7 5.5 %collective-permute-start = (f32[1,4,64,128]{3,2,1,0:T(8,128)S(1)}, f32[1,4,64,128]{3,2,1,0:T(8,128)S(1)}, u32[]{:S(2)}, u32[]{:S(2)}) collective-permute-start(f32[1,4,64,128]{3,2,1,0:T(8,128)S(1)} %get-tuple-element.57), channel_id=1, source_target_pairs={{2,4},{4,2},{6,8},{8,6},{10,12},{12,10},{3,5},{5,3},{7,9},{9,7},{1... | collective-permute-start | bytes 393224 | tf_op jit(solution)/shard_map/ppermute | solution.py:358
  5.5 2.0 %copy-start.1 = (f32[4,4,7,64,64]{4,3,2,1,0:T(8,128)S(1)}, f32[4,4,7,64,64]{4,3,2,1,0:T(8,128)}, u32[]{:S(2)}) copy-start(f32[4,4,7,64,64]{4,3,2,1,0:T(8,128)} %held.1) | copy-start | bytes 5505028
  7.5 0.9 copy-start.2
  8.4 0.7 copy-start.4
  9.1 2.7 %copy-start = (f32[4,4,64,128]{3,2,1,0:T(8,128)S(1)}, f32[4,4,64,128]{3,2,1,0:T(8,128)}, u32[]{:S(2)}) copy-start(f32[4,4,64,128]{3,2,1,0:T(8,128)} %refs_0_.5) | copy-start | bytes 1572868
  9.1 2.7 %copy-start.3 = (s32[4,4,7]{2,1,0:T(4,128)S(1)}, s32[4,4,7]{2,1,0:T(4,128)}, u32[]{:S(2)}) copy-start(s32[4,4,7]{2,1,0:T(4,128)} %cols.5) | copy-start | bytes 1348
  10.2 15.1 %copy-start.5 = (bf16[16,128,512]{2,1,0:T(8,128)(2,1)}, bf16[16,128,512]{2,1,0:T(8,128)(2,1)S(1)}, u32[]{:S(2)}) copy-start(bf16[16,128,512]{2,1,0:T(8,128)(2,1)S(1)} %pack.1.packed) | copy-start | bytes 6291460
  10.2 1.4 %collective-permute-start.3 = (f32[1,4,64,128]{3,2,1,0:T(8,128)S(1)}, f32[1,4,64,128]{3,2,1,0:T(8,128)S(1)}, u32[]{:S(2)}, u32[]{:S(2)}) collective-permute-start(f32[1,4,64,128]{3,2,1,0:T(8,128)S(1)} %collective-permute-done.1.refs_0_), channel_id=1, source_target_pairs={{0,1},{1,0},{2,3},{3,2},{4,5},{5,4},{6,7},{7,6},{8,9},{9,8},{10,11... | collective-permute-start | bytes 393224 | tf_op jit(solution)/shard_map/ppermute | solution.py:342
  10.5 1.4 %collective-permute-start.4 = (f32[1,4,64,128]{3,2,1,0:T(8,128)S(1)}, f32[1,4,64,128]{3,2,1,0:T(8,128)S(1)}, u32[]{:S(2)}, u32[]{:S(2)}) collective-permute-start(f32[1,4,64,128]{3,2,1,0:T(8,128)S(1)} %collective-permute-done.refs_2_), channel_id=1, source_target_pairs={{0,1},{1,0},{2,3},{3,2},{4,5},{5,4},{6,7},{7,6},{8,9},{9,8},{10,11... | collective-permute-start | bytes 393224 | tf_op jit(solution)/shard_map/ppermute | solution.py:342
  13.5 10.1 %collective-permute-start.5 = (f32[4,4,64,128]{3,2,1,0:T(8,128)S(1)}, f32[4,4,64,128]{3,2,1,0:T(8,128)S(1)}, u32[]{:S(2)}, u32[]{:S(2)}) collective-permute-start(f32[4,4,64,128]{3,2,1,0:T(8,128)S(1)} %get-tuple-element.32.own.refs_4_.refs_1_), channel_id=1, source_target_pairs={{0,1},{1,0},{2,3},{3,2},{4,5},{5,4},{6,7},{7,6},{8,9},{9,8},{10,11... | collective-permute-start | bytes 1572872 | tf_op jit(solution)/shard_map/ppermute | solution.py:342
  13.9 8.1 %collective-permute-start.6 = (f32[1,4,64,128]{3,2,1,0:T(8,128)S(1)}, f32[1,4,64,128]{3,2,1,0:T(8,128)S(1)}, u32[]{:S(2)}, u32[]{:S(2)}) collective-permute-start(f32[1,4,64,128]{3,2,1,0:T(8,128)S(1)} %get-tuple-element.33), channel_id=1, source_target_pairs={{0,2},{2,0},{4,6},{6,4},{8,10},{10,8},{12,14},{14,12},{1,3},{3,1},... | collective-permute-start | bytes 393224 | tf_op jit(solution)/shard_map/ppermute | solution.py:357
  18.2 3.9 %collective-permute-start.8 = (f32[1,4,64,128]{3,2,1,0:T(8,128)S(1)}, f32[1,4,64,128]{3,2,1,0:T(8,128)S(1)}, u32[]{:S(2)}, u32[]{:S(2)}) collective-permute-start(f32[1,4,64,128]{3,2,1,0:T(8,128)S(1)} %get-tuple-element.34), channel_id=1, source_target_pairs={{2,4},{4,2},{6,8},{8,6},{10,12},{12,10},{3,5},{5,3},{7,9},{9,7},{1... | collective-permute-start | bytes 393224 | tf_op jit(solution)/shard_map/ppermute | solution.py:358
  22.0 1.3 %collective-permute-start.7 = (f32[1,4,64,128]{3,2,1,0:T(8,128)S(1)}, f32[1,4,64,128]{3,2,1,0:T(8,128)S(1)}, u32[]{:S(2)}, u32[]{:S(2)}) collective-permute-start(f32[1,4,64,128]{3,2,1,0:T(8,128)S(1)} %collective-permute-done.6.refs_0_), channel_id=1, source_target_pairs={{0,1},{1,0},{2,3},{3,2},{4,5},{5,4},{6,7},{7,6},{8,9},{9,8},{10,11... | collective-permute-start | bytes 393224 | tf_op jit(solution)/shard_map/ppermute | solution.py:342
  22.0 1.5 %collective-permute-start.9 = (f32[1,4,64,128]{3,2,1,0:T(8,128)S(1)}, f32[1,4,64,128]{3,2,1,0:T(8,128)S(1)}, u32[]{:S(2)}, u32[]{:S(2)}) collective-permute-start(f32[1,4,64,128]{3,2,1,0:T(8,128)S(1)} %collective-permute-done.8.refs_2_), channel_id=1, source_target_pairs={{0,1},{1,0},{2,3},{3,2},{4,5},{5,4},{6,7},{7,6},{8,9},{9,8},{10,11... | collective-permute-start | bytes 393224 | tf_op jit(solution)/shard_map/ppermute | solution.py:342
  25.3 18.6 %collective-permute-start.10 = (f32[4,4,64,128]{3,2,1,0:T(8,128)S(1)}, f32[4,4,64,128]{3,2,1,0:T(8,128)S(1)}, u32[]{:S(2)}, u32[]{:S(2)}) collective-permute-start(f32[4,4,64,128]{3,2,1,0:T(8,128)S(1)} %get-tuple-element.35.own.refs_2_), channel_id=1, source_target_pairs={{0,1},{1,0},{2,3},{3,2},{4,5},{5,4},{6,7},{7,6},{8,9},{9,8},{10,11... | collective-permute-start | bytes 1572872 | tf_op jit(solution)/shard_map/ppermute | solution.py:342
  25.7 8.3 %collective-permute-start.11 = (f32[1,4,64,128]{3,2,1,0:T(8,128)S(1)}, f32[1,4,64,128]{3,2,1,0:T(8,128)S(1)}, u32[]{:S(2)}, u32[]{:S(2)}) collective-permute-start(f32[1,4,64,128]{3,2,1,0:T(8,128)S(1)} %get-tuple-element.36), channel_id=1, source_target_pairs={{0,2},{2,0},{4,6},{6,4},{8,10},{10,8},{12,14},{14,12},{1,3},{3,1},... | collective-permute-start | bytes 393224 | tf_op jit(solution)/shard_map/ppermute | solution.py:357
  30.0 4.0 %collective-permute-start.13 = (f32[1,4,64,128]{3,2,1,0:T(8,128)S(1)}, f32[1,4,64,128]{3,2,1,0:T(8,128)S(1)}, u32[]{:S(2)}, u32[]{:S(2)}) collective-permute-start(f32[1,4,64,128]{3,2,1,0:T(8,128)S(1)} %get-tuple-element.37), channel_id=1, source_target_pairs={{2,4},{4,2},{6,8},{8,6},{10,12},{12,10},{3,5},{5,3},{7,9},{9,7},{1... | collective-permute-start | bytes 393224 | tf_op jit(solution)/shard_map/ppermute | solution.py:358
  32.3 2.2 %collective-permute-start.16 = (f32[384,128]{1,0:T(8,128)S(1)}, f32[384,128]{1,0:T(8,128)S(1)}, u32[]{:S(2)}, u32[]{:S(2)}) collective-permute-start(f32[384,128]{1,0:T(8,128)S(1)} %get-tuple-element.41), channel_id=1, source_target_pairs={{0,1},{1,0},{2,3},{3,2},{4,5},{5,4},{6,7},{7,6},{8,9},{9,8},{10,11... | collective-permute-start | bytes 589832 | tf_op jit(solution)/shard_map/ppermute | solution.py:342
  34.0 9.9 %collective-permute-start.12 = (f32[1,4,64,128]{3,2,1,0:T(8,128)S(1)}, f32[1,4,64,128]{3,2,1,0:T(8,128)S(1)}, u32[]{:S(2)}, u32[]{:S(2)}) collective-permute-start(f32[1,4,64,128]{3,2,1,0:T(8,128)S(1)} %collective-permute-done.11.refs_0_), channel_id=1, source_target_pairs={{0,1},{1,0},{2,3},{3,2},{4,5},{5,4},{6,7},{7,6},{8,9},{9,8},{10,11... | collective-permute-start | bytes 393224 | tf_op jit(solution)/shard_map/ppermute | solution.py:342
  34.0 9.9 %collective-permute-start.14 = (f32[1,4,64,128]{3,2,1,0:T(8,128)S(1)}, f32[1,4,64,128]{3,2,1,0:T(8,128)S(1)}, u32[]{:S(2)}, u32[]{:S(2)}) collective-permute-start(f32[1,4,64,128]{3,2,1,0:T(8,128)S(1)} %collective-permute-done.13.refs_2_), channel_id=1, source_target_pairs={{0,1},{1,0},{2,3},{3,2},{4,5},{5,4},{6,7},{7,6},{8,9},{9,8},{10,11... | collective-permute-start | bytes 393224 | tf_op jit(solution)/shard_map/ppermute | solution.py:342
  35.2 17.3 %all-to-all-start = ((f32[8,48,128]{2,1,0:T(8,128)}), f32[8,48,128]{2,1,0:T(8,128)S(1)}, u32[]{:S(2)}, u32[]{:S(2)}) async-start(f32[8,48,128]{2,1,0:T(8,128)} %bitcast.4), calls=%async_computation | async-start | bytes 393216 | tf_op jit(solution)/shard_map/all_to_all | solution.py:345
  43.9 1.6 %copy-start.6 = (bf16[16,128,512]{2,1,0:T(8,128)(2,1)S(1)}, bf16[16,128,512]{2,1,0:T(8,128)(2,1)}, u32[]{:S(2)}) copy-start(bf16[16,128,512]{2,1,0:T(8,128)(2,1)} %copy-done.5) | copy-start | bytes 6291460
  48.6 1.4 %collective-permute-start.15 = (f32[256,128]{1,0:T(8,128)S(1)}, f32[256,128]{1,0:T(8,128)S(1)}, u32[]{:S(2)}, u32[]{:S(2)}) collective-permute-start(f32[256,128]{1,0:T(8,128)S(1)} %get-tuple-element.39), channel_id=1, source_target_pairs={{0,1},{1,0},{2,3},{3,2},{4,5},{5,4},{6,7},{7,6},{8,9},{9,8},{10,11... | collective-permute-start | bytes 393224 | tf_op jit(solution)/shard_map/ppermute | solution.py:342
  53.2 11.8 %all-to-all-start.1 = ((f32[8,48,128]{2,1,0:T(8,128)}), f32[8,48,128]{2,1,0:T(8,128)S(1)}, u32[]{:S(2)}, u32[]{:S(2)}) async-start(f32[8,48,128]{2,1,0:T(8,128)} %broadcast_in_dim.2), calls=%async_computation.1 | async-start | bytes 393216 | tf_op jit(solution)/shard_map/all_to_all | solution.py:345
  56.8 7.3 %collective-permute-start.17 = (f32[256,128]{1,0:T(8,128)S(1)}, f32[256,128]{1,0:T(8,128)S(1)}, u32[]{:S(2)}, u32[]{:S(2)}) collective-permute-start(f32[256,128]{1,0:T(8,128)S(1)} %add.28), channel_id=1, source_target_pairs={{0,2},{2,0},{4,6},{6,4},{8,10},{10,8},{12,14},{14,12},{1,3},{3,1},... | collective-permute-start | bytes 393224 | tf_op jit(solution)/shard_map/ppermute | solution.py:348
  65.0 1.4 %collective-permute-start.19 = (f32[384,128]{1,0:T(8,128)S(1)}, f32[384,128]{1,0:T(8,128)S(1)}, u32[]{:S(2)}, u32[]{:S(2)}) collective-permute-start(f32[384,128]{1,0:T(8,128)S(1)} %bitcast.6), channel_id=1, source_target_pairs={{0,1},{1,0},{2,3},{3,2},{4,5},{5,4},{6,7},{7,6},{8,9},{9,8},{10,11... | collective-permute-start | bytes 589832 | tf_op jit(solution)/shard_map/ppermute | solution.py:342
  65.0 5.9 %collective-permute-start.18 = (f32[256,128]{1,0:T(8,128)S(1)}, f32[256,128]{1,0:T(8,128)S(1)}, u32[]{:S(2)}, u32[]{:S(2)}) collective-permute-start(f32[256,128]{1,0:T(8,128)S(1)} %add.30), channel_id=1, source_target_pairs={{0,4},{2,6},{4,0},{6,2},{8,12},{10,14},{12,8},{14,10},{1,5},{3,7},... | collective-permute-start | bytes 393224 | tf_op jit(solution)/shard_map/ppermute | solution.py:348
  70.9 10.6 %collective-permute-start.20 = (f32[256,128]{1,0:T(8,128)S(1)}, f32[256,128]{1,0:T(8,128)S(1)}, u32[]{:S(2)}, u32[]{:S(2)}) collective-permute-start(f32[256,128]{1,0:T(8,128)S(1)} %add.31), channel_id=1, source_target_pairs={{0,8},{2,10},{4,12},{6,14},{8,0},{10,2},{12,4},{14,6},{1,9},{3,11}... | collective-permute-start | bytes 393224 | tf_op jit(solution)/shard_map/ppermute | solution.py:348
  81.6 1.4 %collective-permute-start.21 = (f32[256,128]{1,0:T(8,128)S(1)}, f32[256,128]{1,0:T(8,128)S(1)}, u32[]{:S(2)}, u32[]{:S(2)}) collective-permute-start(f32[256,128]{1,0:T(8,128)S(1)} %add.32.own), channel_id=1, source_target_pairs={{0,1},{1,0},{2,3},{3,2},{4,5},{5,4},{6,7},{7,6},{8,9},{9,8},{10,11... | collective-permute-start | bytes 393224 | tf_op jit(solution)/shard_map/ppermute | solution.py:342

commit v8 on v6

--- a/solution.py
+++ b/solution.py
@@ -178,8 +178,8 @@
     tiles = size // tall
     lanes = lax.broadcasted_iota(jnp.int32, (tall, size), 1)
     sub = lax.broadcasted_iota(jnp.int32, (tall, size), 0)
-    gram = [block[tall * t : tall * (t + 1)] for t in range(tiles)]
-    unit = [jnp.where(lanes == sub + tall * t, 1.0, 0.0) for t in range(tiles)]
+    work = [block[tall * t : tall * (t + 1)] for t in range(tiles)]
+    uppers, inverses = [], []
 
     def spread(x, row):
         return jnp.broadcast_to(x[row : row + 1], (tall, size))
@@ -187,40 +187,44 @@
     def lane(x, at):
         return jnp.broadcast_to(x[:, at : at + 1], (tall, size))
 
-    corner = [lane(gram[0], c) for c in range(tall)]
+    corner = [lane(work[0], c) for c in range(tall)]
     for p in range(tiles):
         at = tall * p
         below = range(p + 1, tiles)
-        cols = [[lane(gram[t], at + c) for t in below] for c in range(tall)]
-        ahead = [lane(gram[p + 1], at + tall + d) for d in range(tall)] if p + 1 < tiles else []
+        cols = [[lane(work[t], at + c) for t in below] for c in range(tall)]
+        ahead = [lane(work[p + 1], at + tall + d) for d in range(tall)] if p + 1 < tiles else []
+        passed = lanes < at + tall
+        upper = work[p]
+        inverse = jnp.where(lanes == sub + at, 1.0, jnp.where(lanes < at, work[p], 0.0))
+        for t in below:
+            work[t] = jnp.where(passed & (lanes >= at), 0.0, work[t])
         scales, tops, lows = [], [], []
         for c in range(tall):
             scale = lax.rsqrt(spread(corner[c], c))
-            square = scale * scale
-            top = jnp.where(sub > c, corner[c], 0.0)
-            weights = [spread(corner[d], c) for d in range(c + 1, tall)]
-            for d in range(c + 1, tall):
-                corner[d] = corner[d] - (top * weights[d - c - 1]) * square
+            weights = [spread(corner[d], c) * scale for d in range(c + 1, tall)]
+            top = jnp.where(sub > c, corner[c], 0.0) * scale
             low = [x * scale for x in cols[c]]
             for d in range(c + 1, tall):
-                weight = weights[d - c - 1] * scale
+                weight = weights[d - c - 1]
+                corner[d] = corner[d] - top * weight
                 cols[d] = [x - m * weight for x, m in zip(cols[d], low)]
             if low:
                 ahead = [x - low[0] * spread(low[0], d) for d, x in enumerate(ahead)]
             scales.append(scale)
-            tops.append(top * scale)
+            tops.append(top)
             lows.append(low)
         for c in range(tall):
-            row_gram = spread(gram[p], c) * scales[c]
-            row_unit = spread(unit[p], c) * scales[c]
-            gram[p] = jnp.where(sub == c, row_gram, gram[p] - tops[c] * row_gram)
-            unit[p] = jnp.where(sub == c, row_unit, unit[p] - tops[c] * row_unit)
+            row_upper = spread(upper, c) * scales[c]
+            row_inverse = spread(inverse, c) * scales[c]
+            upper = jnp.where(sub == c, row_upper, upper - tops[c] * row_upper)
+            inverse = jnp.where(sub == c, row_inverse, inverse - tops[c] * row_inverse)
+            row = jnp.where(passed, row_inverse, row_upper)
             for t, m in zip(below, lows[c]):
-                gram[t] = gram[t] - m * row_gram
-                unit[t] = unit[t] - m * row_unit
+                work[t] = work[t] - m * row
+        uppers.append(jnp.where(lanes >= sub + at, upper, 0.0))
+        inverses.append(inverse)
         corner = ahead
-    upper = [jnp.where(lanes >= sub + tall * t, gram[t], 0.0) for t in range(tiles)]
-    return jnp.concatenate(upper, axis=0), jnp.concatenate(unit, axis=0)
+    return jnp.concatenate(uppers, axis=0), jnp.concatenate(inverses, axis=0)
 
 
 def dot(a, b, right=0):

time: 92 us -> 90.8 us (0.987)
  Pallas kernels: 30.2 us -> 28.8 us
    pallas_call x4, Pallas kernels: 17.8 us -> 16.5 us  [column(): pl.pallas_call(functools.partial(column_kernel, place, first, scale), in_...]
  transfers between devices with their start and end apart: 24 -> 24, of which waited for: 13 -> 13; matrix products, arithmetic and copies ran while one was open for 2% -> 2% of each run, Pallas kernels for 20% -> 19%
where the time goes in v8:
time: 90.8 us; the launch traced here: 90.4 us
  starting transfers between devices  33.6 us (37%)
  Pallas kernels  28.8 us (32%)
  waiting for transfers between devices  19.4 us (21%)
  local copies, waits for them, and re-layouts  6.87 us (8%)
    pallas_call x4, Pallas kernels, column(): pl.pallas_call(functools.partial(column_kernel, place, first, scale), in_...  16.5 us
    all_to_all x2, starting transfers between devices, exchange(): return lax.all_to_all(x, 'trans', 0, 0, tiled=True)  12.2 us
    ppermute x3, starting transfers between devices, local(): near_edge = lax.ppermute(near_layer, 'trans', near)  11.2 us
    ppermute x3, waiting for transfers between devices, double(): other = lax.ppermute(x, 'trans', [(i, i ^ reach) for i in range(count)])  6.2 us
    unnamed x14, local copies, waits for them, and re-layouts  5.19 us
    pallas_call x3, Pallas kernels, step(): pl.pallas_call(functools.partial(step_kernel, before is None, last, cols....  5.05 us
    ppermute x13, waiting for transfers between devices, swap(): return lax.ppermute(x, 'cross', [(0, 1), (1, 0)])  5.01 us
    ppermute x3, starting transfers between devices, double(): other = lax.ppermute(x, 'trans', [(i, i ^ reach) for i in range(count)])  4.8 us
  transfers between devices with their start and end apart: 24, of which 13 were waited for; matrix products, arithmetic and copies ran while one was open for 2% of the time, Pallas kernels for 19%

profile of v8, /device:TPU:0, one launch (start us, length us, event | category | flops | bytes accessed | tf_op | source)
XLA Modules:
  0.0 90.4 jit_solution(13290927768307013325)
XLA Ops:
  0.6 0.5 collective-permute-start.2
  1.1 1.0 %constant_dynamic-slice_fusion = (f32[1,4,64,128]{3,2,1,0:T(8,128)S(1)}, f32[1,4,64,128]{3,2,1,0:T(8,128)S(1)}) fusion(f32[4,4,64,128]{3,2,1,0:T(8,128)} %refs_0_.5, s32[]{:T(128)S(6)} %select_n.15, s32[]{:T(128)S(6)} %select_n.14), kind=kLoop, calls=%fused_computation.1 | loop fusion | bytes 524296 | tf_op jit(solution)/shard_map/dynamic_slice | solution.py:355
  2.1 2.6 %collective-permute-start.1 = (f32[1,4,64,128]{3,2,1,0:T(8,128)S(1)}, f32[1,4,64,128]{3,2,1,0:T(8,128)S(1)}, u32[]{:S(2)}, u32[]{:S(2)}) collective-permute-start(f32[1,4,64,128]{3,2,1,0:T(8,128)S(1)} %get-tuple-element.56), channel_id=1, source_target_pairs={{0,2},{2,0},{4,6},{6,4},{8,10},{10,8},{12,14},{14,12},{1,3},{3,1},... | collective-permute-start | bytes 393224 | tf_op jit(solution)/shard_map/ppermute | solution.py:359
  4.7 0.7 collective-permute-start
  5.5 2.0 %copy-done.1 = f32[4,4,7,64,64]{4,3,2,1,0:T(8,128)S(1)} copy-done((f32[4,4,7,64,64]{4,3,2,1,0:T(8,128)S(1)}, f32[4,4,7,64,64]{4,3,2,1,0:T(8,128)}, u32[]{:S(2)}) %copy-start.1) | copy-done | bytes 1835032
  7.5 0.9 copy-done.2
  8.4 0.7 copy-done.4
  9.1 1.1 %pack.1.packed = bf16[16,128,512]{2,1,0:T(8,128)(2,1)S(1)} custom-call(s32[4]{0:T(128)S(1)} %pad_add_fusion.info, s32[4]{0:T(128)S(1)} %copy-done.4, f32[4,4,7,64,64]{4,3,2,1,0:T(8,128)S(1)} %copy-done.1, f32[4,64,64]{2,1,0:T(8,128)S(1)} %copy-done.2), custom_call_target="tpu_custom_call" | custom-call | flops 2875000064 | tf_op jit(solution)/shard_map/pack/pallas_call | solution.py:53
  10.2 0.2 collective-permute-start.3
  10.5 0.3 collective-permute-start.4
  10.8 0.8 collective-permute-done.3.refs_1_
  11.8 1.7 %step.3 = (f32[4,4,64,128]{3,2,1,0:T(8,128)S(1)}, f32[1,4,64,128]{3,2,1,0:T(8,128)S(1)}, f32[1,4,64,128]{3,2,1,0:T(8,128)S(1)}) custom-call(s32[4]{0:T(128)S(1)} %pad_add_fusion.info, s32[4,4,7]{2,1,0:T(4,128)S(1)} %copy-done.3, bf16[16,128,512]{2,1,0:T(8,128)(2,1)S(1)} %pack.1.packed, f32[4,4,64,128]{3,2,1,0:T(8,128)S(1)} %copy-done, ...), custom_call_target="tpu_custom_call" | custom-call | flops 1955000064 | tf_op jit(solution)/shard_map/step/pallas_call | solution.py:114
  13.5 0.4 collective-permute-start.5
  13.9 4.3 %collective-permute-start.6 = (f32[1,4,64,128]{3,2,1,0:T(8,128)S(1)}, f32[1,4,64,128]{3,2,1,0:T(8,128)S(1)}, u32[]{:S(2)}, u32[]{:S(2)}) collective-permute-start(f32[1,4,64,128]{3,2,1,0:T(8,128)S(1)} %get-tuple-element.33), channel_id=1, source_target_pairs={{0,2},{2,0},{4,6},{6,4},{8,10},{10,8},{12,14},{14,12},{1,3},{3,1},... | collective-permute-start | bytes 393224 | tf_op jit(solution)/shard_map/ppermute | solution.py:359
  18.2 0.7 collective-permute-start.8
  18.8 3.2 %collective-permute-done.6.refs_0_ = f32[1,4,64,128]{3,2,1,0:T(8,128)S(1)} collective-permute-done((f32[1,4,64,128]{3,2,1,0:T(8,128)S(1)}, f32[1,4,64,128]{3,2,1,0:T(8,128)S(1)}, u32[]{:S(2)}, u32[]{:S(2)}) %collective-permute-start.6) | collective-permute-done | bytes 131104 | tf_op jit(solution)/shard_map/ppermute | solution.py:359
  22.0 0.5 collective-permute-start.9
  22.5 0.8 collective-permute-done.7.refs_1_
  23.6 1.7 %step.4 = (f32[4,4,64,128]{3,2,1,0:T(8,128)S(1)}, f32[1,4,64,128]{3,2,1,0:T(8,128)S(1)}, f32[1,4,64,128]{3,2,1,0:T(8,128)S(1)}) custom-call(s32[4]{0:T(128)S(1)} %pad_add_fusion.info, s32[4,4,7]{2,1,0:T(4,128)S(1)} %copy-done.3, bf16[16,128,512]{2,1,0:T(8,128)(2,1)S(1)} %pack.1.packed, f32[4,4,64,128]{3,2,1,0:T(8,128)S(1)} %get-tuple-element.32.own.refs_4_.refs_1_, ...), custom_call_target="tpu_custom_call" | custom-call | flops 1955000064 | tf_op jit(solution)/shard_map/step/pallas_call | solution.py:114
  25.3 0.4 collective-permute-start.10
  25.7 4.3 %collective-permute-start.11 = (f32[1,4,64,128]{3,2,1,0:T(8,128)S(1)}, f32[1,4,64,128]{3,2,1,0:T(8,128)S(1)}, u32[]{:S(2)}, u32[]{:S(2)}) collective-permute-start(f32[1,4,64,128]{3,2,1,0:T(8,128)S(1)} %get-tuple-element.36), channel_id=1, source_target_pairs={{0,2},{2,0},{4,6},{6,4},{8,10},{10,8},{12,14},{14,12},{1,3},{3,1},... | collective-permute-start | bytes 393224 | tf_op jit(solution)/shard_map/ppermute | solution.py:359
  30.0 0.7 collective-permute-start.13
  30.6 1.6 %gram.3 = (f32[384,128]{1,0:T(8,128)S(1)}, f32[384,128]{1,0:T(8,128)S(1)}) custom-call(s32[4]{0:T(128)S(1)} %pad_add_fusion.info, f32[4,4,64,128]{3,2,1,0:T(8,128)S(1)} %copy-done, f32[4,4,64,128]{3,2,1,0:T(8,128)S(1)} %get-tuple-element.32.own.refs_4_.refs_1_, f32[4,4,64,128]{3,2,1,0:T(8,128)S(1)} %get-tuple-element.35.own.refs_2_), custom_call_target="tpu_custom_call" | custom-call | flops 1610000000 | tf_op jit(solution)/shard_map/gram/pallas_call | solution.py:156
  32.4 1.6 %collective-permute-done.11.refs_0_ = f32[1,4,64,128]{3,2,1,0:T(8,128)S(1)} collective-permute-done((f32[1,4,64,128]{3,2,1,0:T(8,128)S(1)}, f32[1,4,64,128]{3,2,1,0:T(8,128)S(1)}, u32[]{:S(2)}, u32[]{:S(2)}) %collective-permute-start.11) | collective-permute-done | bytes 131104 | tf_op jit(solution)/shard_map/ppermute | solution.py:359
  34.0 0.5 collective-permute-start.14
  34.5 0.7 add.29
  35.2 8.7 %all-to-all-start = ((f32[8,48,128]{2,1,0:T(8,128)}), f32[8,48,128]{2,1,0:T(8,128)S(1)}, u32[]{:S(2)}, u32[]{:S(2)}) async-start(f32[8,48,128]{2,1,0:T(8,128)} %bitcast.4), calls=%async_computation | async-start | bytes 393216 | tf_op jit(solution)/shard_map/all_to_all | solution.py:347
  43.9 1.6 %copy-done.6 = bf16[16,128,512]{2,1,0:T(8,128)(2,1)S(1)} copy-done((bf16[16,128,512]{2,1,0:T(8,128)(2,1)S(1)}, bf16[16,128,512]{2,1,0:T(8,128)(2,1)}, u32[]{:S(2)}) %copy-start.6) | copy-done | bytes 2097176
  45.5 1.7 %step.5.refs_3_ = f32[4,4,64,128]{3,2,1,0:T(8,128)S(1)} custom-call(s32[4]{0:T(128)S(1)} %pad_add_fusion.info, s32[4,4,7]{2,1,0:T(4,128)S(1)} %copy-done.3, bf16[16,128,512]{2,1,0:T(8,128)(2,1)S(1)} %copy-done.6, f32[4,4,64,128]{3,2,1,0:T(8,128)S(1)} %get-tuple-element.35.own.refs_2_, f32[4,4,64,128]{3,2,1,0:T(8,128)S(1)} %collective-permute-done.10.other, ...), custom_call_target="tpu_custom_call" | custom-call | flops 1955000064 | tf_op jit(solution)/shard_map/step/pallas_call | solution.py:114
  47.2 1.4 %gram.2 = (f32[256,128]{1,0:T(8,128)S(1)}, f32[256,128]{1,0:T(8,128)S(1)}) custom-call(s32[4]{0:T(128)S(1)} %pad_add_fusion.info, f32[4,4,64,128]{3,2,1,0:T(8,128)S(1)} %copy-done, f32[4,4,64,128]{3,2,1,0:T(8,128)S(1)} %get-tuple-element.32.own.refs_4_.refs_1_, f32[4,4,64,128]{3,2,1,0:T(8,128)S(1)} %get-tuple-element.35.own.refs_2_, ...), custom_call_target="tpu_custom_call" | custom-call | flops 1610000000 | tf_op jit(solution)/shard_map/gram/pallas_call | solution.py:156
  48.6 0.3 collective-permute-start.15
  48.9 1.1 %collective-permute-done.15 = f32[256,128]{1,0:T(8,128)S(1)} collective-permute-done((f32[256,128]{1,0:T(8,128)S(1)}, f32[256,128]{1,0:T(8,128)S(1)}, u32[]{:S(2)}, u32[]{:S(2)}) %collective-permute-start.15) | collective-permute-done | bytes 131104 | tf_op jit(solution)/shard_map/ppermute | solution.py:344
  50.0 2.4 %all-to-all-done = f32[8,48,128]{2,1,0:T(8,128)S(1)} async-done(((f32[8,48,128]{2,1,0:T(8,128)}), f32[8,48,128]{2,1,0:T(8,128)S(1)}, u32[]{:S(2)}, u32[]{:S(2)}) %all-to-all-start) | async-done | bytes 196640 | tf_op jit(solution)/shard_map/all_to_all | solution.py:347
  52.5 0.7 broadcast_in_dim.2
  53.2 3.6 %all-to-all-start.1 = ((f32[8,48,128]{2,1,0:T(8,128)}), f32[8,48,128]{2,1,0:T(8,128)S(1)}, u32[]{:S(2)}, u32[]{:S(2)}) async-start(f32[8,48,128]{2,1,0:T(8,128)} %broadcast_in_dim.2), calls=%async_computation.1 | async-start | bytes 393216 | tf_op jit(solution)/shard_map/all_to_all | solution.py:347
  56.8 2.0 %collective-permute-start.17 = (f32[256,128]{1,0:T(8,128)S(1)}, f32[256,128]{1,0:T(8,128)S(1)}, u32[]{:S(2)}, u32[]{:S(2)}) collective-permute-start(f32[256,128]{1,0:T(8,128)S(1)} %add.28), channel_id=1, source_target_pairs={{0,2},{2,0},{4,6},{6,4},{8,10},{10,8},{12,14},{14,12},{1,3},{3,1},... | collective-permute-start | bytes 393224 | tf_op jit(solution)/shard_map/ppermute | solution.py:350
  58.8 5.3 %collective-permute-done.17 = f32[256,128]{1,0:T(8,128)S(1)} collective-permute-done((f32[256,128]{1,0:T(8,128)S(1)}, f32[256,128]{1,0:T(8,128)S(1)}, u32[]{:S(2)}, u32[]{:S(2)}) %collective-permute-start.17) | collective-permute-done | bytes 131104 | tf_op jit(solution)/shard_map/ppermute | solution.py:350
  64.1 0.9 %all-to-all-done.1 = f32[8,48,128]{2,1,0:T(8,128)S(1)} async-done(((f32[8,48,128]{2,1,0:T(8,128)}), f32[8,48,128]{2,1,0:T(8,128)S(1)}, u32[]{:S(2)}, u32[]{:S(2)}) %all-to-all-start.1) | async-done | bytes 196640 | tf_op jit(solution)/shard_map/all_to_all | solution.py:347
  65.0 0.9 %collective-permute-start.18 = (f32[256,128]{1,0:T(8,128)S(1)}, f32[256,128]{1,0:T(8,128)S(1)}, u32[]{:S(2)}, u32[]{:S(2)}) collective-permute-start(f32[256,128]{1,0:T(8,128)S(1)} %add.30), channel_id=1, source_target_pairs={{0,4},{2,6},{4,0},{6,2},{8,12},{10,14},{12,8},{14,10},{1,5},{3,7},... | collective-permute-start | bytes 393224 | tf_op jit(solution)/shard_map/ppermute | solution.py:350
  66.0 0.5 collective-permute-done.19.other
  66.5 3.6 %column.4 = (f32[128,128]{1,0:T(8,128)S(1)}, f32[128,128]{1,0:T(8,128)S(1)}) custom-call(s32[4]{0:T(128)S(1)} %pad_add_fusion.info, f32[384,128]{1,0:T(8,128)S(1)} %bitcast.7, f32[384,128]{1,0:T(8,128)S(1)} %collective-permute-done.19.other), custom_call_target="tpu_custom_call" | custom-call | flops 4600000000 | tf_op jit(solution)/shard_map/column/pallas_call | solution.py:273
  70.0 0.9 %collective-permute-done.18 = f32[256,128]{1,0:T(8,128)S(1)} collective-permute-done((f32[256,128]{1,0:T(8,128)S(1)}, f32[256,128]{1,0:T(8,128)S(1)}, u32[]{:S(2)}, u32[]{:S(2)}) %collective-permute-start.18) | collective-permute-done | bytes 131104 | tf_op jit(solution)/shard_map/ppermute | solution.py:350
  70.9 1.8 %collective-permute-start.20 = (f32[256,128]{1,0:T(8,128)S(1)}, f32[256,128]{1,0:T(8,128)S(1)}, u32[]{:S(2)}, u32[]{:S(2)}) collective-permute-start(f32[256,128]{1,0:T(8,128)S(1)} %add.31), channel_id=1, source_target_pairs={{0,8},{2,10},{4,12},{6,14},{8,0},{10,2},{12,4},{14,6},{1,9},{3,11}... | collective-permute-start | bytes 393224 | tf_op jit(solution)/shard_map/ppermute | solution.py:350
  72.8 3.9 %column.5 = (f32[256,256]{1,0:T(8,128)S(1)}, f32[256,256]{1,0:T(8,128)S(1)}) custom-call(s32[4]{0:T(128)S(1)} %pad_add_fusion.info, f32[384,128]{1,0:T(8,128)S(1)} %bitcast.8, f32[384,128]{1,0:T(8,128)S(1)} %collective-permute-done.19.other, f32[128,128]{1,0:T(8,128)S(1)} %get-tuple-element.47.refs_0_, f32[128,128]{1,0:T(8,128)S(1)} %get-tuple-element.46.refs_1_), custom_call_target="tpu_custom_call" | custom-call | flops 4600000000 | tf_op jit(solution)/shard_map/column/pallas_call | solution.py:273
  76.6 3.9 %column.6 = (f32[384,384]{1,0:T(8,128)S(1)}, f32[384,384]{1,0:T(8,128)S(1)}) custom-call(s32[4]{0:T(128)S(1)} %pad_add_fusion.info, f32[384,128]{1,0:T(8,128)S(1)} %bitcast.9, f32[384,128]{1,0:T(8,128)S(1)} %collective-permute-done.19.other, f32[256,256]{1,0:T(8,128)S(1)} %get-tuple-element.49.refs_0_, f32[256,256]{1,0:T(8,128)S(1)} %get-tuple-element.50.refs_1_), custom_call_target="tpu_custom_call" | custom-call | flops 4600000000 | tf_op jit(solution)/shard_map/column/pallas_call | solution.py:273
  80.7 1.3 %collective-permute-done.21.other = f32[256,128]{1,0:T(8,128)S(1)} collective-permute-done((f32[256,128]{1,0:T(8,128)S(1)}, f32[256,128]{1,0:T(8,128)S(1)}, u32[]{:S(2)}, u32[]{:S(2)}) %collective-permute-start.21) | collective-permute-done | bytes 131104 | tf_op jit(solution)/shard_map/ppermute | solution.py:344
  82.0 5.1 %column.7 = (f32[512,512]{1,0:T(8,128)}, f32[512,512]{1,0:T(8,128)S(1)}) custom-call(s32[4]{0:T(128)S(1)} %pad_add_fusion.info, f32[256,128]{1,0:T(8,128)S(1)} %add.32.own, f32[256,128]{1,0:T(8,128)S(1)} %collective-permute-done.21.other, f32[384,384]{1,0:T(8,128)S(1)} %get-tuple-element.52.refs_0_, f32[384,384]{1,0:T(8,128)S(1)} %get-tuple-element.51.refs_1_), custom_call_target="tpu_custom_call" | custom-call | flops 4600000000 | tf_op jit(solution)/shard_map/column/pallas_call | solution.py:273
  87.2 3.2 %basis.1 = bf16[4,4,64,512]{3,2,1,0:T(8,128)(2,1)} custom-call(f32[4,4,64,128]{3,2,1,0:T(8,128)S(1)} %copy-done, f32[4,4,64,128]{3,2,1,0:T(8,128)S(1)} %get-tuple-element.32.own.refs_4_.refs_1_, f32[4,4,64,128]{3,2,1,0:T(8,128)S(1)} %get-tuple-element.35.own.refs_2_, f32[4,4,64,128]{3,2,1,0:T(8,128)S(1)} %step.5.refs_3_, ...), custom_call_target="tpu_custom_call" | custom-call | flops 3449999872 | tf_op jit(solution)/shard_map/basis/pallas_call | solution.py:315
  (34 shorter events, 0.8 us)
Async XLA Ops:
  0.6 11.2 %collective-permute-start.2 = (f32[4,4,64,128]{3,2,1,0:T(8,128)}, f32[4,4,64,128]{3,2,1,0:T(8,128)S(1)}, u32[]{:S(2)}, u32[]{:S(2)}) collective-permute-start(f32[4,4,64,128]{3,2,1,0:T(8,128)} %refs_0_.5), channel_id=1, source_target_pairs={{0,1},{1,0},{2,3},{3,2},{4,5},{5,4},{6,7},{7,6},{8,9},{9,8},{10,11... | collective-permute-start | bytes 1572872 | tf_op jit(solution)/shard_map/ppermute | solution.py:344
  2.1 8.1 %collective-permute-start.1 = (f32[1,4,64,128]{3,2,1,0:T(8,128)S(1)}, f32[1,4,64,128]{3,2,1,0:T(8,128)S(1)}, u32[]{:S(2)}, u32[]{:S(2)}) collective-permute-start(f32[1,4,64,128]{3,2,1,0:T(8,128)S(1)} %get-tuple-element.56), channel_id=1, source_target_pairs={{0,2},{2,0},{4,6},{6,4},{8,10},{10,8},{12,14},{14,12},{1,3},{3,1},... | collective-permute-start | bytes 393224 | tf_op jit(solution)/shard_map/ppermute | solution.py:359
  4.7 5.5 %collective-permute-start = (f32[1,4,64,128]{3,2,1,0:T(8,128)S(1)}, f32[1,4,64,128]{3,2,1,0:T(8,128)S(1)}, u32[]{:S(2)}, u32[]{:S(2)}) collective-permute-start(f32[1,4,64,128]{3,2,1,0:T(8,128)S(1)} %get-tuple-element.57), channel_id=1, source_target_pairs={{2,4},{4,2},{6,8},{8,6},{10,12},{12,10},{3,5},{5,3},{7,9},{9,7},{1... | collective-permute-start | bytes 393224 | tf_op jit(solution)/shard_map/ppermute | solution.py:360
  5.5 2.0 %copy-start.1 = (f32[4,4,7,64,64]{4,3,2,1,0:T(8,128)S(1)}, f32[4,4,7,64,64]{4,3,2,1,0:T(8,128)}, u32[]{:S(2)}) copy-start(f32[4,4,7,64,64]{4,3,2,1,0:T(8,128)} %held.1) | copy-start | bytes 5505028
  7.5 0.9 %copy-start.2 = (f32[4,64,64]{2,1,0:T(8,128)S(1)}, f32[4,64,64]{2,1,0:T(8,128)}, u32[]{:S(2)}) copy-start(f32[4,64,64]{2,1,0:T(8,128)} %leads.1) | copy-start | bytes 196612
  8.4 0.7 copy-start.4
  9.1 2.7 %copy-start = (f32[4,4,64,128]{3,2,1,0:T(8,128)S(1)}, f32[4,4,64,128]{3,2,1,0:T(8,128)}, u32[]{:S(2)}) copy-start(f32[4,4,64,128]{3,2,1,0:T(8,128)} %refs_0_.5) | copy-start | bytes 1572868
  9.1 2.7 %copy-start.3 = (s32[4,4,7]{2,1,0:T(4,128)S(1)}, s32[4,4,7]{2,1,0:T(4,128)}, u32[]{:S(2)}) copy-start(s32[4,4,7]{2,1,0:T(4,128)} %cols.5) | copy-start | bytes 1348
  10.2 15.1 %copy-start.5 = (bf16[16,128,512]{2,1,0:T(8,128)(2,1)}, bf16[16,128,512]{2,1,0:T(8,128)(2,1)S(1)}, u32[]{:S(2)}) copy-start(bf16[16,128,512]{2,1,0:T(8,128)(2,1)S(1)} %pack.1.packed) | copy-start | bytes 6291460
  10.2 1.4 %collective-permute-start.3 = (f32[1,4,64,128]{3,2,1,0:T(8,128)S(1)}, f32[1,4,64,128]{3,2,1,0:T(8,128)S(1)}, u32[]{:S(2)}, u32[]{:S(2)}) collective-permute-start(f32[1,4,64,128]{3,2,1,0:T(8,128)S(1)} %collective-permute-done.1.refs_0_), channel_id=1, source_target_pairs={{0,1},{1,0},{2,3},{3,2},{4,5},{5,4},{6,7},{7,6},{8,9},{9,8},{10,11... | collective-permute-start | bytes 393224 | tf_op jit(solution)/shard_map/ppermute | solution.py:344
  10.5 1.4 %collective-permute-start.4 = (f32[1,4,64,128]{3,2,1,0:T(8,128)S(1)}, f32[1,4,64,128]{3,2,1,0:T(8,128)S(1)}, u32[]{:S(2)}, u32[]{:S(2)}) collective-permute-start(f32[1,4,64,128]{3,2,1,0:T(8,128)S(1)} %collective-permute-done.refs_2_), channel_id=1, source_target_pairs={{0,1},{1,0},{2,3},{3,2},{4,5},{5,4},{6,7},{7,6},{8,9},{9,8},{10,11... | collective-permute-start | bytes 393224 | tf_op jit(solution)/shard_map/ppermute | solution.py:344
  13.5 10.1 %collective-permute-start.5 = (f32[4,4,64,128]{3,2,1,0:T(8,128)S(1)}, f32[4,4,64,128]{3,2,1,0:T(8,128)S(1)}, u32[]{:S(2)}, u32[]{:S(2)}) collective-permute-start(f32[4,4,64,128]{3,2,1,0:T(8,128)S(1)} %get-tuple-element.32.own.refs_4_.refs_1_), channel_id=1, source_target_pairs={{0,1},{1,0},{2,3},{3,2},{4,5},{5,4},{6,7},{7,6},{8,9},{9,8},{10,11... | collective-permute-start | bytes 1572872 | tf_op jit(solution)/shard_map/ppermute | solution.py:344
  13.9 8.1 %collective-permute-start.6 = (f32[1,4,64,128]{3,2,1,0:T(8,128)S(1)}, f32[1,4,64,128]{3,2,1,0:T(8,128)S(1)}, u32[]{:S(2)}, u32[]{:S(2)}) collective-permute-start(f32[1,4,64,128]{3,2,1,0:T(8,128)S(1)} %get-tuple-element.33), channel_id=1, source_target_pairs={{0,2},{2,0},{4,6},{6,4},{8,10},{10,8},{12,14},{14,12},{1,3},{3,1},... | collective-permute-start | bytes 393224 | tf_op jit(solution)/shard_map/ppermute | solution.py:359
  18.2 3.9 %collective-permute-start.8 = (f32[1,4,64,128]{3,2,1,0:T(8,128)S(1)}, f32[1,4,64,128]{3,2,1,0:T(8,128)S(1)}, u32[]{:S(2)}, u32[]{:S(2)}) collective-permute-start(f32[1,4,64,128]{3,2,1,0:T(8,128)S(1)} %get-tuple-element.34), channel_id=1, source_target_pairs={{2,4},{4,2},{6,8},{8,6},{10,12},{12,10},{3,5},{5,3},{7,9},{9,7},{1... | collective-permute-start | bytes 393224 | tf_op jit(solution)/shard_map/ppermute | solution.py:360
  22.0 1.3 %collective-permute-start.7 = (f32[1,4,64,128]{3,2,1,0:T(8,128)S(1)}, f32[1,4,64,128]{3,2,1,0:T(8,128)S(1)}, u32[]{:S(2)}, u32[]{:S(2)}) collective-permute-start(f32[1,4,64,128]{3,2,1,0:T(8,128)S(1)} %collective-permute-done.6.refs_0_), channel_id=1, source_target_pairs={{0,1},{1,0},{2,3},{3,2},{4,5},{5,4},{6,7},{7,6},{8,9},{9,8},{10,11... | collective-permute-start | bytes 393224 | tf_op jit(solution)/shard_map/ppermute | solution.py:344
  22.0 1.5 %collective-permute-start.9 = (f32[1,4,64,128]{3,2,1,0:T(8,128)S(1)}, f32[1,4,64,128]{3,2,1,0:T(8,128)S(1)}, u32[]{:S(2)}, u32[]{:S(2)}) collective-permute-start(f32[1,4,64,128]{3,2,1,0:T(8,128)S(1)} %collective-permute-done.8.refs_2_), channel_id=1, source_target_pairs={{0,1},{1,0},{2,3},{3,2},{4,5},{5,4},{6,7},{7,6},{8,9},{9,8},{10,11... | collective-permute-start | bytes 393224 | tf_op jit(solution)/shard_map/ppermute | solution.py:344
  25.3 18.6 %collective-permute-start.10 = (f32[4,4,64,128]{3,2,1,0:T(8,128)S(1)}, f32[4,4,64,128]{3,2,1,0:T(8,128)S(1)}, u32[]{:S(2)}, u32[]{:S(2)}) collective-permute-start(f32[4,4,64,128]{3,2,1,0:T(8,128)S(1)} %get-tuple-element.35.own.refs_2_), channel_id=1, source_target_pairs={{0,1},{1,0},{2,3},{3,2},{4,5},{5,4},{6,7},{7,6},{8,9},{9,8},{10,11... | collective-permute-start | bytes 1572872 | tf_op jit(solution)/shard_map/ppermute | solution.py:344
  25.7 8.3 %collective-permute-start.11 = (f32[1,4,64,128]{3,2,1,0:T(8,128)S(1)}, f32[1,4,64,128]{3,2,1,0:T(8,128)S(1)}, u32[]{:S(2)}, u32[]{:S(2)}) collective-permute-start(f32[1,4,64,128]{3,2,1,0:T(8,128)S(1)} %get-tuple-element.36), channel_id=1, source_target_pairs={{0,2},{2,0},{4,6},{6,4},{8,10},{10,8},{12,14},{14,12},{1,3},{3,1},... | collective-permute-start | bytes 393224 | tf_op jit(solution)/shard_map/ppermute | solution.py:359
  30.0 4.0 %collective-permute-start.13 = (f32[1,4,64,128]{3,2,1,0:T(8,128)S(1)}, f32[1,4,64,128]{3,2,1,0:T(8,128)S(1)}, u32[]{:S(2)}, u32[]{:S(2)}) collective-permute-start(f32[1,4,64,128]{3,2,1,0:T(8,128)S(1)} %get-tuple-element.37), channel_id=1, source_target_pairs={{2,4},{4,2},{6,8},{8,6},{10,12},{12,10},{3,5},{5,3},{7,9},{9,7},{1... | collective-permute-start | bytes 393224 | tf_op jit(solution)/shard_map/ppermute | solution.py:360
  32.3 2.2 %collective-permute-start.16 = (f32[384,128]{1,0:T(8,128)S(1)}, f32[384,128]{1,0:T(8,128)S(1)}, u32[]{:S(2)}, u32[]{:S(2)}) collective-permute-start(f32[384,128]{1,0:T(8,128)S(1)} %get-tuple-element.41), channel_id=1, source_target_pairs={{0,1},{1,0},{2,3},{3,2},{4,5},{5,4},{6,7},{7,6},{8,9},{9,8},{10,11... | collective-permute-start | bytes 589832 | tf_op jit(solution)/shard_map/ppermute | solution.py:344
  34.0 9.9 %collective-permute-start.12 = (f32[1,4,64,128]{3,2,1,0:T(8,128)S(1)}, f32[1,4,64,128]{3,2,1,0:T(8,128)S(1)}, u32[]{:S(2)}, u32[]{:S(2)}) collective-permute-start(f32[1,4,64,128]{3,2,1,0:T(8,128)S(1)} %collective-permute-done.11.refs_0_), channel_id=1, source_target_pairs={{0,1},{1,0},{2,3},{3,2},{4,5},{5,4},{6,7},{7,6},{8,9},{9,8},{10,11... | collective-permute-start | bytes 393224 | tf_op jit(solution)/shard_map/ppermute | solution.py:344
  34.0 9.9 %collective-permute-start.14 = (f32[1,4,64,128]{3,2,1,0:T(8,128)S(1)}, f32[1,4,64,128]{3,2,1,0:T(8,128)S(1)}, u32[]{:S(2)}, u32[]{:S(2)}) collective-permute-start(f32[1,4,64,128]{3,2,1,0:T(8,128)S(1)} %collective-permute-done.13.refs_2_), channel_id=1, source_target_pairs={{0,1},{1,0},{2,3},{3,2},{4,5},{5,4},{6,7},{7,6},{8,9},{9,8},{10,11... | collective-permute-start | bytes 393224 | tf_op jit(solution)/shard_map/ppermute | solution.py:344
  35.2 17.3 %all-to-all-start = ((f32[8,48,128]{2,1,0:T(8,128)}), f32[8,48,128]{2,1,0:T(8,128)S(1)}, u32[]{:S(2)}, u32[]{:S(2)}) async-start(f32[8,48,128]{2,1,0:T(8,128)} %bitcast.4), calls=%async_computation | async-start | bytes 393216 | tf_op jit(solution)/shard_map/all_to_all | solution.py:347
  43.9 1.6 %copy-start.6 = (bf16[16,128,512]{2,1,0:T(8,128)(2,1)S(1)}, bf16[16,128,512]{2,1,0:T(8,128)(2,1)}, u32[]{:S(2)}) copy-start(bf16[16,128,512]{2,1,0:T(8,128)(2,1)} %copy-done.5) | copy-start | bytes 6291460
  48.6 1.4 %collective-permute-start.15 = (f32[256,128]{1,0:T(8,128)S(1)}, f32[256,128]{1,0:T(8,128)S(1)}, u32[]{:S(2)}, u32[]{:S(2)}) collective-permute-start(f32[256,128]{1,0:T(8,128)S(1)} %get-tuple-element.39), channel_id=1, source_target_pairs={{0,1},{1,0},{2,3},{3,2},{4,5},{5,4},{6,7},{7,6},{8,9},{9,8},{10,11... | collective-permute-start | bytes 393224 | tf_op jit(solution)/shard_map/ppermute | solution.py:344
  53.2 11.8 %all-to-all-start.1 = ((f32[8,48,128]{2,1,0:T(8,128)}), f32[8,48,128]{2,1,0:T(8,128)S(1)}, u32[]{:S(2)}, u32[]{:S(2)}) async-start(f32[8,48,128]{2,1,0:T(8,128)} %broadcast_in_dim.2), calls=%async_computation.1 | async-start | bytes 393216 | tf_op jit(solution)/shard_map/all_to_all | solution.py:347
  56.8 7.3 %collective-permute-start.17 = (f32[256,128]{1,0:T(8,128)S(1)}, f32[256,128]{1,0:T(8,128)S(1)}, u32[]{:S(2)}, u32[]{:S(2)}) collective-permute-start(f32[256,128]{1,0:T(8,128)S(1)} %add.28), channel_id=1, source_target_pairs={{0,2},{2,0},{4,6},{6,4},{8,10},{10,8},{12,14},{14,12},{1,3},{3,1},... | collective-permute-start | bytes 393224 | tf_op jit(solution)/shard_map/ppermute | solution.py:350
  65.0 1.4 %collective-permute-start.19 = (f32[384,128]{1,0:T(8,128)S(1)}, f32[384,128]{1,0:T(8,128)S(1)}, u32[]{:S(2)}, u32[]{:S(2)}) collective-permute-start(f32[384,128]{1,0:T(8,128)S(1)} %bitcast.6), channel_id=1, source_target_pairs={{0,1},{1,0},{2,3},{3,2},{4,5},{5,4},{6,7},{7,6},{8,9},{9,8},{10,11... | collective-permute-start | bytes 589832 | tf_op jit(solution)/shard_map/ppermute | solution.py:344
  65.0 5.9 %collective-permute-start.18 = (f32[256,128]{1,0:T(8,128)S(1)}, f32[256,128]{1,0:T(8,128)S(1)}, u32[]{:S(2)}, u32[]{:S(2)}) collective-permute-start(f32[256,128]{1,0:T(8,128)S(1)} %add.30), channel_id=1, source_target_pairs={{0,4},{2,6},{4,0},{6,2},{8,12},{10,14},{12,8},{14,10},{1,5},{3,7},... | collective-permute-start | bytes 393224 | tf_op jit(solution)/shard_map/ppermute | solution.py:350
  70.9 9.6 %collective-permute-start.20 = (f32[256,128]{1,0:T(8,128)S(1)}, f32[256,128]{1,0:T(8,128)S(1)}, u32[]{:S(2)}, u32[]{:S(2)}) collective-permute-start(f32[256,128]{1,0:T(8,128)S(1)} %add.31), channel_id=1, source_target_pairs={{0,8},{2,10},{4,12},{6,14},{8,0},{10,2},{12,4},{14,6},{1,9},{3,11}... | collective-permute-start | bytes 393224 | tf_op jit(solution)/shard_map/ppermute | solution.py:350
  80.6 1.4 %collective-permute-start.21 = (f32[256,128]{1,0:T(8,128)S(1)}, f32[256,128]{1,0:T(8,128)S(1)}, u32[]{:S(2)}, u32[]{:S(2)}) collective-permute-start(f32[256,128]{1,0:T(8,128)S(1)} %add.32.own), channel_id=1, source_target_pairs={{0,1},{1,0},{2,3},{3,2},{4,5},{5,4},{6,7},{7,6},{8,9},{9,8},{10,11... | collective-permute-start | bytes 393224 | tf_op jit(solution)/shard_map/ppermute | solution.py:344

commit v9 on v8

--- a/solution.py
+++ b/solution.py
@@ -283,8 +283,9 @@
 
 
 def basis_kernel(scale, count, *refs):
-    *powers, inverse, out, high, low = refs
+    *powers, inverse, upper, out, upper_out, high, low = refs
     columns = powers[0].shape[-1]
+    upper_out[...] = upper[...]
 
     @pl.when(pl.program_id(0) == 0)
     def _():
@@ -308,22 +309,26 @@
         out[:, :, :, start:stop] = acc.astype(jnp.bfloat16).reshape(out.shape[:3] + (stop - start,))
 
 
-def basis_of(powers, inverse, scale):
+def basis_of(powers, inverse, upper, scale):
     layers, cross_local, size, columns = powers[0].shape
     count = len(powers)
     full = count * columns
+    part = pl.BlockSpec((full // layers, full), lambda i: (i, 0))
     return pl.pallas_call(
         functools.partial(basis_kernel, scale, count),
         grid=(layers,),
         in_specs=[pl.BlockSpec((1, cross_local, size, columns), lambda i: (i, 0, 0, 0))] * count
-        + [pl.BlockSpec(inverse.shape, lambda i: (0, 0))],
-        out_specs=pl.BlockSpec((1, cross_local, size, full), lambda i: (i, 0, 0, 0)),
-        out_shape=jax.ShapeDtypeStruct((layers, cross_local, size, full), jnp.bfloat16),
+        + [pl.BlockSpec(inverse.shape, lambda i: (0, 0)), part],
+        out_specs=[pl.BlockSpec((1, cross_local, size, full), lambda i: (i, 0, 0, 0)), part],
+        out_shape=[
+            jax.ShapeDtypeStruct((layers, cross_local, size, full), jnp.bfloat16),
+            jax.ShapeDtypeStruct(upper.shape, jnp.float32),
+        ],
         scratch_shapes=[pltpu.VMEM((full, full), jnp.bfloat16)] * 2,
         compiler_params=pltpu.CompilerParams(vmem_limit_bytes=VMEM_LIMIT),
         cost_estimate=estimate(3.0),
         name="basis",
-    )(*powers, inverse)
+    )(*powers, inverse, upper)
 
 
 def local(sources, couplings, block_cols, lead_sites, lead_sigma):
@@ -389,7 +394,7 @@
         last = double(last, reach, work)
         reach *= 2
     r_factor, inverse = column(3, 0, info, last, swap(last), third[::-1], 1.0 / scale_rows)
-    return basis_of(powers, inverse, scale_rows), r_factor
+    return tuple(basis_of(powers, inverse, r_factor, scale_rows))
 
 
 def solution(mesh):

time: 90.8 us -> 89.9 us (0.990)
    pallas_call x4, Pallas kernels: 16.5 us -> 15.5 us  [column(): pl.pallas_call(functools.partial(column_kernel, place, first, scale), in_...]
where the time goes in v9:
time: 89.9 us; the launch traced here: 89.5 us
  starting transfers between devices  33.6 us (37%)
  Pallas kernels  28 us (31%)
  waiting for transfers between devices  19.4 us (22%)
  local copies, waits for them, and re-layouts  6.87 us (8%)
    pallas_call x4, Pallas kernels, column(): pl.pallas_call(functools.partial(column_kernel, place, first, scale), in_...  15.5 us
    all_to_all x2, starting transfers between devices, exchange(): return lax.all_to_all(x, 'trans', 0, 0, tiled=True)  12.2 us
    ppermute x3, starting transfers between devices, local(): near_edge = lax.ppermute(near_layer, 'trans', near)  11.2 us
    ppermute x3, waiting for transfers between devices, double(): other = lax.ppermute(x, 'trans', [(i, i ^ reach) for i in range(count)])  6.2 us
    unnamed x14, local copies, waits for them, and re-layouts  5.19 us
    pallas_call x3, Pallas kernels, step(): pl.pallas_call(functools.partial(step_kernel, before is None, last, cols....  5.05 us
    ppermute x13, waiting for transfers between devices, swap(): return lax.ppermute(x, 'cross', [(0, 1), (1, 0)])  5.01 us
    ppermute x3, starting transfers between devices, double(): other = lax.ppermute(x, 'trans', [(i, i ^ reach) for i in range(count)])  4.8 us
  transfers between devices with their start and end apart: 24, of which 13 were waited for; matrix products, arithmetic and copies ran while one was open for 2% of the time, Pallas kernels for 19%

profile of v9, /device:TPU:0, one launch (start us, length us, event | category | flops | bytes accessed | tf_op | source)
XLA Modules:
  0.0 89.5 jit_solution(12000608146862975272)
XLA Ops:
  0.6 0.5 collective-permute-start.2
  1.1 1.0 %constant_dynamic-slice_fusion = (f32[1,4,64,128]{3,2,1,0:T(8,128)S(1)}, f32[1,4,64,128]{3,2,1,0:T(8,128)S(1)}) fusion(f32[4,4,64,128]{3,2,1,0:T(8,128)} %refs_0_.5, s32[]{:T(128)S(6)} %select_n.15, s32[]{:T(128)S(6)} %select_n.14), kind=kLoop, calls=%fused_computation.1 | loop fusion | bytes 524296 | tf_op jit(solution)/shard_map/dynamic_slice | solution.py:360
  2.1 2.6 %collective-permute-start.1 = (f32[1,4,64,128]{3,2,1,0:T(8,128)S(1)}, f32[1,4,64,128]{3,2,1,0:T(8,128)S(1)}, u32[]{:S(2)}, u32[]{:S(2)}) collective-permute-start(f32[1,4,64,128]{3,2,1,0:T(8,128)S(1)} %get-tuple-element.56), channel_id=1, source_target_pairs={{0,2},{2,0},{4,6},{6,4},{8,10},{10,8},{12,14},{14,12},{1,3},{3,1},... | collective-permute-start | bytes 393224 | tf_op jit(solution)/shard_map/ppermute | solution.py:364
  4.7 0.7 collective-permute-start
  5.5 2.0 %copy-done.1 = f32[4,4,7,64,64]{4,3,2,1,0:T(8,128)S(1)} copy-done((f32[4,4,7,64,64]{4,3,2,1,0:T(8,128)S(1)}, f32[4,4,7,64,64]{4,3,2,1,0:T(8,128)}, u32[]{:S(2)}) %copy-start.1) | copy-done | bytes 1835032
  7.5 0.9 %copy-done.2 = f32[4,64,64]{2,1,0:T(8,128)S(1)} copy-done((f32[4,64,64]{2,1,0:T(8,128)S(1)}, f32[4,64,64]{2,1,0:T(8,128)}, u32[]{:S(2)}) %copy-start.2) | copy-done | bytes 65560
  8.4 0.7 copy-done.4
  9.1 1.1 %pack.1.packed = bf16[16,128,512]{2,1,0:T(8,128)(2,1)S(1)} custom-call(s32[4]{0:T(128)S(1)} %pad_add_fusion.info, s32[4]{0:T(128)S(1)} %copy-done.4, f32[4,4,7,64,64]{4,3,2,1,0:T(8,128)S(1)} %copy-done.1, f32[4,64,64]{2,1,0:T(8,128)S(1)} %copy-done.2), custom_call_target="tpu_custom_call" | custom-call | flops 2875000064 | tf_op jit(solution)/shard_map/pack/pallas_call | solution.py:53
  10.2 0.2 collective-permute-start.3
  10.5 0.3 collective-permute-start.4
  10.8 0.8 collective-permute-done.3.refs_1_
  11.8 1.7 %step.3 = (f32[4,4,64,128]{3,2,1,0:T(8,128)S(1)}, f32[1,4,64,128]{3,2,1,0:T(8,128)S(1)}, f32[1,4,64,128]{3,2,1,0:T(8,128)S(1)}) custom-call(s32[4]{0:T(128)S(1)} %pad_add_fusion.info, s32[4,4,7]{2,1,0:T(4,128)S(1)} %copy-done.3, bf16[16,128,512]{2,1,0:T(8,128)(2,1)S(1)} %pack.1.packed, f32[4,4,64,128]{3,2,1,0:T(8,128)S(1)} %copy-done, ...), custom_call_target="tpu_custom_call" | custom-call | flops 1955000064 | tf_op jit(solution)/shard_map/step/pallas_call | solution.py:114
  13.5 0.4 collective-permute-start.5
  13.9 4.3 %collective-permute-start.6 = (f32[1,4,64,128]{3,2,1,0:T(8,128)S(1)}, f32[1,4,64,128]{3,2,1,0:T(8,128)S(1)}, u32[]{:S(2)}, u32[]{:S(2)}) collective-permute-start(f32[1,4,64,128]{3,2,1,0:T(8,128)S(1)} %get-tuple-element.33), channel_id=1, source_target_pairs={{0,2},{2,0},{4,6},{6,4},{8,10},{10,8},{12,14},{14,12},{1,3},{3,1},... | collective-permute-start | bytes 393224 | tf_op jit(solution)/shard_map/ppermute | solution.py:364
  18.2 0.7 collective-permute-start.8
  18.8 3.2 %collective-permute-done.6.refs_0_ = f32[1,4,64,128]{3,2,1,0:T(8,128)S(1)} collective-permute-done((f32[1,4,64,128]{3,2,1,0:T(8,128)S(1)}, f32[1,4,64,128]{3,2,1,0:T(8,128)S(1)}, u32[]{:S(2)}, u32[]{:S(2)}) %collective-permute-start.6) | collective-permute-done | bytes 131104 | tf_op jit(solution)/shard_map/ppermute | solution.py:364
  22.0 0.5 collective-permute-start.9
  22.5 0.8 collective-permute-done.7.refs_1_
  23.6 1.7 %step.4 = (f32[4,4,64,128]{3,2,1,0:T(8,128)S(1)}, f32[1,4,64,128]{3,2,1,0:T(8,128)S(1)}, f32[1,4,64,128]{3,2,1,0:T(8,128)S(1)}) custom-call(s32[4]{0:T(128)S(1)} %pad_add_fusion.info, s32[4,4,7]{2,1,0:T(4,128)S(1)} %copy-done.3, bf16[16,128,512]{2,1,0:T(8,128)(2,1)S(1)} %pack.1.packed, f32[4,4,64,128]{3,2,1,0:T(8,128)S(1)} %get-tuple-element.32.own.refs_4_.refs_1_, ...), custom_call_target="tpu_custom_call" | custom-call | flops 1955000064 | tf_op jit(solution)/shard_map/step/pallas_call | solution.py:114
  25.3 0.4 collective-permute-start.10
  25.7 4.3 %collective-permute-start.11 = (f32[1,4,64,128]{3,2,1,0:T(8,128)S(1)}, f32[1,4,64,128]{3,2,1,0:T(8,128)S(1)}, u32[]{:S(2)}, u32[]{:S(2)}) collective-permute-start(f32[1,4,64,128]{3,2,1,0:T(8,128)S(1)} %get-tuple-element.36), channel_id=1, source_target_pairs={{0,2},{2,0},{4,6},{6,4},{8,10},{10,8},{12,14},{14,12},{1,3},{3,1},... | collective-permute-start | bytes 393224 | tf_op jit(solution)/shard_map/ppermute | solution.py:364
  30.0 0.7 collective-permute-start.13
  30.6 1.6 %gram.3 = (f32[384,128]{1,0:T(8,128)S(1)}, f32[384,128]{1,0:T(8,128)S(1)}) custom-call(s32[4]{0:T(128)S(1)} %pad_add_fusion.info, f32[4,4,64,128]{3,2,1,0:T(8,128)S(1)} %copy-done, f32[4,4,64,128]{3,2,1,0:T(8,128)S(1)} %get-tuple-element.32.own.refs_4_.refs_1_, f32[4,4,64,128]{3,2,1,0:T(8,128)S(1)} %get-tuple-element.35.own.refs_2_), custom_call_target="tpu_custom_call" | custom-call | flops 1610000000 | tf_op jit(solution)/shard_map/gram/pallas_call | solution.py:156
  32.4 1.6 %collective-permute-done.11.refs_0_ = f32[1,4,64,128]{3,2,1,0:T(8,128)S(1)} collective-permute-done((f32[1,4,64,128]{3,2,1,0:T(8,128)S(1)}, f32[1,4,64,128]{3,2,1,0:T(8,128)S(1)}, u32[]{:S(2)}, u32[]{:S(2)}) %collective-permute-start.11) | collective-permute-done | bytes 131104 | tf_op jit(solution)/shard_map/ppermute | solution.py:364
  34.0 0.5 collective-permute-start.14
  34.5 0.7 add.29
  35.2 8.7 %all-to-all-start = ((f32[8,48,128]{2,1,0:T(8,128)}), f32[8,48,128]{2,1,0:T(8,128)S(1)}, u32[]{:S(2)}, u32[]{:S(2)}) async-start(f32[8,48,128]{2,1,0:T(8,128)} %bitcast.4), calls=%async_computation | async-start | bytes 393216 | tf_op jit(solution)/shard_map/all_to_all | solution.py:352
  43.9 1.6 %copy-done.6 = bf16[16,128,512]{2,1,0:T(8,128)(2,1)S(1)} copy-done((bf16[16,128,512]{2,1,0:T(8,128)(2,1)S(1)}, bf16[16,128,512]{2,1,0:T(8,128)(2,1)}, u32[]{:S(2)}) %copy-start.6) | copy-done | bytes 2097176
  45.5 1.7 %step.5.refs_3_ = f32[4,4,64,128]{3,2,1,0:T(8,128)S(1)} custom-call(s32[4]{0:T(128)S(1)} %pad_add_fusion.info, s32[4,4,7]{2,1,0:T(4,128)S(1)} %copy-done.3, bf16[16,128,512]{2,1,0:T(8,128)(2,1)S(1)} %copy-done.6, f32[4,4,64,128]{3,2,1,0:T(8,128)S(1)} %get-tuple-element.35.own.refs_2_, f32[4,4,64,128]{3,2,1,0:T(8,128)S(1)} %collective-permute-done.10.other, ...), custom_call_target="tpu_custom_call" | custom-call | flops 1955000064 | tf_op jit(solution)/shard_map/step/pallas_call | solution.py:114
  47.2 1.4 %gram.2 = (f32[256,128]{1,0:T(8,128)S(1)}, f32[256,128]{1,0:T(8,128)S(1)}) custom-call(s32[4]{0:T(128)S(1)} %pad_add_fusion.info, f32[4,4,64,128]{3,2,1,0:T(8,128)S(1)} %copy-done, f32[4,4,64,128]{3,2,1,0:T(8,128)S(1)} %get-tuple-element.32.own.refs_4_.refs_1_, f32[4,4,64,128]{3,2,1,0:T(8,128)S(1)} %get-tuple-element.35.own.refs_2_, ...), custom_call_target="tpu_custom_call" | custom-call | flops 1610000000 | tf_op jit(solution)/shard_map/gram/pallas_call | solution.py:156
  48.6 0.3 collective-permute-start.15
  48.9 1.1 %collective-permute-done.15 = f32[256,128]{1,0:T(8,128)S(1)} collective-permute-done((f32[256,128]{1,0:T(8,128)S(1)}, f32[256,128]{1,0:T(8,128)S(1)}, u32[]{:S(2)}, u32[]{:S(2)}) %collective-permute-start.15) | collective-permute-done | bytes 131104 | tf_op jit(solution)/shard_map/ppermute | solution.py:349
  50.0 2.4 %all-to-all-done = f32[8,48,128]{2,1,0:T(8,128)S(1)} async-done(((f32[8,48,128]{2,1,0:T(8,128)}), f32[8,48,128]{2,1,0:T(8,128)S(1)}, u32[]{:S(2)}, u32[]{:S(2)}) %all-to-all-start) | async-done | bytes 196640 | tf_op jit(solution)/shard_map/all_to_all | solution.py:352
  52.5 0.7 broadcast_in_dim.2
  53.2 3.6 %all-to-all-start.1 = ((f32[8,48,128]{2,1,0:T(8,128)}), f32[8,48,128]{2,1,0:T(8,128)S(1)}, u32[]{:S(2)}, u32[]{:S(2)}) async-start(f32[8,48,128]{2,1,0:T(8,128)} %broadcast_in_dim.2), calls=%async_computation.1 | async-start | bytes 393216 | tf_op jit(solution)/shard_map/all_to_all | solution.py:352
  56.8 2.0 %collective-permute-start.17 = (f32[256,128]{1,0:T(8,128)S(1)}, f32[256,128]{1,0:T(8,128)S(1)}, u32[]{:S(2)}, u32[]{:S(2)}) collective-permute-start(f32[256,128]{1,0:T(8,128)S(1)} %add.28), channel_id=1, source_target_pairs={{0,2},{2,0},{4,6},{6,4},{8,10},{10,8},{12,14},{14,12},{1,3},{3,1},... | collective-permute-start | bytes 393224 | tf_op jit(solution)/shard_map/ppermute | solution.py:355
  58.8 5.3 %collective-permute-done.17 = f32[256,128]{1,0:T(8,128)S(1)} collective-permute-done((f32[256,128]{1,0:T(8,128)S(1)}, f32[256,128]{1,0:T(8,128)S(1)}, u32[]{:S(2)}, u32[]{:S(2)}) %collective-permute-start.17) | collective-permute-done | bytes 131104 | tf_op jit(solution)/shard_map/ppermute | solution.py:355
  64.1 0.9 %all-to-all-done.1 = f32[8,48,128]{2,1,0:T(8,128)S(1)} async-done(((f32[8,48,128]{2,1,0:T(8,128)}), f32[8,48,128]{2,1,0:T(8,128)S(1)}, u32[]{:S(2)}, u32[]{:S(2)}) %all-to-all-start.1) | async-done | bytes 196640 | tf_op jit(solution)/shard_map/all_to_all | solution.py:352
  65.0 0.9 %collective-permute-start.18 = (f32[256,128]{1,0:T(8,128)S(1)}, f32[256,128]{1,0:T(8,128)S(1)}, u32[]{:S(2)}, u32[]{:S(2)}) collective-permute-start(f32[256,128]{1,0:T(8,128)S(1)} %add.30), channel_id=1, source_target_pairs={{0,4},{2,6},{4,0},{6,2},{8,12},{10,14},{12,8},{14,10},{1,5},{3,7},... | collective-permute-start | bytes 393224 | tf_op jit(solution)/shard_map/ppermute | solution.py:355
  66.0 0.5 collective-permute-done.19.other
  66.5 3.6 %column.4 = (f32[128,128]{1,0:T(8,128)S(1)}, f32[128,128]{1,0:T(8,128)S(1)}) custom-call(s32[4]{0:T(128)S(1)} %pad_add_fusion.info, f32[384,128]{1,0:T(8,128)S(1)} %bitcast.7, f32[384,128]{1,0:T(8,128)S(1)} %collective-permute-done.19.other), custom_call_target="tpu_custom_call" | custom-call | flops 4600000000 | tf_op jit(solution)/shard_map/column/pallas_call | solution.py:273
  70.0 0.9 %collective-permute-done.18 = f32[256,128]{1,0:T(8,128)S(1)} collective-permute-done((f32[256,128]{1,0:T(8,128)S(1)}, f32[256,128]{1,0:T(8,128)S(1)}, u32[]{:S(2)}, u32[]{:S(2)}) %collective-permute-start.18) | collective-permute-done | bytes 131104 | tf_op jit(solution)/shard_map/ppermute | solution.py:355
  70.9 1.8 %collective-permute-start.20 = (f32[256,128]{1,0:T(8,128)S(1)}, f32[256,128]{1,0:T(8,128)S(1)}, u32[]{:S(2)}, u32[]{:S(2)}) collective-permute-start(f32[256,128]{1,0:T(8,128)S(1)} %add.31), channel_id=1, source_target_pairs={{0,8},{2,10},{4,12},{6,14},{8,0},{10,2},{12,4},{14,6},{1,9},{3,11}... | collective-permute-start | bytes 393224 | tf_op jit(solution)/shard_map/ppermute | solution.py:355
  72.8 3.9 %column.5 = (f32[256,256]{1,0:T(8,128)S(1)}, f32[256,256]{1,0:T(8,128)S(1)}) custom-call(s32[4]{0:T(128)S(1)} %pad_add_fusion.info, f32[384,128]{1,0:T(8,128)S(1)} %bitcast.8, f32[384,128]{1,0:T(8,128)S(1)} %collective-permute-done.19.other, f32[128,128]{1,0:T(8,128)S(1)} %get-tuple-element.47.refs_0_, f32[128,128]{1,0:T(8,128)S(1)} %get-tuple-element.46.refs_1_), custom_call_target="tpu_custom_call" | custom-call | flops 4600000000 | tf_op jit(solution)/shard_map/column/pallas_call | solution.py:273
  76.6 3.9 %column.6 = (f32[384,384]{1,0:T(8,128)S(1)}, f32[384,384]{1,0:T(8,128)S(1)}) custom-call(s32[4]{0:T(128)S(1)} %pad_add_fusion.info, f32[384,128]{1,0:T(8,128)S(1)} %bitcast.9, f32[384,128]{1,0:T(8,128)S(1)} %collective-permute-done.19.other, f32[256,256]{1,0:T(8,128)S(1)} %get-tuple-element.49.refs_0_, f32[256,256]{1,0:T(8,128)S(1)} %get-tuple-element.50.refs_1_), custom_call_target="tpu_custom_call" | custom-call | flops 4600000000 | tf_op jit(solution)/shard_map/column/pallas_call | solution.py:273
  80.7 1.3 %collective-permute-done.21.other = f32[256,128]{1,0:T(8,128)S(1)} collective-permute-done((f32[256,128]{1,0:T(8,128)S(1)}, f32[256,128]{1,0:T(8,128)S(1)}, u32[]{:S(2)}, u32[]{:S(2)}) %collective-permute-start.21) | collective-permute-done | bytes 131104 | tf_op jit(solution)/shard_map/ppermute | solution.py:349
  82.0 4.2 %column.7 = (f32[512,512]{1,0:T(8,128)S(1)}, f32[512,512]{1,0:T(8,128)S(1)}) custom-call(s32[4]{0:T(128)S(1)} %pad_add_fusion.info, f32[256,128]{1,0:T(8,128)S(1)} %add.32.own, f32[256,128]{1,0:T(8,128)S(1)} %collective-permute-done.21.other, f32[384,384]{1,0:T(8,128)S(1)} %get-tuple-element.52.refs_0_, f32[384,384]{1,0:T(8,128)S(1)} %get-tuple-element.51.refs_1_), custom_call_target="tpu_custom_call" | custom-call | flops 4600000000 | tf_op jit(solution)/shard_map/column/pallas_call | solution.py:273
  86.2 3.3 %basis.1 = (bf16[4,4,64,512]{3,2,1,0:T(8,128)(2,1)}, f32[512,512]{1,0:T(8,128)}) custom-call(f32[4,4,64,128]{3,2,1,0:T(8,128)S(1)} %copy-done, f32[4,4,64,128]{3,2,1,0:T(8,128)S(1)} %get-tuple-element.32.own.refs_4_.refs_1_, f32[4,4,64,128]{3,2,1,0:T(8,128)S(1)} %get-tuple-element.35.own.refs_2_, f32[4,4,64,128]{3,2,1,0:T(8,128)S(1)} %step.5.refs_3_, ...), custom_call_target="tpu_custom_call" | custom-call | flops 3449999872 | tf_op jit(solution)/shard_map/basis/pallas_call | solution.py:317
  (34 shorter events, 0.8 us)
Async XLA Ops:
  0.6 11.2 %collective-permute-start.2 = (f32[4,4,64,128]{3,2,1,0:T(8,128)}, f32[4,4,64,128]{3,2,1,0:T(8,128)S(1)}, u32[]{:S(2)}, u32[]{:S(2)}) collective-permute-start(f32[4,4,64,128]{3,2,1,0:T(8,128)} %refs_0_.5), channel_id=1, source_target_pairs={{0,1},{1,0},{2,3},{3,2},{4,5},{5,4},{6,7},{7,6},{8,9},{9,8},{10,11... | collective-permute-start | bytes 1572872 | tf_op jit(solution)/shard_map/ppermute | solution.py:349
  2.1 8.1 %collective-permute-start.1 = (f32[1,4,64,128]{3,2,1,0:T(8,128)S(1)}, f32[1,4,64,128]{3,2,1,0:T(8,128)S(1)}, u32[]{:S(2)}, u32[]{:S(2)}) collective-permute-start(f32[1,4,64,128]{3,2,1,0:T(8,128)S(1)} %get-tuple-element.56), channel_id=1, source_target_pairs={{0,2},{2,0},{4,6},{6,4},{8,10},{10,8},{12,14},{14,12},{1,3},{3,1},... | collective-permute-start | bytes 393224 | tf_op jit(solution)/shard_map/ppermute | solution.py:364
  4.7 5.5 %collective-permute-start = (f32[1,4,64,128]{3,2,1,0:T(8,128)S(1)}, f32[1,4,64,128]{3,2,1,0:T(8,128)S(1)}, u32[]{:S(2)}, u32[]{:S(2)}) collective-permute-start(f32[1,4,64,128]{3,2,1,0:T(8,128)S(1)} %get-tuple-element.57), channel_id=1, source_target_pairs={{2,4},{4,2},{6,8},{8,6},{10,12},{12,10},{3,5},{5,3},{7,9},{9,7},{1... | collective-permute-start | bytes 393224 | tf_op jit(solution)/shard_map/ppermute | solution.py:365
  5.5 2.0 %copy-start.1 = (f32[4,4,7,64,64]{4,3,2,1,0:T(8,128)S(1)}, f32[4,4,7,64,64]{4,3,2,1,0:T(8,128)}, u32[]{:S(2)}) copy-start(f32[4,4,7,64,64]{4,3,2,1,0:T(8,128)} %held.1) | copy-start | bytes 5505028
  7.5 0.9 %copy-start.2 = (f32[4,64,64]{2,1,0:T(8,128)S(1)}, f32[4,64,64]{2,1,0:T(8,128)}, u32[]{:S(2)}) copy-start(f32[4,64,64]{2,1,0:T(8,128)} %leads.1) | copy-start | bytes 196612
  8.4 0.7 copy-start.4
  9.1 2.7 %copy-start = (f32[4,4,64,128]{3,2,1,0:T(8,128)S(1)}, f32[4,4,64,128]{3,2,1,0:T(8,128)}, u32[]{:S(2)}) copy-start(f32[4,4,64,128]{3,2,1,0:T(8,128)} %refs_0_.5) | copy-start | bytes 1572868
  9.1 2.7 %copy-start.3 = (s32[4,4,7]{2,1,0:T(4,128)S(1)}, s32[4,4,7]{2,1,0:T(4,128)}, u32[]{:S(2)}) copy-start(s32[4,4,7]{2,1,0:T(4,128)} %cols.5) | copy-start | bytes 1348
  10.2 15.1 %copy-start.5 = (bf16[16,128,512]{2,1,0:T(8,128)(2,1)}, bf16[16,128,512]{2,1,0:T(8,128)(2,1)S(1)}, u32[]{:S(2)}) copy-start(bf16[16,128,512]{2,1,0:T(8,128)(2,1)S(1)} %pack.1.packed) | copy-start | bytes 6291460
  10.2 1.4 %collective-permute-start.3 = (f32[1,4,64,128]{3,2,1,0:T(8,128)S(1)}, f32[1,4,64,128]{3,2,1,0:T(8,128)S(1)}, u32[]{:S(2)}, u32[]{:S(2)}) collective-permute-start(f32[1,4,64,128]{3,2,1,0:T(8,128)S(1)} %collective-permute-done.1.refs_0_), channel_id=1, source_target_pairs={{0,1},{1,0},{2,3},{3,2},{4,5},{5,4},{6,7},{7,6},{8,9},{9,8},{10,11... | collective-permute-start | bytes 393224 | tf_op jit(solution)/shard_map/ppermute | solution.py:349
  10.5 1.4 %collective-permute-start.4 = (f32[1,4,64,128]{3,2,1,0:T(8,128)S(1)}, f32[1,4,64,128]{3,2,1,0:T(8,128)S(1)}, u32[]{:S(2)}, u32[]{:S(2)}) collective-permute-start(f32[1,4,64,128]{3,2,1,0:T(8,128)S(1)} %collective-permute-done.refs_2_), channel_id=1, source_target_pairs={{0,1},{1,0},{2,3},{3,2},{4,5},{5,4},{6,7},{7,6},{8,9},{9,8},{10,11... | collective-permute-start | bytes 393224 | tf_op jit(solution)/shard_map/ppermute | solution.py:349
  13.5 10.1 %collective-permute-start.5 = (f32[4,4,64,128]{3,2,1,0:T(8,128)S(1)}, f32[4,4,64,128]{3,2,1,0:T(8,128)S(1)}, u32[]{:S(2)}, u32[]{:S(2)}) collective-permute-start(f32[4,4,64,128]{3,2,1,0:T(8,128)S(1)} %get-tuple-element.32.own.refs_4_.refs_1_), channel_id=1, source_target_pairs={{0,1},{1,0},{2,3},{3,2},{4,5},{5,4},{6,7},{7,6},{8,9},{9,8},{10,11... | collective-permute-start | bytes 1572872 | tf_op jit(solution)/shard_map/ppermute | solution.py:349
  13.9 8.1 %collective-permute-start.6 = (f32[1,4,64,128]{3,2,1,0:T(8,128)S(1)}, f32[1,4,64,128]{3,2,1,0:T(8,128)S(1)}, u32[]{:S(2)}, u32[]{:S(2)}) collective-permute-start(f32[1,4,64,128]{3,2,1,0:T(8,128)S(1)} %get-tuple-element.33), channel_id=1, source_target_pairs={{0,2},{2,0},{4,6},{6,4},{8,10},{10,8},{12,14},{14,12},{1,3},{3,1},... | collective-permute-start | bytes 393224 | tf_op jit(solution)/shard_map/ppermute | solution.py:364
  18.2 3.9 %collective-permute-start.8 = (f32[1,4,64,128]{3,2,1,0:T(8,128)S(1)}, f32[1,4,64,128]{3,2,1,0:T(8,128)S(1)}, u32[]{:S(2)}, u32[]{:S(2)}) collective-permute-start(f32[1,4,64,128]{3,2,1,0:T(8,128)S(1)} %get-tuple-element.34), channel_id=1, source_target_pairs={{2,4},{4,2},{6,8},{8,6},{10,12},{12,10},{3,5},{5,3},{7,9},{9,7},{1... | collective-permute-start | bytes 393224 | tf_op jit(solution)/shard_map/ppermute | solution.py:365
  22.0 1.3 %collective-permute-start.7 = (f32[1,4,64,128]{3,2,1,0:T(8,128)S(1)}, f32[1,4,64,128]{3,2,1,0:T(8,128)S(1)}, u32[]{:S(2)}, u32[]{:S(2)}) collective-permute-start(f32[1,4,64,128]{3,2,1,0:T(8,128)S(1)} %collective-permute-done.6.refs_0_), channel_id=1, source_target_pairs={{0,1},{1,0},{2,3},{3,2},{4,5},{5,4},{6,7},{7,6},{8,9},{9,8},{10,11... | collective-permute-start | bytes 393224 | tf_op jit(solution)/shard_map/ppermute | solution.py:349
  22.0 1.5 %collective-permute-start.9 = (f32[1,4,64,128]{3,2,1,0:T(8,128)S(1)}, f32[1,4,64,128]{3,2,1,0:T(8,128)S(1)}, u32[]{:S(2)}, u32[]{:S(2)}) collective-permute-start(f32[1,4,64,128]{3,2,1,0:T(8,128)S(1)} %collective-permute-done.8.refs_2_), channel_id=1, source_target_pairs={{0,1},{1,0},{2,3},{3,2},{4,5},{5,4},{6,7},{7,6},{8,9},{9,8},{10,11... | collective-permute-start | bytes 393224 | tf_op jit(solution)/shard_map/ppermute | solution.py:349
  25.3 18.6 %collective-permute-start.10 = (f32[4,4,64,128]{3,2,1,0:T(8,128)S(1)}, f32[4,4,64,128]{3,2,1,0:T(8,128)S(1)}, u32[]{:S(2)}, u32[]{:S(2)}) collective-permute-start(f32[4,4,64,128]{3,2,1,0:T(8,128)S(1)} %get-tuple-element.35.own.refs_2_), channel_id=1, source_target_pairs={{0,1},{1,0},{2,3},{3,2},{4,5},{5,4},{6,7},{7,6},{8,9},{9,8},{10,11... | collective-permute-start | bytes 1572872 | tf_op jit(solution)/shard_map/ppermute | solution.py:349
  25.7 8.3 %collective-permute-start.11 = (f32[1,4,64,128]{3,2,1,0:T(8,128)S(1)}, f32[1,4,64,128]{3,2,1,0:T(8,128)S(1)}, u32[]{:S(2)}, u32[]{:S(2)}) collective-permute-start(f32[1,4,64,128]{3,2,1,0:T(8,128)S(1)} %get-tuple-element.36), channel_id=1, source_target_pairs={{0,2},{2,0},{4,6},{6,4},{8,10},{10,8},{12,14},{14,12},{1,3},{3,1},... | collective-permute-start | bytes 393224 | tf_op jit(solution)/shard_map/ppermute | solution.py:364
  30.0 4.0 %collective-permute-start.13 = (f32[1,4,64,128]{3,2,1,0:T(8,128)S(1)}, f32[1,4,64,128]{3,2,1,0:T(8,128)S(1)}, u32[]{:S(2)}, u32[]{:S(2)}) collective-permute-start(f32[1,4,64,128]{3,2,1,0:T(8,128)S(1)} %get-tuple-element.37), channel_id=1, source_target_pairs={{2,4},{4,2},{6,8},{8,6},{10,12},{12,10},{3,5},{5,3},{7,9},{9,7},{1... | collective-permute-start | bytes 393224 | tf_op jit(solution)/shard_map/ppermute | solution.py:365
  32.3 2.2 %collective-permute-start.16 = (f32[384,128]{1,0:T(8,128)S(1)}, f32[384,128]{1,0:T(8,128)S(1)}, u32[]{:S(2)}, u32[]{:S(2)}) collective-permute-start(f32[384,128]{1,0:T(8,128)S(1)} %get-tuple-element.41), channel_id=1, source_target_pairs={{0,1},{1,0},{2,3},{3,2},{4,5},{5,4},{6,7},{7,6},{8,9},{9,8},{10,11... | collective-permute-start | bytes 589832 | tf_op jit(solution)/shard_map/ppermute | solution.py:349
  34.0 9.9 %collective-permute-start.12 = (f32[1,4,64,128]{3,2,1,0:T(8,128)S(1)}, f32[1,4,64,128]{3,2,1,0:T(8,128)S(1)}, u32[]{:S(2)}, u32[]{:S(2)}) collective-permute-start(f32[1,4,64,128]{3,2,1,0:T(8,128)S(1)} %collective-permute-done.11.refs_0_), channel_id=1, source_target_pairs={{0,1},{1,0},{2,3},{3,2},{4,5},{5,4},{6,7},{7,6},{8,9},{9,8},{10,11... | collective-permute-start | bytes 393224 | tf_op jit(solution)/shard_map/ppermute | solution.py:349
  34.0 9.9 %collective-permute-start.14 = (f32[1,4,64,128]{3,2,1,0:T(8,128)S(1)}, f32[1,4,64,128]{3,2,1,0:T(8,128)S(1)}, u32[]{:S(2)}, u32[]{:S(2)}) collective-permute-start(f32[1,4,64,128]{3,2,1,0:T(8,128)S(1)} %collective-permute-done.13.refs_2_), channel_id=1, source_target_pairs={{0,1},{1,0},{2,3},{3,2},{4,5},{5,4},{6,7},{7,6},{8,9},{9,8},{10,11... | collective-permute-start | bytes 393224 | tf_op jit(solution)/shard_map/ppermute | solution.py:349
  35.2 17.3 %all-to-all-start = ((f32[8,48,128]{2,1,0:T(8,128)}), f32[8,48,128]{2,1,0:T(8,128)S(1)}, u32[]{:S(2)}, u32[]{:S(2)}) async-start(f32[8,48,128]{2,1,0:T(8,128)} %bitcast.4), calls=%async_computation | async-start | bytes 393216 | tf_op jit(solution)/shard_map/all_to_all | solution.py:352
  43.9 1.6 %copy-start.6 = (bf16[16,128,512]{2,1,0:T(8,128)(2,1)S(1)}, bf16[16,128,512]{2,1,0:T(8,128)(2,1)}, u32[]{:S(2)}) copy-start(bf16[16,128,512]{2,1,0:T(8,128)(2,1)} %copy-done.5) | copy-start | bytes 6291460
  48.6 1.4 %collective-permute-start.15 = (f32[256,128]{1,0:T(8,128)S(1)}, f32[256,128]{1,0:T(8,128)S(1)}, u32[]{:S(2)}, u32[]{:S(2)}) collective-permute-start(f32[256,128]{1,0:T(8,128)S(1)} %get-tuple-element.39), channel_id=1, source_target_pairs={{0,1},{1,0},{2,3},{3,2},{4,5},{5,4},{6,7},{7,6},{8,9},{9,8},{10,11... | collective-permute-start | bytes 393224 | tf_op jit(solution)/shard_map/ppermute | solution.py:349
  53.2 11.8 %all-to-all-start.1 = ((f32[8,48,128]{2,1,0:T(8,128)}), f32[8,48,128]{2,1,0:T(8,128)S(1)}, u32[]{:S(2)}, u32[]{:S(2)}) async-start(f32[8,48,128]{2,1,0:T(8,128)} %broadcast_in_dim.2), calls=%async_computation.1 | async-start | bytes 393216 | tf_op jit(solution)/shard_map/all_to_all | solution.py:352
  56.8 7.3 %collective-permute-start.17 = (f32[256,128]{1,0:T(8,128)S(1)}, f32[256,128]{1,0:T(8,128)S(1)}, u32[]{:S(2)}, u32[]{:S(2)}) collective-permute-start(f32[256,128]{1,0:T(8,128)S(1)} %add.28), channel_id=1, source_target_pairs={{0,2},{2,0},{4,6},{6,4},{8,10},{10,8},{12,14},{14,12},{1,3},{3,1},... | collective-permute-start | bytes 393224 | tf_op jit(solution)/shard_map/ppermute | solution.py:355
  65.0 1.4 %collective-permute-start.19 = (f32[384,128]{1,0:T(8,128)S(1)}, f32[384,128]{1,0:T(8,128)S(1)}, u32[]{:S(2)}, u32[]{:S(2)}) collective-permute-start(f32[384,128]{1,0:T(8,128)S(1)} %bitcast.6), channel_id=1, source_target_pairs={{0,1},{1,0},{2,3},{3,2},{4,5},{5,4},{6,7},{7,6},{8,9},{9,8},{10,11... | collective-permute-start | bytes 589832 | tf_op jit(solution)/shard_map/ppermute | solution.py:349
  65.0 5.9 %collective-permute-start.18 = (f32[256,128]{1,0:T(8,128)S(1)}, f32[256,128]{1,0:T(8,128)S(1)}, u32[]{:S(2)}, u32[]{:S(2)}) collective-permute-start(f32[256,128]{1,0:T(8,128)S(1)} %add.30), channel_id=1, source_target_pairs={{0,4},{2,6},{4,0},{6,2},{8,12},{10,14},{12,8},{14,10},{1,5},{3,7},... | collective-permute-start | bytes 393224 | tf_op jit(solution)/shard_map/ppermute | solution.py:355
  70.9 9.6 %collective-permute-start.20 = (f32[256,128]{1,0:T(8,128)S(1)}, f32[256,128]{1,0:T(8,128)S(1)}, u32[]{:S(2)}, u32[]{:S(2)}) collective-permute-start(f32[256,128]{1,0:T(8,128)S(1)} %add.31), channel_id=1, source_target_pairs={{0,8},{2,10},{4,12},{6,14},{8,0},{10,2},{12,4},{14,6},{1,9},{3,11}... | collective-permute-start | bytes 393224 | tf_op jit(solution)/shard_map/ppermute | solution.py:355
  80.6 1.4 %collective-permute-start.21 = (f32[256,128]{1,0:T(8,128)S(1)}, f32[256,128]{1,0:T(8,128)S(1)}, u32[]{:S(2)}, u32[]{:S(2)}) collective-permute-start(f32[256,128]{1,0:T(8,128)S(1)} %add.32.own), channel_id=1, source_target_pairs={{0,1},{1,0},{2,3},{3,2},{4,5},{5,4},{6,7},{7,6},{8,9},{9,8},{10,11... | collective-permute-start | bytes 393224 | tf_op jit(solution)/shard_map/ppermute | solution.py:349

commit v10 on v9

--- a/solution.py
+++ b/solution.py
@@ -24,7 +24,7 @@
     return high, low
 
 
-def pack_kernel(info, sites, held, leads, out):
+def pack_kernel(info, held, leads, out):
     layers, cross_local, slots, size, _ = held.shape
     contacts = leads.shape[0]
     for layer in range(layers):
@@ -34,7 +34,7 @@
             for k in range(contacts):
                 end, flag = (0, info[1]) if k < contacts // 2 else (layers - 1, info[2])
                 if layer == end:
-                    here = jnp.logical_and(flag == 1, sites[k] == place)
+                    here = jnp.logical_and(flag == 1, info[4 + k] == place)
                     lead = lead - leads[k] * jnp.where(here, 1.0, 0.0)
             blocks = [held[layer, q, j] for j in range(slots)] + [lead]
             row = jnp.concatenate(
@@ -46,13 +46,13 @@
             out[layer * cross_local + q, size:] = low
 
 
-def pack(couplings, lead_sites, lead_sigma, info):
+def pack(couplings, lead_sigma, info):
     layers, cross_local, slots, size, _ = couplings.shape
     scalar = pl.BlockSpec(memory_space=pltpu.SMEM)
     whole = pl.BlockSpec(memory_space=pltpu.VMEM)
     return pl.pallas_call(
         pack_kernel,
-        in_specs=[scalar, scalar, whole, whole],
+        in_specs=[scalar, whole, whole],
         out_specs=whole,
         out_shape=jax.ShapeDtypeStruct(
             (layers * cross_local, 2 * size, (slots + 1) * size), jnp.bfloat16
@@ -60,7 +60,7 @@
         compiler_params=pltpu.CompilerParams(vmem_limit_bytes=VMEM_LIMIT),
         cost_estimate=estimate(2.5),
         name="pack",
-    )(info, lead_sites, couplings, lead_sigma)
+    )(info, couplings, lead_sigma)
 
 
 def step_kernel(first, last, slots, info, cols, packed, own, other, *refs):
@@ -337,9 +337,10 @@
     count = lax.axis_size("trans")
     place = lax.axis_index("trans")
     even = 1 - place % 2
-    info = jnp.stack([lax.axis_index("cross"), place == 0, place == count - 1, even])
+    sites = [lead_sites[k] for k in range(lead_sites.shape[0])]
+    info = jnp.stack([lax.axis_index("cross"), place == 0, place == count - 1, even, *sites])
     info = info.astype(jnp.int32)
-    packed = pack(couplings, lead_sites, lead_sigma, info)
+    packed = pack(couplings, lead_sigma, info)
     scale_rows = math.sqrt(count * layers * cross_local * cross_count * size)
 
     near = [(i, i ^ 1) for i in range(count) if i ^ 1 < count]

time: 89.9 us -> 89.9 us (level)
    unnamed x14 -> x12, local copies, waits for them, and re-layouts: 5.19 us -> 4.54 us
  transfers between devices with their start and end apart: 24 -> 24, of which waited for: 13 -> 13; matrix products, arithmetic and copies ran while one was open for 2% -> 3% of each run, Pallas kernels for 19% -> 19%
where the time goes in v10:
time: 89.9 us; the launch traced here: 89.5 us
  starting transfers between devices  33.6 us (37%)
  Pallas kernels  28 us (31%)
  waiting for transfers between devices  19.4 us (22%)
  local copies, waits for them, and re-layouts  6.95 us (8%)
    pallas_call x4, Pallas kernels, column(): pl.pallas_call(functools.partial(column_kernel, place, first, scale), in_...  15.5 us
    all_to_all x2, starting transfers between devices, exchange(): return lax.all_to_all(x, 'trans', 0, 0, tiled=True)  12.2 us
    ppermute x3, starting transfers between devices, local(): near_edge = lax.ppermute(near_layer, 'trans', near)  11.2 us
    ppermute x3, waiting for transfers between devices, double(): other = lax.ppermute(x, 'trans', [(i, i ^ reach) for i in range(count)])  6.2 us
    pallas_call x3, Pallas kernels, step(): pl.pallas_call(functools.partial(step_kernel, before is None, last, cols....  5.05 us
    ppermute x13, waiting for transfers between devices, swap(): return lax.ppermute(x, 'cross', [(0, 1), (1, 0)])  5.01 us
    ppermute x3, starting transfers between devices, double(): other = lax.ppermute(x, 'trans', [(i, i ^ reach) for i in range(count)])  4.8 us
    ppermute x3, waiting for transfers between devices, local(): near_edge = lax.ppermute(near_layer, 'trans', near)  4.77 us
  transfers between devices with their start and end apart: 24, of which 13 were waited for; matrix products, arithmetic and copies ran while one was open for 3% of the time, Pallas kernels for 19%

profile of v10, /device:TPU:0, one launch (start us, length us, event | category | flops | bytes accessed | tf_op | source)
XLA Modules:
  0.0 89.5 jit_solution(4159780973693843095)
XLA Ops:
  0.6 0.5 collective-permute-start.2
  1.1 1.0 %constant_dynamic-slice_fusion = (f32[1,4,64,128]{3,2,1,0:T(8,128)S(1)}, f32[1,4,64,128]{3,2,1,0:T(8,128)S(1)}) fusion(f32[4,4,64,128]{3,2,1,0:T(8,128)} %refs_0_.5, s32[]{:T(128)S(6)} %select_n.15, s32[]{:T(128)S(6)} %select_n.14), kind=kLoop, calls=%fused_computation | loop fusion | bytes 524296 | tf_op jit(solution)/shard_map/dynamic_slice | solution.py:361
  2.1 2.6 %collective-permute-start.1 = (f32[1,4,64,128]{3,2,1,0:T(8,128)S(1)}, f32[1,4,64,128]{3,2,1,0:T(8,128)S(1)}, u32[]{:S(2)}, u32[]{:S(2)}) collective-permute-start(f32[1,4,64,128]{3,2,1,0:T(8,128)S(1)} %get-tuple-element.56), channel_id=1, source_target_pairs={{0,2},{2,0},{4,6},{6,4},{8,10},{10,8},{12,14},{14,12},{1,3},{3,1},... | collective-permute-start | bytes 393224 | tf_op jit(solution)/shard_map/ppermute | solution.py:365
  4.7 0.7 collective-permute-start
  5.4 0.7 stack.27.info
  6.1 2.0 %copy-done.1 = f32[4,4,7,64,64]{4,3,2,1,0:T(8,128)S(1)} copy-done((f32[4,4,7,64,64]{4,3,2,1,0:T(8,128)S(1)}, f32[4,4,7,64,64]{4,3,2,1,0:T(8,128)}, u32[]{:S(2)}) %copy-start.1) | copy-done | bytes 1835032
  8.2 0.9 %copy-done.2 = f32[4,64,64]{2,1,0:T(8,128)S(1)} copy-done((f32[4,64,64]{2,1,0:T(8,128)S(1)}, f32[4,64,64]{2,1,0:T(8,128)}, u32[]{:S(2)}) %copy-start.2) | copy-done | bytes 65560
  9.1 1.1 %pack.1.packed = bf16[16,128,512]{2,1,0:T(8,128)(2,1)S(1)} custom-call(s32[8]{0:T(128)S(1)} %stack.27.info, f32[4,4,7,64,64]{4,3,2,1,0:T(8,128)S(1)} %copy-done.1, f32[4,64,64]{2,1,0:T(8,128)S(1)} %copy-done.2), custom_call_target="tpu_custom_call" | custom-call | flops 2875000064 | tf_op jit(solution)/shard_map/pack/pallas_call | solution.py:53
  10.2 0.2 collective-permute-start.3
  10.5 0.3 collective-permute-start.4
  10.8 0.8 collective-permute-done.3.refs_1_
  11.8 1.7 %step.3 = (f32[4,4,64,128]{3,2,1,0:T(8,128)S(1)}, f32[1,4,64,128]{3,2,1,0:T(8,128)S(1)}, f32[1,4,64,128]{3,2,1,0:T(8,128)S(1)}) custom-call(s32[8]{0:T(128)S(1)} %stack.27.info, s32[4,4,7]{2,1,0:T(4,128)S(1)} %copy-done.3, bf16[16,128,512]{2,1,0:T(8,128)(2,1)S(1)} %pack.1.packed, f32[4,4,64,128]{3,2,1,0:T(8,128)S(1)} %copy-done, ...), custom_call_target="tpu_custom_call" | custom-call | flops 1955000064 | tf_op jit(solution)/shard_map/step/pallas_call | solution.py:114
  13.5 0.4 collective-permute-start.5
  13.9 4.3 %collective-permute-start.6 = (f32[1,4,64,128]{3,2,1,0:T(8,128)S(1)}, f32[1,4,64,128]{3,2,1,0:T(8,128)S(1)}, u32[]{:S(2)}, u32[]{:S(2)}) collective-permute-start(f32[1,4,64,128]{3,2,1,0:T(8,128)S(1)} %get-tuple-element.33), channel_id=1, source_target_pairs={{0,2},{2,0},{4,6},{6,4},{8,10},{10,8},{12,14},{14,12},{1,3},{3,1},... | collective-permute-start | bytes 393224 | tf_op jit(solution)/shard_map/ppermute | solution.py:365
  18.2 0.7 collective-permute-start.8
  18.8 3.2 %collective-permute-done.6.refs_0_ = f32[1,4,64,128]{3,2,1,0:T(8,128)S(1)} collective-permute-done((f32[1,4,64,128]{3,2,1,0:T(8,128)S(1)}, f32[1,4,64,128]{3,2,1,0:T(8,128)S(1)}, u32[]{:S(2)}, u32[]{:S(2)}) %collective-permute-start.6) | collective-permute-done | bytes 131104 | tf_op jit(solution)/shard_map/ppermute | solution.py:365
  22.0 0.5 collective-permute-start.9
  22.5 0.8 collective-permute-done.7.refs_1_
  23.6 1.7 %step.4 = (f32[4,4,64,128]{3,2,1,0:T(8,128)S(1)}, f32[1,4,64,128]{3,2,1,0:T(8,128)S(1)}, f32[1,4,64,128]{3,2,1,0:T(8,128)S(1)}) custom-call(s32[8]{0:T(128)S(1)} %stack.27.info, s32[4,4,7]{2,1,0:T(4,128)S(1)} %copy-done.3, bf16[16,128,512]{2,1,0:T(8,128)(2,1)S(1)} %pack.1.packed, f32[4,4,64,128]{3,2,1,0:T(8,128)S(1)} %get-tuple-element.32.own.refs_4_.refs_1_, ...), custom_call_target="tpu_custom_call" | custom-call | flops 1955000064 | tf_op jit(solution)/shard_map/step/pallas_call | solution.py:114
  25.3 0.4 collective-permute-start.10
  25.7 4.3 %collective-permute-start.11 = (f32[1,4,64,128]{3,2,1,0:T(8,128)S(1)}, f32[1,4,64,128]{3,2,1,0:T(8,128)S(1)}, u32[]{:S(2)}, u32[]{:S(2)}) collective-permute-start(f32[1,4,64,128]{3,2,1,0:T(8,128)S(1)} %get-tuple-element.36), channel_id=1, source_target_pairs={{0,2},{2,0},{4,6},{6,4},{8,10},{10,8},{12,14},{14,12},{1,3},{3,1},... | collective-permute-start | bytes 393224 | tf_op jit(solution)/shard_map/ppermute | solution.py:365
  30.0 0.7 collective-permute-start.13
  30.6 1.6 %gram.3 = (f32[384,128]{1,0:T(8,128)S(1)}, f32[384,128]{1,0:T(8,128)S(1)}) custom-call(s32[8]{0:T(128)S(1)} %stack.27.info, f32[4,4,64,128]{3,2,1,0:T(8,128)S(1)} %copy-done, f32[4,4,64,128]{3,2,1,0:T(8,128)S(1)} %get-tuple-element.32.own.refs_4_.refs_1_, f32[4,4,64,128]{3,2,1,0:T(8,128)S(1)} %get-tuple-element.35.own.refs_2_), custom_call_target="tpu_custom_call" | custom-call | flops 1610000000 | tf_op jit(solution)/shard_map/gram/pallas_call | solution.py:156
  32.4 1.6 %collective-permute-done.11.refs_0_ = f32[1,4,64,128]{3,2,1,0:T(8,128)S(1)} collective-permute-done((f32[1,4,64,128]{3,2,1,0:T(8,128)S(1)}, f32[1,4,64,128]{3,2,1,0:T(8,128)S(1)}, u32[]{:S(2)}, u32[]{:S(2)}) %collective-permute-start.11) | collective-permute-done | bytes 131104 | tf_op jit(solution)/shard_map/ppermute | solution.py:365
  34.0 0.5 collective-permute-start.14
  34.5 0.7 add.29
  35.2 8.7 %all-to-all-start = ((f32[8,48,128]{2,1,0:T(8,128)}), f32[8,48,128]{2,1,0:T(8,128)S(1)}, u32[]{:S(2)}, u32[]{:S(2)}) async-start(f32[8,48,128]{2,1,0:T(8,128)} %bitcast.4), calls=%async_computation | async-start | bytes 393216 | tf_op jit(solution)/shard_map/all_to_all | solution.py:353
  43.9 1.6 %copy-done.5 = bf16[16,128,512]{2,1,0:T(8,128)(2,1)S(1)} copy-done((bf16[16,128,512]{2,1,0:T(8,128)(2,1)S(1)}, bf16[16,128,512]{2,1,0:T(8,128)(2,1)}, u32[]{:S(2)}) %copy-start.5) | copy-done | bytes 2097176
  45.5 1.7 %step.5.refs_3_ = f32[4,4,64,128]{3,2,1,0:T(8,128)S(1)} custom-call(s32[8]{0:T(128)S(1)} %stack.27.info, s32[4,4,7]{2,1,0:T(4,128)S(1)} %copy-done.3, bf16[16,128,512]{2,1,0:T(8,128)(2,1)S(1)} %copy-done.5, f32[4,4,64,128]{3,2,1,0:T(8,128)S(1)} %get-tuple-element.35.own.refs_2_, f32[4,4,64,128]{3,2,1,0:T(8,128)S(1)} %collective-permute-done.10.other, ...), custom_call_target="tpu_custom_call" | custom-call | flops 1955000064 | tf_op jit(solution)/shard_map/step/pallas_call | solution.py:114
  47.2 1.4 %gram.2 = (f32[256,128]{1,0:T(8,128)S(1)}, f32[256,128]{1,0:T(8,128)S(1)}) custom-call(s32[8]{0:T(128)S(1)} %stack.27.info, f32[4,4,64,128]{3,2,1,0:T(8,128)S(1)} %copy-done, f32[4,4,64,128]{3,2,1,0:T(8,128)S(1)} %get-tuple-element.32.own.refs_4_.refs_1_, f32[4,4,64,128]{3,2,1,0:T(8,128)S(1)} %get-tuple-element.35.own.refs_2_, f32[4,4,64,128]{3,2,1,0:T(8,128)S(1)} %step.5.refs_3_), custom_call_target="tpu_custom_call" | custom-call | flops 1610000000 | tf_op jit(solution)/shard_map/gram/pallas_call | solution.py:156
  48.6 0.3 collective-permute-start.15
  48.9 1.1 %collective-permute-done.15 = f32[256,128]{1,0:T(8,128)S(1)} collective-permute-done((f32[256,128]{1,0:T(8,128)S(1)}, f32[256,128]{1,0:T(8,128)S(1)}, u32[]{:S(2)}, u32[]{:S(2)}) %collective-permute-start.15) | collective-permute-done | bytes 131104 | tf_op jit(solution)/shard_map/ppermute | solution.py:350
  50.0 2.4 %all-to-all-done = f32[8,48,128]{2,1,0:T(8,128)S(1)} async-done(((f32[8,48,128]{2,1,0:T(8,128)}), f32[8,48,128]{2,1,0:T(8,128)S(1)}, u32[]{:S(2)}, u32[]{:S(2)}) %all-to-all-start) | async-done | bytes 196640 | tf_op jit(solution)/shard_map/all_to_all | solution.py:353
  52.5 0.7 broadcast_in_dim.2
  53.2 3.6 %all-to-all-start.1 = ((f32[8,48,128]{2,1,0:T(8,128)}), f32[8,48,128]{2,1,0:T(8,128)S(1)}, u32[]{:S(2)}, u32[]{:S(2)}) async-start(f32[8,48,128]{2,1,0:T(8,128)} %broadcast_in_dim.2), calls=%async_computation.1 | async-start | bytes 393216 | tf_op jit(solution)/shard_map/all_to_all | solution.py:353
  56.8 2.0 %collective-permute-start.17 = (f32[256,128]{1,0:T(8,128)S(1)}, f32[256,128]{1,0:T(8,128)S(1)}, u32[]{:S(2)}, u32[]{:S(2)}) collective-permute-start(f32[256,128]{1,0:T(8,128)S(1)} %add.28), channel_id=1, source_target_pairs={{0,2},{2,0},{4,6},{6,4},{8,10},{10,8},{12,14},{14,12},{1,3},{3,1},... | collective-permute-start | bytes 393224 | tf_op jit(solution)/shard_map/ppermute | solution.py:356
  58.8 5.3 %collective-permute-done.17 = f32[256,128]{1,0:T(8,128)S(1)} collective-permute-done((f32[256,128]{1,0:T(8,128)S(1)}, f32[256,128]{1,0:T(8,128)S(1)}, u32[]{:S(2)}, u32[]{:S(2)}) %collective-permute-start.17) | collective-permute-done | bytes 131104 | tf_op jit(solution)/shard_map/ppermute | solution.py:356
  64.1 0.9 %all-to-all-done.1 = f32[8,48,128]{2,1,0:T(8,128)S(1)} async-done(((f32[8,48,128]{2,1,0:T(8,128)}), f32[8,48,128]{2,1,0:T(8,128)S(1)}, u32[]{:S(2)}, u32[]{:S(2)}) %all-to-all-start.1) | async-done | bytes 196640 | tf_op jit(solution)/shard_map/all_to_all | solution.py:353
  65.0 0.9 %collective-permute-start.18 = (f32[256,128]{1,0:T(8,128)S(1)}, f32[256,128]{1,0:T(8,128)S(1)}, u32[]{:S(2)}, u32[]{:S(2)}) collective-permute-start(f32[256,128]{1,0:T(8,128)S(1)} %add.30), channel_id=1, source_target_pairs={{0,4},{2,6},{4,0},{6,2},{8,12},{10,14},{12,8},{14,10},{1,5},{3,7},... | collective-permute-start | bytes 393224 | tf_op jit(solution)/shard_map/ppermute | solution.py:356
  66.0 0.5 collective-permute-done.19.other
  66.4 3.6 %column.4 = (f32[128,128]{1,0:T(8,128)S(1)}, f32[128,128]{1,0:T(8,128)S(1)}) custom-call(s32[8]{0:T(128)S(1)} %stack.27.info, f32[384,128]{1,0:T(8,128)S(1)} %bitcast.7, f32[384,128]{1,0:T(8,128)S(1)} %collective-permute-done.19.other), custom_call_target="tpu_custom_call" | custom-call | flops 4600000000 | tf_op jit(solution)/shard_map/column/pallas_call | solution.py:273
  70.0 0.9 %collective-permute-done.18 = f32[256,128]{1,0:T(8,128)S(1)} collective-permute-done((f32[256,128]{1,0:T(8,128)S(1)}, f32[256,128]{1,0:T(8,128)S(1)}, u32[]{:S(2)}, u32[]{:S(2)}) %collective-permute-start.18) | collective-permute-done | bytes 131104 | tf_op jit(solution)/shard_map/ppermute | solution.py:356
  70.9 1.8 %collective-permute-start.20 = (f32[256,128]{1,0:T(8,128)S(1)}, f32[256,128]{1,0:T(8,128)S(1)}, u32[]{:S(2)}, u32[]{:S(2)}) collective-permute-start(f32[256,128]{1,0:T(8,128)S(1)} %add.31), channel_id=1, source_target_pairs={{0,8},{2,10},{4,12},{6,14},{8,0},{10,2},{12,4},{14,6},{1,9},{3,11}... | collective-permute-start | bytes 393224 | tf_op jit(solution)/shard_map/ppermute | solution.py:356
  72.8 3.8 %column.5 = (f32[256,256]{1,0:T(8,128)S(1)}, f32[256,256]{1,0:T(8,128)S(1)}) custom-call(s32[8]{0:T(128)S(1)} %stack.27.info, f32[384,128]{1,0:T(8,128)S(1)} %bitcast.8, f32[384,128]{1,0:T(8,128)S(1)} %collective-permute-done.19.other, f32[128,128]{1,0:T(8,128)S(1)} %get-tuple-element.47.refs_0_, f32[128,128]{1,0:T(8,128)S(1)} %get-tuple-element.46.refs_1_), custom_call_target="tpu_custom_call" | custom-call | flops 4600000000 | tf_op jit(solution)/shard_map/column/pallas_call | solution.py:273
  76.6 3.9 %column.6 = (f32[384,384]{1,0:T(8,128)S(1)}, f32[384,384]{1,0:T(8,128)S(1)}) custom-call(s32[8]{0:T(128)S(1)} %stack.27.info, f32[384,128]{1,0:T(8,128)S(1)} %bitcast.9, f32[384,128]{1,0:T(8,128)S(1)} %collective-permute-done.19.other, f32[256,256]{1,0:T(8,128)S(1)} %get-tuple-element.49.refs_0_, f32[256,256]{1,0:T(8,128)S(1)} %get-tuple-element.50.refs_1_), custom_call_target="tpu_custom_call" | custom-call | flops 4600000000 | tf_op jit(solution)/shard_map/column/pallas_call | solution.py:273
  80.7 1.3 %collective-permute-done.21.other = f32[256,128]{1,0:T(8,128)S(1)} collective-permute-done((f32[256,128]{1,0:T(8,128)S(1)}, f32[256,128]{1,0:T(8,128)S(1)}, u32[]{:S(2)}, u32[]{:S(2)}) %collective-permute-start.21) | collective-permute-done | bytes 131104 | tf_op jit(solution)/shard_map/ppermute | solution.py:350
  82.0 4.2 %column.7 = (f32[512,512]{1,0:T(8,128)S(1)}, f32[512,512]{1,0:T(8,128)S(1)}) custom-call(s32[8]{0:T(128)S(1)} %stack.27.info, f32[256,128]{1,0:T(8,128)S(1)} %add.32.own, f32[256,128]{1,0:T(8,128)S(1)} %collective-permute-done.21.other, f32[384,384]{1,0:T(8,128)S(1)} %get-tuple-element.52.refs_0_, f32[384,384]{1,0:T(8,128)S(1)} %get-tuple-element.51.refs_1_), custom_call_target="tpu_custom_call" | custom-call | flops 4600000000 | tf_op jit(solution)/shard_map/column/pallas_call | solution.py:273
  86.2 3.3 %basis.1 = (bf16[4,4,64,512]{3,2,1,0:T(8,128)(2,1)}, f32[512,512]{1,0:T(8,128)}) custom-call(f32[4,4,64,128]{3,2,1,0:T(8,128)S(1)} %copy-done, f32[4,4,64,128]{3,2,1,0:T(8,128)S(1)} %get-tuple-element.32.own.refs_4_.refs_1_, f32[4,4,64,128]{3,2,1,0:T(8,128)S(1)} %get-tuple-element.35.own.refs_2_, f32[4,4,64,128]{3,2,1,0:T(8,128)S(1)} %step.5.refs_3_, ...), custom_call_target="tpu_custom_call" | custom-call | flops 3449999872 | tf_op jit(solution)/shard_map/basis/pallas_call | solution.py:317
  (32 shorter events, 0.7 us)
Async XLA Ops:
  0.6 11.2 %collective-permute-start.2 = (f32[4,4,64,128]{3,2,1,0:T(8,128)}, f32[4,4,64,128]{3,2,1,0:T(8,128)S(1)}, u32[]{:S(2)}, u32[]{:S(2)}) collective-permute-start(f32[4,4,64,128]{3,2,1,0:T(8,128)} %refs_0_.5), channel_id=1, source_target_pairs={{0,1},{1,0},{2,3},{3,2},{4,5},{5,4},{6,7},{7,6},{8,9},{9,8},{10,11... | collective-permute-start | bytes 1572872 | tf_op jit(solution)/shard_map/ppermute | solution.py:350
  2.1 8.1 %collective-permute-start.1 = (f32[1,4,64,128]{3,2,1,0:T(8,128)S(1)}, f32[1,4,64,128]{3,2,1,0:T(8,128)S(1)}, u32[]{:S(2)}, u32[]{:S(2)}) collective-permute-start(f32[1,4,64,128]{3,2,1,0:T(8,128)S(1)} %get-tuple-element.56), channel_id=1, source_target_pairs={{0,2},{2,0},{4,6},{6,4},{8,10},{10,8},{12,14},{14,12},{1,3},{3,1},... | collective-permute-start | bytes 393224 | tf_op jit(solution)/shard_map/ppermute | solution.py:365
  4.7 5.5 %collective-permute-start = (f32[1,4,64,128]{3,2,1,0:T(8,128)S(1)}, f32[1,4,64,128]{3,2,1,0:T(8,128)S(1)}, u32[]{:S(2)}, u32[]{:S(2)}) collective-permute-start(f32[1,4,64,128]{3,2,1,0:T(8,128)S(1)} %get-tuple-element.57), channel_id=1, source_target_pairs={{2,4},{4,2},{6,8},{8,6},{10,12},{12,10},{3,5},{5,3},{7,9},{9,7},{1... | collective-permute-start | bytes 393224 | tf_op jit(solution)/shard_map/ppermute | solution.py:366
  6.1 2.0 %copy-start.1 = (f32[4,4,7,64,64]{4,3,2,1,0:T(8,128)S(1)}, f32[4,4,7,64,64]{4,3,2,1,0:T(8,128)}, u32[]{:S(2)}) copy-start(f32[4,4,7,64,64]{4,3,2,1,0:T(8,128)} %held.1) | copy-start | bytes 5505028
  8.2 0.9 %copy-start.2 = (f32[4,64,64]{2,1,0:T(8,128)S(1)}, f32[4,64,64]{2,1,0:T(8,128)}, u32[]{:S(2)}) copy-start(f32[4,64,64]{2,1,0:T(8,128)} %leads.1) | copy-start | bytes 196612
  9.1 2.7 %copy-start = (f32[4,4,64,128]{3,2,1,0:T(8,128)S(1)}, f32[4,4,64,128]{3,2,1,0:T(8,128)}, u32[]{:S(2)}) copy-start(f32[4,4,64,128]{3,2,1,0:T(8,128)} %refs_0_.5) | copy-start | bytes 1572868
  9.1 2.7 %copy-start.3 = (s32[4,4,7]{2,1,0:T(4,128)S(1)}, s32[4,4,7]{2,1,0:T(4,128)}, u32[]{:S(2)}) copy-start(s32[4,4,7]{2,1,0:T(4,128)} %cols.5) | copy-start | bytes 1348
  10.2 15.1 %copy-start.4 = (bf16[16,128,512]{2,1,0:T(8,128)(2,1)}, bf16[16,128,512]{2,1,0:T(8,128)(2,1)S(1)}, u32[]{:S(2)}) copy-start(bf16[16,128,512]{2,1,0:T(8,128)(2,1)S(1)} %pack.1.packed) | copy-start | bytes 6291460
  10.2 1.4 %collective-permute-start.3 = (f32[1,4,64,128]{3,2,1,0:T(8,128)S(1)}, f32[1,4,64,128]{3,2,1,0:T(8,128)S(1)}, u32[]{:S(2)}, u32[]{:S(2)}) collective-permute-start(f32[1,4,64,128]{3,2,1,0:T(8,128)S(1)} %collective-permute-done.1.refs_0_), channel_id=1, source_target_pairs={{0,1},{1,0},{2,3},{3,2},{4,5},{5,4},{6,7},{7,6},{8,9},{9,8},{10,11... | collective-permute-start | bytes 393224 | tf_op jit(solution)/shard_map/ppermute | solution.py:350
  10.5 1.4 %collective-permute-start.4 = (f32[1,4,64,128]{3,2,1,0:T(8,128)S(1)}, f32[1,4,64,128]{3,2,1,0:T(8,128)S(1)}, u32[]{:S(2)}, u32[]{:S(2)}) collective-permute-start(f32[1,4,64,128]{3,2,1,0:T(8,128)S(1)} %collective-permute-done.refs_2_), channel_id=1, source_target_pairs={{0,1},{1,0},{2,3},{3,2},{4,5},{5,4},{6,7},{7,6},{8,9},{9,8},{10,11... | collective-permute-start | bytes 393224 | tf_op jit(solution)/shard_map/ppermute | solution.py:350
  13.5 10.1 %collective-permute-start.5 = (f32[4,4,64,128]{3,2,1,0:T(8,128)S(1)}, f32[4,4,64,128]{3,2,1,0:T(8,128)S(1)}, u32[]{:S(2)}, u32[]{:S(2)}) collective-permute-start(f32[4,4,64,128]{3,2,1,0:T(8,128)S(1)} %get-tuple-element.32.own.refs_4_.refs_1_), channel_id=1, source_target_pairs={{0,1},{1,0},{2,3},{3,2},{4,5},{5,4},{6,7},{7,6},{8,9},{9,8},{10,11... | collective-permute-start | bytes 1572872 | tf_op jit(solution)/shard_map/ppermute | solution.py:350
  13.9 8.1 %collective-permute-start.6 = (f32[1,4,64,128]{3,2,1,0:T(8,128)S(1)}, f32[1,4,64,128]{3,2,1,0:T(8,128)S(1)}, u32[]{:S(2)}, u32[]{:S(2)}) collective-permute-start(f32[1,4,64,128]{3,2,1,0:T(8,128)S(1)} %get-tuple-element.33), channel_id=1, source_target_pairs={{0,2},{2,0},{4,6},{6,4},{8,10},{10,8},{12,14},{14,12},{1,3},{3,1},... | collective-permute-start | bytes 393224 | tf_op jit(solution)/shard_map/ppermute | solution.py:365
  18.2 3.9 %collective-permute-start.8 = (f32[1,4,64,128]{3,2,1,0:T(8,128)S(1)}, f32[1,4,64,128]{3,2,1,0:T(8,128)S(1)}, u32[]{:S(2)}, u32[]{:S(2)}) collective-permute-start(f32[1,4,64,128]{3,2,1,0:T(8,128)S(1)} %get-tuple-element.34), channel_id=1, source_target_pairs={{2,4},{4,2},{6,8},{8,6},{10,12},{12,10},{3,5},{5,3},{7,9},{9,7},{1... | collective-permute-start | bytes 393224 | tf_op jit(solution)/shard_map/ppermute | solution.py:366
  22.0 1.3 %collective-permute-start.7 = (f32[1,4,64,128]{3,2,1,0:T(8,128)S(1)}, f32[1,4,64,128]{3,2,1,0:T(8,128)S(1)}, u32[]{:S(2)}, u32[]{:S(2)}) collective-permute-start(f32[1,4,64,128]{3,2,1,0:T(8,128)S(1)} %collective-permute-done.6.refs_0_), channel_id=1, source_target_pairs={{0,1},{1,0},{2,3},{3,2},{4,5},{5,4},{6,7},{7,6},{8,9},{9,8},{10,11... | collective-permute-start | bytes 393224 | tf_op jit(solution)/shard_map/ppermute | solution.py:350
  22.0 1.5 %collective-permute-start.9 = (f32[1,4,64,128]{3,2,1,0:T(8,128)S(1)}, f32[1,4,64,128]{3,2,1,0:T(8,128)S(1)}, u32[]{:S(2)}, u32[]{:S(2)}) collective-permute-start(f32[1,4,64,128]{3,2,1,0:T(8,128)S(1)} %collective-permute-done.8.refs_2_), channel_id=1, source_target_pairs={{0,1},{1,0},{2,3},{3,2},{4,5},{5,4},{6,7},{7,6},{8,9},{9,8},{10,11... | collective-permute-start | bytes 393224 | tf_op jit(solution)/shard_map/ppermute | solution.py:350
  25.3 18.6 %collective-permute-start.10 = (f32[4,4,64,128]{3,2,1,0:T(8,128)S(1)}, f32[4,4,64,128]{3,2,1,0:T(8,128)S(1)}, u32[]{:S(2)}, u32[]{:S(2)}) collective-permute-start(f32[4,4,64,128]{3,2,1,0:T(8,128)S(1)} %get-tuple-element.35.own.refs_2_), channel_id=1, source_target_pairs={{0,1},{1,0},{2,3},{3,2},{4,5},{5,4},{6,7},{7,6},{8,9},{9,8},{10,11... | collective-permute-start | bytes 1572872 | tf_op jit(solution)/shard_map/ppermute | solution.py:350
  25.7 8.3 %collective-permute-start.11 = (f32[1,4,64,128]{3,2,1,0:T(8,128)S(1)}, f32[1,4,64,128]{3,2,1,0:T(8,128)S(1)}, u32[]{:S(2)}, u32[]{:S(2)}) collective-permute-start(f32[1,4,64,128]{3,2,1,0:T(8,128)S(1)} %get-tuple-element.36), channel_id=1, source_target_pairs={{0,2},{2,0},{4,6},{6,4},{8,10},{10,8},{12,14},{14,12},{1,3},{3,1},... | collective-permute-start | bytes 393224 | tf_op jit(solution)/shard_map/ppermute | solution.py:365
  30.0 4.0 %collective-permute-start.13 = (f32[1,4,64,128]{3,2,1,0:T(8,128)S(1)}, f32[1,4,64,128]{3,2,1,0:T(8,128)S(1)}, u32[]{:S(2)}, u32[]{:S(2)}) collective-permute-start(f32[1,4,64,128]{3,2,1,0:T(8,128)S(1)} %get-tuple-element.37), channel_id=1, source_target_pairs={{2,4},{4,2},{6,8},{8,6},{10,12},{12,10},{3,5},{5,3},{7,9},{9,7},{1... | collective-permute-start | bytes 393224 | tf_op jit(solution)/shard_map/ppermute | solution.py:366
  32.3 2.2 %collective-permute-start.16 = (f32[384,128]{1,0:T(8,128)S(1)}, f32[384,128]{1,0:T(8,128)S(1)}, u32[]{:S(2)}, u32[]{:S(2)}) collective-permute-start(f32[384,128]{1,0:T(8,128)S(1)} %get-tuple-element.41), channel_id=1, source_target_pairs={{0,1},{1,0},{2,3},{3,2},{4,5},{5,4},{6,7},{7,6},{8,9},{9,8},{10,11... | collective-permute-start | bytes 589832 | tf_op jit(solution)/shard_map/ppermute | solution.py:350
  34.0 9.9 %collective-permute-start.12 = (f32[1,4,64,128]{3,2,1,0:T(8,128)S(1)}, f32[1,4,64,128]{3,2,1,0:T(8,128)S(1)}, u32[]{:S(2)}, u32[]{:S(2)}) collective-permute-start(f32[1,4,64,128]{3,2,1,0:T(8,128)S(1)} %collective-permute-done.11.refs_0_), channel_id=1, source_target_pairs={{0,1},{1,0},{2,3},{3,2},{4,5},{5,4},{6,7},{7,6},{8,9},{9,8},{10,11... | collective-permute-start | bytes 393224 | tf_op jit(solution)/shard_map/ppermute | solution.py:350
  34.0 9.9 %collective-permute-start.14 = (f32[1,4,64,128]{3,2,1,0:T(8,128)S(1)}, f32[1,4,64,128]{3,2,1,0:T(8,128)S(1)}, u32[]{:S(2)}, u32[]{:S(2)}) collective-permute-start(f32[1,4,64,128]{3,2,1,0:T(8,128)S(1)} %collective-permute-done.13.refs_2_), channel_id=1, source_target_pairs={{0,1},{1,0},{2,3},{3,2},{4,5},{5,4},{6,7},{7,6},{8,9},{9,8},{10,11... | collective-permute-start | bytes 393224 | tf_op jit(solution)/shard_map/ppermute | solution.py:350
  35.2 17.3 %all-to-all-start = ((f32[8,48,128]{2,1,0:T(8,128)}), f32[8,48,128]{2,1,0:T(8,128)S(1)}, u32[]{:S(2)}, u32[]{:S(2)}) async-start(f32[8,48,128]{2,1,0:T(8,128)} %bitcast.4), calls=%async_computation | async-start | bytes 393216 | tf_op jit(solution)/shard_map/all_to_all | solution.py:353
  43.9 1.6 %copy-start.5 = (bf16[16,128,512]{2,1,0:T(8,128)(2,1)S(1)}, bf16[16,128,512]{2,1,0:T(8,128)(2,1)}, u32[]{:S(2)}) copy-start(bf16[16,128,512]{2,1,0:T(8,128)(2,1)} %copy-done.4) | copy-start | bytes 6291460
  48.6 1.4 %collective-permute-start.15 = (f32[256,128]{1,0:T(8,128)S(1)}, f32[256,128]{1,0:T(8,128)S(1)}, u32[]{:S(2)}, u32[]{:S(2)}) collective-permute-start(f32[256,128]{1,0:T(8,128)S(1)} %get-tuple-element.39), channel_id=1, source_target_pairs={{0,1},{1,0},{2,3},{3,2},{4,5},{5,4},{6,7},{7,6},{8,9},{9,8},{10,11... | collective-permute-start | bytes 393224 | tf_op jit(solution)/shard_map/ppermute | solution.py:350
  53.2 11.8 %all-to-all-start.1 = ((f32[8,48,128]{2,1,0:T(8,128)}), f32[8,48,128]{2,1,0:T(8,128)S(1)}, u32[]{:S(2)}, u32[]{:S(2)}) async-start(f32[8,48,128]{2,1,0:T(8,128)} %broadcast_in_dim.2), calls=%async_computation.1 | async-start | bytes 393216 | tf_op jit(solution)/shard_map/all_to_all | solution.py:353
  56.8 7.3 %collective-permute-start.17 = (f32[256,128]{1,0:T(8,128)S(1)}, f32[256,128]{1,0:T(8,128)S(1)}, u32[]{:S(2)}, u32[]{:S(2)}) collective-permute-start(f32[256,128]{1,0:T(8,128)S(1)} %add.28), channel_id=1, source_target_pairs={{0,2},{2,0},{4,6},{6,4},{8,10},{10,8},{12,14},{14,12},{1,3},{3,1},... | collective-permute-start | bytes 393224 | tf_op jit(solution)/shard_map/ppermute | solution.py:356
  65.0 1.4 %collective-permute-start.19 = (f32[384,128]{1,0:T(8,128)S(1)}, f32[384,128]{1,0:T(8,128)S(1)}, u32[]{:S(2)}, u32[]{:S(2)}) collective-permute-start(f32[384,128]{1,0:T(8,128)S(1)} %bitcast.6), channel_id=1, source_target_pairs={{0,1},{1,0},{2,3},{3,2},{4,5},{5,4},{6,7},{7,6},{8,9},{9,8},{10,11... | collective-permute-start | bytes 589832 | tf_op jit(solution)/shard_map/ppermute | solution.py:350
  65.0 5.9 %collective-permute-start.18 = (f32[256,128]{1,0:T(8,128)S(1)}, f32[256,128]{1,0:T(8,128)S(1)}, u32[]{:S(2)}, u32[]{:S(2)}) collective-permute-start(f32[256,128]{1,0:T(8,128)S(1)} %add.30), channel_id=1, source_target_pairs={{0,4},{2,6},{4,0},{6,2},{8,12},{10,14},{12,8},{14,10},{1,5},{3,7},... | collective-permute-start | bytes 393224 | tf_op jit(solution)/shard_map/ppermute | solution.py:356
  70.9 9.6 %collective-permute-start.20 = (f32[256,128]{1,0:T(8,128)S(1)}, f32[256,128]{1,0:T(8,128)S(1)}, u32[]{:S(2)}, u32[]{:S(2)}) collective-permute-start(f32[256,128]{1,0:T(8,128)S(1)} %add.31), channel_id=1, source_target_pairs={{0,8},{2,10},{4,12},{6,14},{8,0},{10,2},{12,4},{14,6},{1,9},{3,11}... | collective-permute-start | bytes 393224 | tf_op jit(solution)/shard_map/ppermute | solution.py:356
  80.6 1.4 %collective-permute-start.21 = (f32[256,128]{1,0:T(8,128)S(1)}, f32[256,128]{1,0:T(8,128)S(1)}, u32[]{:S(2)}, u32[]{:S(2)}) collective-permute-start(f32[256,128]{1,0:T(8,128)S(1)} %add.32.own), channel_id=1, source_target_pairs={{0,1},{1,0},{2,3},{3,2},{4,5},{5,4},{6,7},{7,6},{8,9},{9,8},{10,11... | collective-permute-start | bytes 393224 | tf_op jit(solution)/shard_map/ppermute | solution.py:350
